TPU v7x, 32 devices: a whole 2x2x4 slice. The times are simulated.
32 devices in a mesh: dp: 8 (over z, y), tensor: 4 (over x, core).
Axes of the slice: x: 2, y: 2, z: 4, core: 2. Of those that a mesh axis runs over, the one named last changes fastest.
Arguments:
- tokens: bfloat16 [16, 1024, 1024], P('dp', 'tensor'), may hold values from -6 to 6
- doc_ids: int32 [16, 1024], P('dp'), may hold values from 0 to 3, as said below
- targets: int32 [16, 1024], P('dp'), may hold values from 0 to 63, as said below
- cotangent: bfloat16 [16, 1024, 1024], P('dp', 'tensor'), may hold values from -6 to 6
- ln1_gain: bfloat16 [1024], replicated, may hold values from 0.5 to 1.5
- ln1_bias: bfloat16 [1024], replicated, may hold values from -1.25 to 1.25
- qkv_weight: bfloat16 [3, 1024, 1024], P(None, None, 'tensor'), may hold values from -0.1875 to 0.1875
- query_bias: bfloat16 [1024], P('tensor'), may hold values from -3 to 3
- value_bias: bfloat16 [1024], P('tensor'), may hold values from -0.125 to 0.125
- output_weight: bfloat16 [1024, 1024], P('tensor'), may hold values from -1.5 to 1.5
- out_bias: bfloat16 [1024], replicated, may hold values from -1.25 to 1.25
- ln2_gain: bfloat16 [1024], replicated, may hold values from 0.5 to 1.5
- ln2_bias: bfloat16 [1024], replicated, may hold values from -1.25 to 1.25
- up_weight: bfloat16 [1024, 4096], P(None, 'tensor'), may hold values from -0.1875 to 0.1875
- up_bias: bfloat16 [4096], P('tensor'), may hold values from -1.25 to 1.25
- down_weight: bfloat16 [4096, 1024], P('tensor'), may hold values from -0.09375 to 0.09375
- down_bias: bfloat16 [1024], replicated, may hold values from -1.25 to 1.25
Outputs:
- activations: bfloat16 [16, 1024, 1024], P('dp', 'tensor')
- loss: float32 [16, 1024], P('dp', 'tensor')
- input_grad: float32 [16, 1024, 1024], P('dp', 'tensor')
- ln1_gain_grad: float32 [1024], replicated
- ln1_bias_grad: float32 [1024], replicated
- qkv_weight_grad: float32 [3, 1024, 1024], P(None, None, 'tensor')
- query_bias_grad: float32 [1024], P('tensor')
- value_bias_grad: float32 [1024], P('tensor')
- out_weight_grad: float32 [1024, 1024], P('tensor')
- out_bias_grad: float32 [1024], replicated
- ln2_gain_grad: float32 [1024], replicated
- ln2_bias_grad: float32 [1024], replicated
- up_weight_grad: float32 [1024, 4096], P(None, 'tensor')
- up_bias_grad: float32 [4096], P('tensor')
- down_weight_grad: float32 [4096, 1024], P('tensor')
- down_bias_grad: float32 [1024], replicated
Inputs may be any that keep to these rules, and one draw needn't show every extreme that they name: `doc_ids`: segment numbers never fall along a sequence and start at 0. Among the 2 sequences of each index of dp exactly one, drawn from the seed, is a single document; each other sequence ends with segment 3. `targets`: each aligned block of 64 positions of a sequence holds every target once.
All inputs are finite; a program needn't handle non-finite values.
Results may differ from a plain program's by a relative error of at most 0.02.
Values may be sent and summed in bfloat16 or wider, within the bound.
No kernel may reach another device: no remote copies, remote signals or barrier semaphores. Data moves between devices by JAX's collectives and lax.ppermute only.
A program may use at most 192 MiB of HBM per device.

v0:
```python
import math

import jax
import jax.numpy as jnp
from jax import lax
from jax.sharding import PartitionSpec as P

HEADS = 8


NORM_EPS = 1e-05
CONTRAST_SCALE = 32.0
CONTRAST_WEIGHT = 64.0
NEGATIVE = -1e30


def positions(places, features):
    paired = (jnp.arange(features, dtype=jnp.int32) // 2).astype(places.dtype)
    angles = places[:, None] * jnp.exp(paired * (-2.0 * math.log(10000.0) / features))[None, :]
    is_odd = jnp.arange(features, dtype=jnp.int32) % 2 == 1
    return jnp.where(is_odd[None, :], jnp.cos(angles), jnp.sin(angles))


def layer_norm(values, gain_vec, shift_vec):
    centered = values - jnp.mean(values, axis=-1, keepdims=True)
    variance = jnp.mean(centered * centered, axis=-1, keepdims=True)
    return centered * lax.rsqrt(variance + NORM_EPS) * gain_vec + shift_vec


def rms_unit(values):
    return values * lax.rsqrt(jnp.mean(values * values, axis=-1, keepdims=True) + NORM_EPS)


def gelu_tanh(values):
    return jax.nn.gelu(values, approximate=True)


def norm_rows(values):
    return lax.all_gather(values, "tensor", axis=1, tiled=True)


def grad_rows(values):
    return lax.all_gather(values, "tensor", axis=1, tiled=True)


def rows_again(values):
    return lax.all_gather(values, "tensor", axis=1, tiled=True)


def soft_parts(scores, allowed):
    masked = jnp.where(allowed, scores, NEGATIVE)
    row_top = jnp.max(masked, axis=-1, keepdims=True)
    exp_terms = jnp.where(allowed, jnp.exp(masked - row_top), 0.0)
    row_total = jnp.sum(exp_terms, axis=-1, keepdims=True)
    return ((row_top + jnp.log(row_total))[:, 0], exp_terms / row_total)


def block_mask(documents, row_start, block_rows):
    columns = jnp.arange(documents.shape[0], dtype=jnp.int32)
    row_ids = row_start + jnp.arange(block_rows, dtype=jnp.int32)
    own_docs = lax.dynamic_slice_in_dim(documents, row_start, block_rows, 0)
    return (own_docs[:, None] == documents[None, :]) & (row_ids[:, None] >= columns[None, :])


def attend_forward(queries, key_rows, value_rows, documents):
    length = queries.shape[0]
    block_rows = min(512, length)
    score_scale = queries.shape[2] ** (-0.5)

    def one_block(block_index):
        row_start = block_index * block_rows
        query_block = lax.dynamic_slice_in_dim(queries, row_start, block_rows, 0)
        allowed = block_mask(documents, row_start, block_rows)[None]
        scores = (
            jnp.einsum("qhd,khd->hqk", query_block, key_rows, preferred_element_type=jnp.float32)
            * score_scale
        )
        masked = jnp.where(allowed, scores, NEGATIVE)
        row_top = jnp.max(masked, axis=-1, keepdims=True)
        exp_terms = jnp.where(allowed, jnp.exp(masked - row_top), 0.0)
        row_total = jnp.sum(exp_terms, axis=-1, keepdims=True)
        weights = (exp_terms / row_total).astype(jnp.bfloat16)
        mixed_block = jnp.einsum(
            "hqk,khd->qhd", weights, value_rows, preferred_element_type=jnp.float32
        )
        return (mixed_block.astype(jnp.bfloat16), (row_top + jnp.log(row_total))[..., 0])

    blocks, log_totals = lax.map(one_block, jnp.arange(length // block_rows, dtype=jnp.int32))
    return (blocks.reshape(length, -1), log_totals)


def attend_backward(queries, key_rows, value_rows, documents, log_totals, grad_out):
    length = queries.shape[0]
    block_rows = min(512, length)
    score_scale = queries.shape[2] ** (-0.5)

    def one_block(running, block_index):
        grad_keys, grad_values = running
        row_start = block_index * block_rows
        query_block = lax.dynamic_slice_in_dim(queries, row_start, block_rows, 0)
        grad_block = lax.dynamic_slice_in_dim(grad_out, row_start, block_rows, 0)
        allowed = block_mask(documents, row_start, block_rows)[None]
        scores = (
            jnp.einsum("qhd,khd->hqk", query_block, key_rows, preferred_element_type=jnp.float32)
            * score_scale
        )
        masked = jnp.where(allowed, scores, NEGATIVE)
        weights = jnp.where(allowed, jnp.exp(masked - log_totals[block_index][..., None]), 0.0)
        grad_weights = jnp.einsum(
            "qhd,khd->hqk", grad_block, value_rows, preferred_element_type=jnp.float32
        )
        centered = jnp.sum(weights * grad_weights, axis=-1, keepdims=True)
        grad_scores = (weights * (grad_weights - centered)).astype(jnp.bfloat16)
        grad_query = (
            jnp.einsum("hqk,khd->qhd", grad_scores, key_rows, preferred_element_type=jnp.float32)
            * score_scale
        )
        grad_keys = (
            grad_keys
            + jnp.einsum(
                "hqk,qhd->khd", grad_scores, query_block, preferred_element_type=jnp.float32
            )
            * score_scale
        )
        grad_values = grad_values + jnp.einsum(
            "hqk,qhd->khd",
            weights.astype(jnp.bfloat16),
            grad_block,
            preferred_element_type=jnp.float32,
        )
        return ((grad_keys, grad_values), grad_query)

    zero_rows = jnp.zeros(key_rows.shape, jnp.float32)
    (grad_keys, grad_values), grad_blocks = lax.scan(
        one_block, (zero_rows, zero_rows), jnp.arange(length // block_rows, dtype=jnp.int32)
    )
    return (grad_blocks.reshape(key_rows.shape), grad_keys, grad_values)


def shards(
    tokens,
    doc_ids,
    targets,
    cotangent,
    ln1_gain,
    ln1_bias,
    qkv_weight,
    query_bias,
    value_bias,
    output_weight,
    out_bias,
    ln2_gain,
    ln2_bias,
    up_weight,
    up_bias,
    down_weight,
    down_bias,
):
    seq_count, part_rows, features = tokens.shape
    length = doc_ids.shape[1]
    first_row = lax.axis_index("tensor") * part_rows
    head_size = features // HEADS
    local_width = qkv_weight.shape[2]
    head_count = local_width // head_size
    gain_one = ln1_gain.astype(jnp.float32)
    shift_one = ln1_bias.astype(jnp.float32)
    gain_two = ln2_gain.astype(jnp.float32)
    shift_two = ln2_bias.astype(jnp.float32)
    output_offset = out_bias.astype(jnp.float32)
    up_shift = up_bias.astype(jnp.float32)
    down_shift = down_bias.astype(jnp.float32)
    places = (first_row + jnp.arange(part_rows, dtype=jnp.int32)).astype(jnp.float32)
    hidden_state = tokens.astype(jnp.float32) + positions(places, features)[None]
    normed_one, pull_one = jax.vjp(layer_norm, hidden_state, gain_one, shift_one)
    low_one = normed_one.astype(jnp.bfloat16)
    rows_one = norm_rows(low_one)
    qkv_shift = jnp.stack(
        [
            query_bias.astype(jnp.float32),
            jnp.zeros((local_width,), jnp.float32),
            value_bias.astype(jnp.float32),
        ]
    )

    def project_qkv(gathered):
        qkv_values = (
            jnp.einsum("snd,cde->csne", gathered, qkv_weight, preferred_element_type=jnp.float32)
            + qkv_shift[:, None, None, :]
        )
        return qkv_values.astype(jnp.bfloat16).reshape(3, seq_count, length, head_count, head_size)

    qkv_low = project_qkv(rows_one)
    attended_rows, log_totals = lax.map(
        lambda packed: attend_forward(*packed), (qkv_low[0], qkv_low[1], qkv_low[2], doc_ids)
    )
    row_portion = attended_rows
    attn_own = jnp.transpose(
        lax.psum_scatter(
            jnp.einsum(
                "rac,cw->arw", row_portion, output_weight, preferred_element_type=jnp.float32
            ).astype(jnp.bfloat16),
            "tensor",
            scatter_dimension=0,
            tiled=True,
        ).astype(jnp.float32),
        (1, 0, 2),
    )
    residual_stream = hidden_state + attn_own + output_offset
    normed_two, pull_two = jax.vjp(layer_norm, residual_stream, gain_two, shift_two)
    low_two = normed_two.astype(jnp.bfloat16)
    rows_two = norm_rows(low_two)

    def feed_up(gathered):
        return (
            jnp.einsum("snd,df->snf", gathered, up_weight, preferred_element_type=jnp.float32)
            + up_shift
        )

    up_value = feed_up(rows_two)
    hidden_act = gelu_tanh(up_value).astype(jnp.bfloat16)
    row_portion = hidden_act
    ffn_own = jnp.transpose(
        lax.psum_scatter(
            jnp.einsum(
                "snf,fd->nsd", row_portion, down_weight, preferred_element_type=jnp.float32
            ).astype(jnp.bfloat16),
            "tensor",
            scatter_dimension=0,
            tiled=True,
        ).astype(jnp.float32),
        (1, 0, 2),
    )
    output = residual_stream + ffn_own + down_shift
    unit_value, pull_unit = jax.vjp(rms_unit, output)
    unit_low = unit_value.astype(jnp.bfloat16)
    key_all = lax.all_gather(unit_low, "tensor", axis=1, tiled=True).reshape(
        seq_count * length, features
    )
    seq_base = jnp.arange(seq_count, dtype=jnp.int32)[:, None] * length
    groups_all = (seq_base + doc_ids).reshape(-1)
    labels_all = targets.reshape(-1)
    own_groups = (seq_base + lax.dynamic_slice_in_dim(doc_ids, first_row, part_rows, 1)).reshape(-1)
    own_labels = lax.dynamic_slice_in_dim(targets, first_row, part_rows, 1).reshape(-1)
    own_units = unit_low.reshape(seq_count * part_rows, features)
    local_rows = seq_count * part_rows
    block_rows = min(512, local_rows)
    factor = CONTRAST_SCALE / features

    def contrast_block(running, block_index):
        scores = (
            jnp.einsum("qd,kd->qk", own_units, key_all, preferred_element_type=jnp.float32) * factor
        )
        memory = own_groups[:, None] != groups_all[None, :]
        positive = memory & (own_labels[:, None] == labels_all[None, :])
        log_all, share_all = soft_parts(scores, memory)
        log_pos, share_pos = soft_parts(scores, positive)
        grad_scores = (CONTRAST_WEIGHT * (share_all - share_pos)).astype(jnp.bfloat16)
        grad_units = (
            jnp.einsum("qk,kd->qd", grad_scores, key_all, preferred_element_type=jnp.float32)
            * factor
        )
        running = (
            running
            + jnp.einsum("qk,qd->kd", grad_scores, own_units, preferred_element_type=jnp.float32)
            * factor
        )
        return (running, (log_all - log_pos, grad_units))

    key_grads, (losses, unit_grads) = lax.scan(
        contrast_block,
        jnp.zeros(key_all.shape, jnp.float32),
        jnp.arange(local_rows // block_rows, dtype=jnp.int32),
    )
    own_key_grads = lax.psum_scatter(
        key_grads.reshape(seq_count, length, features).astype(jnp.bfloat16),
        "tensor",
        scatter_dimension=1,
        tiled=True,
    ).astype(jnp.float32)
    grad_unit = unit_grads.reshape(seq_count, part_rows, features) + own_key_grads
    grad_output = pull_unit(grad_unit)[0] + cotangent.astype(jnp.float32)
    grad_out_rows = grad_rows(grad_output.astype(jnp.bfloat16))
    rows_two = rows_again(low_two)
    up_value = feed_up(rows_two)
    hidden_act = gelu_tanh(up_value).astype(jnp.bfloat16)
    grad_hidden = jnp.einsum(
        "snd,fd->snf", grad_out_rows, down_weight, preferred_element_type=jnp.float32
    )
    grad_up = jax.vjp(gelu_tanh, up_value)[1](grad_hidden)[0].astype(jnp.bfloat16)
    grad_down_w = jnp.einsum(
        "snf,snd->fd", hidden_act, grad_out_rows, preferred_element_type=jnp.float32
    )
    grad_up_w = jnp.einsum("snd,snf->df", rows_two, grad_up, preferred_element_type=jnp.float32)
    grad_up_b = jnp.sum(grad_up, axis=(0, 1), dtype=jnp.float32)
    row_portion = grad_up
    grad_normed_two = jnp.transpose(
        lax.psum_scatter(
            jnp.einsum(
                "snf,df->nsd", row_portion, up_weight, preferred_element_type=jnp.float32
            ).astype(jnp.bfloat16),
            "tensor",
            scatter_dimension=0,
            tiled=True,
        ).astype(jnp.float32),
        (1, 0, 2),
    )
    grad_middle, grad_gain_two, grad_shift_two = pull_two(grad_normed_two)
    grad_residual = grad_output + grad_middle
    residual_grad_rows = grad_rows(grad_residual.astype(jnp.bfloat16))
    grad_attended = jnp.einsum(
        "qhw,jw->qhj", residual_grad_rows, output_weight, preferred_element_type=jnp.float32
    ).astype(jnp.bfloat16)
    grad_out_w = jnp.einsum(
        "yak,yac->kc", attended_rows, residual_grad_rows, preferred_element_type=jnp.float32
    )
    rows_one = rows_again(low_one)
    qkv_low = project_qkv(rows_one)
    grad_heads = grad_attended.reshape(seq_count, length, head_count, head_size)
    grad_query, grad_keys, grad_values = lax.map(
        lambda packed: attend_backward(*packed),
        (qkv_low[0], qkv_low[1], qkv_low[2], doc_ids, log_totals, grad_heads),
    )
    grad_qkv = (
        jnp.stack([grad_query, grad_keys, grad_values])
        .reshape(3, seq_count, length, local_width)
        .astype(jnp.bfloat16)
    )
    grad_qkv_w = jnp.einsum("snd,csne->cde", rows_one, grad_qkv, preferred_element_type=jnp.float32)
    grad_query_b = jnp.sum(grad_qkv[0], axis=(0, 1), dtype=jnp.float32)
    grad_value_b = jnp.sum(grad_qkv[2], axis=(0, 1), dtype=jnp.float32)
    row_portion = grad_qkv
    grad_normed_one = jnp.transpose(
        lax.psum_scatter(
            jnp.einsum(
                "csne,cde->nsd", row_portion, qkv_weight, preferred_element_type=jnp.float32
            ).astype(jnp.bfloat16),
            "tensor",
            scatter_dimension=0,
            tiled=True,
        ).astype(jnp.float32),
        (1, 0, 2),
    )
    grad_hidden_in, grad_gain_one, grad_shift_one = pull_one(grad_normed_one)
    input_grad = grad_residual + grad_hidden_in
    small_sums = lax.psum(
        jnp.stack(
            [
                grad_gain_one,
                grad_shift_one,
                jnp.sum(grad_residual, axis=(0, 1)),
                grad_gain_two,
                grad_shift_two,
                jnp.sum(grad_output, axis=(0, 1)),
            ]
        ),
        ("dp", "tensor"),
    )
    grad_qkv_w, grad_query_b, grad_value_b, grad_out_w, grad_up_w, grad_up_b, grad_down_w = (
        lax.psum(grad_qkv_w.astype(jnp.bfloat16), "dp").astype(jnp.float32),
        lax.psum(grad_query_b.astype(jnp.bfloat16), "dp").astype(jnp.float32),
        lax.psum(grad_value_b.astype(jnp.bfloat16), "dp").astype(jnp.float32),
        lax.psum(grad_out_w.astype(jnp.bfloat16), "dp").astype(jnp.float32),
        lax.psum(grad_up_w.astype(jnp.bfloat16), "dp").astype(jnp.float32),
        lax.psum(grad_up_b.astype(jnp.bfloat16), "dp").astype(jnp.float32),
        lax.psum(grad_down_w.astype(jnp.bfloat16), "dp").astype(jnp.float32),
    )
    return (
        output.astype(jnp.bfloat16),
        losses.reshape(seq_count, part_rows),
        input_grad,
        small_sums[0],
        small_sums[1],
        grad_qkv_w,
        grad_query_b,
        grad_value_b,
        grad_out_w,
        small_sums[2],
        small_sums[3],
        small_sums[4],
        grad_up_w,
        grad_up_b,
        grad_down_w,
        small_sums[5],
    )


def solution(mesh):
    in_specs = (
        P("dp", "tensor", None),
        P("dp", None),
        P("dp", None),
        P("dp", "tensor", None),
        P(),
        P(),
        P(None, None, "tensor"),
        P("tensor"),
        P("tensor"),
        P("tensor", None),
        P(),
        P(),
        P(),
        P(None, "tensor"),
        P("tensor"),
        P("tensor", None),
        P(),
    )
    out_specs = (
        P("dp", "tensor", None),
        P("dp", "tensor"),
        P("dp", "tensor", None),
        P(),
        P(),
        P(None, None, "tensor"),
        P("tensor"),
        P("tensor"),
        P("tensor", None),
        P(),
        P(),
        P(),
        P(None, "tensor"),
        P("tensor"),
        P("tensor", None),
        P(),
    )
    return jax.shard_map(shards, mesh=mesh, in_specs=in_specs, out_specs=out_specs, check_vma=False)
```

profile of v0, /device:TPU:0, one launch (start us, length us, event | category | flops | bytes accessed | tf_op | source)
XLA Modules:
  0.0 914.0 jit_solution(8420058338397921991)
XLA Ops:
  8.9 3.7 fusion.84
  19.4 36.9 %all-gather.6.cloned.1.call-done = bf16[2,1024,1024]{2,1,0:T(8,128)(2,1)} async-done(((bf16[2,256,1024]{2,1,0:T(8,128)(2,1)}), bf16[2,1024,1024]{2,1,0:T(8,128)(2,1)}) %all-gather.6.cloned.1.call-update) | async-done | bytes 4194320 | tf_op jit(solution)/shard_map/all_gather | solution.py:39
  56.3 6.1 fusion.47
  64.1 2.3 copy.40
  70.0 40.6 %while.60 = (s32[]{:T(128)}, bf16[2,1024,256]{2,1,0:T(8,128)(2,1)}, f32[2,2,2,512]{3,2,1,0:T(2,128)S(1)}, bf16[2,1024,2,128]{3,1,2,0:T(8,128)(2,1)}, s32[2,1024]...) while((s32[]{:T(128)}, bf16[2,1024,256]{2,1,0:T(8,128)(2,1)}, ...), condition=%wide.region_7.8_spmd, body=%wide.region_2.7_spmd.sunk | while | flops 553254400 | bytes 28383784 | solution.py:193
  73.2 14.9 %while.63 = (s32[]{:T(128)}, bf16[2,512,2,128]{3,2,1,0:T(2,128)(2,1)}, f32[2,2,512]{2,1,0:T(2,128)S(1)}, s32[2]{0:T(128)S(1)}, s32[1024]{0:T(1024)S(1)}, /*index...) while((s32[]{:T(128)}, ...), condition=%wide.region_6.6_spmd, body=%wide.region_3.5_spmd.sunk | while | flops 553254400 | bytes 23116064 | solution.py:88
  93.5 14.9 %while.63 = (s32[]{:T(128)}, bf16[2,512,2,128]{3,2,1,0:T(2,128)(2,1)}, f32[2,2,512]{2,1,0:T(2,128)S(1)}, s32[2]{0:T(128)S(1)}, s32[1024]{0:T(1024)S(1)}, /*index...) while((s32[]{:T(128)}, ...), condition=%wide.region_6.6_spmd, body=%wide.region_3.5_spmd.sunk | while | flops 553254400 | bytes 23116064 | solution.py:88
  110.6 4.7 convert_bitcast_fusion.2
  115.5 44.5 %reduce-scatter.6.cloned.1.call-done = bf16[256,2,1024]{2,0,1:T(8,128)(2,1)} async-done(((bf16[1024,2,1024]{2,0,1:T(8,128)(2,1)}), bf16[256,2,1024]{2,0,1:T(8,128)(2,1)}) %reduce-scatter.6.cloned.1.call-update) | async-done | bytes 1048592 | tf_op jit(solution)/shard_map/reduce_scatter | solution.py:198
  165.1 34.4 %all-gather.8.cloned.1.call-done = bf16[2,1024,1024]{2,1,0:T(8,128)(2,1)} async-done(((bf16[2,256,1024]{2,1,0:T(8,128)(2,1)}), bf16[2,1024,1024]{2,1,0:T(8,128)(2,1)}) %all-gather.8.cloned.1.call-update) | async-done | bytes 4194320 | tf_op jit(solution)/shard_map/all_gather | solution.py:39
  199.4 6.9 fusion.67
  206.3 3.3 copy-done.70
  209.6 7.0 convert_bitcast_fusion.1
  217.3 44.0 %reduce-scatter.8.cloned.1.call-done = bf16[256,2,1024]{2,0,1:T(8,128)(2,1)} async-done(((bf16[1024,2,1024]{2,0,1:T(8,128)(2,1)}), bf16[256,2,1024]{2,0,1:T(8,128)(2,1)}) %reduce-scatter.8.cloned.1.call-update) | async-done | bytes 1048592 | tf_op jit(solution)/shard_map/reduce_scatter | solution.py:223
  266.3 34.4 %all-gather.10.cloned.1.call-done = bf16[2,1024,1024]{2,1,0:T(8,128)(2,1)} async-done(((bf16[2,256,1024]{2,1,0:T(8,128)(2,1)}), bf16[2,1024,1024]{2,1,0:T(8,128)(2,1)}) %all-gather.10.cloned.1.call-update) | async-done | bytes 4194320 | tf_op jit(solution)/shard_map/all_gather | solution.py:236
  300.7 5.8 fusion.46
  306.5 3.3 fusion.56
  309.8 3.6 multiply_convert_fusion.3
  313.5 4.4 multiply_convert_fusion.1
  318.0 6.6 convolution_multiply_fusion.2
  324.6 38.0 %reduce-scatter.10.cloned.1.call-done = bf16[2,256,1024]{2,1,0:T(8,128)(2,1)} async-done(((bf16[2,1024,1024]{2,1,0:T(8,128)(2,1)}), bf16[2,256,1024]{2,1,0:T(8,128)(2,1)}) %reduce-scatter.10.cloned.1.call-update) | async-done | bytes 1048592 | tf_op jit(solution)/shard_map/reduce_scatter | solution.py:274
  362.6 3.0 multiply_reduce_fusion.1
  366.7 2.4 fusion.102
  372.0 34.2 %all-gather.12.cloned.1.call-done = bf16[2,1024,1024]{2,1,0:T(8,128)(2,1)} async-done(((bf16[2,256,1024]{2,1,0:T(8,128)(2,1)}), bf16[2,1024,1024]{2,1,0:T(8,128)(2,1)}) %all-gather.12.cloned.1.call-update) | async-done | bytes 4194320 | tf_op jit(solution)/shard_map/all_gather | solution.py:43
  406.2 13.3 %fusion.110 = (bf16[1024]{0:T(1024)(128)(2,1)}, bf16[2,1024,1024]{2,1,0:T(8,128)(2,1)S(1)}) fusion(f32[2,1024,1024]{2,1,0:T(8,128)} %copy-done.70, f32[1024]{0:T(1024)S(1)} %convert_element_type.195, bf16[2,1024,1024]{2,1,0:T(8,128)(2,1)} %all-gather.12.cloned.1.call-done, bf16[1024,1024]{1,0:T(8,128)(2,1)S(1)} %copy-done), kind=kOutput, calls=%fused_computation.196 | convolution fusion | flops 4341103616 | bytes 18880512 | tf_op jit(solution)/shard_map/snd,fd->snf/dot_general | solution.py:286
  421.5 6.2 convert_bitcast_fusion
  427.8 44.6 %reduce-scatter.12.cloned.1.call-done = bf16[256,2,1024]{2,0,1:T(8,128)(2,1)} async-done(((bf16[1024,2,1024]{2,0,1:T(8,128)(2,1)}), bf16[256,2,1024]{2,0,1:T(8,128)(2,1)}) %reduce-scatter.12.cloned.1.call-update) | async-done | bytes 1048592 | tf_op jit(solution)/shard_map/reduce_scatter | solution.py:297
  474.3 3.0 fusion.60
  481.4 9.5 %bitcast_convert_fusion.2 = bf16[1024,1024]{1,0:T(8,128)(2,1)} fusion(bf16[2,1024,1024]{2,1,0:T(8,128)(2,1)} %all-gather.8.cloned.1.call-done, bf16[2,1024,1024]{2,1,0:T(8,128)(2,1)} %copy-done.69), kind=kOutput, calls=%fused_computation.78 | convolution fusion | flops 4296015872 | bytes 10485760 | tf_op jit(solution)/shard_map/snd,snf->df/dot_general | solution.py:293
  490.9 11.0 %bitcast_convert_fusion.1 = bf16[1024,1024]{1,0:T(8,128)(2,1)} fusion(bf16[2,1024,1024]{2,1,0:T(8,128)(2,1)S(1)} %copy-done.65, f32[2,1024,1024]{2,1,0:T(8,128)} %copy-done.70, f32[1024]{0:T(1024)S(1)} %convert_element_type.195), kind=kOutput, calls=%fused_computation.77 | convolution fusion | flops 4316987392 | bytes 14684160 | tf_op jit(solution)/shard_map/snf,snd->fd/dot_general | solution.py:290
  501.8 13.9 %all-gather.14.cloned.1.call-done = bf16[2,1024,1024]{2,1,0:T(8,128)(2,1)} async-done(((bf16[2,256,1024]{2,1,0:T(8,128)(2,1)}), bf16[2,1024,1024]{2,1,0:T(8,128)(2,1)}) %all-gather.14.cloned.1.call-update) | async-done | bytes 4194320 | tf_op jit(solution)/shard_map/all_gather | solution.py:43
  515.8 4.4 convolution_convert_fusion
  520.2 59.9 %while.62 = (s32[]{:T(128)}, bf16[2,1024,2,128]{3,2,1,0:T(2,128)(2,1)}, bf16[2,1024,2,128]{1,3,2,0:T(8,128)(2,1)}, bf16[2,1024,2,128]{1,3,2,0:T(8,128)(2,1)}, bf...) while((s32[]{:T(128)}, ...), condition=%wide.region_26.27_spmd, body=%wide.region_22.26_spmd.sunk | while | flops 1355808256 | bytes 59042532 | solution.py:319
  526.7 20.3 %while.64 = (s32[]{:T(128)}, f32[1024,2,128]{0,2,1:T(8,128)S(1)}, f32[1024,2,128]{0,2,1:T(8,128)S(1)}, bf16[2,512,2,128]{3,2,1,0:T(2,128)(2,1)}, s32[2]{0:T(128)...) while((s32[]{:T(128)}, f32[1024,2,128]{0,2,1:T(8,128)S(1)}, ...), condition=%wide.region_25.25_spmd.clone, body=%wide.region_23.24_spmd.clone.sunk | while | flops 1355808256 | bytes 48531856 | solution.py:134
  556.5 20.3 %while.64 = (s32[]{:T(128)}, f32[1024,2,128]{0,2,1:T(8,128)S(1)}, f32[1024,2,128]{0,2,1:T(8,128)S(1)}, bf16[2,512,2,128]{3,2,1,0:T(2,128)(2,1)}, s32[2]{0:T(128)...) while((s32[]{:T(128)}, f32[1024,2,128]{0,2,1:T(8,128)S(1)}, ...), condition=%wide.region_25.25_spmd.clone, body=%wide.region_23.24_spmd.clone.sunk | while | flops 1355808256 | bytes 48531856 | solution.py:134
  581.7 2.5 stack.53
  585.6 4.4 fusion.82
  590.0 6.8 fusion.79
  598.0 7.1 fusion.40
  609.0 22.6 %all-reduce = (bf16[256]{0:T(256)(128)(2,1)S(1)}, bf16[256]{0:T(256)(128)(2,1)S(1)}, bf16[1024]{0:T(1024)(128)(2,1)S(1)}) all-reduce(bf16[256]{0:T(256)(128)(2,1)S(1)} %bitcast.316, bf16[256]{0:T(256)(128)(2,1)S(1)} %bitcast.315, bf16[1024]{0:T(1024)(128)(2,1)S(1)} %copy-done.64), channel_id=1, replica_groups=mesh['dp'=8,'tensor'=4] {'dp'}, use_global_device_ids=true, to_apply=%region_39.40 | all-reduce | flops 1536 | bytes 6144 | tf_op jit(solution)/shard_map/psum | solution.py:360
  633.3 178.3 %all-reduce.4.cloned.1.call-done = (bf16[3,1024,256]{1,2,0:T(8,128)(2,1)}, bf16[256,1024]{1,0:T(8,128)(2,1)}, bf16[1024,1024]{1,0:T(8,128)(2,1)}, bf16[1024,1024]{1,0:T(8,128)(2,1)}) async-done(((bf16[3,1024,256]{1,2,0:T(8,128)(2,1)}, bf16[256,1024]{1,0:T(8,128)(2,1)}, bf16[1024,1024]{1,0:T(8,128)(2,1)}, bf16[1024,1024]{1,0:T(8,128)(2,1)}), (bf16[3,1024,256]{1,2,0:T(8,128)(2,1)}, ...) | async-done | bytes 6291472 | tf_op jit(solution)/shard_map/psum | solution.py:359
  813.9 3.1 copy.53
  817.0 2.6 convert_element_type.225
  819.6 2.9 convert_element_type.228
  822.5 35.2 %reduce-scatter.14.cloned.1.call-done = bf16[256,2,1024]{2,0,1:T(8,128)(2,1)} async-done(((bf16[1024,2,1024]{2,0,1:T(8,128)(2,1)}), bf16[256,2,1024]{2,0,1:T(8,128)(2,1)}) %reduce-scatter.14.cloned.1.call-update) | async-done | bytes 1048592 | tf_op jit(solution)/shard_map/reduce_scatter | solution.py:333
  859.8 2.5 fusion.61
  862.6 39.5 %psum.56 = f32[6,1024]{1,0:T(8,128)S(1)} all-reduce(f32[6,1024]{1,0:T(8,128)S(1)} %stack.63), channel_id=1, replica_groups=mesh['dp'=8,'tensor'=4] {'dp','tensor'}, use_global_device_ids=true, to_apply=%region_36.37 | all-reduce | flops 6144 | bytes 49152 | tf_op jit(solution)/shard_map/psum | solution.py:345
  902.7 4.3 add_add_fusion.3
  (398 shorter events, 139.0 us)
Async XLA Ops:
  7.2 202.4 %copy-start = (bf16[1024,1024]{1,0:T(8,128)(2,1)S(1)}, bf16[1024,1024]{1,0:T(8,128)(2,1)}, u32[]{:S(2)}) copy-start(bf16[1024,1024]{1,0:T(8,128)(2,1)} %param.40) | copy-start | bytes 6291460
  7.2 10.3 %copy-start.8 = (bf16[2,256,1024]{2,1,0:T(8,128)(2,1)S(1)}, bf16[2,256,1024]{2,1,0:T(8,128)(2,1)}, u32[]{:S(2)}) copy-start(bf16[2,256,1024]{2,1,0:T(8,128)(2,1)} %param.25) | copy-start | bytes 3145732
  7.2 49.1 %all-gather.6.cloned.1.call-start = ((), (), s32[]{:S(2)}) async-start(), calls=%async_computation.5 | async-start | bytes 5242880 | tf_op jit(solution)/shard_map/all_gather | solution.py:39
  8.2 8.7 copy-start.39
  12.6 6.6 copy-start.67
  12.6 6.6 copy-start.68
  19.0 141.0 %reduce-scatter.6.cloned.1.call-start = ((), (), s32[]{:S(2)}) async-start(), calls=%async_computation.6 | async-start | bytes 5242880 | tf_op jit(solution)/shard_map/reduce_scatter | solution.py:198
  64.1 5.9 copy-start.38
  110.6 4.8 copy-start.59
  110.6 4.8 copy-start.60
  110.6 4.8 copy-start.61
  110.6 49.4 %copy-start.6 = (f32[256,1024]{1,0:T(8,128)S(1)}, f32[256,1024]{1,0:T(8,128)}, u32[]{:S(2)}) copy-start(f32[256,1024]{1,0:T(8,128)} %copy-done.5) | copy-start | bytes 3145732
  115.3 84.1 %all-gather.8.cloned.1.call-start = ((), (), s32[]{:S(2)}) async-start(), calls=%async_computation.7 | async-start | bytes 5242880 | tf_op jit(solution)/shard_map/all_gather | solution.py:39
  164.8 96.5 %reduce-scatter.8.cloned.1.call-start = ((), (), s32[]{:S(2)}) async-start(), calls=%async_computation.8 | async-start | bytes 5242880 | tf_op jit(solution)/shard_map/reduce_scatter | solution.py:223
  216.6 84.1 %all-gather.10.cloned.1.call-start = ((), (), s32[]{:S(2)}) async-start(), calls=%async_computation.9 | async-start | bytes 5242880 | tf_op jit(solution)/shard_map/all_gather | solution.py:236
  217.3 48.8 %copy-start.58 = (s32[2,1024]{1,0:T(2,128)S(1)}, s32[2,1024]{1,0:T(2,128)}, u32[]{:S(2)}) copy-start(s32[2,1024]{1,0:T(2,128)} %param.27) | copy-start | bytes 24580
  266.1 96.6 %reduce-scatter.10.cloned.1.call-start = ((), (), s32[]{:S(2)}) async-start(), calls=%async_computation.10 | async-start | bytes 5242880 | tf_op jit(solution)/shard_map/reduce_scatter | solution.py:274
  306.5 7.0 copy-start.45
  306.5 7.0 copy-start.47
  309.8 8.1 copy-start.49
  309.8 8.1 copy-start.51
  313.5 4.4 copy-start.32
  318.0 88.2 %all-gather.12.cloned.1.call-start = ((), (), s32[]{:S(2)}) async-start(), calls=%async_computation.11 | async-start | bytes 5242880 | tf_op jit(solution)/shard_map/all_gather | solution.py:43
  318.0 47.6 %copy-start.36 = (bf16[2,256,1024]{2,1,0:T(8,128)(2,1)S(1)}, bf16[2,256,1024]{2,1,0:T(8,128)(2,1)}, u32[]{:S(2)}) copy-start(bf16[2,256,1024]{2,1,0:T(8,128)(2,1)} %param.28) | copy-start | bytes 3145732
  371.5 100.9 %reduce-scatter.12.cloned.1.call-start = ((), (), s32[]{:S(2)}) async-start(), calls=%async_computation.12 | async-start | bytes 5242880 | tf_op jit(solution)/shard_map/reduce_scatter | solution.py:297
  406.2 15.3 %copy-start.66 = (bf16[1024,1024]{1,0:T(8,128)(2,1)S(1)}, bf16[1024,1024]{1,0:T(8,128)(2,1)}, u32[]{:S(2)}) copy-start(bf16[1024,1024]{1,0:T(8,128)(2,1)} %param.38) | copy-start | bytes 6291460
  427.8 44.7 %copy-start.4 = (f32[2,256,1024]{2,1,0:T(8,128)S(1)}, f32[2,256,1024]{2,1,0:T(8,128)}, u32[]{:S(2)}) copy-start(f32[2,256,1024]{2,1,0:T(8,128)} %copy-done.3) | copy-start | bytes 6291460
  427.8 88.0 %all-gather.14.cloned.1.call-start = ((), (), s32[]{:S(2)}) async-start(), calls=%async_computation.13 | async-start | bytes 5242880 | tf_op jit(solution)/shard_map/all_gather | solution.py:43
  472.4 4.8 copy-start.14
  472.4 4.8 copy-start.15
  481.1 330.5 %all-reduce.4.cloned.1.call-start = ((), (), s32[]{:S(2)}) async-start(), calls=%async_computation.15 | async-start | bytes 12582912 | tf_op jit(solution)/shard_map/psum | solution.py:359
  481.4 9.5 %copy-start.65 = (bf16[2,1024,1024]{2,1,0:T(8,128)(2,1)S(1)}, bf16[2,1024,1024]{2,1,0:T(8,128)(2,1)}, u32[]{:S(2)}) copy-start(bf16[2,1024,1024]{2,1,0:T(8,128)(2,1)} %all-gather.12.cloned.1.call-done) | copy-start | bytes 12582916
  490.9 24.9 %copy-start.37 = (bf16[256,1024]{1,0:T(8,128)(2,1)S(1)}, bf16[256,1024]{1,0:T(8,128)(2,1)}, u32[]{:S(2)}) copy-start(bf16[256,1024]{1,0:T(8,128)(2,1)} %param.34) | copy-start | bytes 1572868
  580.1 5.5 copy-start.24
  585.6 4.4 copy-start.35
  596.8 261.0 %reduce-scatter.14.cloned.1.call-start = ((), (), s32[]{:S(2)}) async-start(), calls=%async_computation.14 | async-start | bytes 5242880 | tf_op jit(solution)/shard_map/reduce_scatter | solution.py:333
  811.6 5.3 copy-start.31
  819.6 38.2 %copy-start.7 = (f32[256,1024]{1,0:T(8,128)S(1)}, f32[256,1024]{1,0:T(8,128)}, u32[]{:S(2)}) copy-start(f32[256,1024]{1,0:T(8,128)} %copy-done.5) | copy-start | bytes 3145732
  819.6 38.2 %copy-start.9 = (bf16[2,256,1024]{2,1,0:T(8,128)(2,1)S(1)}, bf16[2,256,1024]{2,1,0:T(8,128)(2,1)}, u32[]{:S(2)}) copy-start(bf16[2,256,1024]{2,1,0:T(8,128)(2,1)} %param.25) | copy-start | bytes 3145732
  819.6 38.2 %copy-start.40 = (f32[1024]{0:T(1024)S(1)}, f32[1024]{0:T(1024)}, u32[]{:S(2)}) copy-start(f32[1024]{0:T(1024)} %copy-done.39) | copy-start | bytes 12292
  819.6 38.2 %copy-start.42 = (f32[2,256]{1,0:T(2,128)S(1)}, f32[2,256]{1,0:T(2,128)}, u32[]{:S(2)}) copy-start(f32[2,256]{1,0:T(2,128)} %copy-done.41) | copy-start | bytes 6148
  819.6 40.2 %copy-start.54 = (f32[2,256]{1,0:T(2,128)S(1)}, f32[2,256]{1,0:T(2,128)}, u32[]{:S(2)}) copy-start(f32[2,256]{1,0:T(2,128)} %copy-done.53) | copy-start | bytes 6148
  819.6 40.2 %copy-start.44 = (f32[2,256]{1,0:T(2,128)S(1)}, f32[2,256]{1,0:T(2,128)}, u32[]{:S(2)}) copy-start(f32[2,256]{1,0:T(2,128)} %copy-done.43) | copy-start | bytes 6148
  822.5 40.0 %copy-start.55 = (f32[1024]{0:T(1024)S(1)}, f32[1024]{0:T(1024)}, u32[]{:S(2)}) copy-start(f32[1024]{0:T(1024)} %get-tuple-element.403) | copy-start | bytes 12292
  822.5 40.0 %copy-start.56 = (f32[1024]{0:T(1024)S(1)}, f32[1024]{0:T(1024)}, u32[]{:S(2)}) copy-start(f32[1024]{0:T(1024)} %get-tuple-element.401) | copy-start | bytes 12292
  822.5 40.0 %copy-start.57 = (f32[1024]{0:T(1024)S(1)}, f32[1024]{0:T(1024)}, u32[]{:S(2)}) copy-start(f32[1024]{0:T(1024)} %get-tuple-element.318) | copy-start | bytes 12292
  857.8 4.5 copy-start.17
  862.3 44.7 %copy-start.1 = (bf16[1024,1024]{1,0:T(8,128)(2,1)S(1)}, bf16[1024,1024]{1,0:T(8,128)(2,1)}, u32[]{:S(2)}) copy-start(bf16[1024,1024]{1,0:T(8,128)(2,1)} %param.40) | copy-start | bytes 6291460
  (55 other events, 100.0 us)
Sparse Core Ops, SparseCore 0:
  19.1 37.1 all-gather.5
  115.5 44.4 reduce-scatter.5
  164.9 34.4 all-gather.7
  216.7 44.5 reduce-scatter.7
  266.2 34.4 all-gather.9
  318.1 44.4 reduce-scatter.9
  371.7 34.4 all-gather.11
  427.9 44.4 reduce-scatter.11
  481.2 34.4 all-gather.13
  596.9 214.6 all-reduce.3
  814.3 43.4 reduce-scatter.13
where the time goes:
time: 920 us; the launch traced here: 914 us
  waiting for transfers between devices  539 us (59%)
  matrix products  136 us (15%)
  local copies, waits for them, and re-layouts  76.1 us (8%)
  other arithmetic  72.1 us (8%)
  blocking collectives  62.1 us (7%)
  between operations  15 us (2%)
  loops' own time  12.7 us (1%)
    psum x1, waiting for transfers between devices, shards(): lax.psum(grad_qkv_w.astype(jnp.bfloat16), 'dp').astype(jnp.float32)  178 us
    all_gather x2, waiting for transfers between devices, norm_rows(): return lax.all_gather(values, 'tensor', axis=1, tiled=True)  71.3 us
    all_gather x2, waiting for transfers between devices, grad_rows(): return lax.all_gather(values, 'tensor', axis=1, tiled=True)  48.1 us
    reduce_scatter x1, waiting for transfers between devices, shards(): lax.psum_scatter(jnp.einsum('snf,df->nsd', row_portion, up_weight, prefer...  44.6 us
    reduce_scatter x1, waiting for transfers between devices, shards(): lax.psum_scatter(jnp.einsum('rac,cw->arw', row_portion, output_weight, pr...  44.5 us
    reduce_scatter x1, waiting for transfers between devices, shards(): lax.psum_scatter(jnp.einsum('snf,fd->nsd', row_portion, down_weight, pref...  44 us
    psum x1, blocking collectives, shards(): lax.psum(jnp.stack([grad_gain_one, grad_shift_one, jnp.sum(grad_residual,...  39.5 us
    reduce_scatter x1, waiting for transfers between devices, shards(): lax.psum_scatter(key_grads.reshape(seq_count, length, features).astype(jn...  38 us
  transfers between devices with their start and end apart: 11, of which 11 were waited for; matrix products, arithmetic and copies ran while one was open for 6% of the time, Pallas kernels for 0%

commit v1 on v0

v1 whole, which is shorter than its diff:
```python
import functools
import math

import jax
import jax.numpy as jnp
from jax import lax
from jax.experimental import pallas as pl
from jax.experimental.pallas import tpu as pltpu
from jax.sharding import PartitionSpec as P

HEADS = 8
NORM_EPS = 1e-05
CONTRAST_SCALE = 32.0
CONTRAST_WEIGHT = 64.0
NEGATIVE = -1e30
LOG2E = math.log2(math.e)
F32 = jnp.float32
BF16 = jnp.bfloat16
MIB = 1 << 20
NN = (((1,), (0,)), ((), ()))
NT = (((1,), (1,)), ((), ()))
TN = (((0,), (0,)), ((), ()))
VMEM = pltpu.VMEM


def dot(a, b, dims=NN):
    return lax.dot_general(a, b, dims, preferred_element_type=F32)


def whole(shape):
    return pl.BlockSpec(shape, lambda *_: (0,) * len(shape))


def kernel_call(body, outs, out_specs, in_specs, grid=(1,), scratch=(), flops=0, nbytes=0, trans=0,
                limit=40, aliases=None, prefetch=0):
    return pl.pallas_call(
        body,
        out_shape=outs,
        grid_spec=pltpu.PrefetchScalarGridSpec(
            num_scalar_prefetch=prefetch,
            grid=grid,
            in_specs=in_specs,
            out_specs=out_specs,
            scratch_shapes=scratch,
        ),
        input_output_aliases=aliases or {},
        cost_estimate=pl.CostEstimate(flops=int(flops), bytes_accessed=int(nbytes), transcendentals=int(trans)),
        compiler_params=pltpu.CompilerParams(vmem_limit_bytes=limit * MIB),
    )


def struct(shape, dtype):
    return jax.ShapeDtypeStruct(shape, dtype)


def into(shape, dtype, block, index, previous):
    out = struct(shape, dtype)
    spec = pl.BlockSpec(block, lambda *_: index)
    return out, spec, ([] if previous is None else [previous])


def norm_stats(v):
    centered = v - jnp.mean(v, axis=-1, keepdims=True)
    rstd = lax.rsqrt(jnp.mean(centered * centered, axis=-1, keepdims=True) + NORM_EPS)
    return centered * rstd, rstd


def first_norm(seq, tokens, tables, gain, shift):
    rows, feats = tokens.shape[1:]
    fine = tables[2].shape[0]

    def body(tok, pa, qa, cb, sb, g, b, h_out, a_out):
        for c in range(rows // fine):
            at = pl.ds(c * fine, fine)
            pos = pa[c : c + 1, :] * cb[...] + qa[c : c + 1, :] * sb[...]
            h = tok[0, at, :].astype(F32) + pos
            h_out[at, :] = h
            z, _ = norm_stats(h)
            a_out[at, :] = (z * g[...] + b[...]).astype(BF16)

    return kernel_call(
        body,
        (struct((rows, feats), F32), struct((rows, feats), BF16)),
        (whole((rows, feats)), whole((rows, feats))),
        [pl.BlockSpec((1, rows, feats), lambda *_: (seq, 0, 0))]
        + [whole(t.shape) for t in tables]
        + [whole((1, feats))] * 2,
        nbytes=rows * feats * 8,
        flops=rows * feats * 20,
        limit=16,
    )(tokens, *tables, gain, shift)


def second_norm(h, keep, core, cross, offset, gain, shift):
    rows, feats = h.shape
    step = 64

    def body(h_ref, k_ref, c_ref, x_ref, o_ref, g, b, r_out, n_out):
        for c in range(rows // step):
            at = pl.ds(c * step, step)
            r = (
                h_ref[at, :]
                + (k_ref[0, at, :].astype(F32) + c_ref[0, at, :].astype(F32) + x_ref[at, :].astype(F32))
                + o_ref[...]
            )
            r_out[at, :] = r
            z, _ = norm_stats(r)
            n_out[at, :] = (z * g[...] + b[...]).astype(BF16)

    block = pl.BlockSpec((1, rows, feats), lambda *_: (0, 0, 0))
    return kernel_call(
        body,
        (struct((rows, feats), F32), struct((rows, feats), BF16)),
        (whole((rows, feats)), whole((rows, feats))),
        [whole((rows, feats)), block, block, whole((rows, feats))] + [whole((1, feats))] * 3,
        nbytes=rows * feats * 16,
        flops=rows * feats * 20,
        limit=16,
    )(h, keep, core, cross, offset, gain, shift)


def output_rows(seq, seqs, r1, keep, core, cross, offset, previous):
    rows, feats = r1.shape
    step = 64

    def body(r_ref, k_ref, c_ref, x_ref, o_ref, *rest):
        act_out, n_out, q_out = rest[-3:]
        for c in range(rows // step):
            at = pl.ds(c * step, step)
            y = (
                r_ref[at, :]
                + (k_ref[0, at, :].astype(F32) + c_ref[0, at, :].astype(F32) + x_ref[at, :].astype(F32))
                + o_ref[...]
            )
            act_out[0, at, :] = y.astype(BF16)
            q = lax.rsqrt(jnp.mean(y * y, axis=-1, keepdims=True) + NORM_EPS)
            n_out[at, :] = (y * q).astype(BF16)
            q_out[at, :] = jnp.broadcast_to(q, (step, 128))

    block = pl.BlockSpec((1, rows, feats), lambda *_: (0, 0, 0))
    act, act_spec, extra = into((seqs, rows, feats), BF16, (1, rows, feats), (seq, 0, 0), previous)
    return kernel_call(
        body,
        (act, struct((rows, feats), BF16), struct((rows, 128), F32)),
        (act_spec, whole((rows, feats)), whole((rows, 128))),
        [whole((rows, feats)), block, block, whole((rows, feats)), whole((1, feats))]
        + [pl.BlockSpec(memory_space=pl.ANY)] * len(extra),
        nbytes=rows * feats * 14,
        flops=rows * feats * 12,
        limit=16,
        aliases={5: 0} if extra else None,
    )(r1, keep, core, cross, offset, *extra)


def norm_backward(seq, seqs, v, keep, core, cross, gain, base, final, previous):
    rows, feats = v.shape
    step = 64

    def body(v_ref, k_ref, c_ref, x_ref, g, base_ref, *rest):
        if final:
            out, sums = rest[-2:]
        else:
            out, low, sums = rest[-3:]
        acc = [jnp.zeros((8, feats), F32) for _ in range(4)]
        for c in range(rows // step):
            at = pl.ds(c * step, step)
            got = k_ref[0, at, :].astype(F32) + c_ref[0, at, :].astype(F32) + x_ref[at, :].astype(F32)
            z, rstd = norm_stats(v_ref[at, :])
            w = got * g[...]
            inner = rstd * (w - jnp.mean(w, axis=-1, keepdims=True) - z * jnp.mean(w * z, axis=-1, keepdims=True))
            old = base_ref[at, :] if final else base_ref[0, at, :]
            new = old + inner
            if final:
                out[0, at, :] = new
            else:
                out[at, :] = new
                low[at, :] = new.astype(BF16)
            terms = [got * z, got] + ([] if final else [new, old])
            for k, term in enumerate(terms):
                acc[k] = acc[k] + jnp.sum(term.reshape(step // 8, 8, feats), axis=0)
        for k in range(4):
            sums[k : k + 1, :] = jnp.sum(acc[k], axis=0, keepdims=True)

    block = pl.BlockSpec((1, rows, feats), lambda *_: (0, 0, 0))
    if final:
        out, spec, extra = into((seqs, rows, feats), F32, (1, rows, feats), (seq, 0, 0), previous)
        outs, specs = (out, struct((4, feats), F32)), (spec, whole((4, feats)))
        base_spec = whole((rows, feats))
    else:
        extra = []
        outs = (struct((rows, feats), F32), struct((rows, feats), BF16), struct((4, feats), F32))
        specs = (whole((rows, feats)), whole((rows, feats)), whole((4, feats)))
        base_spec = pl.BlockSpec((1, rows, feats), lambda *_: (seq, 0, 0))
    return kernel_call(
        body,
        outs,
        specs,
        [whole((rows, feats)), block, block, whole((rows, feats)), whole((1, feats)), base_spec]
        + [pl.BlockSpec(memory_space=pl.ANY)] * len(extra),
        nbytes=rows * feats * 20,
        flops=rows * feats * 30,
        limit=20,
        aliases={6: 0} if extra else None,
    )(v, keep, core, cross, gain, base, *extra)


def pick(refs, index, out):
    for k, ref in enumerate(refs):

        @pl.when(index == k)
        def _(ref=ref):
            out[...] = ref[...].reshape(out.shape)


def attend_forward(seq, seqs, place, docs_row, docs_col, blocks, wqkv, q_shift, v_shift, wo, previous):
    rows, feats = blocks[0].shape
    parts = len(blocks)
    length = rows * parts
    width = wqkv.shape[2]
    size = feats // HEADS
    heads = width // size
    scale = LOG2E * size ** (-0.5)

    def body(t_ref, dr, dc, x0, x1, x2, x3, w, qb, vb, wo_ref, *rest):
        keep, send, cat, qkv, att, lse, keys, vals = rest[-8:]
        i = pl.program_id(0)
        rel = lax.bitwise_xor(i, t_ref[0])
        pick((x0, x1, x2, x3), rel, cat)
        x = cat[0]
        q = (dot(x, w[0]) + qb[...]).astype(BF16)
        k = dot(x, w[1]).astype(BF16)
        v = (dot(x, w[2]) + vb[...]).astype(BF16)
        qkv[0], qkv[1], qkv[2] = q, k, v
        at = pl.ds(pl.multiple_of(i * rows, rows), rows)
        keys[at, :] = k
        vals[at, :] = v

        for step in range(parts):

            @pl.when(i == step)
            def _(step=step):
                span = (step + 1) * rows
                same = dc[step * rows : span, :] == dr[:, :span]
                before = lax.broadcasted_iota(jnp.int32, (rows, span), 0) + step * rows >= lax.broadcasted_iota(
                    jnp.int32, (rows, span), 1
                )
                allowed = same & before
                for hd in range(heads):
                    cols = slice(hd * size, (hd + 1) * size)
                    s = jnp.where(allowed, dot(qkv[0, :, cols], keys[:span, cols], NT) * scale, NEGATIVE)
                    top = jnp.max(s, axis=-1, keepdims=True)
                    e = jnp.exp2(s - top)
                    total = jnp.sum(e, axis=-1, keepdims=True)
                    o = dot(e.astype(BF16), vals[:span, cols]) / total
                    att[0, :, cols] = o.astype(BF16)
                    lse[:, hd * 128 : (hd + 1) * 128] = jnp.broadcast_to(top + jnp.log2(total), (rows, 128))

        partial = dot(att[0], wo_ref[...]).astype(BF16)

        @pl.when(lax.rem(rel, 2) == 0)
        def _():
            keep[0] = partial

        @pl.when(lax.rem(rel, 2) == 1)
        def _():
            send[0] = partial

    rel_of = lambda i, t: lax.bitwise_xor(i, t[0])
    pair = pl.BlockSpec((1, rows, feats), lambda i, t: (lax.div(rel_of(i, t), 2), 0, 0))
    extra = [] if previous is None else list(previous)
    return kernel_call(
        body,
        (
            struct((2, rows, feats), BF16),
            struct((2, rows, feats), BF16),
            struct((seqs, length, feats), BF16),
            struct((3, length, width), BF16),
            struct((seqs, length, width), BF16),
            struct((length, heads * 128), F32),
        ),
        (
            pair,
            pair,
            pl.BlockSpec((1, rows, feats), lambda i, t: (seq, rel_of(i, t), 0)),
            pl.BlockSpec((3, rows, width), lambda i, t: (0, i, 0)),
            pl.BlockSpec((1, rows, width), lambda i, t: (seq, rel_of(i, t), 0)),
            pl.BlockSpec((rows, heads * 128), lambda i, t: (i, 0)),
        ),
        [
            whole((1, length)),
            whole((length, 1)),
            *[whole((rows, feats))] * 4,
            whole(wqkv.shape),
            whole((1, width)),
            whole((1, width)),
            whole(wo.shape),
        ]
        + [pl.BlockSpec(memory_space=pl.ANY)] * len(extra),
        grid=(parts,),
        scratch=[VMEM((length, width), BF16), VMEM((length, width), BF16)],
        flops=2 * length * feats * width * 4 + 5 * length * length * width // 2 * 2,
        nbytes=length * feats * 8,
        trans=length * length * heads // 2,
        prefetch=1,
        aliases={11: 2, 12: 4} if extra else None,
    )(place, docs_row, docs_col, *blocks, wqkv, q_shift, v_shift, wo, *extra)


def attend_backward(seq, seqs, place, docs_row, docs_col, blocks, qkv, att, lse, wqkv, wo, previous):
    rows, feats = blocks[0].shape
    parts = len(blocks)
    length = rows * parts
    width = wqkv.shape[2]
    size = feats // HEADS
    heads = width // size
    root = size ** (-0.5)
    scale = LOG2E * root

    def body(t_ref, dr, dc, x0, x1, x2, x3, qkv_ref, att_ref, lse_ref, w, wo_ref, *rest):
        keep, send, cat, gq_out, gk_out, gv_out, sums, gk, gv, ga, gq = rest[-11:]
        s_id = pl.program_id(0)
        i = parts - 1 - s_id
        rel = lax.bitwise_xor(i, t_ref[0])
        pick((x0, x1, x2, x3), rel, cat)

        @pl.when(s_id == 0)
        def _():
            gk[...] = jnp.zeros_like(gk)
            gv[...] = jnp.zeros_like(gv)
            sums[...] = jnp.zeros_like(sums)

        ga[...] = dot(cat[0], wo_ref[...], NT).astype(BF16)

        for step in range(parts):

            @pl.when(i == step)
            def _(step=step):
                span = (step + 1) * rows
                own = slice(step * rows, span)
                same = dc[own, :] == dr[:, :span]
                before = lax.broadcasted_iota(jnp.int32, (rows, span), 0) + step * rows >= lax.broadcasted_iota(
                    jnp.int32, (rows, span), 1
                )
                allowed = same & before
                for hd in range(heads):
                    cols = slice(hd * size, (hd + 1) * size)
                    q = qkv_ref[0, own, cols]
                    k = qkv_ref[1, :span, cols]
                    g = ga[:, cols]
                    s = dot(q, k, NT) * scale - lse_ref[:, hd * 128 : hd * 128 + 1]
                    p = jnp.exp2(jnp.where(allowed, s, NEGATIVE))
                    gp = dot(g, qkv_ref[2, :span, cols], NT)
                    row = jnp.sum(g.astype(F32) * att_ref[0, :, cols].astype(F32), axis=-1, keepdims=True)
                    gs = (p * (gp - row)).astype(BF16)
                    gq[:, cols] = (dot(gs, k) * root).astype(BF16)
                    gk[:span, cols] += dot(gs, q, TN)
                    gv[:span, cols] += dot(p.astype(BF16), g, TN)

        at = pl.ds(pl.multiple_of(i * rows, rows), rows)
        low_k = (gk[at, :] * root).astype(BF16)
        low_v = gv[at, :].astype(BF16)
        gq_out[0], gk_out[0], gv_out[0] = gq[...], low_k, low_v
        sums[0:1, :] += jnp.sum(gq[...].astype(F32), axis=0, keepdims=True)
        sums[1:2, :] += jnp.sum(low_v.astype(F32), axis=0, keepdims=True)
        partial = (dot(gq[...], w[0], NT) + dot(low_k, w[1], NT) + dot(low_v, w[2], NT)).astype(BF16)

        @pl.when(lax.rem(rel, 2) == 0)
        def _():
            keep[0] = partial

        @pl.when(lax.rem(rel, 2) == 1)
        def _():
            send[0] = partial

    rel_of = lambda s, t: lax.bitwise_xor(parts - 1 - s, t[0])
    pair = pl.BlockSpec((1, rows, feats), lambda s, t: (lax.div(rel_of(s, t), 2), 0, 0))
    part = pl.BlockSpec((1, rows, width), lambda s, t: (seq, rel_of(s, t), 0))
    extra = [] if previous is None else list(previous)
    return kernel_call(
        body,
        (
            struct((2, rows, feats), BF16),
            struct((2, rows, feats), BF16),
            struct((seqs, length, feats), BF16),
            *[struct((seqs, length, width), BF16)] * 3,
            struct((2, width), F32),
        ),
        (
            pair,
            pair,
            pl.BlockSpec((1, rows, feats), lambda s, t: (seq, rel_of(s, t), 0)),
            part,
            part,
            part,
            whole((2, width)),
        ),
        [
            whole((1, length)),
            whole((length, 1)),
            *[whole((rows, feats))] * 4,
            whole((3, length, width)),
            part,
            pl.BlockSpec((rows, heads * 128), lambda s, t: (parts - 1 - s, 0)),
            whole(wqkv.shape),
            whole(wo.shape),
        ]
        + [pl.BlockSpec(memory_space=pl.ANY)] * len(extra),
        grid=(parts,),
        scratch=[
            VMEM((length, width), F32),
            VMEM((length, width), F32),
            VMEM((rows, width), BF16),
            VMEM((rows, width), BF16),
        ],
        flops=2 * length * feats * width * 4 + 5 * length * length * width,
        nbytes=length * feats * 8,
        trans=length * length * heads // 2,
        prefetch=1,
        aliases={12: 2, 13: 3, 14: 4, 15: 5} if extra else None,
    )(place, docs_row, docs_col, *blocks, qkv, att, lse, wqkv, wo, *extra)


ORDER = (1, 3, 0, 2)


def ordered(s):
    return lax.select(s < 2, 2 * s + 1, 2 * s - 4)


def pair_specs(rows, feats):
    send = pl.BlockSpec((1, rows, feats), lambda s: (lax.min(s, 1), 0, 0))
    keep = pl.BlockSpec((1, rows, feats), lambda s: (lax.max(s - 2, 0), 0, 0))
    return keep, send


def feed_forward(seq, seqs, blocks, w_up, b_up, w_down, previous):
    rows, feats = blocks[0].shape
    units = w_up.shape[1]
    root = math.sqrt(2.0 / math.pi)

    def body(x0, x1, x2, x3, up, bu, down, *rest):
        keep, send, cat, act, slope = rest[-5:]
        s = pl.program_id(0)
        pick([(x0, x1, x2, x3)[k] for k in ORDER], s, cat)
        u = dot(cat[0], up[...]) + bu[...]
        sq = u * u
        th = jnp.tanh(root * u * (1.0 + 0.044715 * sq))
        half = 0.5 * (1.0 + th)
        g = (u * half).astype(BF16)
        act[0] = g
        slope[0] = (half + (0.5 * root) * u * (1.0 - th * th) * (1.0 + (3 * 0.044715) * sq)).astype(BF16)
        partial = dot(g, down[...]).astype(BF16)

        @pl.when(s < 2)
        def _():
            send[0] = partial

        @pl.when(s >= 2)
        def _():
            keep[0] = partial

    extra = [] if previous is None else list(previous)
    keep, send = pair_specs(rows, feats)
    part = lambda cols: pl.BlockSpec((1, rows, cols), lambda s: (seq, ordered(s), 0))
    length = rows * len(blocks)
    return kernel_call(
        body,
        (
            struct((2, rows, feats), BF16),
            struct((2, rows, feats), BF16),
            struct((seqs, length, feats), BF16),
            struct((seqs, length, units), BF16),
            struct((seqs, length, units), BF16),
        ),
        (keep, send, part(feats), part(units), part(units)),
        [*[whole((rows, feats))] * 4, whole(w_up.shape), whole((1, units)), whole(w_down.shape)]
        + [pl.BlockSpec(memory_space=pl.ANY)] * len(extra),
        grid=(4,),
        flops=4 * length * feats * units,
        nbytes=length * feats * 14,
        trans=length * units,
        aliases={7: 2, 8: 3, 9: 4} if extra else None,
    )(*blocks, w_up, b_up, w_down, *extra)


def feed_backward(seq, seqs, own, got, slope, w_up, w_down, previous):
    rows, feats = own.shape[1:]
    units = w_up.shape[1]

    def body(own_ref, got_ref, slope_ref, up, down, *rest):
        keep, send, cat, grad, sums = rest[-5:]
        s = pl.program_id(0)
        pick([got_ref.at[0], got_ref.at[1], own_ref.at[0], own_ref.at[1]], s, cat)
        gu = (dot(cat[0], down[...], NT) * slope_ref[0].astype(F32)).astype(BF16)
        grad[0] = gu
        total = jnp.sum(gu.astype(F32), axis=0, keepdims=True)

        @pl.when(s == 0)
        def _():
            sums[...] = total

        @pl.when(s > 0)
        def _():
            sums[...] += total

        partial = dot(gu, up[...], NT).astype(BF16)

        @pl.when(s < 2)
        def _():
            send[0] = partial

        @pl.when(s >= 2)
        def _():
            keep[0] = partial

    extra = [] if previous is None else list(previous)
    keep, send = pair_specs(rows, feats)
    part = lambda cols: pl.BlockSpec((1, rows, cols), lambda s: (seq, ordered(s), 0))
    length = rows * 4
    return kernel_call(
        body,
        (
            struct((2, rows, feats), BF16),
            struct((2, rows, feats), BF16),
            struct((seqs, length, feats), BF16),
            struct((seqs, length, units), BF16),
            struct((1, units), F32),
        ),
        (keep, send, part(feats), part(units), whole((1, units))),
        [whole((2, rows, feats)), whole((2, rows, feats)), part(units), whole(w_up.shape), whole(w_down.shape)]
        + [pl.BlockSpec(memory_space=pl.ANY)] * len(extra),
        grid=(4,),
        flops=4 * length * feats * units,
        nbytes=length * feats * 14,
        aliases={5: 2, 6: 3} if extra else None,
    )(own, got, slope, w_up, w_down, *extra)


def column(row):
    return jnp.transpose(jnp.broadcast_to(row, (8, row.shape[1])))[:, :1]


def contrast_scores(place, docs, labels, units):
    rows, feats = units[0].shape
    factor = CONTRAST_SCALE / feats * LOG2E
    count = len(units)

    def body(t_ref, doc_ref, lab_ref, *rest):
        refs, (exps, col_out, row_out, both) = rest[:count], rest[count:]
        s = pl.program_id(0)
        t = t_ref[0]

        @pl.when(s == 0)
        def _():
            for k in range(count):
                both[k] = refs[k][...]

        seq = lax.div(s, 2)
        part = lax.rem(s, 2) * 2
        mine = both[seq * 4 + part]
        own_at = lax.bitwise_xor(part, t)
        own_doc = column(doc_ref[seq, own_at])
        own_lab = column(lab_ref[seq, own_at])
        total = jnp.zeros((rows, 1), F32)
        total_pos = jnp.zeros((rows, 1), F32)
        for k in range(count):
            other = k // 4
            e = jnp.exp2(dot(mine, both[k], NT) * factor)
            at = lax.bitwise_xor(jnp.int32(k % 4), t)
            memory = (own_doc != doc_ref[other, at]) | (seq != other)
            e = jnp.where(memory, e, 0.0)
            total += jnp.sum(e, axis=-1, keepdims=True)
            total_pos += jnp.sum(jnp.where(own_lab == lab_ref[other, at], e, 0.0), axis=-1, keepdims=True)
            exps[:, k * rows : (k + 1) * rows] = e.astype(BF16)
        lanes = lax.broadcasted_iota(jnp.int32, (rows, 128), 1)
        wide = jnp.where(lanes == 0, total, total_pos)
        col_out[...] = wide
        row_out[...] = jnp.transpose(wide)[:8, :]

    return kernel_call(
        body,
        (
            struct((4 * rows, count * rows), BF16),
            struct((4 * rows, 128), F32),
            struct((8, 4 * rows), F32),
        ),
        (
            pl.BlockSpec((rows, count * rows), lambda s, t: (s, 0)),
            pl.BlockSpec((rows, 128), lambda s, t: (s, 0)),
            pl.BlockSpec((8, rows), lambda s, t: (0, s)),
        ),
        [whole(docs.shape), whole(labels.shape)] + [whole((rows, feats))] * count,
        grid=(4,),
        scratch=[VMEM((count, rows, feats), BF16)],
        flops=2 * 4 * rows * count * rows * feats,
        nbytes=count * rows * feats * 4,
        trans=4 * rows * count * rows,
        prefetch=1,
    )(place, docs, labels, *units)


def contrast_grads(place, labels, units, exps, col_sums, row_own, row_got, q_own, q_got, cot, cot_got):
    rows, feats = units[0].shape
    factor = CONTRAST_SCALE / feats
    count = len(units)
    seqs = count // 4

    def body(t_ref, lab_ref, *rest):
        refs = rest[:count]
        (e_ref, col, own, got, qo, qg, ct, cg, full, low0, low1, both, grad) = rest[count:]
        s = pl.program_id(0)
        t = t_ref[0]

        @pl.when(s == 0)
        def _():
            for k in range(count):
                both[k * rows : (k + 1) * rows, :] = refs[k][...]

        seq = lax.div(s, 2)
        half = lax.rem(s, 2)
        part = half * 2
        own_lab = column(lab_ref[seq, lax.bitwise_xor(part, t)])
        inv = CONTRAST_WEIGHT / col[...]
        all_i, pos_i = inv[:, 0:1], inv[:, 1:2]
        for k in range(count):
            other, piece = k // 4, k % 4
            source = own if piece % 2 == 0 else got
            at = (other * 2 + piece // 2) * rows
            inv_j = CONTRAST_WEIGHT / source[0:2, at : at + rows]
            same = own_lab == lab_ref[other, lax.bitwise_xor(jnp.int32(piece), t)]
            coef = (all_i + inv_j[0:1]) - jnp.where(same, pos_i + inv_j[1:2], 0.0)
            cols = slice(k * rows, (k + 1) * rows)
            grad[:, cols] = (e_ref[:, cols].astype(F32) * coef).astype(BF16)
        gn = dot(grad[...], both[...]) * factor
        n = both[pl.ds(pl.multiple_of((seq * 4 + part) * rows, rows), rows), :].astype(F32)
        inner = gn - n * jnp.mean(gn * n, axis=-1, keepdims=True)

        @pl.when(half == 0)
        def _():
            gy = ct[0].astype(F32) + qo[0, :, 0:1] * inner
            full[0] = gy
            low = gy.astype(BF16)

            @pl.when(seq == 0)
            def _():
                low0[0] = low

            @pl.when(seq == 1)
            def _():
                low1[0] = low

        @pl.when(half == 1)
        def _():
            low = (cg[0].astype(F32) + qg[0, :, 0:1] * inner).astype(BF16)

            @pl.when(seq == 0)
            def _():
                low0[0] = low

            @pl.when(seq == 1)
            def _():
                low1[0] = low

    per_seq = lambda cols: pl.BlockSpec((1, rows, cols), lambda s, t: (lax.div(s, 2), 0, 0))
    return kernel_call(
        body,
        (
            struct((seqs, rows, feats), F32),
            struct((2, rows, feats), BF16),
            struct((2, rows, feats), BF16),
        ),
        (
            per_seq(feats),
            pl.BlockSpec((1, rows, feats), lambda s, t: (lax.min(s, 1), 0, 0)),
            pl.BlockSpec((1, rows, feats), lambda s, t: (lax.max(s - 2, 0), 0, 0)),
        ),
        [whole(labels.shape)]
        + [whole((rows, feats))] * count
        + [
            pl.BlockSpec((rows, count * rows), lambda s, t: (s, 0)),
            pl.BlockSpec((rows, 128), lambda s, t: (s, 0)),
            whole((8, 4 * rows)),
            whole((8, 4 * rows)),
            per_seq(128),
            per_seq(128),
            per_seq(feats),
            per_seq(feats),
        ],
        grid=(4,),
        scratch=[VMEM((count * rows, feats), BF16), VMEM((rows, count * rows), BF16)],
        flops=2 * 4 * rows * count * rows * feats,
        nbytes=count * rows * feats * 5,
        prefetch=1,
    )(place, labels, *units, exps, col_sums, row_own, row_got, q_own, q_got, cot, cot_got)


def swap(value, axis, size, bit):
    return lax.ppermute(value, axis, [(i, i ^ bit) for i in range(size)])


CORE, CROSS = 1, 2


def tensor_swap(value, bit):
    return swap(value, "tensor", 4, bit)


def gather_rows(value):
    cross = tensor_swap(value, CROSS)
    core = tensor_swap(value, CORE)
    return [value, core, cross, tensor_swap(cross, CORE)]


def scatter_rows(keep, send):
    core = tensor_swap(send, CORE)
    cross = tensor_swap((keep[1].astype(F32) + core[1].astype(F32)).astype(BF16), CROSS)
    return keep, core, cross


def sum_over_dp(value, size, bits):
    me = lax.axis_index("dp")
    for bit in bits:
        half = value.shape[0] // 2
        high = (me & bit) != 0
        keep = lax.dynamic_slice_in_dim(value, jnp.where(high, half, 0), half, 0)
        send = lax.dynamic_slice_in_dim(value, jnp.where(high, 0, half), half, 0)
        got = swap(send, "dp", size, bit)
        value = (keep.astype(F32) + got.astype(F32)).astype(BF16)
    for bit in reversed(bits):
        high = (me & bit) != 0
        got = swap(value, "dp", size, bit)
        value = jnp.concatenate([jnp.where(high, got, value), jnp.where(high, value, got)])
    return value


def sum_pair(first, second, size):
    bits = [1 << k for k in range(size.bit_length() - 1)]
    other = bits[1::-1] + bits[2:]
    return sum_over_dp(first, size, bits), sum_over_dp(second, size, other)


def shards(
    dp_size,
    tokens,
    doc_ids,
    targets,
    cotangent,
    ln1_gain,
    ln1_bias,
    qkv_weight,
    query_bias,
    value_bias,
    output_weight,
    out_bias,
    ln2_gain,
    ln2_bias,
    up_weight,
    up_bias,
    down_weight,
    down_bias,
):
    seqs, rows, feats = tokens.shape
    length = doc_ids.shape[1]
    parts = length // rows
    me = lax.axis_index("tensor")
    place = me.reshape(1).astype(jnp.int32)
    vec = lambda v: v.astype(F32).reshape(1, -1)
    gain_one, shift_one, gain_two, shift_two = vec(ln1_gain), vec(ln1_bias), vec(ln2_gain), vec(ln2_bias)
    out_offset, down_offset, up_shift = vec(out_bias), vec(down_bias), vec(up_bias)
    q_shift, v_shift = vec(query_bias), vec(value_bias)

    fine = 16
    paired = (jnp.arange(feats, dtype=jnp.int32) // 2).astype(F32)
    freq = jnp.exp(paired * (-2.0 * math.log(10000.0) / feats))[None, :]
    odd = (jnp.arange(feats, dtype=jnp.int32) % 2 == 1)[None, :]
    coarse_at = (me * rows + fine * jnp.arange(rows // fine, dtype=jnp.int32)).astype(F32)[:, None] * freq
    fine_at = jnp.arange(fine, dtype=jnp.int32).astype(F32)[:, None] * freq
    sin_a, cos_a = jnp.sin(coarse_at), jnp.cos(coarse_at)
    tables = (jnp.where(odd, cos_a, sin_a), jnp.where(odd, -sin_a, cos_a), jnp.cos(fine_at), jnp.sin(fine_at))

    docs_f, labels_f = doc_ids.astype(F32), targets.astype(F32)
    docs4 = docs_f.reshape(seqs, parts, 1, rows)
    labels4 = labels_f.reshape(seqs, parts, 1, rows)
    each = range(seqs)
    docs_row = [docs_f[s : s + 1] for s in each]
    docs_col = [docs_f[s].reshape(length, 1) for s in each]

    hidden, normed = zip(*[first_norm(s, tokens, tables, gain_one, shift_one) for s in each])
    rows_one = [gather_rows(v) for v in normed]
    kept, shared = [], None
    attn = []
    for s in each:
        keep, send, cat_one, qkv, att, lse = attend_forward(
            s, seqs, place, docs_row[s], docs_col[s], rows_one[s], qkv_weight, q_shift, v_shift, output_weight, shared
        )
        shared = (cat_one, att)
        kept.append((qkv, lse))
        attn.append(scatter_rows(keep, send))
    cot_got = jnp.stack([tensor_swap(cotangent[s], CROSS) for s in each])
    stream, normed_two = zip(
        *[second_norm(hidden[s], *attn[s], out_offset, gain_two, shift_two) for s in each]
    )
    rows_two = [gather_rows(v) for v in normed_two]
    fed, ffn = None, []
    for s in each:
        keep, send, cat_two, hidden_act, slope = feed_forward(
            s, seqs, rows_two[s], up_weight, up_shift, down_weight, fed
        )
        fed = (cat_two, hidden_act, slope)
        ffn.append(scatter_rows(keep, send))
    activations, units, scales = None, [], []
    for s in each:
        activations, unit, scale = output_rows(s, seqs, stream[s], *ffn[s], down_offset, activations)
        units.append(unit)
        scales.append(scale)
    units_all = [block for unit in units for block in gather_rows(unit)]
    scales_own = jnp.stack(scales)
    scales_got = tensor_swap(scales_own, CROSS)

    exps, col_sums, row_sums = contrast_scores(place, docs4, labels4, units_all)
    row_got = tensor_swap(row_sums, CORE)
    grad_y, *low_y = contrast_grads(
        place, labels4, units_all, exps, col_sums, row_sums, row_got, scales_own, scales_got, cotangent, cot_got
    )
    own_cols = col_sums.reshape(seqs, 2, rows, 128)[:, 0, :, :2]
    loss = jnp.log(own_cols[..., 0]) - jnp.log(own_cols[..., 1])

    got_y = [tensor_swap(v, CORE) for v in low_y]
    back, gb, up_sums = None, [], []
    for s in each:
        keep, send, cat_y, grad_up, sums = feed_backward(
            s, seqs, low_y[s], got_y[s], slope, up_weight, down_weight, back
        )
        back = (cat_y, grad_up)
        up_sums.append(sums)
        gb.append(scatter_rows(keep, send))
    grad_down_w = jnp.einsum("snf,snd->fd", hidden_act, cat_y, preferred_element_type=F32).astype(BF16)
    grad_up_w = jnp.einsum("snd,snf->df", cat_two, grad_up, preferred_element_type=F32).astype(BF16)
    grad_down_w, grad_up_w = sum_pair(grad_down_w, grad_up_w, dp_size)

    grad_r, low_r, sums_two = zip(
        *[norm_backward(s, seqs, stream[s], *gb[s], gain_two, grad_y, False, None) for s in each]
    )
    rows_r = [gather_rows(v) for v in low_r]
    back, ga, head_sums = None, [], []
    for s in each:
        keep, send, *back, sums = attend_backward(
            s, seqs, place, docs_row[s], docs_col[s], rows_r[s], kept[s][0], att, kept[s][1], qkv_weight,
            output_weight, back,
        )
        head_sums.append(sums)
        ga.append(scatter_rows(keep, send))
    cat_r, *grad_qkv = back
    grad_out_w = jnp.einsum("yak,yac->kc", att, cat_r, preferred_element_type=F32).astype(BF16)
    grad_qkv_w = [
        jnp.einsum("snd,sne->de", cat_one, g, preferred_element_type=F32).astype(BF16) for g in grad_qkv
    ]
    first = jnp.concatenate([grad_qkv_w[0], grad_qkv_w[1]], axis=1)
    second = jnp.concatenate([grad_qkv_w[2], grad_out_w.reshape(feats, -1)], axis=1)
    first, second = sum_pair(first, second, dp_size)
    width = grad_out_w.shape[0]
    grad_qkv_w = jnp.stack([first[:, :width], first[:, width:], second[:, :width]]).astype(F32)
    grad_out_w = second[:, width:].reshape(width, feats).astype(F32)

    input_grad, sums_one = None, []
    for s in each:
        input_grad, sums = norm_backward(s, seqs, hidden[s], *ga[s], gain_one, grad_r[s], True, input_grad)
        sums_one.append(sums)
    total = lambda items: functools.reduce(jnp.add, items)
    heads_sum = total(head_sums)
    heads_row = jnp.pad(heads_sum.reshape(1, -1), ((0, 0), (0, feats - heads_sum.size)))
    small = jnp.concatenate([total(sums_one)[:2], total(sums_two), total(up_sums), heads_row])
    bit = 1
    while bit < dp_size:
        small = small + swap(small, "dp", dp_size, bit)
        bit *= 2
    local, small = small[6:], small[:6]
    for bit in (CORE, CROSS):
        small = small + tensor_swap(small, bit)
    return (
        activations,
        loss,
        input_grad,
        small[0],
        small[1],
        grad_qkv_w,
        local[1, : heads_sum.shape[1]],
        local[1, heads_sum.shape[1] : 2 * heads_sum.shape[1]],
        grad_out_w,
        small[4],
        small[2],
        small[3],
        grad_up_w.astype(F32),
        local[0],
        grad_down_w.astype(F32),
        small[5],
    )


def solution(mesh):
    in_specs = (
        P("dp", "tensor", None),
        P("dp", None),
        P("dp", None),
        P("dp", "tensor", None),
        P(),
        P(),
        P(None, None, "tensor"),
        P("tensor"),
        P("tensor"),
        P("tensor", None),
        P(),
        P(),
        P(),
        P(None, "tensor"),
        P("tensor"),
        P("tensor", None),
        P(),
    )
    out_specs = (
        P("dp", "tensor", None),
        P("dp", "tensor"),
        P("dp", "tensor", None),
        P(),
        P(),
        P(None, None, "tensor"),
        P("tensor"),
        P("tensor"),
        P("tensor", None),
        P(),
        P(),
        P(),
        P(None, "tensor"),
        P("tensor"),
        P("tensor", None),
        P(),
    )
    return jax.shard_map(
        functools.partial(shards, mesh.shape["dp"]),
        mesh=mesh,
        in_specs=in_specs,
        out_specs=out_specs,
        check_vma=False,
    )
```

time: 920 us -> 532 us (0.58)
  waiting for transfers between devices: 539 us -> 243 us
  Pallas kernels: 0 us -> 114 us
  matrix products: 136 us -> 23.4 us
  starting transfers between devices: 1.67 us -> 68 us
  blocking collectives: 62.1 us -> 0 us
  other arithmetic: 72.1 us -> 29 us
  local copies, waits for them, and re-layouts: 76.1 us -> 49.4 us
  between operations: 15 us -> 2.09 us
  loops' own time: 12.7 us -> 0 us
    ppermute x0 -> x75, waiting for transfers between devices: none -> 243 us  [swap(): return lax.ppermute(value, axis, [(i, i ^ bit) for i in range(size)])]
    reduce_scatter x5 -> x0, waiting for transfers between devices: 206 us -> none  [the longest x1 44.6 us: shards(): lax.psum_scatter(jnp.einsum('snf,df->nsd', row_portion, up_weight, prefer...]
    psum x1 -> x0, waiting for transfers between devices: 178 us -> none  [shards(): lax.psum(grad_qkv_w.astype(jnp.bfloat16), 'dp').astype(jnp.float32)]
    all_gather x5 -> x0, waiting for transfers between devices: 154 us -> none  [the longest x2 71.3 us: norm_rows(): return lax.all_gather(values, 'tensor', axis=1, tiled=True)]
    pallas_call x0 -> x20, Pallas kernels: none -> 114 us  [the longest x2 22.1 us: attend_backward(): kernel_call(body, (struct((2, rows, feats), BF16), struct((2, rows, feats...]
    dot_general x43 -> x6, matrix products: 136 us -> 23.4 us  [the longest x1 7.83 us: shards(): jnp.einsum('snd,snf->df', cat_two, grad_up, preferred_element_type=F32)]
    ppermute x0 -> x75, starting transfers between devices: none -> 68 us  [swap(): return lax.ppermute(value, axis, [(i, i ^ bit) for i in range(size)])]
    psum x2 -> x0, blocking collectives: 62.1 us -> none  [the longest x1 39.5 us: shards(): lax.psum(jnp.stack([grad_gain_one, grad_shift_one, jnp.sum(grad_residual,...]
  transfers between devices with their start and end apart: 11 -> 75, of which waited for: 11 -> 34; matrix products, arithmetic and copies ran while one was open for 6% -> 12% of each run, Pallas kernels for 0% -> 19%
where the time goes in v1:
time: 532 us; the launch traced here: 528 us
  waiting for transfers between devices  243 us (46%)
  Pallas kernels  114 us (21%)
  starting transfers between devices  68 us (13%)
  local copies, waits for them, and re-layouts  49.4 us (9%)
  other arithmetic  29 us (5%)
  matrix products  23.4 us (4%)
    ppermute x75, waiting for transfers between devices, swap(): return lax.ppermute(value, axis, [(i, i ^ bit) for i in range(size)])  243 us
    ppermute x75, starting transfers between devices, swap(): return lax.ppermute(value, axis, [(i, i ^ bit) for i in range(size)])  68 us
    unnamed x177, local copies, waits for them, and re-layouts  34.9 us
    pallas_call x2, Pallas kernels, attend_backward(): kernel_call(body, (struct((2, rows, feats), BF16), struct((2, rows, feats...  22.1 us
    pallas_call x2, Pallas kernels, attend_forward(): kernel_call(body, (struct((2, rows, feats), BF16), struct((2, rows, feats...  19.9 us
    pallas_call x2, Pallas kernels, feed_backward(): kernel_call(body, (struct((2, rows, feats), BF16), struct((2, rows, feats...  19.1 us
    pallas_call x2, Pallas kernels, feed_forward(): kernel_call(body, (struct((2, rows, feats), BF16), struct((2, rows, feats...  18.6 us
    pallas_call x1, Pallas kernels, contrast_grads(): kernel_call(body, (struct((seqs, rows, feats), F32), struct((2, rows, fea...  11.1 us
  transfers between devices with their start and end apart: 75, of which 34 were waited for; matrix products, arithmetic and copies ran while one was open for 12% of the time, Pallas kernels for 19%

profile of v1, /device:TPU:0, one launch (start us, length us, event | category | flops | bytes accessed | tf_op | source)
XLA Modules:
  0.0 528.1 jit_solution(3927827264128094304)
XLA Ops:
  4.4 3.0 collective-permute-start.4
  10.5 9.6 %collective-permute-done.4.x2 = bf16[256,1024]{1,0:T(8,128)(2,1)S(1)} collective-permute-done((bf16[256,1024]{1,0:T(8,128)(2,1)S(1)}, bf16[256,1024]{1,0:T(8,128)(2,1)S(1)}, u32[]{:S(2)}, u32[]{:S(2)}) %collective-permute-start.4) | collective-permute-done | bytes 524320 | tf_op jit(solution)/shard_map/ppermute | solution.py:698
  22.7 8.0 %collective-permute-done.1.x2 = bf16[256,1024]{1,0:T(8,128)(2,1)} collective-permute-done((bf16[256,1024]{1,0:T(8,128)(2,1)}, bf16[256,1024]{1,0:T(8,128)(2,1)}, u32[]{:S(2)}, u32[]{:S(2)}) %collective-permute-start.1) | collective-permute-done | bytes 524320 | tf_op jit(solution)/shard_map/ppermute | solution.py:698
  41.0 9.5 %shard_map.290 = (bf16[2,256,1024]{2,1,0:T(8,128)(2,1)S(1)}, bf16[2,256,1024]{2,1,0:T(8,128)(2,1)}, bf16[2,1024,1024]{2,1,0:T(8,128)(2,1)}, bf16[3,1024,256]{2,1...) custom-call(s32[1]{0:T(128)} %bitcast.2.t_ref, f32[1,1024]{1,0:T(1,128)S(1)} %get-tuple-element.240.dr, ...), custom_call_target="tpu_custom_call" | custom-call | flops 3489660928 | bytes 8388608 | tf_op jit(solution)/shard_map/pallas_call | solution.py:271
  57.6 10.5 %shard_map.291 = (bf16[2,256,1024]{2,1,0:T(8,128)(2,1)S(1)}, bf16[2,256,1024]{2,1,0:T(8,128)(2,1)S(1)}, bf16[2,1024,1024]{2,1,0:T(8,128)(2,1)}, bf16[3,1024,256]...) custom-call(s32[1]{0:T(128)} %bitcast.2.t_ref, ...), custom_call_target="tpu_custom_call", output_to_operand_aliasing={{2}: (11, {}), {4}: (12, {})} | custom-call | flops 3489660928 | bytes 8388608 | tf_op jit(solution)/shard_map/pallas_call | solution.py:271
  73.8 12.2 %collective-permute-done.12.x_ref = bf16[256,1024]{1,0:T(8,128)(2,1)S(1)} collective-permute-done((bf16[256,1024]{1,0:T(8,128)(2,1)S(1)}, bf16[256,1024]{1,0:T(8,128)(2,1)S(1)}, u32[]{:S(2)}, u32[]{:S(2)}) %collective-permute-start.12) | collective-permute-done | bytes 524320 | tf_op jit(solution)/shard_map/ppermute | solution.py:698
  90.7 6.6 %collective-permute-done.7.x_ref = bf16[256,1024]{1,0:T(8,128)(2,1)S(1)} collective-permute-done((bf16[256,1024]{1,0:T(8,128)(2,1)S(1)}, bf16[256,1024]{1,0:T(8,128)(2,1)S(1)}, u32[]{:S(2)}, u32[]{:S(2)}) %collective-permute-start.7) | collective-permute-done | bytes 524320 | tf_op jit(solution)/shard_map/ppermute | solution.py:698
  99.6 8.8 %collective-permute-done.14.x2 = bf16[256,1024]{1,0:T(8,128)(2,1)S(1)} collective-permute-done((bf16[256,1024]{1,0:T(8,128)(2,1)S(1)}, bf16[256,1024]{1,0:T(8,128)(2,1)S(1)}, u32[]{:S(2)}, u32[]{:S(2)}) %collective-permute-start.14) | collective-permute-done | bytes 524320 | tf_op jit(solution)/shard_map/ppermute | solution.py:698
  109.0 10.3 %collective-permute-done.9.x2 = bf16[256,1024]{1,0:T(8,128)(2,1)S(1)} collective-permute-done((bf16[256,1024]{1,0:T(8,128)(2,1)S(1)}, bf16[256,1024]{1,0:T(8,128)(2,1)S(1)}, u32[]{:S(2)}, u32[]{:S(2)}) %collective-permute-start.9) | collective-permute-done | bytes 524320 | tf_op jit(solution)/shard_map/ppermute | solution.py:698
  119.3 9.6 %shard_map.294 = (bf16[2,256,1024]{2,1,0:T(8,128)(2,1)S(1)}, bf16[2,256,1024]{2,1,0:T(8,128)(2,1)S(1)}, bf16[2,1024,1024]{2,1,0:T(8,128)(2,1)S(1)}, bf16[2,1024,1024]{2,1,0:T(8,128)(2,1)}, bf16[2,1024,1024]{2,1,0:T(8,128)(2,1)}) custom-call(bf16[256,1024]{1,0:T(8,128)(2,1)S(1)} %get-tuple-element.104.x0, bf16[256,1024]{1,0:T(8,128)(2,1)S(1)} %collective-permute-done.13.x1, ...), custom_call_target="tpu_custom_call" | custom-call | flops 4294967296 | bytes 14680064 | tf_op jit(solution)/shard_map/pallas_call | solution.py:466
  129.4 9.0 %shard_map.295 = (bf16[2,256,1024]{2,1,0:T(8,128)(2,1)S(1)}, bf16[2,256,1024]{2,1,0:T(8,128)(2,1)S(1)}, bf16[2,1024,1024]{2,1,0:T(8,128)(2,1)S(1)}, bf16[2,1024,1024]{2,1,0:T(8,128)(2,1)}, bf16[2,1024,1024]{2,1,0:T(8,128)(2,1)}) custom-call(bf16[256,1024]{1,0:T(8,128)(2,1)S(1)} %get-tuple-element.100.x0, ...), custom_call_target="tpu_custom_call", output_to_operand_aliasing={{2}: (7, {}), {3}: (8, {}), {4}: (9, {})} | custom-call | flops 4294967296 | bytes 14680064 | tf_op jit(solution)/shard_map/pallas_call | solution.py:466
  143.2 10.3 %collective-permute-done.19.x_ref = bf16[256,1024]{1,0:T(8,128)(2,1)S(1)} collective-permute-done((bf16[256,1024]{1,0:T(8,128)(2,1)S(1)}, bf16[256,1024]{1,0:T(8,128)(2,1)S(1)}, u32[]{:S(2)}, u32[]{:S(2)}) %collective-permute-start.19) | collective-permute-done | bytes 524320 | tf_op jit(solution)/shard_map/ppermute | solution.py:698
  156.4 8.4 %collective-permute-done.17.x_ref = bf16[256,1024]{1,0:T(8,128)(2,1)S(1)} collective-permute-done((bf16[256,1024]{1,0:T(8,128)(2,1)S(1)}, bf16[256,1024]{1,0:T(8,128)(2,1)S(1)}, u32[]{:S(2)}, u32[]{:S(2)}) %collective-permute-start.17) | collective-permute-done | bytes 524320 | tf_op jit(solution)/shard_map/ppermute | solution.py:698
  168.3 7.8 %collective-permute-done.21.rest_2_ = bf16[256,1024]{1,0:T(8,128)(2,1)} collective-permute-done((bf16[256,1024]{1,0:T(8,128)(2,1)S(1)}, bf16[256,1024]{1,0:T(8,128)(2,1)}, u32[]{:S(2)}, u32[]{:S(2)}) %collective-permute-start.21) | collective-permute-done | bytes 524320 | tf_op jit(solution)/shard_map/ppermute | solution.py:698
  176.1 10.8 %collective-permute-done.24.rest_6_ = bf16[256,1024]{1,0:T(8,128)(2,1)} collective-permute-done((bf16[256,1024]{1,0:T(8,128)(2,1)}, bf16[256,1024]{1,0:T(8,128)(2,1)}, u32[]{:S(2)}, u32[]{:S(2)}) %collective-permute-start.24) | collective-permute-done | bytes 524320 | tf_op jit(solution)/shard_map/ppermute | solution.py:698
  194.8 8.5 %shard_map.298 = (bf16[1024,2048]{1,0:T(8,128)(2,1)S(1)}, f32[1024,128]{1,0:T(8,128)S(1)}, f32[8,1024]{1,0:T(8,128)S(1)}) custom-call(s32[1]{0:T(128)} %bitcast.2.t_ref, f32[2,4,1,256]{3,2,1,0:T(1,128)S(1)} %reshape.218.doc_ref, f32[2,4,1,256]{3,2,1,0:T(1,128)S(1)} %reshape.189.lab_ref, bf16[256,1024]{1,0:T(8,128)(2,1)S(1)} %copy-done.52, ...), custom_call_target="tpu_custom_call" | custom-call | flops 4294967296 | bytes 8388608 | tf_op jit(solution)/shard_map/pallas_call | solution.py:580
  205.4 8.8 %collective-permute-done.28 = bf16[256,1024]{1,0:T(8,128)(2,1)} collective-permute-done((bf16[256,1024]{1,0:T(8,128)(2,1)}, bf16[256,1024]{1,0:T(8,128)(2,1)}, u32[]{:S(2)}, u32[]{:S(2)}) %collective-permute-start.28) | collective-permute-done | bytes 524320 | tf_op jit(solution)/shard_map/ppermute | solution.py:698
  215.5 3.8 collective-permute-done.27.rest_13_
  219.4 11.1 %shard_map.299 = (f32[2,256,1024]{2,1,0:T(8,128)S(1)}, bf16[2,256,1024]{2,1,0:T(8,128)(2,1)}, bf16[2,256,1024]{2,1,0:T(8,128)(2,1)}) custom-call(s32[1]{0:T(128)} %bitcast.2.t_ref, f32[2,4,1,256]{3,2,1,0:T(1,128)S(1)} %reshape.189.lab_ref, bf16[256,1024]{1,0:T(8,128)(2,1)S(1)} %copy-done.53, bf16[256,1024]{1,0:T(8,128)(2,1)S(1)} %copy-done.55, ...), custom_call_target="tpu_custom_call" | custom-call | flops 4294967296 | bytes 10485760 | tf_op jit(solution)/shard_map/pallas_call | solution.py:665
  232.3 2.5 collective-permute-done.31.got_ref
  236.4 9.7 %shard_map.300 = (bf16[2,256,1024]{2,1,0:T(8,128)(2,1)S(1)}, bf16[2,256,1024]{2,1,0:T(8,128)(2,1)}, bf16[2,1024,1024]{2,1,0:T(8,128)(2,1)S(1)}, bf16[2,1024,1024]{2,1,0:T(8,128)(2,1)}, f32[1,1024]{1,0:T(1,128)S(1)}) custom-call(bf16[2,256,1024]{2,1,0:T(8,128)(2,1)} %get-tuple-element.124.own_ref, bf16[2,256,1024]{2,1,0:T(8,128)(2,1)} %collective-permute-done.31.got_ref, ...), custom_call_target="tpu_custom_call" | custom-call | flops 4294967296 | bytes 14680064 | tf_op jit(solution)/shard_map/pallas_call | solution.py:520
  246.3 9.4 %shard_map.301 = (bf16[2,256,1024]{2,1,0:T(8,128)(2,1)S(1)}, bf16[2,256,1024]{2,1,0:T(8,128)(2,1)S(1)}, bf16[2,1024,1024]{2,1,0:T(8,128)(2,1)S(1)}, bf16[2,1024,1024]{2,1,0:T(8,128)(2,1)}, f32[1,1024]{1,0:T(1,128)S(1)}) custom-call(bf16[2,256,1024]{2,1,0:T(8,128)(2,1)} %get-tuple-element.122.own_ref, ...), custom_call_target="tpu_custom_call", output_to_operand_aliasing={{2}: (5, {}), {3}: (6, {})} | custom-call | flops 4294967296 | bytes 14680064 | tf_op jit(solution)/shard_map/pallas_call | solution.py:520
  255.7 7.8 %bitcast_convert_fusion.1 = bf16[1024,1024]{1,0:T(8,128)(2,1)S(1)} fusion(bf16[2,1024,1024]{2,1,0:T(8,128)(2,1)S(1)} %copy-done.6, bf16[2,1024,1024]{2,1,0:T(8,128)(2,1)} %get-tuple-element.165), kind=kOutput, calls=%fused_computation.1 | convolution fusion | flops 4296015872 | bytes 10485760 | tf_op jit(solution)/shard_map/snd,snf->df/dot_general | solution.py:838
  266.5 4.8 bitcast_convert_fusion
  278.4 12.1 %collective-permute-done.63 = bf16[512,1024]{1,0:T(8,128)(2,1)} collective-permute-done((bf16[512,1024]{1,0:T(8,128)(2,1)}, bf16[512,1024]{1,0:T(8,128)(2,1)}, u32[]{:S(2)}, u32[]{:S(2)}) %collective-permute-start.63) | collective-permute-done | bytes 1048608 | tf_op jit(solution)/shard_map/ppermute | solution.py:698
  294.3 5.8 %collective-permute-done.69 = bf16[512,1024]{1,0:T(8,128)(2,1)} collective-permute-done((bf16[512,1024]{1,0:T(8,128)(2,1)}, bf16[512,1024]{1,0:T(8,128)(2,1)}, u32[]{:S(2)}, u32[]{:S(2)}) %collective-permute-start.69) | collective-permute-done | bytes 1048608 | tf_op jit(solution)/shard_map/ppermute | solution.py:698
  306.4 3.9 collective-permute-done.64
  310.5 2.7 collective-permute-start.65
  314.6 4.9 collective-permute-start.71
  319.4 11.5 %collective-permute-done.65 = bf16[128,1024]{1,0:T(8,128)(2,1)S(1)} collective-permute-done((bf16[128,1024]{1,0:T(8,128)(2,1)S(1)}, bf16[128,1024]{1,0:T(8,128)(2,1)S(1)}, u32[]{:S(2)}, u32[]{:S(2)}) %collective-permute-start.65) | collective-permute-done | bytes 262176 | tf_op jit(solution)/shard_map/ppermute | solution.py:698
  334.6 7.6 %collective-permute-done.71 = bf16[128,1024]{1,0:T(8,128)(2,1)S(1)} collective-permute-done((bf16[128,1024]{1,0:T(8,128)(2,1)S(1)}, bf16[128,1024]{1,0:T(8,128)(2,1)S(1)}, u32[]{:S(2)}, u32[]{:S(2)}) %collective-permute-start.71) | collective-permute-done | bytes 262176 | tf_op jit(solution)/shard_map/ppermute | solution.py:698
  342.4 10.6 %collective-permute-done.66 = bf16[128,1024]{1,0:T(8,128)(2,1)S(1)} collective-permute-done((bf16[128,1024]{1,0:T(8,128)(2,1)S(1)}, bf16[128,1024]{1,0:T(8,128)(2,1)S(1)}, u32[]{:S(2)}, u32[]{:S(2)}) %collective-permute-start.66) | collective-permute-done | bytes 262176 | tf_op jit(solution)/shard_map/ppermute | solution.py:698
  355.5 2.6 collective-permute-done.72
  359.2 10.9 %shard_map.304 = (bf16[2,256,1024]{2,1,0:T(8,128)(2,1)S(1)}, bf16[2,256,1024]{2,1,0:T(8,128)(2,1)}, bf16[2,1024,1024]{2,1,0:T(8,128)(2,1)}, bf16[2,1024,256]{2,1...) custom-call(s32[1]{0:T(128)} %bitcast.2.t_ref, ...), custom_call_target="tpu_custom_call" | custom-call | flops 3489660928 | bytes 8388608 | tf_op jit(solution)/shard_map/pallas_call | solution.py:379
  370.2 11.1 %shard_map.305 = (bf16[2,256,1024]{2,1,0:T(8,128)(2,1)S(1)}, bf16[2,256,1024]{2,1,0:T(8,128)(2,1)}, bf16[2,1024,1024]{2,1,0:T(8,128)(2,1)}, bf16[2,1024,256]{2,1...) custom-call(s32[1]{0:T(128)} %bitcast.2.t_ref, ...), custom_call_target="tpu_custom_call", output_to_operand_aliasing={{2}: (12, {}), {3}: (13, {}), {4}: (14, {}), {5}: (15, {})} | custom-call | flops 3489660928 | bytes 8388608 | tf_op jit(solution)/shard_map/pallas_call | solution.py:379
  384.9 4.3 fusion.3
  393.3 3.9 fusion.2
  406.7 5.4 %collective-permute-done.57 = bf16[512,512]{0,1:T(8,128)(2,1)S(1)} collective-permute-done((bf16[512,512]{0,1:T(8,128)(2,1)S(1)}, bf16[512,512]{0,1:T(8,128)(2,1)S(1)}, u32[]{:S(2)}, u32[]{:S(2)}) %collective-permute-start.57) | collective-permute-done | bytes 524320 | tf_op jit(solution)/shard_map/ppermute | solution.py:698
  413.9 3.0 collective-permute-done.51
  418.8 25.2 %collective-permute-done.58 = bf16[256,512]{0,1:T(8,128)(2,1)S(1)} collective-permute-done((bf16[256,512]{0,1:T(8,128)(2,1)S(1)}, bf16[256,512]{0,1:T(8,128)(2,1)S(1)}, u32[]{:S(2)}, u32[]{:S(2)}) %collective-permute-start.58) | collective-permute-done | bytes 262176 | tf_op jit(solution)/shard_map/ppermute | solution.py:698
  444.6 6.7 %collective-permute-done.52 = bf16[256,512]{0,1:T(8,128)(2,1)S(1)} collective-permute-done((bf16[256,512]{0,1:T(8,128)(2,1)S(1)}, bf16[256,512]{0,1:T(8,128)(2,1)S(1)}, u32[]{:S(2)}, u32[]{:S(2)}) %collective-permute-start.52) | collective-permute-done | bytes 262176 | tf_op jit(solution)/shard_map/ppermute | solution.py:698
  452.8 5.7 %collective-permute-done.59 = bf16[128,512]{0,1:T(8,128)(2,1)S(1)} collective-permute-done((bf16[128,512]{0,1:T(8,128)(2,1)S(1)}, bf16[128,512]{0,1:T(8,128)(2,1)S(1)}, u32[]{:S(2)}, u32[]{:S(2)}) %collective-permute-start.59) | collective-permute-done | bytes 131104 | tf_op jit(solution)/shard_map/ppermute | solution.py:698
  458.7 8.3 %collective-permute-done.53 = bf16[128,512]{0,1:T(8,128)(2,1)S(1)} collective-permute-done((bf16[128,512]{0,1:T(8,128)(2,1)S(1)}, bf16[128,512]{0,1:T(8,128)(2,1)S(1)}, u32[]{:S(2)}, u32[]{:S(2)}) %collective-permute-start.53) | collective-permute-done | bytes 131104 | tf_op jit(solution)/shard_map/ppermute | solution.py:698
  467.1 3.0 collective-permute-start.54
  481.6 7.8 %collective-permute-done.45.x_ref = bf16[256,1024]{1,0:T(8,128)(2,1)S(1)} collective-permute-done((bf16[256,1024]{1,0:T(8,128)(2,1)S(1)}, bf16[256,1024]{1,0:T(8,128)(2,1)S(1)}, u32[]{:S(2)}, u32[]{:S(2)}) %collective-permute-start.45) | collective-permute-done | bytes 524320 | tf_op jit(solution)/shard_map/ppermute | solution.py:698
  489.4 2.9 shard_map.306
  503.3 4.4 collective-permute-done.48
  515.3 6.8 %collective-permute-done.56 = bf16[512,512]{0,1:T(8,128)(2,1)S(1)} collective-permute-done((bf16[512,512]{0,1:T(8,128)(2,1)S(1)}, bf16[512,512]{0,1:T(8,128)(2,1)S(1)}, u32[]{:S(2)}, u32[]{:S(2)}) %collective-permute-start.56) | collective-permute-done | bytes 524320 | tf_op jit(solution)/shard_map/ppermute | solution.py:698
  (404 shorter events, 154.1 us)
Async XLA Ops:
  4.4 15.8 %collective-permute-start.4 = (bf16[256,1024]{1,0:T(8,128)(2,1)S(1)}, bf16[256,1024]{1,0:T(8,128)(2,1)S(1)}, u32[]{:S(2)}, u32[]{:S(2)}) collective-permute-start(bf16[256,1024]{1,0:T(8,128)(2,1)S(1)} %get-tuple-element.94.x0), channel_id=1, source_target_pairs={{0,2},{1,3},{2,0},{3,1},{4,6},{5,7},{6,4},{7,5},{8,10},{9,11},{10,... | collective-permute-start | bytes 1572872 | tf_op jit(solution)/shard_map/ppermute | solution.py:698
  9.7 21.0 %collective-permute-start.1 = (bf16[256,1024]{1,0:T(8,128)(2,1)}, bf16[256,1024]{1,0:T(8,128)(2,1)}, u32[]{:S(2)}, u32[]{:S(2)}) collective-permute-start(bf16[256,1024]{1,0:T(8,128)(2,1)} %get-tuple-element.93.x0), channel_id=1, source_target_pairs={{0,2},{1,3},{2,0},{3,1},{4,6},{5,7},{6,4},{7,5},{8,10},{9,11},{10,... | collective-permute-start | bytes 1572872 | tf_op jit(solution)/shard_map/ppermute | solution.py:698
  9.7 22.0 %collective-permute-start.3 = (bf16[256,1024]{1,0:T(8,128)(2,1)S(1)}, bf16[256,1024]{1,0:T(8,128)(2,1)S(1)}, u32[]{:S(2)}, u32[]{:S(2)}) collective-permute-start(bf16[256,1024]{1,0:T(8,128)(2,1)S(1)} %get-tuple-element.94.x0), channel_id=1, source_target_pairs={{0,1},{1,0},{2,3},{3,2},{4,5},{5,4},{6,7},{7,6},{8,9},{9,8},{10,11... | collective-permute-start | bytes 1572872 | tf_op jit(solution)/shard_map/ppermute | solution.py:698
  20.2 34.0 %collective-permute-start = (bf16[256,1024]{1,0:T(8,128)(2,1)}, bf16[256,1024]{1,0:T(8,128)(2,1)}, u32[]{:S(2)}, u32[]{:S(2)}) collective-permute-start(bf16[256,1024]{1,0:T(8,128)(2,1)} %get-tuple-element.93.x0), channel_id=1, source_target_pairs={{0,1},{1,0},{2,3},{3,2},{4,5},{5,4},{6,7},{7,6},{8,9},{9,8},{10,11... | collective-permute-start | bytes 1572872 | tf_op jit(solution)/shard_map/ppermute | solution.py:698
  30.7 23.5 %collective-permute-start.2 = (bf16[256,1024]{1,0:T(8,128)(2,1)}, bf16[256,1024]{1,0:T(8,128)(2,1)}, u32[]{:S(2)}, u32[]{:S(2)}) collective-permute-start(bf16[256,1024]{1,0:T(8,128)(2,1)} %collective-permute-done.1.x2), channel_id=1, source_target_pairs={{0,1},{1,0},{2,3},{3,2},{4,5},{5,4},{6,7},{7,6},{8,9},{9,8},{10,11... | collective-permute-start | bytes 1572872 | tf_op jit(solution)/shard_map/ppermute | solution.py:698
  52.6 16.6 %collective-permute-start.11 = (bf16[2,256,1024]{2,1,0:T(8,128)(2,1)}, bf16[2,256,1024]{2,1,0:T(8,128)(2,1)}, u32[]{:S(2)}, u32[]{:S(2)}) collective-permute-start(bf16[2,256,1024]{2,1,0:T(8,128)(2,1)} %get-tuple-element.103), channel_id=1, source_target_pairs={{0,1},{1,0},{2,3},{3,2},{4,5},{5,4},{6,7},{7,6},{8,9},{9,8},{10,11... | collective-permute-start | bytes 3145736 | tf_op jit(solution)/shard_map/ppermute | solution.py:698
  73.2 24.0 %collective-permute-start.7 = (bf16[256,1024]{1,0:T(8,128)(2,1)S(1)}, bf16[256,1024]{1,0:T(8,128)(2,1)S(1)}, u32[]{:S(2)}, u32[]{:S(2)}) collective-permute-start(bf16[256,1024]{1,0:T(8,128)(2,1)S(1)} %fusion.4), channel_id=1, source_target_pairs={{0,2},{1,3},{2,0},{3,1},{4,6},{5,7},{6,4},{7,5},{8,10},{9,11},{10,... | collective-permute-start | bytes 1572872 | tf_op jit(solution)/shard_map/ppermute | solution.py:698
  88.8 19.6 %collective-permute-start.14 = (bf16[256,1024]{1,0:T(8,128)(2,1)S(1)}, bf16[256,1024]{1,0:T(8,128)(2,1)S(1)}, u32[]{:S(2)}, u32[]{:S(2)}) collective-permute-start(bf16[256,1024]{1,0:T(8,128)(2,1)S(1)} %get-tuple-element.104.x0), channel_id=1, source_target_pairs={{0,2},{1,3},{2,0},{3,1},{4,6},{5,7},{6,4},{7,5},{8,10},{9,11},{10,... | collective-permute-start | bytes 1572872 | tf_op jit(solution)/shard_map/ppermute | solution.py:698
  97.8 21.5 %collective-permute-start.9 = (bf16[256,1024]{1,0:T(8,128)(2,1)S(1)}, bf16[256,1024]{1,0:T(8,128)(2,1)S(1)}, u32[]{:S(2)}, u32[]{:S(2)}) collective-permute-start(bf16[256,1024]{1,0:T(8,128)(2,1)S(1)} %get-tuple-element.100.x0), channel_id=1, source_target_pairs={{0,2},{1,3},{2,0},{3,1},{4,6},{5,7},{6,4},{7,5},{8,10},{9,11},{10,... | collective-permute-start | bytes 1572872 | tf_op jit(solution)/shard_map/ppermute | solution.py:698
  99.6 19.6 %collective-permute-start.13 = (bf16[256,1024]{1,0:T(8,128)(2,1)S(1)}, bf16[256,1024]{1,0:T(8,128)(2,1)S(1)}, u32[]{:S(2)}, u32[]{:S(2)}) collective-permute-start(bf16[256,1024]{1,0:T(8,128)(2,1)S(1)} %get-tuple-element.104.x0), channel_id=1, source_target_pairs={{0,1},{1,0},{2,3},{3,2},{4,5},{5,4},{6,7},{7,6},{8,9},{9,8},{10,11... | collective-permute-start | bytes 1572872 | tf_op jit(solution)/shard_map/ppermute | solution.py:698
  108.5 20.9 %collective-permute-start.8 = (bf16[256,1024]{1,0:T(8,128)(2,1)S(1)}, bf16[256,1024]{1,0:T(8,128)(2,1)S(1)}, u32[]{:S(2)}, u32[]{:S(2)}) collective-permute-start(bf16[256,1024]{1,0:T(8,128)(2,1)S(1)} %get-tuple-element.100.x0), channel_id=1, source_target_pairs={{0,1},{1,0},{2,3},{3,2},{4,5},{5,4},{6,7},{7,6},{8,9},{9,8},{10,11... | collective-permute-start | bytes 1572872 | tf_op jit(solution)/shard_map/ppermute | solution.py:698
  141.3 23.4 %collective-permute-start.17 = (bf16[256,1024]{1,0:T(8,128)(2,1)S(1)}, bf16[256,1024]{1,0:T(8,128)(2,1)S(1)}, u32[]{:S(2)}, u32[]{:S(2)}) collective-permute-start(bf16[256,1024]{1,0:T(8,128)(2,1)S(1)} %fusion.6), channel_id=1, source_target_pairs={{0,2},{1,3},{2,0},{3,1},{4,6},{5,7},{6,4},{7,5},{8,10},{9,11},{10,... | collective-permute-start | bytes 1572872 | tf_op jit(solution)/shard_map/ppermute | solution.py:698
  154.6 21.4 %collective-permute-start.21 = (bf16[256,1024]{1,0:T(8,128)(2,1)S(1)}, bf16[256,1024]{1,0:T(8,128)(2,1)}, u32[]{:S(2)}, u32[]{:S(2)}) collective-permute-start(bf16[256,1024]{1,0:T(8,128)(2,1)S(1)} %get-tuple-element.115.rest_0_), channel_id=1, source_target_pairs={{0,2},{1,3},{2,0},{3,1},{4,6},{5,7},{6,4},{7,5},{8,10},{9,11},{10,... | collective-permute-start | bytes 1572872 | tf_op jit(solution)/shard_map/ppermute | solution.py:698
  166.0 20.9 %collective-permute-start.24 = (bf16[256,1024]{1,0:T(8,128)(2,1)}, bf16[256,1024]{1,0:T(8,128)(2,1)}, u32[]{:S(2)}, u32[]{:S(2)}) collective-permute-start(bf16[256,1024]{1,0:T(8,128)(2,1)} %get-tuple-element.116.rest_4_), channel_id=1, source_target_pairs={{0,2},{1,3},{2,0},{3,1},{4,6},{5,7},{6,4},{7,5},{8,10},{9,11},{10,... | collective-permute-start | bytes 1572872 | tf_op jit(solution)/shard_map/ppermute | solution.py:698
  167.8 21.9 %collective-permute-start.20 = (bf16[256,1024]{1,0:T(8,128)(2,1)S(1)}, bf16[256,1024]{1,0:T(8,128)(2,1)S(1)}, u32[]{:S(2)}, u32[]{:S(2)}) collective-permute-start(bf16[256,1024]{1,0:T(8,128)(2,1)S(1)} %get-tuple-element.115.rest_0_), channel_id=1, source_target_pairs={{0,1},{1,0},{2,3},{3,2},{4,5},{5,4},{6,7},{7,6},{8,9},{9,8},{10,11... | collective-permute-start | bytes 1572872 | tf_op jit(solution)/shard_map/ppermute | solution.py:698
  167.8 23.1 %collective-permute-start.23 = (bf16[256,1024]{1,0:T(8,128)(2,1)}, bf16[256,1024]{1,0:T(8,128)(2,1)}, u32[]{:S(2)}, u32[]{:S(2)}) collective-permute-start(bf16[256,1024]{1,0:T(8,128)(2,1)} %get-tuple-element.116.rest_4_), channel_id=1, source_target_pairs={{0,1},{1,0},{2,3},{3,2},{4,5},{5,4},{6,7},{7,6},{8,9},{9,8},{10,11... | collective-permute-start | bytes 1572872 | tf_op jit(solution)/shard_map/ppermute | solution.py:698
  176.1 16.7 %collective-permute-start.22 = (bf16[256,1024]{1,0:T(8,128)(2,1)}, bf16[256,1024]{1,0:T(8,128)(2,1)}, u32[]{:S(2)}, u32[]{:S(2)}) collective-permute-start(bf16[256,1024]{1,0:T(8,128)(2,1)} %collective-permute-done.21.rest_2_), channel_id=1, source_target_pairs={{0,1},{1,0},{2,3},{3,2},{4,5},{5,4},{6,7},{7,6},{8,9},{9,8},{10,11... | collective-permute-start | bytes 1572872 | tf_op jit(solution)/shard_map/ppermute | solution.py:698
  188.0 17.5 %collective-permute-start.29 = (bf16[256,1024]{1,0:T(8,128)(2,1)}, bf16[256,1024]{1,0:T(8,128)(2,1)}, u32[]{:S(2)}, u32[]{:S(2)}) collective-permute-start(bf16[256,1024]{1,0:T(8,128)(2,1)} %get-tuple-element.217), channel_id=1, source_target_pairs={{0,2},{1,3},{2,0},{3,1},{4,6},{5,7},{6,4},{7,5},{8,10},{9,11},{10,... | collective-permute-start | bytes 1572872 | tf_op jit(solution)/shard_map/ppermute | solution.py:698
  190.5 23.7 %collective-permute-start.28 = (bf16[256,1024]{1,0:T(8,128)(2,1)}, bf16[256,1024]{1,0:T(8,128)(2,1)}, u32[]{:S(2)}, u32[]{:S(2)}) collective-permute-start(bf16[256,1024]{1,0:T(8,128)(2,1)} %get-tuple-element.216), channel_id=1, source_target_pairs={{0,2},{1,3},{2,0},{3,1},{4,6},{5,7},{6,4},{7,5},{8,10},{9,11},{10,... | collective-permute-start | bytes 1572872 | tf_op jit(solution)/shard_map/ppermute | solution.py:698
  190.9 28.5 %collective-permute-start.27 = (f32[2,256,128]{2,1,0:T(8,128)S(1)}, f32[2,256,128]{2,1,0:T(8,128)S(1)}, u32[]{:S(2)}, u32[]{:S(2)}) collective-permute-start(f32[2,256,128]{2,1,0:T(8,128)S(1)} %pad_maximum_fusion.9.rest_12_), channel_id=1, source_target_pairs={{0,2},{1,3},{2,0},{3,1},{4,6},{5,7},{6,4},{7,5},{8,10},{9,11},{10,... | collective-permute-start | bytes 786440 | tf_op jit(solution)/shard_map/ppermute | solution.py:698
  246.1 29.4 %collective-permute-start.37 = (bf16[2,256,1024]{2,1,0:T(8,128)(2,1)}, bf16[2,256,1024]{2,1,0:T(8,128)(2,1)}, u32[]{:S(2)}, u32[]{:S(2)}) collective-permute-start(bf16[2,256,1024]{2,1,0:T(8,128)(2,1)} %get-tuple-element.135), channel_id=1, source_target_pairs={{0,1},{1,0},{2,3},{3,2},{4,5},{5,4},{6,7},{7,6},{8,9},{9,8},{10,11... | collective-permute-start | bytes 3145736 | tf_op jit(solution)/shard_map/ppermute | solution.py:698
  264.7 25.8 %collective-permute-start.63 = (bf16[512,1024]{1,0:T(8,128)(2,1)}, bf16[512,1024]{1,0:T(8,128)(2,1)}, u32[]{:S(2)}, u32[]{:S(2)}) collective-permute-start(bf16[512,1024]{1,0:T(8,128)(2,1)} %constant_dynamic-slice_fusion.5), channel_id=1, source_target_pairs={{0,8},{4,12},{8,0},{12,4},{16,24},{20,28},{24,16},{28,20},{1,9},{5... | collective-permute-start | bytes 3145736 | tf_op jit(solution)/shard_map/ppermute | solution.py:698
  273.7 26.3 %collective-permute-start.69 = (bf16[512,1024]{1,0:T(8,128)(2,1)}, bf16[512,1024]{1,0:T(8,128)(2,1)}, u32[]{:S(2)}, u32[]{:S(2)}) collective-permute-start(bf16[512,1024]{1,0:T(8,128)(2,1)} %constant_dynamic-slice_fusion.2), channel_id=1, source_target_pairs={{0,4},{4,0},{8,12},{12,8},{16,20},{20,16},{24,28},{28,24},{1,5},{5... | collective-permute-start | bytes 3145736 | tf_op jit(solution)/shard_map/ppermute | solution.py:698
  275.4 26.5 %collective-permute-start.32 = (bf16[2,256,1024]{2,1,0:T(8,128)(2,1)}, bf16[2,256,1024]{2,1,0:T(8,128)(2,1)S(1)}, u32[]{:S(2)}, u32[]{:S(2)}) collective-permute-start(bf16[2,256,1024]{2,1,0:T(8,128)(2,1)} %copy-done.50), channel_id=1, source_target_pairs={{0,1},{1,0},{2,3},{3,2},{4,5},{5,4},{6,7},{7,6},{8,9},{9,8},{10,11... | collective-permute-start | bytes 3145736 | tf_op jit(solution)/shard_map/ppermute | solution.py:698
  276.8 27.2 %collective-permute-start.38 = (bf16[256,1024]{1,0:T(8,128)(2,1)S(1)}, bf16[256,1024]{1,0:T(8,128)(2,1)S(1)}, u32[]{:S(2)}, u32[]{:S(2)}) collective-permute-start(bf16[256,1024]{1,0:T(8,128)(2,1)S(1)} %fusion.9), channel_id=1, source_target_pairs={{0,2},{1,3},{2,0},{3,1},{4,6},{5,7},{6,4},{7,5},{8,10},{9,11},{10,... | collective-permute-start | bytes 1572872 | tf_op jit(solution)/shard_map/ppermute | solution.py:698
  292.5 17.8 %collective-permute-start.64 = (bf16[256,1024]{1,0:T(8,128)(2,1)S(1)}, bf16[256,1024]{1,0:T(8,128)(2,1)S(1)}, u32[]{:S(2)}, u32[]{:S(2)}) collective-permute-start(bf16[256,1024]{1,0:T(8,128)(2,1)S(1)} %constant_dynamic-slice_fusion.4), channel_id=1, source_target_pairs={{0,4},{4,0},{8,12},{12,8},{16,20},{20,16},{24,28},{28,24},{1,5},{5... | collective-permute-start | bytes 1572872 | tf_op jit(solution)/shard_map/ppermute | solution.py:698
  302.1 29.7 %collective-permute-start.33 = (bf16[256,1024]{1,0:T(8,128)(2,1)S(1)}, bf16[256,1024]{1,0:T(8,128)(2,1)S(1)}, u32[]{:S(2)}, u32[]{:S(2)}) collective-permute-start(bf16[256,1024]{1,0:T(8,128)(2,1)S(1)} %fusion.8), channel_id=1, source_target_pairs={{0,2},{1,3},{2,0},{3,1},{4,6},{5,7},{6,4},{7,5},{8,10},{9,11},{10,... | collective-permute-start | bytes 1572872 | tf_op jit(solution)/shard_map/ppermute | solution.py:698
  306.1 36.2 %collective-permute-start.40 = (bf16[256,1024]{1,0:T(8,128)(2,1)S(1)}, bf16[256,1024]{1,0:T(8,128)(2,1)S(1)}, u32[]{:S(2)}, u32[]{:S(2)}) collective-permute-start(bf16[256,1024]{1,0:T(8,128)(2,1)S(1)} %get-tuple-element.136.x0), channel_id=1, source_target_pairs={{0,2},{1,3},{2,0},{3,1},{4,6},{5,7},{6,4},{7,5},{8,10},{9,11},{10,... | collective-permute-start | bytes 1572872 | tf_op jit(solution)/shard_map/ppermute | solution.py:698
  310.5 20.5 %collective-permute-start.65 = (bf16[128,1024]{1,0:T(8,128)(2,1)S(1)}, bf16[128,1024]{1,0:T(8,128)(2,1)S(1)}, u32[]{:S(2)}, u32[]{:S(2)}) collective-permute-start(bf16[128,1024]{1,0:T(8,128)(2,1)S(1)} %constant_dynamic-slice_fusion.3), channel_id=1, source_target_pairs={{0,16},{4,20},{8,24},{12,28},{16,0},{20,4},{24,8},{28,12},{1,17},{... | collective-permute-start | bytes 786440 | tf_op jit(solution)/shard_map/ppermute | solution.py:698
  314.6 27.6 %collective-permute-start.71 = (bf16[128,1024]{1,0:T(8,128)(2,1)S(1)}, bf16[128,1024]{1,0:T(8,128)(2,1)S(1)}, u32[]{:S(2)}, u32[]{:S(2)}) collective-permute-start(bf16[128,1024]{1,0:T(8,128)(2,1)S(1)} %constant_dynamic-slice_fusion), channel_id=1, source_target_pairs={{0,16},{4,20},{8,24},{12,28},{16,0},{20,4},{24,8},{28,12},{1,17},{... | collective-permute-start | bytes 786440 | tf_op jit(solution)/shard_map/ppermute | solution.py:698
  331.0 21.9 %collective-permute-start.66 = (bf16[128,1024]{1,0:T(8,128)(2,1)S(1)}, bf16[128,1024]{1,0:T(8,128)(2,1)S(1)}, u32[]{:S(2)}, u32[]{:S(2)}) collective-permute-start(bf16[128,1024]{1,0:T(8,128)(2,1)S(1)} %add_convert_fusion.15), channel_id=1, source_target_pairs={{0,16},{4,20},{8,24},{12,28},{16,0},{20,4},{24,8},{28,12},{1,17},{... | collective-permute-start | bytes 786440 | tf_op jit(solution)/shard_map/ppermute | solution.py:698
  332.9 37.3 %collective-permute-start.34 = (bf16[256,1024]{1,0:T(8,128)(2,1)S(1)}, bf16[256,1024]{1,0:T(8,128)(2,1)S(1)}, u32[]{:S(2)}, u32[]{:S(2)}) collective-permute-start(bf16[256,1024]{1,0:T(8,128)(2,1)S(1)} %get-tuple-element.130.x0), channel_id=1, source_target_pairs={{0,1},{1,0},{2,3},{3,2},{4,5},{5,4},{6,7},{7,6},{8,9},{9,8},{10,11... | collective-permute-start | bytes 1572872 | tf_op jit(solution)/shard_map/ppermute | solution.py:698
  333.0 20.9 %collective-permute-start.35 = (bf16[256,1024]{1,0:T(8,128)(2,1)S(1)}, bf16[256,1024]{1,0:T(8,128)(2,1)S(1)}, u32[]{:S(2)}, u32[]{:S(2)}) collective-permute-start(bf16[256,1024]{1,0:T(8,128)(2,1)S(1)} %get-tuple-element.130.x0), channel_id=1, source_target_pairs={{0,2},{1,3},{2,0},{3,1},{4,6},{5,7},{6,4},{7,5},{8,10},{9,11},{10,... | collective-permute-start | bytes 1572872 | tf_op jit(solution)/shard_map/ppermute | solution.py:698
  342.2 16.9 %collective-permute-start.39 = (bf16[256,1024]{1,0:T(8,128)(2,1)S(1)}, bf16[256,1024]{1,0:T(8,128)(2,1)S(1)}, u32[]{:S(2)}, u32[]{:S(2)}) collective-permute-start(bf16[256,1024]{1,0:T(8,128)(2,1)S(1)} %get-tuple-element.136.x0), channel_id=1, source_target_pairs={{0,1},{1,0},{2,3},{3,2},{4,5},{5,4},{6,7},{7,6},{8,9},{9,8},{10,11... | collective-permute-start | bytes 1572872 | tf_op jit(solution)/shard_map/ppermute | solution.py:698
  342.3 15.8 %collective-permute-start.72 = (bf16[128,1024]{1,0:T(8,128)(2,1)S(1)}, bf16[128,1024]{1,0:T(8,128)(2,1)S(1)}, u32[]{:S(2)}, u32[]{:S(2)}) collective-permute-start(bf16[128,1024]{1,0:T(8,128)(2,1)S(1)} %add_convert_fusion.14), channel_id=1, source_target_pairs={{0,16},{4,20},{8,24},{12,28},{16,0},{20,4},{24,8},{28,12},{1,17},{... | collective-permute-start | bytes 786440 | tf_op jit(solution)/shard_map/ppermute | solution.py:698
  353.9 48.2 %collective-permute-start.67 = (bf16[256,1024]{1,0:T(8,128)(2,1)}, bf16[256,1024]{1,0:T(8,128)(2,1)}, u32[]{:S(2)}, u32[]{:S(2)}) collective-permute-start(bf16[256,1024]{1,0:T(8,128)(2,1)} %pad_maximum_fusion.7), channel_id=1, source_target_pairs={{0,4},{4,0},{8,12},{12,8},{16,20},{20,16},{24,28},{28,24},{1,5},{5... | collective-permute-start | bytes 1572872 | tf_op jit(solution)/shard_map/ppermute | solution.py:698
  359.1 46.1 %collective-permute-start.73 = (bf16[256,1024]{1,0:T(8,128)(2,1)}, bf16[256,1024]{1,0:T(8,128)(2,1)}, u32[]{:S(2)}, u32[]{:S(2)}) collective-permute-start(bf16[256,1024]{1,0:T(8,128)(2,1)} %pad_maximum_fusion.8), channel_id=1, source_target_pairs={{0,8},{4,12},{8,0},{12,4},{16,24},{20,28},{24,16},{28,20},{1,9},{5... | collective-permute-start | bytes 1572872 | tf_op jit(solution)/shard_map/ppermute | solution.py:698
  384.3 82.7 %collective-permute-start.42 = (bf16[2,256,1024]{2,1,0:T(8,128)(2,1)}, bf16[2,256,1024]{2,1,0:T(8,128)(2,1)S(1)}, u32[]{:S(2)}, u32[]{:S(2)}) collective-permute-start(bf16[2,256,1024]{2,1,0:T(8,128)(2,1)} %get-tuple-element.144), channel_id=1, source_target_pairs={{0,1},{1,0},{2,3},{3,2},{4,5},{5,4},{6,7},{7,6},{8,9},{9,8},{10,11... | collective-permute-start | bytes 3145736 | tf_op jit(solution)/shard_map/ppermute | solution.py:698
  384.8 85.5 %collective-permute-start.44 = (bf16[2,256,1024]{2,1,0:T(8,128)(2,1)}, bf16[2,256,1024]{2,1,0:T(8,128)(2,1)}, u32[]{:S(2)}, u32[]{:S(2)}) collective-permute-start(bf16[2,256,1024]{2,1,0:T(8,128)(2,1)} %get-tuple-element.147), channel_id=1, source_target_pairs={{0,1},{1,0},{2,3},{3,2},{4,5},{5,4},{6,7},{7,6},{8,9},{9,8},{10,11... | collective-permute-start | bytes 3145736 | tf_op jit(solution)/shard_map/ppermute | solution.py:698
  402.1 14.9 %collective-permute-start.51 = (bf16[512,512]{0,1:T(8,128)(2,1)S(1)}, bf16[512,512]{0,1:T(8,128)(2,1)S(1)}, u32[]{:S(2)}, u32[]{:S(2)}) collective-permute-start(bf16[512,512]{0,1:T(8,128)(2,1)S(1)} %fusion.18), channel_id=1, source_target_pairs={{0,4},{4,0},{8,12},{12,8},{16,20},{20,16},{24,28},{28,24},{1,5},{5... | collective-permute-start | bytes 1572872 | tf_op jit(solution)/shard_map/ppermute | solution.py:698
  405.1 68.0 %collective-permute-start.68 = (bf16[512,1024]{1,0:T(8,128)(2,1)S(1)}, bf16[512,1024]{1,0:T(8,128)(2,1)S(1)}, u32[]{:S(2)}, u32[]{:S(2)}) collective-permute-start(bf16[512,1024]{1,0:T(8,128)(2,1)S(1)} %pad_maximum_fusion.1), channel_id=1, source_target_pairs={{0,8},{4,12},{8,0},{12,4},{16,24},{20,28},{24,16},{28,20},{1,9},{5... | collective-permute-start | bytes 3145736 | tf_op jit(solution)/shard_map/ppermute | solution.py:698
  412.1 64.6 %collective-permute-start.74 = (bf16[512,1024]{1,0:T(8,128)(2,1)S(1)}, bf16[512,1024]{1,0:T(8,128)(2,1)S(1)}, u32[]{:S(2)}, u32[]{:S(2)}) collective-permute-start(bf16[512,1024]{1,0:T(8,128)(2,1)S(1)} %pad_maximum_fusion.2), channel_id=1, source_target_pairs={{0,4},{4,0},{8,12},{12,8},{16,20},{20,16},{24,28},{28,24},{1,5},{5... | collective-permute-start | bytes 3145736 | tf_op jit(solution)/shard_map/ppermute | solution.py:698
  417.0 27.0 %collective-permute-start.58 = (bf16[256,512]{0,1:T(8,128)(2,1)S(1)}, bf16[256,512]{0,1:T(8,128)(2,1)S(1)}, u32[]{:S(2)}, u32[]{:S(2)}) collective-permute-start(bf16[256,512]{0,1:T(8,128)(2,1)S(1)} %constant_dynamic-slice_fusion.7), channel_id=1, source_target_pairs={{0,4},{4,0},{8,12},{12,8},{16,20},{20,16},{24,28},{28,24},{1,5},{5... | collective-permute-start | bytes 786440 | tf_op jit(solution)/shard_map/ppermute | solution.py:698
  470.3 22.1 %collective-permute-start.43 = (bf16[256,1024]{1,0:T(8,128)(2,1)S(1)}, bf16[256,1024]{1,0:T(8,128)(2,1)S(1)}, u32[]{:S(2)}, u32[]{:S(2)}) collective-permute-start(bf16[256,1024]{1,0:T(8,128)(2,1)S(1)} %fusion.10), channel_id=1, source_target_pairs={{0,2},{1,3},{2,0},{3,1},{4,6},{5,7},{6,4},{7,5},{8,10},{9,11},{10,... | collective-permute-start | bytes 1572872 | tf_op jit(solution)/shard_map/ppermute | solution.py:698
  473.2 16.3 %collective-permute-start.45 = (bf16[256,1024]{1,0:T(8,128)(2,1)S(1)}, bf16[256,1024]{1,0:T(8,128)(2,1)S(1)}, u32[]{:S(2)}, u32[]{:S(2)}) collective-permute-start(bf16[256,1024]{1,0:T(8,128)(2,1)S(1)} %fusion.11), channel_id=1, source_target_pairs={{0,2},{1,3},{2,0},{3,1},{4,6},{5,7},{6,4},{7,5},{8,10},{9,11},{10,... | collective-permute-start | bytes 1572872 | tf_op jit(solution)/shard_map/ppermute | solution.py:698
  479.8 16.2 %collective-permute-start.61 = (bf16[256,512]{0,1:T(8,128)(2,1)S(1)}, bf16[256,512]{0,1:T(8,128)(2,1)S(1)}, u32[]{:S(2)}, u32[]{:S(2)}) collective-permute-start(bf16[256,512]{0,1:T(8,128)(2,1)S(1)} %pad_maximum_fusion.11), channel_id=1, source_target_pairs={{0,4},{4,0},{8,12},{12,8},{16,20},{20,16},{24,28},{28,24},{1,5},{5... | collective-permute-start | bytes 786440 | tf_op jit(solution)/shard_map/ppermute | solution.py:698
  481.5 21.7 %collective-permute-start.55 = (bf16[256,512]{0,1:T(8,128)(2,1)S(1)}, bf16[256,512]{0,1:T(8,128)(2,1)S(1)}, u32[]{:S(2)}, u32[]{:S(2)}) collective-permute-start(bf16[256,512]{0,1:T(8,128)(2,1)S(1)} %pad_maximum_fusion.10), channel_id=1, source_target_pairs={{0,8},{4,12},{8,0},{12,4},{16,24},{20,28},{24,16},{28,20},{1,9},{5... | collective-permute-start | bytes 786440 | tf_op jit(solution)/shard_map/ppermute | solution.py:698
  498.7 15.3 %collective-permute-start.62 = (bf16[512,512]{0,1:T(8,128)(2,1)S(1)}, bf16[512,512]{0,1:T(8,128)(2,1)S(1)}, u32[]{:S(2)}, u32[]{:S(2)}) collective-permute-start(bf16[512,512]{0,1:T(8,128)(2,1)S(1)} %pad_maximum_fusion.6), channel_id=1, source_target_pairs={{0,8},{4,12},{8,0},{12,4},{16,24},{20,28},{24,16},{28,20},{1,9},{5... | collective-permute-start | bytes 1572872 | tf_op jit(solution)/shard_map/ppermute | solution.py:698
  (114 other events, 1434.0 us)

commit v2 on v1

v2 whole, which is shorter than its diff:
```python
import functools
import math

import jax
import jax.numpy as jnp
from jax import lax
from jax.experimental import pallas as pl
from jax.experimental.pallas import tpu as pltpu
from jax.sharding import PartitionSpec as P

HEADS = 8
NORM_EPS = 1e-05
CONTRAST_SCALE = 32.0
CONTRAST_WEIGHT = 64.0
NEGATIVE = -1e30
LOG2E = math.log2(math.e)
F32 = jnp.float32
BF16 = jnp.bfloat16
MIB = 1 << 20
LIMIT, SMALL = 40, 16
COST = 0.02
NN = (((1,), (0,)), ((), ()))
NT = (((1,), (1,)), ((), ()))
TN = (((0,), (0,)), ((), ()))
VMEM = pltpu.VMEM


def dot(a, b, dims=NN):
    return lax.dot_general(a, b, dims, preferred_element_type=F32)


def whole(shape):
    return pl.BlockSpec(shape, lambda *_: (0,) * len(shape))


def kernel_call(body, outs, out_specs, in_specs, grid=(1,), scratch=(), flops=0, nbytes=0, trans=0,
                limit=LIMIT, aliases=None, prefetch=0, name=None):
    return pl.pallas_call(
        body,
        out_shape=outs,
        grid_spec=pltpu.PrefetchScalarGridSpec(
            num_scalar_prefetch=prefetch,
            grid=grid,
            in_specs=in_specs,
            out_specs=out_specs,
            scratch_shapes=scratch,
        ),
        name=name,
        input_output_aliases=aliases or {},
        cost_estimate=pl.CostEstimate(
            flops=int(flops * COST), bytes_accessed=int(nbytes * COST), transcendentals=int(trans * COST)
        ),
        compiler_params=pltpu.CompilerParams(vmem_limit_bytes=limit * MIB),
    )


def struct(shape, dtype):
    return jax.ShapeDtypeStruct(shape, dtype)


ANY = pl.BlockSpec(memory_space=pl.ANY)
HBM = pl.BlockSpec(memory_space=pltpu.HBM)
DMA = pltpu.SemaphoreType.DMA


def move(src, dst, sem):
    copy = pltpu.make_async_copy(src, dst, sem)
    copy.start()
    return copy


def column(row):
    return jnp.transpose(jnp.broadcast_to(row, (8, row.shape[1])))[:, :1]


def norm_stats(v):
    centered = v - jnp.mean(v, axis=-1, keepdims=True)
    rstd = lax.rsqrt(jnp.mean(centered * centered, axis=-1, keepdims=True) + NORM_EPS)
    return centered * rstd, rstd


ROW_STEPS = 4


def row_blocks(rows, cols):
    return pl.BlockSpec((rows // ROW_STEPS, cols), lambda i: (i, 0))


def first_norm(seq, tokens, tables, gain, shift):
    rows, feats = tokens.shape[1:]
    fine = tables[2].shape[0]
    step = rows // ROW_STEPS

    def body(tok, pa, qa, cb, sb, g, b, h_out, a_out):
        i = pl.program_id(0)
        for c in range(step // fine):
            at = pl.ds(c * fine, fine)
            row = pl.ds(i * (step // fine) + c, 1)
            pos = pa[row, :] * cb[...] + qa[row, :] * sb[...]
            h = tok[0, at, :].astype(F32) + pos
            h_out[at, :] = h
            z, _ = norm_stats(h)
            a_out[at, :] = (z * g[...] + b[...]).astype(BF16)

    return kernel_call(
        body,
        (struct((rows, feats), F32), struct((rows, feats), BF16)),
        (row_blocks(rows, feats), row_blocks(rows, feats)),
        [pl.BlockSpec((1, step, feats), lambda i: (seq, i, 0))]
        + [whole(t.shape) for t in tables]
        + [whole((1, feats))] * 2,
        grid=(ROW_STEPS,),
        nbytes=rows * feats * 8,
        limit=SMALL,
        name="first_norm",
    )(tokens, *tables, gain, shift)


def joined(parts, at):
    return functools.reduce(jnp.add, [p[at, :].astype(F32) for p in parts])


def second_norm(h, parts, offset, gain, shift):
    rows, feats = h.shape
    chunk = 32
    step = rows // ROW_STEPS

    def body(h_ref, k_ref, c_ref, x_ref, o_ref, g, b, r_out, n_out):
        for c in range(step // chunk):
            at = pl.ds(c * chunk, chunk)
            r = h_ref[at, :] + joined((k_ref, c_ref, x_ref), at) + o_ref[...]
            r_out[at, :] = r
            z, _ = norm_stats(r)
            n_out[at, :] = (z * g[...] + b[...]).astype(BF16)

    block = row_blocks(rows, feats)
    return kernel_call(
        body,
        (struct((rows, feats), F32), struct((rows, feats), BF16)),
        (block, block),
        [block] * 4 + [whole((1, feats))] * 3,
        grid=(ROW_STEPS,),
        nbytes=rows * feats * 16,
        limit=SMALL,
        name="second_norm",
    )(h, *parts, offset, gain, shift)


EXTRA = 16


def output_rows(seq, seqs, r1, parts, offset, previous):
    rows, feats = r1.shape
    step, chunk = 128, 32

    def body(r_ref, k_ref, c_ref, x_ref, o_ref, *rest):
        act_out, n_out, q_all = rest[-3:]
        i = pl.program_id(0)
        for c in range(step // chunk):
            at = pl.ds(c * chunk, chunk)
            y = r_ref[at, :] + joined((k_ref, c_ref, x_ref), at) + o_ref[...]
            act_out[0, at, :] = y.astype(BF16)
            q = lax.rsqrt(jnp.mean(y * y, axis=-1, keepdims=True) + NORM_EPS)
            n_out[pl.ds(pl.multiple_of(i * step + c * chunk, chunk), chunk), :] = (y * q).astype(BF16)
            q_all[at, :] = jnp.broadcast_to(q, (chunk, step))

        @pl.when(i == 0)
        def _():
            n_out[rows:, :] = jnp.zeros((EXTRA, feats), BF16)

        row = jnp.transpose(q_all[...])[:EXTRA, :]
        high = row.astype(BF16).astype(F32)
        which = lax.broadcasted_iota(jnp.int32, (EXTRA, step), 0)
        lanes = pl.ds(pl.multiple_of(i * step, step), step)
        n_out[rows:, lanes] = jnp.where(which == 0, high, jnp.where(which == 1, row - high, 0.0)).astype(BF16)

    block = pl.BlockSpec((step, feats), lambda i: (i, 0))
    extra = [] if previous is None else [previous]
    return kernel_call(
        body,
        (struct((seqs, rows, feats), BF16), struct((rows + EXTRA, feats), BF16)),
        (pl.BlockSpec((1, step, feats), lambda i: (seq, i, 0)), whole((rows + EXTRA, feats))),
        [block] * 4 + [whole((1, feats))] + [ANY] * len(extra),
        grid=(rows // step,),
        scratch=[VMEM((step, step), F32)],
        nbytes=rows * feats * 14,
        aliases={5: 0} if extra else None,
        limit=SMALL,
        name="output_rows",
    )(r1, *parts, offset, *extra)


def norm_backward(seq, seqs, v, parts, gain, base, final, previous):
    rows, feats = v.shape
    chunk = 16
    step = rows // ROW_STEPS

    def body(v_ref, k_ref, c_ref, x_ref, g, base_ref, *rest):
        if final:
            out, sums = rest[-2:]
        else:
            out, low, sums = rest[-3:]
        acc = [jnp.zeros((8, feats), F32) for _ in range(2 if final else 4)]
        for c in range(step // chunk):
            at = pl.ds(c * chunk, chunk)
            got = joined((k_ref, c_ref, x_ref), at)
            z, rstd = norm_stats(v_ref[at, :])
            w = got * g[...]
            inner = rstd * (w - jnp.mean(w, axis=-1, keepdims=True) - z * jnp.mean(w * z, axis=-1, keepdims=True))
            old = base_ref[at, :] if final else base_ref[0, at, :]
            new = old + inner
            if final:
                out[0, at, :] = new
            else:
                out[at, :] = new
                low[at, :] = new.astype(BF16)
            terms = [got * z, got] + ([] if final else [new, old])
            for k, term in enumerate(terms):
                acc[k] = acc[k] + jnp.sum(term.reshape(chunk // 8, 8, feats), axis=0)

        @pl.when(pl.program_id(0) == 0)
        def _():
            sums[...] = jnp.zeros_like(sums)

        for k, term in enumerate(acc):
            sums[k : k + 1, :] += jnp.sum(term, axis=0, keepdims=True)

    block = row_blocks(rows, feats)
    extra = [] if previous is None else [previous]
    seq_block = pl.BlockSpec((1, step, feats), lambda i: (seq, i, 0))
    if final:
        outs, specs = (struct((seqs, rows, feats), F32), struct((4, feats), F32)), (seq_block, whole((4, feats)))
    else:
        outs = (struct((rows, feats), F32), struct((rows, feats), BF16), struct((4, feats), F32))
        specs = (block, block, whole((4, feats)))
    return kernel_call(
        body,
        outs,
        specs,
        [block] * 4 + [whole((1, feats)), block if final else seq_block] + [ANY] * len(extra),
        grid=(ROW_STEPS,),
        nbytes=rows * feats * 20,
        aliases={6: 0} if extra else None,
        limit=SMALL,
        name="norm_backward",
    )(v, *parts, gain, base, *extra)


def send_block(refs, rel, src, sems):
    for r, ref in enumerate(refs):

        @pl.when(rel == r)
        def _(r=r, ref=ref):
            pltpu.make_async_copy(src, ref, sems.at[r]).start()


def wait_blocks(refs, src, sems):
    for r, ref in enumerate(refs):
        pltpu.make_async_copy(src, ref, sems.at[r]).wait()


def lane_pair(first, second, rows):
    lanes = lax.broadcasted_iota(jnp.int32, (rows, 128), 1)
    return jnp.where(lanes == 0, first, second)


def attend_forward(seq, seqs, place, docs_row, blocks, wqkv, q_shift, v_shift, wo, previous):
    rows, feats = blocks[0].shape
    parts = len(blocks)
    length = rows * parts
    width = wqkv.shape[2]
    size = feats // HEADS
    heads = width // size
    scale = LOG2E * size ** (-0.5)

    def body(t_ref, dr, qb, vb, *rest):
        x_refs, (w_ref, wo_ref), rest = rest[:4], rest[4:6], rest[6:]
        p_refs, (cat, qkv_out, att_out, lse_out), rest = rest[-19:-15], rest[-15:-11], rest[-11:]
        xs, w, wov, qkv, att, lse, ps, in_sem, p_sem, c_sem, o_sem = rest
        t = t_ref[0]
        load_w = move(w_ref, w, in_sem.at[4])
        for r in range(parts):
            at = lax.bitwise_xor(jnp.int32(r), t)
            move(x_refs[r], xs.at[at], in_sem.at[at])
        load_wo = move(wo_ref, wov, in_sem.at[5])
        pending = []

        def project(i):
            pltpu.make_async_copy(x_refs[0], xs.at[i], in_sem.at[i]).wait()
            rel = lax.bitwise_xor(jnp.int32(i), t)
            pending.append(move(xs.at[i], cat.at[seq, pl.ds(pl.multiple_of(rel * rows, rows), rows)], c_sem.at[i]))
            x = xs[i]
            at = slice(i * rows, (i + 1) * rows)
            qkv[0, at, :] = (dot(x, w[0]) + qb[...]).astype(BF16)
            qkv[1, at, :] = dot(x, w[1]).astype(BF16)
            qkv[2, at, :] = (dot(x, w[2]) + vb[...]).astype(BF16)

        load_w.wait()
        project(0)
        load_wo.wait()
        for i in range(parts):
            if i + 1 < parts:
                project(i + 1)
            span = (i + 1) * rows
            own = slice(i * rows, span)
            same = column(dr[:, own]) == dr[:, :span]
            before = lax.broadcasted_iota(jnp.int32, (rows, span), 0) + i * rows >= lax.broadcasted_iota(
                jnp.int32, (rows, span), 1
            )
            allowed = same & before
            logs = []
            for hd in range(heads):
                cols = slice(hd * size, (hd + 1) * size)
                s = jnp.where(allowed, dot(qkv[0, own, cols], qkv[1, :span, cols], NT) * scale, NEGATIVE)
                top = jnp.max(s, axis=-1, keepdims=True)
                e = jnp.exp2(s - top)
                total = jnp.sum(e, axis=-1, keepdims=True)
                att[i, :, cols] = (dot(e.astype(BF16), qkv[2, :span, cols]) / total).astype(BF16)
                logs.append(top + jnp.log2(total))
            lse[own, :] = lane_pair(logs[0], logs[-1], rows)
            ps[i] = dot(att[i], wov[...]).astype(BF16)
            rel = lax.bitwise_xor(jnp.int32(i), t)
            send_block(p_refs, rel, ps.at[i], p_sem)
            pending.append(
                move(att.at[i], att_out.at[seq, pl.ds(pl.multiple_of(rel * rows, rows), rows)], o_sem.at[i])
            )
        pending.append(move(qkv, qkv_out, in_sem.at[4]))
        pending.append(move(lse, lse_out, in_sem.at[5]))
        for copy in pending:
            copy.wait()
        wait_blocks(p_refs, ps.at[0], p_sem)

    extra = [] if previous is None else list(previous)
    return kernel_call(
        body,
        (
            *[struct((rows, feats), BF16)] * 4,
            struct((seqs, length, feats), BF16),
            struct((3, length, width), BF16),
            struct((seqs, length, width), BF16),
            struct((length, 128), F32),
        ),
        (ANY,) * 4 + (HBM,) * 4,
        [pl.BlockSpec(memory_space=pltpu.SMEM), whole((1, length)), whole((1, width)), whole((1, width))]
        + [ANY] * 4
        + [HBM] * (2 + len(extra)),
        scratch=[
            VMEM((parts, rows, feats), BF16),
            VMEM(wqkv.shape, BF16),
            VMEM(wo.shape, BF16),
            VMEM((3, length, width), BF16),
            VMEM((parts, rows, width), BF16),
            VMEM((length, 128), F32),
            VMEM((parts, rows, feats), BF16),
            DMA((6,)),
            DMA((4,)),
            DMA((4,)),
            DMA((4,)),
        ],
        flops=2 * length * feats * width * 4 + 5 * length * length * width,
        nbytes=length * feats * 8,
        trans=length * length * heads // 2,
        aliases={10: 4, 11: 6} if extra else None,
        name="attend_forward",
    )(place, docs_row, q_shift, v_shift, *blocks, wqkv, wo, *extra)


def attend_backward(seq, seqs, place, docs_row, blocks, qkv, att, lse, wqkv, wo, previous):
    rows, feats = blocks[0].shape
    parts = len(blocks)
    length = rows * parts
    width = wqkv.shape[2]
    size = feats // HEADS
    heads = width // size
    root = size ** (-0.5)
    scale = LOG2E * root

    def body(t_ref, dr, *rest):
        x_refs, (qkv_ref, att_ref, lse_ref, w_ref, wo_ref), rest = rest[:4], rest[4:9], rest[9:]
        p_refs, (cat, gq_out, gk_out, gv_out, sums), rest = rest[-23:-19], rest[-19:-14], rest[-14:]
        xs, w, wov, qkvv, attv, lsev, gk, gv, ga, low, ps, in_sem, p_sem, o_sem = rest
        t = t_ref[0]
        load_wo = move(wo_ref, wov, in_sem.at[4])
        for r in (3, 2, 1, 0):
            at = lax.bitwise_xor(jnp.int32(r), t)
            move(x_refs[r], xs.at[at], in_sem.at[at])
        loads = [move(qkv_ref, qkvv, in_sem.at[5]), move(lse_ref, lsev, in_sem.at[6])]
        for i in range(parts):
            rel = lax.bitwise_xor(jnp.int32(i), t)
            at = pl.ds(pl.multiple_of(rel * rows, rows), rows)
            loads.append(move(att_ref.at[seq, at], attv.at[i], in_sem.at[8 + i]))
        load_w = move(w_ref, w, in_sem.at[7])
        pending = []

        def project(i):
            pltpu.make_async_copy(x_refs[0], xs.at[i], in_sem.at[i]).wait()
            rel = lax.bitwise_xor(jnp.int32(i), t)
            pending.append(
                move(xs.at[i], cat.at[seq, pl.ds(pl.multiple_of(rel * rows, rows), rows)], o_sem.at[i])
            )
            ga[i] = dot(xs[i], wov[...], NT).astype(BF16)

        load_wo.wait()
        project(parts - 1)
        for copy in loads:
            copy.wait()
        load_w.wait()
        q_sum = jnp.zeros((1, width), F32)
        v_sum = jnp.zeros((1, width), F32)
        for i in reversed(range(parts)):
            if i:
                project(i - 1)
            span = (i + 1) * rows
            own = slice(i * rows, span)
            same = column(dr[:, own]) == dr[:, :span]
            before = lax.broadcasted_iota(jnp.int32, (rows, span), 0) + i * rows >= lax.broadcasted_iota(
                jnp.int32, (rows, span), 1
            )
            allowed = same & before
            for hd in range(heads):
                cols = slice(hd * size, (hd + 1) * size)
                q = qkvv[0, own, cols]
                k = qkvv[1, :span, cols]
                g = ga[i, :, cols]
                s = dot(q, k, NT) * scale - lsev[own, hd : hd + 1]
                p = jnp.exp2(jnp.where(allowed, s, NEGATIVE))
                gp = dot(g, qkvv[2, :span, cols], NT)
                row = jnp.sum(g.astype(F32) * attv[i, :, cols].astype(F32), axis=-1, keepdims=True)
                gs = (p * (gp - row)).astype(BF16)
                low[0, own, cols] = (dot(gs, k) * root).astype(BF16)
                new_k = dot(gs, q, TN)
                new_v = dot(p.astype(BF16), g, TN)
                if i == parts - 1:
                    gk[:span, cols] = new_k
                    gv[:span, cols] = new_v
                else:
                    gk[:span, cols] += new_k
                    gv[:span, cols] += new_v
            low[1, own, :] = (gk[own, :] * root).astype(BF16)
            low[2, own, :] = gv[own, :].astype(BF16)
            q_sum += jnp.sum(low[0, own, :].astype(F32), axis=0, keepdims=True)
            v_sum += jnp.sum(low[2, own, :].astype(F32), axis=0, keepdims=True)
            ps[i] = (
                dot(low[0, own, :], w[0], NT) + dot(low[1, own, :], w[1], NT) + dot(low[2, own, :], w[2], NT)
            ).astype(BF16)
            rel = lax.bitwise_xor(jnp.int32(i), t)
            send_block(p_refs, rel, ps.at[i], p_sem)
            at = pl.ds(pl.multiple_of(rel * rows, rows), rows)
            for c, out in enumerate((gq_out, gk_out, gv_out)):
                pending.append(move(low.at[c, own], out.at[seq, at], o_sem.at[4 + 3 * i + c]))
        sums[0:1, :] = q_sum
        sums[1:2, :] = v_sum
        for copy in pending:
            copy.wait()
        wait_blocks(p_refs, ps.at[0], p_sem)

    extra = [] if previous is None else list(previous)
    return kernel_call(
        body,
        (
            *[struct((rows, feats), BF16)] * 4,
            struct((seqs, length, feats), BF16),
            *[struct((seqs, length, width), BF16)] * 3,
            struct((2, width), F32),
        ),
        (ANY,) * 4 + (HBM,) * 4 + (whole((2, width)),),
        [pl.BlockSpec(memory_space=pltpu.SMEM), whole((1, length))] + [ANY] * 4 + [HBM] * (5 + len(extra)),
        scratch=[
            VMEM((parts, rows, feats), BF16),
            VMEM(wqkv.shape, BF16),
            VMEM(wo.shape, BF16),
            VMEM((3, length, width), BF16),
            VMEM((parts, rows, width), BF16),
            VMEM((length, 128), F32),
            VMEM((length, width), F32),
            VMEM((length, width), F32),
            VMEM((parts, rows, width), BF16),
            VMEM((3, length, width), BF16),
            VMEM((parts, rows, feats), BF16),
            DMA((12,)),
            DMA((4,)),
            DMA((16,)),
        ],
        flops=2 * length * feats * width * 4 + 10 * length * length * width,
        nbytes=length * feats * 8,
        trans=length * length * heads // 2,
        aliases={11: 4, 12: 5, 13: 6, 14: 7} if extra else None,
        name="attend_backward",
    )(place, docs_row, *blocks, qkv, att, lse, wqkv, wo, *extra)


ORDER = (3, 1, 2, 0)


def feed_forward(seq, seqs, blocks, w_up, b_up, w_down, previous):
    rows, feats = blocks[0].shape
    parts = len(blocks)
    length = rows * parts
    units = w_up.shape[1]
    root = math.sqrt(2.0 / math.pi)

    def body(bu, *rest):
        x_refs, (up_ref, down_ref), rest = rest[:4], rest[4:6], rest[6:]
        p_refs, (cat, act_out, slope_out), rest = rest[-17:-13], rest[-13:-10], rest[-10:]
        xs, up, down, u, act, slope, ps, in_sem, p_sem, o_sem = rest
        load_up = move(up_ref, up, in_sem.at[4])
        loads = {r: move(x_refs[r], xs.at[r], in_sem.at[r]) for r in ORDER}
        load_down = move(down_ref, down, in_sem.at[5])
        pending = []

        def project(k):
            r = ORDER[k]
            loads[r].wait()
            pending.append(move(xs.at[r], cat.at[seq, pl.ds(r * rows, rows)], o_sem.at[r]))
            u[k % 2] = dot(xs[r], up[...]) + bu[...]

        load_up.wait()
        project(0)
        load_down.wait()
        for k, r in enumerate(ORDER):
            if k + 1 < parts:
                project(k + 1)
            v = u[k % 2]
            sq = v * v
            th = jnp.tanh(v * (root + (root * 0.044715) * sq))
            half = 0.5 + 0.5 * th
            g = (v * half).astype(BF16)
            act[r] = g
            slope[r] = (half + v * (1.0 - th * th) * (0.5 * root + (1.5 * 0.044715 * root) * sq)).astype(BF16)
            ps[r] = dot(g, down[...]).astype(BF16)
            at = pl.ds(r * rows, rows)
            pending.append(move(ps.at[r], p_refs[r], p_sem.at[r]))
            pending.append(move(act.at[r], act_out.at[seq, at], o_sem.at[4 + r]))
            pending.append(move(slope.at[r], slope_out.at[seq, at], o_sem.at[8 + r]))
        for copy in pending:
            copy.wait()

    extra = [] if previous is None else list(previous)
    return kernel_call(
        body,
        (
            *[struct((rows, feats), BF16)] * 4,
            struct((seqs, length, feats), BF16),
            struct((seqs, length, units), BF16),
            struct((seqs, length, units), BF16),
        ),
        (ANY,) * 4 + (HBM,) * 3,
        [whole((1, units))] + [ANY] * 4 + [HBM] * (2 + len(extra)),
        scratch=[
            VMEM((parts, rows, feats), BF16),
            VMEM(w_up.shape, BF16),
            VMEM(w_down.shape, BF16),
            VMEM((2, rows, units), F32),
            VMEM((parts, rows, units), BF16),
            VMEM((parts, rows, units), BF16),
            VMEM((parts, rows, feats), BF16),
            DMA((6,)),
            DMA((4,)),
            DMA((12,)),
        ],
        flops=4 * length * feats * units,
        nbytes=length * feats * 14,
        trans=length * units,
        aliases={7: 4, 8: 5, 9: 6} if extra else None,
        name="feed_forward",
    )(b_up, *blocks, w_up, w_down, *extra)


def feed_backward(seq, seqs, own, got, slope, w_up, w_down, previous):
    rows, feats = own.shape[1:]
    parts = 4
    length = rows * parts
    units = w_up.shape[1]

    def body(own_ref, got_ref, slope_ref, up_ref, down_ref, *rest):
        p_refs, (grad_out, sums), rest = rest[-16:-12], rest[-12:-10], rest[-10:]
        ys, up, down, slopes, u, grad, ps, in_sem, p_sem, o_sem = rest
        load_down = move(down_ref, down, in_sem.at[4])
        loads, slope_loads = {}, {}
        for r in ORDER:
            loads[r] = move((got_ref if r % 2 else own_ref).at[r // 2], ys.at[r], in_sem.at[r])
            slope_loads[r] = move(slope_ref.at[seq, pl.ds(r * rows, rows)], slopes.at[r], in_sem.at[6 + r])
        load_up = move(up_ref, up, in_sem.at[5])
        pending = []

        def project(k):
            r = ORDER[k]
            loads[r].wait()
            slope_loads[r].wait()
            u[k % 2] = dot(ys[r], down[...], NT)

        load_down.wait()
        project(0)
        load_up.wait()
        total = jnp.zeros((8, units), F32)
        for k, r in enumerate(ORDER):
            if k + 1 < parts:
                project(k + 1)
            gu = (u[k % 2] * slopes[r].astype(F32)).astype(BF16)
            grad[r] = gu
            total += jnp.sum(gu.astype(F32).reshape(rows // 8, 8, units), axis=0)
            ps[r] = dot(gu, up[...], NT).astype(BF16)
            pending.append(move(ps.at[r], p_refs[r], p_sem.at[r]))
            pending.append(move(grad.at[r], grad_out.at[seq, pl.ds(r * rows, rows)], o_sem.at[4 + r]))
        sums[...] = jnp.sum(total, axis=0, keepdims=True)
        for copy in pending:
            copy.wait()

    extra = [] if previous is None else [previous]
    return kernel_call(
        body,
        (
            *[struct((rows, feats), BF16)] * 4,
            struct((seqs, length, units), BF16),
            struct((1, units), F32),
        ),
        (ANY,) * 4 + (HBM, whole((1, units))),
        [ANY] * 2 + [HBM] * (3 + len(extra)),
        scratch=[
            VMEM((parts, rows, feats), BF16),
            VMEM(w_up.shape, BF16),
            VMEM(w_down.shape, BF16),
            VMEM((parts, rows, units), BF16),
            VMEM((2, rows, units), F32),
            VMEM((parts, rows, units), BF16),
            VMEM((parts, rows, feats), BF16),
            DMA((10,)),
            DMA((4,)),
            DMA((8,)),
        ],
        flops=4 * length * feats * units,
        nbytes=length * feats * 14,
        aliases={5: 4} if extra else None,
        name="feed_backward",
    )(own, got, slope, w_up, w_down, *extra)


def contrast_scores(place, docs, labels, units):
    rows, feats = units[0].shape[0] - EXTRA, units[0].shape[1]
    factor = CONTRAST_SCALE / feats * LOG2E
    count = len(units)
    seqs = count // 4

    def body(t_ref, doc_ref, lab_ref, *rest):
        refs, (exp_out, col_out, row_out, loss_out, both, exps, in_sem, out_sem) = rest[:count], rest[count:]
        t = t_ref[0]
        loads = [move(refs[k].at[pl.ds(0, rows)], both.at[k], in_sem.at[k]) for k in range(count)]
        pending = []
        for s in range(4):
            seq, part = s // 2, s % 2 * 2
            if s == 0:
                loads[0].wait()
            own_at = lax.bitwise_xor(jnp.int32(part), t)
            own_doc = column(doc_ref[seq, own_at])
            own_lab = column(lab_ref[seq, own_at])
            total = jnp.zeros((rows, 128), F32)
            total_pos = jnp.zeros((rows, 128), F32)
            for k in range(count):
                if s == 0 and k:
                    loads[k].wait()
                other = k // 4
                e = jnp.exp2(dot(both[seq * 4 + part], both[k], NT) * factor)
                at = lax.bitwise_xor(jnp.int32(k % 4), t)
                if seq == other:
                    e = jnp.where(own_doc != doc_ref[other, at], e, 0.0)
                picked = jnp.where(own_lab == lab_ref[other, at], e, 0.0)
                for c in range(rows // 128):
                    lanes = slice(c * 128, (c + 1) * 128)
                    total += e[:, lanes]
                    total_pos += picked[:, lanes]
                exps[s, :, k * rows : (k + 1) * rows] = e.astype(BF16)
            pending.append(move(exps.at[s], exp_out.at[s], out_sem.at[s]))
            wide = lane_pair(
                jnp.sum(total, axis=-1, keepdims=True), jnp.sum(total_pos, axis=-1, keepdims=True), rows
            )
            col_out[s * rows : (s + 1) * rows, :] = wide
            flat = jnp.transpose(wide)[:8, :]
            row_out[:, s * rows : (s + 1) * rows] = flat
            if part == 0:
                logs = jnp.log(flat)
                loss_out[seq : seq + 1, :] = logs[0:1] - logs[1:2]
        for copy in pending:
            copy.wait()

    return kernel_call(
        body,
        (
            struct((4, rows, count * rows), BF16),
            struct((4 * rows, 128), F32),
            struct((8, 4 * rows), F32),
            struct((seqs, rows), F32),
        ),
        (HBM, whole((4 * rows, 128)), whole((8, 4 * rows)), whole((seqs, rows))),
        [pl.BlockSpec(memory_space=pltpu.SMEM), whole(docs.shape), whole(labels.shape)] + [ANY] * count,
        scratch=[VMEM((count, rows, feats), BF16), VMEM((4, rows, count * rows), BF16), DMA((count,)), DMA((4,))],
        flops=2 * 4 * rows * count * rows * feats,
        nbytes=count * rows * feats * 4,
        trans=4 * rows * count * rows,
        name="contrast_scores",
    )(place, docs, labels, *units)


def contrast_grads(place, labels, units, exps, col_sums, row_own, row_got, cot, cot_got):
    rows, feats = units[0].shape[0] - EXTRA, units[0].shape[1]
    factor = CONTRAST_SCALE / feats
    count = len(units)
    seqs = count // 4

    def body(t_ref, lab_ref, col, own, got, *rest):
        refs, (e_ref, cot_ref, *other_refs), rest = rest[:count], rest[count : count + 4], rest[count + 4 :]
        full, low0, low1, both, exps, scales, cots, grad, full_v, low_v, in_sem, e_sem, q_sem, c_sem, o_sem = rest
        t = t_ref[0]
        e_loads = [move(e_ref.at[0], exps.at[0], e_sem.at[0])]
        loads = [
            move(refs[k].at[pl.ds(0, rows)], both.at[pl.ds(k * rows, rows)], in_sem.at[k]) for k in range(count)
        ]
        e_loads += [move(e_ref.at[s], exps.at[s], e_sem.at[s]) for s in range(1, 4)]
        small = []
        for s in range(4):
            seq, half = s // 2, s % 2
            small.append(
                (
                    move(refs[seq * 4 + half * 2].at[pl.ds(rows, EXTRA)], scales.at[s], q_sem.at[s]),
                    move(other_refs[seq] if half else cot_ref.at[seq], cots.at[s], c_sem.at[s]),
                )
            )
        pending = []

        def weigh(s):
            seq, half = s // 2, s % 2
            own_lab = column(lab_ref[seq, lax.bitwise_xor(jnp.int32(half * 2), t)])
            inv = CONTRAST_WEIGHT / col[s * rows : (s + 1) * rows, :]
            all_i, pos_i = inv[:, 0:1], inv[:, 1:2]
            e_loads[s].wait()
            for k in range(count):
                other, piece = k // 4, k % 4
                source = own if piece % 2 == 0 else got
                at = (other * 2 + piece // 2) * rows
                inv_j = CONTRAST_WEIGHT / source[0:2, at : at + rows]
                same = own_lab == lab_ref[other, lax.bitwise_xor(jnp.int32(piece), t)]
                coef = (all_i + inv_j[0:1]) - jnp.where(same, pos_i + inv_j[1:2], 0.0)
                cols = slice(k * rows, (k + 1) * rows)
                grad[s % 2, :, cols] = (exps[s, :, cols].astype(F32) * coef).astype(BF16)

        weigh(0)
        for copy in loads:
            copy.wait()
        for s in range(4):
            seq, half = s // 2, s % 2
            if s + 1 < 4:
                weigh(s + 1)
            gn = dot(grad[s % 2], both[...]) * factor
            first = (seq * 4 + half * 2) * rows
            n = both[first : first + rows, :].astype(F32)
            inner = gn - n * jnp.mean(gn * n, axis=-1, keepdims=True)
            for copy in small[s]:
                copy.wait()
            pieces = scales[s, :, :rows].astype(F32)
            gy = cots[s].astype(F32) + column(pieces[0:1] + pieces[1:2]) * inner
            low_v[s] = gy.astype(BF16)
            pending.append(move(low_v.at[s], (low1 if seq else low0).at[half], o_sem.at[s]))
            if half == 0:
                full_v[seq] = gy
                pending.append(move(full_v.at[seq], full.at[seq], o_sem.at[4 + seq]))
        for copy in pending:
            copy.wait()

    return kernel_call(
        body,
        (
            struct((seqs, rows, feats), F32),
            struct((2, rows, feats), BF16),
            struct((2, rows, feats), BF16),
        ),
        (ANY,) * 3,
        [
            pl.BlockSpec(memory_space=pltpu.SMEM),
            whole(labels.shape),
            whole((4 * rows, 128)),
            whole((8, 4 * rows)),
            whole((8, 4 * rows)),
        ]
        + [ANY] * count
        + [HBM] * 2
        + [ANY] * 2,
        scratch=[
            VMEM((count * rows, feats), BF16),
            VMEM((4, rows, count * rows), BF16),
            VMEM((4, EXTRA, feats), BF16),
            VMEM((4, rows, feats), BF16),
            VMEM((2, rows, count * rows), BF16),
            VMEM((seqs, rows, feats), F32),
            VMEM((4, rows, feats), BF16),
            DMA((count,)),
            DMA((4,)),
            DMA((4,)),
            DMA((4,)),
            DMA((4 + seqs,)),
        ],
        flops=2 * 4 * rows * count * rows * feats,
        nbytes=count * rows * feats * 5,
        name="contrast_grads",
    )(place, labels, col_sums, row_own, row_got, *units, exps, cot, *cot_got)


def down_grad(act, own, got, flags, bit):
    seqs, length, units = act.shape
    rows, feats = own[0].shape[1:]
    tiles = units // TILE

    def body(flag, a_ref, *rest):
        own_refs, got_refs = rest[:seqs], rest[seqs : 2 * seqs]
        other_ref, kept_ref, a, b, out, a_sem, b_sem, o_sem = rest[2 * seqs :]
        b_loads = []
        for s in range(seqs):
            for r in range(4):
                src = (got_refs if r % 2 else own_refs)[s].at[r // 2]
                b_loads.append(move(src, b.at[s, pl.ds(r * rows, rows)], b_sem.at[4 * s + r]))
        columns = [pl.ds(i * TILE, TILE) for i in range(tiles)]
        a_loads = [move(a_ref.at[:, :, columns[i]], a.at[i], a_sem.at[i]) for i in range(tiles)]
        for copy in b_loads:
            copy.wait()
        stores = []
        for i in range(tiles):
            a_loads[i].wait()
            out[i] = functools.reduce(jnp.add, [dot(a[i, s], b[s], TN) for s in range(seqs)]).astype(BF16)
            stores.append(
                send_half(i, tiles, flag[bit], out.at[i], other_ref, kept_ref, pl.ds(0, feats), o_sem.at[i])
            )
        for copy in stores:
            copy.wait()

    return kernel_call(
        body,
        (struct((units // 2, feats), BF16),) * 2,
        (ANY,) * 2,
        [pl.BlockSpec(memory_space=pltpu.SMEM), HBM] + [ANY] * (2 * seqs),
        scratch=[
            VMEM((tiles, seqs, length, TILE), BF16),
            VMEM((seqs, length, feats), BF16),
            VMEM((tiles, TILE, feats), BF16),
            DMA((tiles,)),
            DMA((4 * seqs,)),
            DMA((tiles,)),
        ],
        flops=2 * seqs * length * units * feats,
        nbytes=4 * seqs * length * feats,
        name="down_grad",
    )(flags, act, *own, *got)


TILE = 256


def send_half(tile, tiles, high, src, to_other, kept, at, sem):
    upper = tile >= tiles // 2
    rows = pl.ds((tile % (tiles // 2)) * TILE, TILE)

    @pl.when(high == int(upper))
    def _():
        pltpu.make_async_copy(src, kept.at[rows, at], sem).start()

    @pl.when(high != int(upper))
    def _():
        pltpu.make_async_copy(src, to_other.at[rows, at], sem).start()

    return pltpu.make_async_copy(src, kept.at[rows, at], sem)


def weight_grad(lhs, rhs, flags, bit):
    seqs, length, out_rows = lhs.shape
    cols = rhs.shape[2]
    tiles = out_rows // TILE

    def body(flag, a_ref, b_ref, other_ref, kept_ref, a, b, out, a_sem, b_sem, o_sem):
        b_loads = [move(b_ref.at[s], b.at[s], b_sem.at[s]) for s in range(seqs)]
        columns = [pl.ds(i * TILE, TILE) for i in range(tiles)]
        a_loads = [move(a_ref.at[:, :, columns[i]], a.at[i], a_sem.at[i]) for i in range(tiles)]
        for copy in b_loads:
            copy.wait()
        stores = []
        for i in range(tiles):
            a_loads[i].wait()
            out[i] = functools.reduce(jnp.add, [dot(a[i, s], b[s], TN) for s in range(seqs)]).astype(BF16)
            stores.append(
                send_half(i, tiles, flag[bit], out.at[i], other_ref, kept_ref, pl.ds(0, cols), o_sem.at[i])
            )
        for copy in stores:
            copy.wait()

    return kernel_call(
        body,
        (struct((out_rows // 2, cols), BF16),) * 2,
        (ANY,) * 2,
        [pl.BlockSpec(memory_space=pltpu.SMEM)] + [HBM] * 2,
        scratch=[
            VMEM((tiles, seqs, length, TILE), BF16),
            VMEM((seqs, length, cols), BF16),
            VMEM((tiles, TILE, cols), BF16),
            DMA((tiles,)),
            DMA((seqs,)),
            DMA((tiles,)),
        ],
        flops=2 * seqs * length * out_rows * cols,
        nbytes=4 * seqs * length * cols,
        name="weight_grad",
    )(flags, lhs, rhs)


def head_grads(lhs, grads, att, rows_r, flags, bits):
    seqs, length, feats = lhs.shape
    width = att.shape[2]
    tiles = feats // width

    def body(*refs):
        flag, a_ref, *g_refs, r_ref = refs[:7]
        first_refs, second_refs = refs[7:9], refs[9:11]
        a, g, r, first, second, a_sem, g_sem, r_sem, o_sem = refs[11:]
        columns = [pl.ds(i * width, width) for i in range(tiles)]
        g_loads = [move(ref, g.at[n], g_sem.at[n]) for n, ref in enumerate(g_refs)]
        a_loads, r_loads = [], []
        for i in range(tiles):
            a_loads.append(move(a_ref.at[:, :, columns[i]], a.at[i], a_sem.at[i]))
            r_loads.append(move(r_ref.at[:, :, columns[i]], r.at[i], r_sem.at[i]))
        for copy in g_loads:
            copy.wait()

        def total(x, y):
            return functools.reduce(jnp.add, [dot(x[s], y[s], TN) for s in range(seqs)]).astype(BF16)

        stores = []
        for i in range(tiles):
            a_loads[i].wait()
            first[i, :, :width] = total(a[i], g[0])
            first[i, :, width:] = total(a[i], g[1])
            second[i, :, :width] = total(a[i], g[2])
            r_loads[i].wait()
            second[i, :, width:] = total(g[3], r[i])
            for n, (src, outs) in enumerate(((first, first_refs), (second, second_refs))):
                stores.append(
                    send_half(i, tiles, flag[bits[n]], src.at[i], *outs, pl.ds(0, 2 * width), o_sem.at[2 * i + n])
                )
        for copy in stores:
            copy.wait()

    return kernel_call(
        body,
        (struct((feats // 2, 2 * width), BF16),) * 4,
        (ANY,) * 4,
        [pl.BlockSpec(memory_space=pltpu.SMEM)] + [HBM] * 6,
        scratch=[
            VMEM((tiles, seqs, length, width), BF16),
            VMEM((4, seqs, length, width), BF16),
            VMEM((tiles, seqs, length, width), BF16),
            VMEM((tiles, width, 2 * width), BF16),
            VMEM((tiles, width, 2 * width), BF16),
            DMA((tiles,)),
            DMA((4,)),
            DMA((tiles,)),
            DMA((2 * tiles,)),
        ],
        flops=2 * seqs * length * feats * width * 4,
        nbytes=4 * seqs * length * feats,
        name="head_grads",
    )(flags, lhs, *grads, att, rows_r)


def halve_step(flags, bit, keep, got):
    rows, cols = keep.shape
    half = rows // 2

    def body(flag, k_ref, g_ref, *outs):
        if bit is None:
            outs[0][...] = (k_ref[...].astype(F32) + g_ref[...].astype(F32)).astype(BF16)
            return
        for high in (0, 1):

            @pl.when(flag[bit] == high)
            def _(high=high):
                for out, upper in ((outs[0], 1 - high), (outs[1], high)):
                    at = slice(upper * half, (upper + 1) * half)
                    out[...] = (k_ref[at, :].astype(F32) + g_ref[at, :].astype(F32)).astype(BF16)

    shape = (rows, cols) if bit is None else (half, cols)
    return kernel_call(
        body,
        (struct(shape, BF16),) * (1 if bit is None else 2),
        (whole(shape),) * (1 if bit is None else 2),
        [pl.BlockSpec(memory_space=pltpu.SMEM)] + [whole((rows, cols))] * 2,
        nbytes=rows * cols * 6,
        limit=SMALL,
        name="halve_step",
    )(flags, keep, got)


def join_step(flags, bit, own, got, dtype):
    rows, cols = own.shape
    steps = 2 if dtype == F32 else 1
    part = rows // steps

    def body(flag, own_ref, got_ref, out):
        for high in (0, 1):

            @pl.when(flag[bit] == high)
            def _(high=high):
                out[high] = own_ref[...].astype(dtype)
                out[1 - high] = got_ref[...].astype(dtype)

    block = pl.BlockSpec((part, cols), lambda i: (i, 0))
    return kernel_call(
        body,
        struct((2, rows, cols), dtype),
        pl.BlockSpec((2, part, cols), lambda i: (0, i, 0)),
        [pl.BlockSpec(memory_space=pltpu.SMEM), block, block],
        grid=(steps,),
        nbytes=rows * cols * 8,
        limit=SMALL,
        name="join_step",
    )(flags, own, got).reshape(2 * rows, cols)


def head_outputs(flags, bits, first, second):
    feats = 2 * first[0].shape[0]
    width = first[0].shape[1] // 2
    tile = width

    def body(h_ref, a_ref, b_ref, c_ref, d_ref, qkv, out):
        mine = (lax.div(pl.program_id(0) * tile, feats // 2) == h_ref[bits[0]])

        for case, x in ((True, a_ref), (False, b_ref)):
            @pl.when(mine == case)
            def _(x=x):
                qkv[0] = x[:, :width].astype(F32)
                qkv[1] = x[:, width:].astype(F32)

        mine_two = (lax.div(pl.program_id(0) * tile, feats // 2) == h_ref[bits[1]])
        for case, y in ((True, c_ref), (False, d_ref)):
            @pl.when(mine_two == case)
            def _(y=y):
                qkv[2] = y[:, :width].astype(F32)
                out[...] = y[:, width:].astype(F32)

    half = pl.BlockSpec((tile, 2 * width), lambda i, h: (lax.rem(i, feats // 2 // tile), 0))
    return kernel_call(
        body,
        (struct((3, feats, width), F32), struct((width, feats), F32)),
        (pl.BlockSpec((3, tile, width), lambda i, h: (0, i, 0)), pl.BlockSpec((width, tile), lambda i, h: (0, i))),
        [half] * 4,
        grid=(feats // tile,),
        nbytes=10 * feats * width * 4,
        prefetch=1,
        limit=SMALL,
        name="head_outputs",
    )(flags, *first, *second)


def swap(value, axis, size, bit):
    return lax.ppermute(value, axis, [(i, i ^ bit) for i in range(size)])


CORE, CROSS = 1, 2


def tensor_swap(value, bit):
    return swap(value, "tensor", 4, bit)


def tie(value, *earlier):
    return lax.optimization_barrier((value, *earlier))[0] if earlier else value


class Gather:
    def __init__(self, value):
        self.value = value
        self.cross = tensor_swap(value, CROSS)
        self.core = tensor_swap(value, CORE)

    def blocks(self, *earlier):
        return [self.value, self.core, self.cross, tensor_swap(tie(self.cross, *earlier), CORE)]


class Scatter:
    def __init__(self, blocks):
        self.own, self.other = blocks[0], blocks[2]
        self.core_other = tensor_swap(blocks[3], CORE)
        self.core_own = tensor_swap(blocks[1], CORE)
        self.mark = blocks[3]

    def cross(self, *earlier):
        block = (tie(self.other, *earlier).astype(F32) + self.core_other.astype(F32)).astype(BF16)
        self.parts = (self.own, self.core_own, tensor_swap(block, CROSS))
        return block


class DpSum:
    def __init__(self, send, keep, flags, size, order):
        self.send, self.value, self.flags, self.size = send, keep, flags, size
        self.left = [(bit, True) for bit in order] + [(bit, False) for bit in reversed(order)]
        self.got, self.now = None, None

    def advance(self, *earlier):
        if self.now is not None and self.now[1]:
            more = self.left and self.left[0][1]
            parts = halve_step(self.flags, self.left[0][0] if more else None, tie(self.value, *earlier), self.got)
            self.send, self.value = parts if more else (parts[0], parts[0])
        elif self.now is not None:
            self.send = self.value = join_step(self.flags, self.now[0], tie(self.value, *earlier), self.got, BF16)
        self.now = self.left.pop(0)
        self.got = swap(self.send, "dp", self.size, 1 << self.now[0])
        return self.send

    def halves(self):
        return self.value, self.got


def shards(
    dp_size,
    tokens,
    doc_ids,
    targets,
    cotangent,
    ln1_gain,
    ln1_bias,
    qkv_weight,
    query_bias,
    value_bias,
    output_weight,
    out_bias,
    ln2_gain,
    ln2_bias,
    up_weight,
    up_bias,
    down_weight,
    down_bias,
):
    seqs, rows, feats = tokens.shape
    length = doc_ids.shape[1]
    parts = length // rows
    me = lax.axis_index("tensor")
    place = me.reshape(1).astype(jnp.int32)
    vec = lambda v: v.astype(F32).reshape(1, -1)
    gain_one, shift_one, gain_two, shift_two = vec(ln1_gain), vec(ln1_bias), vec(ln2_gain), vec(ln2_bias)
    out_offset, down_offset, up_shift = vec(out_bias), vec(down_bias), vec(up_bias)
    q_shift, v_shift = vec(query_bias), vec(value_bias)

    fine = 16
    paired = (jnp.arange(feats, dtype=jnp.int32) // 2).astype(F32)
    freq = jnp.exp(paired * (-2.0 * math.log(10000.0) / feats))[None, :]
    odd = (jnp.arange(feats, dtype=jnp.int32) % 2 == 1)[None, :]
    coarse_at = (me * rows + fine * jnp.arange(rows // fine, dtype=jnp.int32)).astype(F32)[:, None] * freq
    fine_at = jnp.arange(fine, dtype=jnp.int32).astype(F32)[:, None] * freq
    sin_a, cos_a = jnp.sin(coarse_at), jnp.cos(coarse_at)
    tables = (jnp.where(odd, cos_a, sin_a), jnp.where(odd, -sin_a, cos_a), jnp.cos(fine_at), jnp.sin(fine_at))

    docs_f, labels_f = doc_ids.astype(F32), targets.astype(F32)
    docs4 = docs_f.reshape(seqs, parts, 1, rows)
    labels4 = labels_f.reshape(seqs, parts, 1, rows)
    docs_row = [docs_f[s : s + 1] for s in range(seqs)]

    hidden, stream, grad_r = [None] * 2, [None] * 2, [None] * 2
    kept, up_sums, head_sums, sums_one, sums_two = [None] * 2, [None] * 2, [None] * 2, [None] * 2, [None] * 2
    shared = {"attend": None, "feed": None, "act": None, "up": None, "heads": None, "input": None}

    def attend(s, gathered, *earlier):
        *blocks, cat, qkv, att, logs = attend_forward(
            s, seqs, tie(place, *earlier), docs_row[s], gathered, qkv_weight, q_shift, v_shift, output_weight,
            shared["attend"],
        )
        shared["attend"], kept[s] = (cat, att), (qkv, logs)
        return Scatter(blocks)

    def middle_rows(s, scatter, *earlier):
        stream[s], normed = second_norm(hidden[s], scatter.parts, tie(out_offset, *earlier), gain_two, shift_two)
        return normed, Gather(normed)

    def feed(s, gathered, *earlier):
        *blocks, cat, act, slope = feed_forward(
            s, seqs, gathered, up_weight, tie(up_shift, *earlier), down_weight, shared["feed"]
        )
        shared["feed"] = (cat, act, slope)
        return Scatter(blocks)

    def last_rows(s, scatter, *earlier):
        shared["act"], unit = output_rows(
            s, seqs, stream[s], scatter.parts, tie(down_offset, *earlier), shared["act"]
        )
        return unit, Gather(unit)

    hidden[0], normed_a = first_norm(0, tokens, tables, gain_one, shift_one)
    rows_a = Gather(normed_a)
    hidden[1], normed_b = first_norm(1, tie(tokens, normed_a), tables, gain_one, shift_one)
    rows_b = Gather(normed_b)
    at_a = attend(0, rows_a.blocks(normed_b))
    block = at_a.cross(rows_b.cross)
    at_b = attend(1, rows_b.blocks(), block)
    normed, rows_a = middle_rows(0, at_a, at_b.mark)
    block = at_b.cross(normed)
    ff_a = feed(0, rows_a.blocks(), block)
    normed, rows_b = middle_rows(1, at_b, ff_a.mark)
    block = ff_a.cross(normed)
    ff_b = feed(1, rows_b.blocks(), block)
    unit, units_a = last_rows(0, ff_a, ff_b.mark)
    block = ff_b.cross(unit)
    unit, units_b = last_rows(1, ff_b, block)
    cots = [tensor_swap(tie(cotangent[s], unit), CROSS) for s in range(2)]
    cat_one, att = shared["attend"]
    cat_two, hidden_act, slope = shared["feed"]

    units = units_a.blocks() + units_b.blocks()
    exps, col_sums, row_sums, loss = contrast_scores(place, docs4, labels4, units)
    row_got = tensor_swap(row_sums, CORE)
    grad_y, *low_y = contrast_grads(
        place, labels4, units, exps, col_sums, row_sums, row_got, cotangent, cots
    )
    got_y = [tensor_swap(v, CORE) for v in low_y]

    def feed_back(s, *earlier):
        *blocks, shared["up"], up_sums[s] = feed_backward(
            s, seqs, low_y[s], got_y[s], slope, tie(up_weight, *earlier), down_weight, shared["up"]
        )
        return Scatter(blocks)

    def middle_back(s, scatter, *earlier):
        grad_r[s], low, sums_two[s] = norm_backward(
            s, seqs, stream[s], scatter.parts, tie(gain_two, *earlier), grad_y, False, None
        )
        return low, Gather(low)

    def attend_back(s, gathered, *earlier):
        *blocks, cat, gq, gk, gv, head_sums[s] = attend_backward(
            s, seqs, tie(place, *earlier), docs_row[s], gathered, kept[s][0], att, kept[s][1], qkv_weight,
            output_weight, shared["heads"],
        )
        shared["heads"] = (cat, gq, gk, gv)
        return Scatter(blocks)

    def first_back(s, scatter, *earlier):
        shared["input"], sums_one[s] = norm_backward(
            s, seqs, hidden[s], scatter.parts, tie(gain_one, *earlier), grad_r[s], True, shared["input"]
        )
        return sums_one[s]

    bits = list(range(dp_size.bit_length() - 1))
    other_bits = bits[1::-1] + bits[2:]
    flags = (lax.axis_index("dp") >> jnp.arange(len(bits), dtype=jnp.int32)) & 1
    fb_a = feed_back(0)
    block = fb_a.cross()
    fb_b = feed_back(1, block)
    block = fb_b.cross()
    low, rows_a = middle_back(0, fb_a, block)
    down_sum = DpSum(*down_grad(tie(hidden_act, low), low_y, got_y, flags, bits[0]), flags, dp_size, bits)
    sent = down_sum.advance()
    low, rows_b = middle_back(1, fb_b, sent)
    up_sum = DpSum(*weight_grad(tie(cat_two, low), shared["up"], flags, bits[0]), flags, dp_size, bits)
    sent = up_sum.advance()
    ab_a = attend_back(0, rows_a.blocks(sent), sent)
    sent = down_sum.advance(ab_a.mark)
    block = ab_a.cross(sent)
    ab_b = attend_back(1, rows_b.blocks(block), block)
    sent = up_sum.advance(down_sum.advance(ab_b.mark))
    sums = first_back(0, ab_a, sent)
    block = ab_b.cross(sums)
    cat_r, *grad_qkv = shared["heads"]
    first_send, first_keep, second_send, second_keep = head_grads(
        tie(cat_one, block), grad_qkv, att, cat_r, flags, (bits[0], other_bits[0])
    )
    first = DpSum(first_send, first_keep, flags, dp_size, bits)
    second = DpSum(second_send, second_keep, flags, dp_size, other_bits)
    sent = (first.advance(), second.advance())
    sent = up_sum.advance(down_sum.advance(*sent))
    sums = first_back(1, ab_b, sent)
    sent = (sums,)

    total = lambda items: functools.reduce(jnp.add, items)
    heads_sum = total(head_sums)
    heads_row = jnp.pad(heads_sum.reshape(1, -1), ((0, 0), (0, feats - heads_sum.size)))
    small = jnp.concatenate([total(sums_one)[:2], total(sums_two), total(up_sums), heads_row])
    swaps = [("dp", dp_size, 1 << bit) for bit in bits] + [("tensor", 4, CORE), ("tensor", 4, CROSS)]
    local = None
    while swaps or first.left or up_sum.left or down_sum.left:
        if swaps:
            axis, size, bit = swaps.pop(0)
            if axis == "tensor" and local is None:
                local, small = small[6:], small[:6]
            small = small + swap(tie(small, *sent), axis, size, bit)
        sent = ()
        if first.left:
            sent += (first.advance(small), second.advance(small))
        for other in (down_sum, up_sum):
            if other.left:
                sent += (other.advance(small, *sent),)
    grad_qkv_w, grad_out_w = head_outputs(flags, (bits[0], other_bits[0]), first.halves(), second.halves())
    grad_down_w = join_step(flags, bits[0], *down_sum.halves(), F32)
    grad_up_w = join_step(flags, bits[0], *up_sum.halves(), F32)
    return (
        shared["act"],
        loss,
        shared["input"],
        small[0],
        small[1],
        grad_qkv_w,
        local[1, : heads_sum.shape[1]],
        local[1, heads_sum.shape[1] : 2 * heads_sum.shape[1]],
        grad_out_w,
        small[4],
        small[2],
        small[3],
        grad_up_w,
        local[0],
        grad_down_w,
        small[5],
    )


def solution(mesh):
    in_specs = (
        P("dp", "tensor", None),
        P("dp", None),
        P("dp", None),
        P("dp", "tensor", None),
        P(),
        P(),
        P(None, None, "tensor"),
        P("tensor"),
        P("tensor"),
        P("tensor", None),
        P(),
        P(),
        P(),
        P(None, "tensor"),
        P("tensor"),
        P("tensor", None),
        P(),
    )
    out_specs = (
        P("dp", "tensor", None),
        P("dp", "tensor"),
        P("dp", "tensor", None),
        P(),
        P(),
        P(None, None, "tensor"),
        P("tensor"),
        P("tensor"),
        P("tensor", None),
        P(),
        P(),
        P(),
        P(None, "tensor"),
        P("tensor"),
        P("tensor", None),
        P(),
    )
    return jax.shard_map(
        functools.partial(shards, mesh.shape["dp"]),
        mesh=mesh,
        in_specs=in_specs,
        out_specs=out_specs,
        check_vma=False,
    )
```

time: 532 us -> 470 us (0.88)
  Pallas kernels: 114 us -> 167 us
  waiting for transfers between devices: 243 us -> 202 us
  matrix products: 23.4 us -> 0 us
  local copies, waits for them, and re-layouts: 49.4 us -> 26 us
  other arithmetic: 29 us -> 6.44 us
  starting transfers between devices: 68 us -> 62.2 us
    pallas_call x15 -> x41, Pallas kernels: 98.7 us -> 151 us  [the longest x2 26.2 us: attend_forward(): kernel_call(body, (*[struct((rows, feats), BF16)] * 4, struct((seqs, leng...]
    ppermute x75 -> x82, waiting for transfers between devices: 243 us -> 202 us  [swap(): return lax.ppermute(value, axis, [(i, i ^ bit) for i in range(size)])]
    dot_general x6 -> x0, matrix products: 23.4 us -> none  [the longest x1 7.83 us: shards(): jnp.einsum('snd,snf->df', cat_two, grad_up, preferred_element_type=F32)]
    convert_element_type x24 -> x8, other arithmetic: 16.4 us -> 2.38 us  [cross(): (tie(self.other, *earlier).astype(F32) + self.core_other.astype(F32)).ast...]
    unnamed x177 -> x137, local copies, waits for them, and re-layouts: 34.9 us -> 23.1 us
    ppermute x75 -> x82, starting transfers between devices: 68 us -> 62.2 us  [swap(): return lax.ppermute(value, axis, [(i, i ^ bit) for i in range(size)])]
  transfers between devices with their start and end apart: 75 -> 82, of which waited for: 34 -> 34; matrix products, arithmetic and copies ran while one was open for 12% -> 2% of each run, Pallas kernels for 19% -> 30%
where the time goes in v2:
time: 470 us; the launch traced here: 466 us
  waiting for transfers between devices  202 us (43%)
  Pallas kernels  167 us (36%)
  starting transfers between devices  62.2 us (13%)
  local copies, waits for them, and re-layouts  26 us (6%)
  other arithmetic  6.44 us (1%)
    ppermute x82, waiting for transfers between devices, swap(): return lax.ppermute(value, axis, [(i, i ^ bit) for i in range(size)])  202 us
    ppermute x82, starting transfers between devices, swap(): return lax.ppermute(value, axis, [(i, i ^ bit) for i in range(size)])  62.2 us
    pallas_call x2, Pallas kernels, attend_forward(): kernel_call(body, (*[struct((rows, feats), BF16)] * 4, struct((seqs, leng...  26.2 us
    pallas_call x2, Pallas kernels, attend_backward(): kernel_call(body, (*[struct((rows, feats), BF16)] * 4, struct((seqs, leng...  23.8 us
    unnamed x137, local copies, waits for them, and re-layouts  23.1 us
    pallas_call x2, Pallas kernels, feed_forward(): kernel_call(body, (*[struct((rows, feats), BF16)] * 4, struct((seqs, leng...  16.8 us
    pallas_call x2, Pallas kernels, feed_backward(): kernel_call(body, (*[struct((rows, feats), BF16)] * 4, struct((seqs, leng...  15.2 us
    pallas_call x1, Pallas kernels, contrast_grads(): kernel_call(body, (struct((seqs, rows, feats), F32), struct((2, rows, fea...  12.2 us
  transfers between devices with their start and end apart: 82, of which 34 were waited for; matrix products, arithmetic and copies ran while one was open for 2% of the time, Pallas kernels for 30%

profile of v2, /device:TPU:0, one launch (start us, length us, event | category | flops | bytes accessed | tf_op | source)
XLA Modules:
  0.0 466.1 jit_solution(10051871711717078170)
XLA Ops:
  4.9 3.0 collective-permute-start.1
  9.0 10.9 %collective-permute-done.1.rest_2_ = bf16[256,1024]{1,0:T(8,128)(2,1)S(1)} collective-permute-done((bf16[256,1024]{1,0:T(8,128)(2,1)S(1)}, bf16[256,1024]{1,0:T(8,128)(2,1)S(1)}, u32[]{:S(2)}, u32[]{:S(2)}) %collective-permute-start.1) | collective-permute-done | bytes 524320 | tf_op jit(solution)/shard_map/ppermute | solution.py:1058
  26.1 8.2 %attend_forward.2 = (bf16[256,1024]{1,0:T(8,128)(2,1)S(1)}, bf16[256,1024]{1,0:T(8,128)(2,1)S(1)}, bf16[256,1024]{1,0:T(8,128)(2,1)S(1)}, bf16[256,1024]{1,0:T(8...) custom-call(s32[1]{0:T(128)} %bitcast.2.t_ref, ...), custom_call_target="tpu_custom_call" | custom-call | flops 69793216 | bytes 167772 | tf_op jit(solution)/shard_map/attend_forward/pallas_call | solution.py:334
  38.5 18.0 %attend_forward.3 = (bf16[256,1024]{1,0:T(8,128)(2,1)S(1)}, bf16[256,1024]{1,0:T(8,128)(2,1)S(1)}, bf16[256,1024]{1,0:T(8,128)(2,1)S(1)}, bf16[256,1024]{1,0:T(8...) custom-call(s32[1]{0:T(128)} %bitcast.2.t_ref, ...), custom_call_target="tpu_custom_call", output_to_operand_aliasing={{4}: (10, {}), {6}: (11, {})} | custom-call | flops 69793216 | bytes 167772 | tf_op jit(solution)/shard_map/attend_forward/pallas_call | solution.py:334
  61.9 12.7 %collective-permute-done.13.rest_2_ = bf16[256,1024]{1,0:T(8,128)(2,1)S(1)} collective-permute-done((bf16[256,1024]{1,0:T(8,128)(2,1)S(1)}, bf16[256,1024]{1,0:T(8,128)(2,1)S(1)}, u32[]{:S(2)}, u32[]{:S(2)}) %collective-permute-start.13) | collective-permute-done | bytes 524320 | tf_op jit(solution)/shard_map/ppermute | solution.py:1058
  76.5 8.3 %feed_forward.2 = (bf16[256,1024]{1,0:T(8,128)(2,1)S(1)}, bf16[256,1024]{1,0:T(8,128)(2,1)S(1)}, bf16[256,1024]{1,0:T(8,128)(2,1)S(1)}, bf16[256,1024]{1,0:T(8,1...) custom-call(f32[1,1024]{1,0:T(1,128)S(1)} %bitcast.68, ...), custom_call_target="tpu_custom_call" | custom-call | flops 85899344 | bytes 293601 | tf_op jit(solution)/shard_map/feed_forward/pallas_call | solution.py:539
  84.8 4.4 collective-permute-done.11.x_ref
  91.4 12.4 %collective-permute-done.17.rest_2_ = bf16[256,1024]{1,0:T(8,128)(2,1)S(1)} collective-permute-done((bf16[256,1024]{1,0:T(8,128)(2,1)S(1)}, bf16[256,1024]{1,0:T(8,128)(2,1)S(1)}, u32[]{:S(2)}, u32[]{:S(2)}) %collective-permute-start.17) | collective-permute-done | bytes 524320 | tf_op jit(solution)/shard_map/ppermute | solution.py:1058
  105.7 8.5 %feed_forward.3 = (bf16[256,1024]{1,0:T(8,128)(2,1)S(1)}, bf16[256,1024]{1,0:T(8,128)(2,1)S(1)}, bf16[256,1024]{1,0:T(8,128)(2,1)S(1)}, bf16[256,1024]{1,0:T(8,1...) custom-call(f32[1,1024]{1,0:T(1,128)S(1)} %bitcast.69, ...), custom_call_target="tpu_custom_call", output_to_operand_aliasing={{4}: (7, {}), {5}: (8, {}), {6}: (9, {})} | custom-call | flops 85899344 | bytes 293601 | tf_op jit(solution)/shard_map/feed_forward/pallas_call | solution.py:539
  114.9 3.6 collective-permute-done.21.x_ref
  122.0 12.8 %collective-permute-done.23.x_ref = bf16[256,1024]{1,0:T(8,128)(2,1)S(1)} collective-permute-done((bf16[256,1024]{1,0:T(8,128)(2,1)S(1)}, bf16[256,1024]{1,0:T(8,128)(2,1)S(1)}, u32[]{:S(2)}, u32[]{:S(2)}) %collective-permute-start.23) | collective-permute-done | bytes 524320 | tf_op jit(solution)/shard_map/ppermute | solution.py:1058
  137.0 10.0 %collective-permute-done.25.rest_2_ = bf16[272,1024]{1,0:T(8,128)(2,1)} collective-permute-done((bf16[272,1024]{1,0:T(8,128)(2,1)S(1)}, bf16[272,1024]{1,0:T(8,128)(2,1)}, u32[]{:S(2)}, u32[]{:S(2)}) %collective-permute-start.25) | collective-permute-done | bytes 557088 | tf_op jit(solution)/shard_map/ppermute | solution.py:1058
  147.4 9.5 %collective-permute-done.28.rest_6_ = bf16[272,1024]{1,0:T(8,128)(2,1)} collective-permute-done((bf16[272,1024]{1,0:T(8,128)(2,1)}, bf16[272,1024]{1,0:T(8,128)(2,1)}, u32[]{:S(2)}, u32[]{:S(2)}) %collective-permute-start.28) | collective-permute-done | bytes 557088 | tf_op jit(solution)/shard_map/ppermute | solution.py:1058
  163.2 9.8 %contrast_scores.1 = (bf16[4,256,2048]{2,1,0:T(8,128)(2,1)S(1)}, f32[1024,128]{1,0:T(8,128)S(1)}, f32[8,1024]{1,0:T(8,128)S(1)}, f32[2,256]{1,0:T(2,128)}) custom-call(s32[1]{0:T(128)} %bitcast.2.t_ref, f32[2,4,1,256]{3,2,1,0:T(1,128)S(1)} %reshape.208.doc_ref, f32[2,4,1,256]{3,2,1,0:T(1,128)S(1)} %reshape.178.lab_ref, bf16[272,1024]{1,0:T(8,128)(2,1)S(1)} %copy-done.39, ...), custom_call_target="tpu_custom_call" | custom-call | flops 85899344 | bytes 167772 | tf_op jit(solution)/shard_map/contrast_scores/pallas_call | solution.py:685
  175.1 8.8 %collective-permute-done.32.rest_11_ = bf16[256,1024]{1,0:T(8,128)(2,1)} collective-permute-done((bf16[256,1024]{1,0:T(8,128)(2,1)}, bf16[256,1024]{1,0:T(8,128)(2,1)}, u32[]{:S(2)}, u32[]{:S(2)}) %collective-permute-start.32) | collective-permute-done | bytes 524320 | tf_op jit(solution)/shard_map/ppermute | solution.py:1058
  184.0 12.2 %contrast_grads.1 = (f32[2,256,1024]{2,1,0:T(8,128)S(1)}, bf16[2,256,1024]{2,1,0:T(8,128)(2,1)S(1)}, bf16[2,256,1024]{2,1,0:T(8,128)(2,1)S(1)}) custom-call(s32[1]{0:T(128)} %bitcast.2.t_ref, f32[2,4,1,256]{3,2,1,0:T(1,128)S(1)} %reshape.178.lab_ref, f32[1024,128]{1,0:T(8,128)S(1)} %get-tuple-element.233.col, f32[8,1024]{1,0:T(8,128)S(1)} %get-tuple-element.234.own, ...), custom_call_target="tpu_custom_call" | custom-call | flops 85899344 | bytes 209715 | tf_op jit(solution)/shard_map/contrast_grads/pallas_call | solution.py:768
  199.0 7.5 %feed_backward.2 = (bf16[256,1024]{1,0:T(8,128)(2,1)S(1)}, bf16[256,1024]{1,0:T(8,128)(2,1)S(1)}, bf16[256,1024]{1,0:T(8,128)(2,1)S(1)}, bf16[256,1024]{1,0:T(8,...) custom-call(bf16[2,256,1024]{2,1,0:T(8,128)(2,1)S(1)} %get-tuple-element.240.own_ref.rest_0_, ...), custom_call_target="tpu_custom_call" | custom-call | flops 85899344 | bytes 293601 | tf_op jit(solution)/shard_map/feed_backward/pallas_call | solution.py:610
  208.7 7.6 %feed_backward.3 = (bf16[256,1024]{1,0:T(8,128)(2,1)S(1)}, bf16[256,1024]{1,0:T(8,128)(2,1)}, bf16[256,1024]{1,0:T(8,128)(2,1)S(1)}, bf16[256,1024]{1,0:T(8,128)...) custom-call(bf16[2,256,1024]{2,1,0:T(8,128)(2,1)S(1)} %get-tuple-element.238, ...), custom_call_target="tpu_custom_call", output_to_operand_aliasing={{4}: (5, {})} | custom-call | flops 85899344 | bytes 293601 | tf_op jit(solution)/shard_map/feed_backward/pallas_call | solution.py:610
  222.0 11.7 %collective-permute-done.40.x_ref = bf16[256,1024]{1,0:T(8,128)(2,1)S(1)} collective-permute-done((bf16[256,1024]{1,0:T(8,128)(2,1)S(1)}, bf16[256,1024]{1,0:T(8,128)(2,1)S(1)}, u32[]{:S(2)}, u32[]{:S(2)}) %collective-permute-start.40) | collective-permute-done | bytes 524320 | tf_op jit(solution)/shard_map/ppermute | solution.py:1058
  233.7 2.3 norm_backward.4
  242.3 7.7 %down_grad.1 = (bf16[512,1024]{1,0:T(8,128)(2,1)}, bf16[512,1024]{1,0:T(8,128)(2,1)S(1)}) custom-call(s32[3]{0:T(128)S(1)} %shift-right-arithmetic_and_fusion.flag.refs_0_.h_ref, bf16[2,1024,1024]{2,1,0:T(8,128)(2,1)S(1)} %copy-done.8, bf16[2,256,1024]{2,1,0:T(8,128)(2,1)S(1)} %copy-done.25, bf16[2,256,1024]{2,1,0:T(8,128)(2,1)S(1)} %copy-done.18, ...), custom_call_target="tpu_custom_call" | custom-call | flops 85899344 | bytes 167772 | tf_op jit(solution)/shard_map/down_grad/pallas_call | solution.py:833
  250.1 3.6 norm_backward.5
  253.8 6.8 %weight_grad.1 = (bf16[512,1024]{1,0:T(8,128)(2,1)S(1)}, bf16[512,1024]{1,0:T(8,128)(2,1)S(1)}) custom-call(s32[3]{0:T(128)S(1)} %shift-right-arithmetic_and_fusion.flag.refs_0_.h_ref, bf16[2,1024,1024]{2,1,0:T(8,128)(2,1)S(1)} %copy-done.7, bf16[2,1024,1024]{2,1,0:T(8,128)(2,1)S(1)} %copy-done.10), custom_call_target="tpu_custom_call" | custom-call | flops 85899344 | bytes 167772 | tf_op jit(solution)/shard_map/weight_grad/pallas_call | solution.py:891
  263.9 12.1 %attend_backward.2 = (bf16[256,1024]{1,0:T(8,128)(2,1)S(1)}, bf16[256,1024]{1,0:T(8,128)(2,1)S(1)}, bf16[256,1024]{1,0:T(8,128)(2,1)S(1)}, bf16[256,1024]{1,0:T(...) custom-call(s32[1]{0:T(128)} %bitcast.2.t_ref, ...), custom_call_target="tpu_custom_call" | custom-call | flops 96636768 | bytes 167772 | tf_op jit(solution)/shard_map/attend_backward/pallas_call | solution.py:458
  278.3 8.2 %collective-permute-done.44.g_ref = bf16[512,1024]{1,0:T(8,128)(2,1)S(1)} collective-permute-done((bf16[512,1024]{1,0:T(8,128)(2,1)}, bf16[512,1024]{1,0:T(8,128)(2,1)S(1)}, u32[]{:S(2)}, u32[]{:S(2)}) %collective-permute-start.44) | collective-permute-done | bytes 1048608 | tf_op jit(solution)/shard_map/ppermute | solution.py:1058
  287.5 3.1 collective-permute-done.47.rest_2_
  295.6 11.7 %attend_backward.3 = (bf16[256,1024]{1,0:T(8,128)(2,1)S(1)}, bf16[256,1024]{1,0:T(8,128)(2,1)S(1)}, bf16[256,1024]{1,0:T(8,128)(2,1)S(1)}, bf16[256,1024]{1,0:T(...) custom-call(s32[1]{0:T(128)} %bitcast.2.t_ref, ...), custom_call_target="tpu_custom_call", output_to_operand_aliasing={{4}: (11, {}), {5}: (12, {}), {6}: (13, {}), {7}: (14, {})} | custom-call | flops 96636768 | bytes 167772 | tf_op jit(solution)/shard_map/attend_backward/pallas_call | solution.py:458
  308.4 8.0 %collective-permute-done.53.g_ref = bf16[512,1024]{1,0:T(8,128)(2,1)S(1)} collective-permute-done((bf16[512,1024]{1,0:T(8,128)(2,1)}, bf16[512,1024]{1,0:T(8,128)(2,1)S(1)}, u32[]{:S(2)}, u32[]{:S(2)}) %collective-permute-start.53) | collective-permute-done | bytes 1048608 | tf_op jit(solution)/shard_map/ppermute | solution.py:1058
  319.0 2.4 norm_backward.6
  323.3 2.6 collective-permute-start.56
  326.0 9.6 %head_grads.1 = (bf16[512,512]{1,0:T(8,128)(2,1)S(1)}, bf16[512,512]{1,0:T(8,128)(2,1)S(1)}, bf16[512,512]{1,0:T(8,128)(2,1)S(1)}, bf16[512,512]{1,0:T(8,128)(2,1)S(1)}) custom-call(s32[3]{0:T(128)S(1)} %shift-right-arithmetic_and_fusion.flag.refs_0_.h_ref, bf16[2,1024,1024]{2,1,0:T(8,128)(2,1)S(1)} %copy-done.12, ...), custom_call_target="tpu_custom_call" | custom-call | flops 85899344 | bytes 167772 | tf_op jit(solution)/shard_map/head_grads/pallas_call | solution.py:946
  336.5 2.7 collective-permute-start.60
  342.8 2.5 norm_backward.7
  346.1 4.0 collective-permute-done.58
  350.9 4.8 %collective-permute-done.60.g_ref = bf16[512,512]{1,0:T(8,128)(2,1)S(1)} collective-permute-done((bf16[512,512]{1,0:T(8,128)(2,1)S(1)}, bf16[512,512]{1,0:T(8,128)(2,1)S(1)}, u32[]{:S(2)}, u32[]{:S(2)}) %collective-permute-start.60) | collective-permute-done | bytes 524320 | tf_op jit(solution)/shard_map/ppermute | solution.py:1058
  359.1 2.4 collective-permute-start.62
  362.0 15.2 %collective-permute-done.62.g_ref = bf16[128,1024]{1,0:T(8,128)(2,1)S(1)} collective-permute-done((bf16[128,1024]{1,0:T(8,128)(2,1)S(1)}, bf16[128,1024]{1,0:T(8,128)(2,1)S(1)}, u32[]{:S(2)}, u32[]{:S(2)}) %collective-permute-start.62) | collective-permute-done | bytes 262176 | tf_op jit(solution)/shard_map/ppermute | solution.py:1058
  377.7 3.5 collective-permute-start.67
  381.2 5.7 %collective-permute-done.63 = f32[8,1024]{1,0:T(8,128)S(1)} collective-permute-done((f32[8,1024]{1,0:T(8,128)S(1)}, f32[8,1024]{1,0:T(8,128)S(1)}, u32[]{:S(2)}, u32[]{:S(2)}) %collective-permute-start.63) | collective-permute-done | bytes 32800 | tf_op jit(solution)/shard_map/ppermute | solution.py:1058
  396.1 11.3 %collective-permute-done.68 = f32[8,1024]{1,0:T(8,128)S(1)} collective-permute-done((f32[8,1024]{1,0:T(8,128)S(1)}, f32[8,1024]{1,0:T(8,128)S(1)}, u32[]{:S(2)}, u32[]{:S(2)}) %collective-permute-start.68) | collective-permute-done | bytes 32800 | tf_op jit(solution)/shard_map/ppermute | solution.py:1058
  409.4 3.4 collective-permute-start.73
  413.0 9.9 %collective-permute-done.73.got_ref = bf16[128,512]{1,0:T(8,128)(2,1)S(1)} collective-permute-done((bf16[128,512]{1,0:T(8,128)(2,1)S(1)}, bf16[128,512]{1,0:T(8,128)(2,1)S(1)}, u32[]{:S(2)}, u32[]{:S(2)}) %collective-permute-start.73) | collective-permute-done | bytes 131104 | tf_op jit(solution)/shard_map/ppermute | solution.py:1058
  428.0 3.9 collective-permute-done.75
  434.0 16.3 %collective-permute-done.78.got_ref = bf16[256,512]{1,0:T(8,128)(2,1)S(1)} collective-permute-done((bf16[256,512]{1,0:T(8,128)(2,1)S(1)}, bf16[256,512]{1,0:T(8,128)(2,1)S(1)}, u32[]{:S(2)}, u32[]{:S(2)}) %collective-permute-start.78) | collective-permute-done | bytes 262176 | tf_op jit(solution)/shard_map/ppermute | solution.py:1058
  453.9 2.7 join_step.19
  457.7 2.5 collective-permute-done.79.d_ref
  460.2 3.0 head_outputs.1
  463.2 2.7 join_step.18
  (340 shorter events, 109.3 us)
Async XLA Ops:
  4.9 14.9 %collective-permute-start.1 = (bf16[256,1024]{1,0:T(8,128)(2,1)S(1)}, bf16[256,1024]{1,0:T(8,128)(2,1)S(1)}, u32[]{:S(2)}, u32[]{:S(2)}) collective-permute-start(bf16[256,1024]{1,0:T(8,128)(2,1)S(1)} %get-tuple-element.185.rest_0_), channel_id=1, source_target_pairs={{0,2},{1,3},{2,0},{3,1},{4,6},{5,7},{6,4},{7,5},{8,10},{9,11},{10,... | collective-permute-start | bytes 1572872 | tf_op jit(solution)/shard_map/ppermute | solution.py:1058
  7.9 15.7 %collective-permute-start = (bf16[256,1024]{1,0:T(8,128)(2,1)S(1)}, bf16[256,1024]{1,0:T(8,128)(2,1)S(1)}, u32[]{:S(2)}, u32[]{:S(2)}) collective-permute-start(bf16[256,1024]{1,0:T(8,128)(2,1)S(1)} %get-tuple-element.185.rest_0_), channel_id=1, source_target_pairs={{0,1},{1,0},{2,3},{3,2},{4,5},{5,4},{6,7},{7,6},{8,9},{9,8},{10,11... | collective-permute-start | bytes 1572872 | tf_op jit(solution)/shard_map/ppermute | solution.py:1058
  19.8 15.7 %collective-permute-start.3 = (bf16[256,1024]{1,0:T(8,128)(2,1)S(1)}, bf16[256,1024]{1,0:T(8,128)(2,1)S(1)}, u32[]{:S(2)}, u32[]{:S(2)}) collective-permute-start(bf16[256,1024]{1,0:T(8,128)(2,1)S(1)} %get-tuple-element.188.rest_0_), channel_id=1, source_target_pairs={{0,2},{1,3},{2,0},{3,1},{4,6},{5,7},{6,4},{7,5},{8,10},{9,11},{10,... | collective-permute-start | bytes 1572872 | tf_op jit(solution)/shard_map/ppermute | solution.py:1058
  35.8 22.6 %collective-permute-start.8 = (bf16[256,1024]{1,0:T(8,128)(2,1)S(1)}, bf16[256,1024]{1,0:T(8,128)(2,1)S(1)}, u32[]{:S(2)}, u32[]{:S(2)}) collective-permute-start(bf16[256,1024]{1,0:T(8,128)(2,1)S(1)} %get-tuple-element.201), channel_id=1, source_target_pairs={{0,1},{1,0},{2,3},{3,2},{4,5},{5,4},{6,7},{7,6},{8,9},{9,8},{10,11... | collective-permute-start | bytes 1572872 | tf_op jit(solution)/shard_map/ppermute | solution.py:1058
  37.1 21.3 %collective-permute-start.9 = (bf16[256,1024]{1,0:T(8,128)(2,1)S(1)}, bf16[256,1024]{1,0:T(8,128)(2,1)S(1)}, u32[]{:S(2)}, u32[]{:S(2)}) collective-permute-start(bf16[256,1024]{1,0:T(8,128)(2,1)S(1)} %add_convert_fusion.7), channel_id=1, source_target_pairs={{0,2},{1,3},{2,0},{3,1},{4,6},{5,7},{6,4},{7,5},{8,10},{9,11},{10,... | collective-permute-start | bytes 1572872 | tf_op jit(solution)/shard_map/ppermute | solution.py:1058
  60.5 14.1 %collective-permute-start.13 = (bf16[256,1024]{1,0:T(8,128)(2,1)S(1)}, bf16[256,1024]{1,0:T(8,128)(2,1)S(1)}, u32[]{:S(2)}, u32[]{:S(2)}) collective-permute-start(bf16[256,1024]{1,0:T(8,128)(2,1)S(1)} %get-tuple-element.204.rest_0_), channel_id=1, source_target_pairs={{0,2},{1,3},{2,0},{3,1},{4,6},{5,7},{6,4},{7,5},{8,10},{9,11},{10,... | collective-permute-start | bytes 1572872 | tf_op jit(solution)/shard_map/ppermute | solution.py:1058
  61.4 23.4 %collective-permute-start.7 = (bf16[256,1024]{1,0:T(8,128)(2,1)S(1)}, bf16[256,1024]{1,0:T(8,128)(2,1)S(1)}, u32[]{:S(2)}, u32[]{:S(2)}) collective-permute-start(bf16[256,1024]{1,0:T(8,128)(2,1)S(1)} %get-tuple-element.197), channel_id=1, source_target_pairs={{0,1},{1,0},{2,3},{3,2},{4,5},{5,4},{6,7},{7,6},{8,9},{9,8},{10,11... | collective-permute-start | bytes 1572872 | tf_op jit(solution)/shard_map/ppermute | solution.py:1058
  74.7 14.4 %collective-permute-start.11 = (bf16[256,1024]{1,0:T(8,128)(2,1)S(1)}, bf16[256,1024]{1,0:T(8,128)(2,1)S(1)}, u32[]{:S(2)}, u32[]{:S(2)}) collective-permute-start(bf16[256,1024]{1,0:T(8,128)(2,1)S(1)} %add_convert_fusion.6), channel_id=1, source_target_pairs={{0,2},{1,3},{2,0},{3,1},{4,6},{5,7},{6,4},{7,5},{8,10},{9,11},{10,... | collective-permute-start | bytes 1572872 | tf_op jit(solution)/shard_map/ppermute | solution.py:1058
  90.9 14.3 %collective-permute-start.16 = (bf16[256,1024]{1,0:T(8,128)(2,1)S(1)}, bf16[256,1024]{1,0:T(8,128)(2,1)S(1)}, u32[]{:S(2)}, u32[]{:S(2)}) collective-permute-start(bf16[256,1024]{1,0:T(8,128)(2,1)S(1)} %get-tuple-element.211.rest_0_), channel_id=1, source_target_pairs={{0,1},{1,0},{2,3},{3,2},{4,5},{5,4},{6,7},{7,6},{8,9},{9,8},{10,11... | collective-permute-start | bytes 1572872 | tf_op jit(solution)/shard_map/ppermute | solution.py:1058
  104.5 13.9 %collective-permute-start.21 = (bf16[256,1024]{1,0:T(8,128)(2,1)S(1)}, bf16[256,1024]{1,0:T(8,128)(2,1)S(1)}, u32[]{:S(2)}, u32[]{:S(2)}) collective-permute-start(bf16[256,1024]{1,0:T(8,128)(2,1)S(1)} %add_convert_fusion.5), channel_id=1, source_target_pairs={{0,2},{1,3},{2,0},{3,1},{4,6},{5,7},{6,4},{7,5},{8,10},{9,11},{10,... | collective-permute-start | bytes 1572872 | tf_op jit(solution)/shard_map/ppermute | solution.py:1058
  119.9 14.9 %collective-permute-start.23 = (bf16[256,1024]{1,0:T(8,128)(2,1)S(1)}, bf16[256,1024]{1,0:T(8,128)(2,1)S(1)}, u32[]{:S(2)}, u32[]{:S(2)}) collective-permute-start(bf16[256,1024]{1,0:T(8,128)(2,1)S(1)} %add_convert_fusion.4), channel_id=1, source_target_pairs={{0,2},{1,3},{2,0},{3,1},{4,6},{5,7},{6,4},{7,5},{8,10},{9,11},{10,... | collective-permute-start | bytes 1572872 | tf_op jit(solution)/shard_map/ppermute | solution.py:1058
  120.6 26.3 %collective-permute-start.25 = (bf16[272,1024]{1,0:T(8,128)(2,1)S(1)}, bf16[272,1024]{1,0:T(8,128)(2,1)}, u32[]{:S(2)}, u32[]{:S(2)}) collective-permute-start(bf16[272,1024]{1,0:T(8,128)(2,1)S(1)} %get-tuple-element.225.rest_0_), channel_id=1, source_target_pairs={{0,2},{1,3},{2,0},{3,1},{4,6},{5,7},{6,4},{7,5},{8,10},{9,11},{10,... | collective-permute-start | bytes 1671176 | tf_op jit(solution)/shard_map/ppermute | solution.py:1058
  136.4 20.6 %collective-permute-start.28 = (bf16[272,1024]{1,0:T(8,128)(2,1)}, bf16[272,1024]{1,0:T(8,128)(2,1)}, u32[]{:S(2)}, u32[]{:S(2)}) collective-permute-start(bf16[272,1024]{1,0:T(8,128)(2,1)} %get-tuple-element.230.rest_4_), channel_id=1, source_target_pairs={{0,2},{1,3},{2,0},{3,1},{4,6},{5,7},{6,4},{7,5},{8,10},{9,11},{10,... | collective-permute-start | bytes 1671176 | tf_op jit(solution)/shard_map/ppermute | solution.py:1058
  136.9 21.7 %collective-permute-start.24 = (bf16[272,1024]{1,0:T(8,128)(2,1)S(1)}, bf16[272,1024]{1,0:T(8,128)(2,1)S(1)}, u32[]{:S(2)}, u32[]{:S(2)}) collective-permute-start(bf16[272,1024]{1,0:T(8,128)(2,1)S(1)} %get-tuple-element.225.rest_0_), channel_id=1, source_target_pairs={{0,1},{1,0},{2,3},{3,2},{4,5},{5,4},{6,7},{7,6},{8,9},{9,8},{10,11... | collective-permute-start | bytes 1671176 | tf_op jit(solution)/shard_map/ppermute | solution.py:1058
  146.9 14.1 %collective-permute-start.26 = (bf16[272,1024]{1,0:T(8,128)(2,1)}, bf16[272,1024]{1,0:T(8,128)(2,1)}, u32[]{:S(2)}, u32[]{:S(2)}) collective-permute-start(bf16[272,1024]{1,0:T(8,128)(2,1)} %collective-permute-done.25.rest_2_), channel_id=1, source_target_pairs={{0,1},{1,0},{2,3},{3,2},{4,5},{5,4},{6,7},{7,6},{8,9},{9,8},{10,11... | collective-permute-start | bytes 1671176 | tf_op jit(solution)/shard_map/ppermute | solution.py:1058
  146.9 14.1 %collective-permute-start.27 = (bf16[272,1024]{1,0:T(8,128)(2,1)}, bf16[272,1024]{1,0:T(8,128)(2,1)}, u32[]{:S(2)}, u32[]{:S(2)}) collective-permute-start(bf16[272,1024]{1,0:T(8,128)(2,1)} %get-tuple-element.230.rest_4_), channel_id=1, source_target_pairs={{0,1},{1,0},{2,3},{3,2},{4,5},{5,4},{6,7},{7,6},{8,9},{9,8},{10,11... | collective-permute-start | bytes 1671176 | tf_op jit(solution)/shard_map/ppermute | solution.py:1058
  158.0 17.0 %collective-permute-start.31 = (bf16[256,1024]{1,0:T(8,128)(2,1)}, bf16[256,1024]{1,0:T(8,128)(2,1)}, u32[]{:S(2)}, u32[]{:S(2)}) collective-permute-start(bf16[256,1024]{1,0:T(8,128)(2,1)} %get-tuple-element.236), channel_id=1, source_target_pairs={{0,2},{1,3},{2,0},{3,1},{4,6},{5,7},{6,4},{7,5},{8,10},{9,11},{10,... | collective-permute-start | bytes 1572872 | tf_op jit(solution)/shard_map/ppermute | solution.py:1058
  159.5 24.5 %collective-permute-start.32 = (bf16[256,1024]{1,0:T(8,128)(2,1)}, bf16[256,1024]{1,0:T(8,128)(2,1)}, u32[]{:S(2)}, u32[]{:S(2)}) collective-permute-start(bf16[256,1024]{1,0:T(8,128)(2,1)} %get-tuple-element.237), channel_id=1, source_target_pairs={{0,2},{1,3},{2,0},{3,1},{4,6},{5,7},{6,4},{7,5},{8,10},{9,11},{10,... | collective-permute-start | bytes 1572872 | tf_op jit(solution)/shard_map/ppermute | solution.py:1058
  218.9 14.8 %collective-permute-start.40 = (bf16[256,1024]{1,0:T(8,128)(2,1)S(1)}, bf16[256,1024]{1,0:T(8,128)(2,1)S(1)}, u32[]{:S(2)}, u32[]{:S(2)}) collective-permute-start(bf16[256,1024]{1,0:T(8,128)(2,1)S(1)} %add_convert_fusion.3), channel_id=1, source_target_pairs={{0,2},{1,3},{2,0},{3,1},{4,6},{5,7},{6,4},{7,5},{8,10},{9,11},{10,... | collective-permute-start | bytes 1572872 | tf_op jit(solution)/shard_map/ppermute | solution.py:1058
  219.5 30.5 %collective-permute-start.36 = (bf16[256,1024]{1,0:T(8,128)(2,1)}, bf16[256,1024]{1,0:T(8,128)(2,1)}, u32[]{:S(2)}, u32[]{:S(2)}) collective-permute-start(bf16[256,1024]{1,0:T(8,128)(2,1)} %get-tuple-element.246), channel_id=1, source_target_pairs={{0,1},{1,0},{2,3},{3,2},{4,5},{5,4},{6,7},{7,6},{8,9},{9,8},{10,11... | collective-permute-start | bytes 1572872 | tf_op jit(solution)/shard_map/ppermute | solution.py:1058
  221.3 28.7 %collective-permute-start.38 = (bf16[256,1024]{1,0:T(8,128)(2,1)}, bf16[256,1024]{1,0:T(8,128)(2,1)}, u32[]{:S(2)}, u32[]{:S(2)}) collective-permute-start(bf16[256,1024]{1,0:T(8,128)(2,1)} %add_convert_fusion.2), channel_id=1, source_target_pairs={{0,2},{1,3},{2,0},{3,1},{4,6},{5,7},{6,4},{7,5},{8,10},{9,11},{10,... | collective-permute-start | bytes 1572872 | tf_op jit(solution)/shard_map/ppermute | solution.py:1058
  237.0 23.5 %collective-permute-start.42 = (bf16[256,1024]{1,0:T(8,128)(2,1)}, bf16[256,1024]{1,0:T(8,128)(2,1)}, u32[]{:S(2)}, u32[]{:S(2)}) collective-permute-start(bf16[256,1024]{1,0:T(8,128)(2,1)} %get-tuple-element.254.rest_0_), channel_id=1, source_target_pairs={{0,2},{1,3},{2,0},{3,1},{4,6},{5,7},{6,4},{7,5},{8,10},{9,11},{10,... | collective-permute-start | bytes 1572872 | tf_op jit(solution)/shard_map/ppermute | solution.py:1058
  237.6 24.3 %collective-permute-start.41 = (bf16[256,1024]{1,0:T(8,128)(2,1)}, bf16[256,1024]{1,0:T(8,128)(2,1)S(1)}, u32[]{:S(2)}, u32[]{:S(2)}) collective-permute-start(bf16[256,1024]{1,0:T(8,128)(2,1)} %get-tuple-element.254.rest_0_), channel_id=1, source_target_pairs={{0,1},{1,0},{2,3},{3,2},{4,5},{5,4},{6,7},{7,6},{8,9},{9,8},{10,11... | collective-permute-start | bytes 1572872 | tf_op jit(solution)/shard_map/ppermute | solution.py:1058
  261.1 25.4 %collective-permute-start.44 = (bf16[512,1024]{1,0:T(8,128)(2,1)}, bf16[512,1024]{1,0:T(8,128)(2,1)S(1)}, u32[]{:S(2)}, u32[]{:S(2)}) collective-permute-start(bf16[512,1024]{1,0:T(8,128)(2,1)} %get-tuple-element.256), channel_id=1, source_target_pairs={{0,4},{4,0},{8,12},{12,8},{16,20},{20,16},{24,28},{28,24},{1,5},{5... | collective-permute-start | bytes 3145736 | tf_op jit(solution)/shard_map/ppermute | solution.py:1058
  276.7 13.9 %collective-permute-start.47 = (bf16[256,1024]{1,0:T(8,128)(2,1)S(1)}, bf16[256,1024]{1,0:T(8,128)(2,1)S(1)}, u32[]{:S(2)}, u32[]{:S(2)}) collective-permute-start(bf16[256,1024]{1,0:T(8,128)(2,1)S(1)} %get-tuple-element.258.rest_0_), channel_id=1, source_target_pairs={{0,2},{1,3},{2,0},{3,1},{4,6},{5,7},{6,4},{7,5},{8,10},{9,11},{10,... | collective-permute-start | bytes 1572872 | tf_op jit(solution)/shard_map/ppermute | solution.py:1058
  278.3 14.8 %collective-permute-start.46 = (bf16[256,1024]{1,0:T(8,128)(2,1)S(1)}, bf16[256,1024]{1,0:T(8,128)(2,1)S(1)}, u32[]{:S(2)}, u32[]{:S(2)}) collective-permute-start(bf16[256,1024]{1,0:T(8,128)(2,1)S(1)} %get-tuple-element.258.rest_0_), channel_id=1, source_target_pairs={{0,1},{1,0},{2,3},{3,2},{4,5},{5,4},{6,7},{7,6},{8,9},{9,8},{10,11... | collective-permute-start | bytes 1572872 | tf_op jit(solution)/shard_map/ppermute | solution.py:1058
  290.6 25.8 %collective-permute-start.53 = (bf16[512,1024]{1,0:T(8,128)(2,1)}, bf16[512,1024]{1,0:T(8,128)(2,1)S(1)}, u32[]{:S(2)}, u32[]{:S(2)}) collective-permute-start(bf16[512,1024]{1,0:T(8,128)(2,1)} %copy-done.61), channel_id=1, source_target_pairs={{0,4},{4,0},{8,12},{12,8},{16,20},{20,16},{24,28},{28,24},{1,5},{5... | collective-permute-start | bytes 3145736 | tf_op jit(solution)/shard_map/ppermute | solution.py:1058
  291.5 16.1 %collective-permute-start.52 = (bf16[256,1024]{1,0:T(8,128)(2,1)S(1)}, bf16[256,1024]{1,0:T(8,128)(2,1)S(1)}, u32[]{:S(2)}, u32[]{:S(2)}) collective-permute-start(bf16[256,1024]{1,0:T(8,128)(2,1)S(1)} %get-tuple-element.271), channel_id=1, source_target_pairs={{0,8},{4,12},{8,0},{12,4},{16,24},{20,28},{24,16},{28,20},{1,9},{5... | collective-permute-start | bytes 1572872 | tf_op jit(solution)/shard_map/ppermute | solution.py:1058
  293.1 25.9 %collective-permute-start.50 = (bf16[256,1024]{1,0:T(8,128)(2,1)S(1)}, bf16[256,1024]{1,0:T(8,128)(2,1)S(1)}, u32[]{:S(2)}, u32[]{:S(2)}) collective-permute-start(bf16[256,1024]{1,0:T(8,128)(2,1)S(1)} %get-tuple-element.285), channel_id=1, source_target_pairs={{0,1},{1,0},{2,3},{3,2},{4,5},{5,4},{6,7},{7,6},{8,9},{9,8},{10,11... | collective-permute-start | bytes 1572872 | tf_op jit(solution)/shard_map/ppermute | solution.py:1058
  293.1 25.9 %collective-permute-start.51 = (bf16[256,1024]{1,0:T(8,128)(2,1)S(1)}, bf16[256,1024]{1,0:T(8,128)(2,1)S(1)}, u32[]{:S(2)}, u32[]{:S(2)}) collective-permute-start(bf16[256,1024]{1,0:T(8,128)(2,1)S(1)} %add_convert_fusion.1), channel_id=1, source_target_pairs={{0,2},{1,3},{2,0},{3,1},{4,6},{5,7},{6,4},{7,5},{8,10},{9,11},{10,... | collective-permute-start | bytes 1572872 | tf_op jit(solution)/shard_map/ppermute | solution.py:1058
  307.4 14.1 %collective-permute-start.54 = (bf16[256,1024]{1,0:T(8,128)(2,1)S(1)}, bf16[256,1024]{1,0:T(8,128)(2,1)S(1)}, u32[]{:S(2)}, u32[]{:S(2)}) collective-permute-start(bf16[256,1024]{1,0:T(8,128)(2,1)S(1)} %get-tuple-element.288), channel_id=1, source_target_pairs={{0,1},{1,0},{2,3},{3,2},{4,5},{5,4},{6,7},{7,6},{8,9},{9,8},{10,11... | collective-permute-start | bytes 1572872 | tf_op jit(solution)/shard_map/ppermute | solution.py:1058
  317.4 22.4 %collective-permute-start.57 = (bf16[256,1024]{1,0:T(8,128)(2,1)S(1)}, bf16[256,1024]{1,0:T(8,128)(2,1)S(1)}, u32[]{:S(2)}, u32[]{:S(2)}) collective-permute-start(bf16[256,1024]{1,0:T(8,128)(2,1)S(1)} %get-tuple-element.292), channel_id=1, source_target_pairs={{0,8},{4,12},{8,0},{12,4},{16,24},{20,28},{24,16},{28,20},{1,9},{5... | collective-permute-start | bytes 1572872 | tf_op jit(solution)/shard_map/ppermute | solution.py:1058
  319.0 23.7 %collective-permute-start.49 = (bf16[256,1024]{1,0:T(8,128)(2,1)S(1)}, bf16[256,1024]{1,0:T(8,128)(2,1)S(1)}, u32[]{:S(2)}, u32[]{:S(2)}) collective-permute-start(bf16[256,1024]{1,0:T(8,128)(2,1)S(1)} %get-tuple-element.282), channel_id=1, source_target_pairs={{0,1},{1,0},{2,3},{3,2},{4,5},{5,4},{6,7},{7,6},{8,9},{9,8},{10,11... | collective-permute-start | bytes 1572872 | tf_op jit(solution)/shard_map/ppermute | solution.py:1058
  321.7 21.1 %collective-permute-start.55 = (bf16[256,1024]{1,0:T(8,128)(2,1)S(1)}, bf16[256,1024]{1,0:T(8,128)(2,1)S(1)}, u32[]{:S(2)}, u32[]{:S(2)}) collective-permute-start(bf16[256,1024]{1,0:T(8,128)(2,1)S(1)} %add_convert_fusion), channel_id=1, source_target_pairs={{0,2},{1,3},{2,0},{3,1},{4,6},{5,7},{6,4},{7,5},{8,10},{9,11},{10,... | collective-permute-start | bytes 1572872 | tf_op jit(solution)/shard_map/ppermute | solution.py:1058
  335.6 14.6 %collective-permute-start.59 = (bf16[512,512]{1,0:T(8,128)(2,1)S(1)}, bf16[512,512]{1,0:T(8,128)(2,1)S(1)}, u32[]{:S(2)}, u32[]{:S(2)}) collective-permute-start(bf16[512,512]{1,0:T(8,128)(2,1)S(1)} %get-tuple-element.305), channel_id=1, source_target_pairs={{0,4},{4,0},{8,12},{12,8},{16,20},{20,16},{24,28},{28,24},{1,5},{5... | collective-permute-start | bytes 1572872 | tf_op jit(solution)/shard_map/ppermute | solution.py:1058
  336.5 19.2 %collective-permute-start.60 = (bf16[512,512]{1,0:T(8,128)(2,1)S(1)}, bf16[512,512]{1,0:T(8,128)(2,1)S(1)}, u32[]{:S(2)}, u32[]{:S(2)}) collective-permute-start(bf16[512,512]{1,0:T(8,128)(2,1)S(1)} %get-tuple-element.306), channel_id=1, source_target_pairs={{0,8},{4,12},{8,0},{12,4},{16,24},{20,28},{24,16},{28,20},{1,9},{5... | collective-permute-start | bytes 1572872 | tf_op jit(solution)/shard_map/ppermute | solution.py:1058
  339.8 16.6 %collective-permute-start.61 = (bf16[128,1024]{1,0:T(8,128)(2,1)S(1)}, bf16[128,1024]{1,0:T(8,128)(2,1)S(1)}, u32[]{:S(2)}, u32[]{:S(2)}) collective-permute-start(bf16[128,1024]{1,0:T(8,128)(2,1)S(1)} %halve_step.15.own_ref), channel_id=1, source_target_pairs={{0,16},{4,20},{8,24},{12,28},{16,0},{20,4},{24,8},{28,12},{1,17},{... | collective-permute-start | bytes 786440 | tf_op jit(solution)/shard_map/ppermute | solution.py:1058
  357.0 31.1 %collective-permute-start.66 = (bf16[256,1024]{1,0:T(8,128)(2,1)S(1)}, bf16[256,1024]{1,0:T(8,128)(2,1)S(1)}, u32[]{:S(2)}, u32[]{:S(2)}) collective-permute-start(bf16[256,1024]{1,0:T(8,128)(2,1)S(1)} %bitcast.42), channel_id=1, source_target_pairs={{0,8},{4,12},{8,0},{12,4},{16,24},{20,28},{24,16},{28,20},{1,9},{5... | collective-permute-start | bytes 1572872 | tf_op jit(solution)/shard_map/ppermute | solution.py:1058
  359.1 18.0 %collective-permute-start.62 = (bf16[128,1024]{1,0:T(8,128)(2,1)S(1)}, bf16[128,1024]{1,0:T(8,128)(2,1)S(1)}, u32[]{:S(2)}, u32[]{:S(2)}) collective-permute-start(bf16[128,1024]{1,0:T(8,128)(2,1)S(1)} %get-tuple-element.309), channel_id=1, source_target_pairs={{0,16},{4,20},{8,24},{12,28},{16,0},{20,4},{24,8},{28,12},{1,17},{... | collective-permute-start | bytes 786440 | tf_op jit(solution)/shard_map/ppermute | solution.py:1058
  361.6 25.3 %collective-permute-start.64 = (bf16[256,512]{1,0:T(8,128)(2,1)S(1)}, bf16[256,512]{1,0:T(8,128)(2,1)S(1)}, u32[]{:S(2)}, u32[]{:S(2)}) collective-permute-start(bf16[256,512]{1,0:T(8,128)(2,1)S(1)} %get-tuple-element.324), channel_id=1, source_target_pairs={{0,8},{4,12},{8,0},{12,4},{16,24},{20,28},{24,16},{28,20},{1,9},{5... | collective-permute-start | bytes 786440 | tf_op jit(solution)/shard_map/ppermute | solution.py:1058
  361.6 25.9 %collective-permute-start.65 = (bf16[256,512]{1,0:T(8,128)(2,1)S(1)}, bf16[256,512]{1,0:T(8,128)(2,1)S(1)}, u32[]{:S(2)}, u32[]{:S(2)}) collective-permute-start(bf16[256,512]{1,0:T(8,128)(2,1)S(1)} %get-tuple-element.327), channel_id=1, source_target_pairs={{0,4},{4,0},{8,12},{12,8},{16,20},{20,16},{24,28},{28,24},{1,5},{5... | collective-permute-start | bytes 786440 | tf_op jit(solution)/shard_map/ppermute | solution.py:1058
  390.6 18.0 %collective-permute-start.71 = (bf16[256,1024]{1,0:T(8,128)(2,1)S(1)}, bf16[256,1024]{1,0:T(8,128)(2,1)S(1)}, u32[]{:S(2)}, u32[]{:S(2)}) collective-permute-start(bf16[256,1024]{1,0:T(8,128)(2,1)S(1)} %bitcast.44), channel_id=1, source_target_pairs={{0,8},{4,12},{8,0},{12,4},{16,24},{20,28},{24,16},{28,20},{1,9},{5... | collective-permute-start | bytes 1572872 | tf_op jit(solution)/shard_map/ppermute | solution.py:1058
  391.9 15.5 %collective-permute-start.69 = (bf16[128,512]{1,0:T(8,128)(2,1)S(1)}, bf16[128,512]{1,0:T(8,128)(2,1)S(1)}, u32[]{:S(2)}, u32[]{:S(2)}) collective-permute-start(bf16[128,512]{1,0:T(8,128)(2,1)S(1)} %get-tuple-element.334), channel_id=1, source_target_pairs={{0,16},{4,20},{8,24},{12,28},{16,0},{20,4},{24,8},{28,12},{1,17},{... | collective-permute-start | bytes 393224 | tf_op jit(solution)/shard_map/ppermute | solution.py:1058
  393.2 14.8 %collective-permute-start.70 = (bf16[128,512]{1,0:T(8,128)(2,1)S(1)}, bf16[128,512]{1,0:T(8,128)(2,1)S(1)}, u32[]{:S(2)}, u32[]{:S(2)}) collective-permute-start(bf16[128,512]{1,0:T(8,128)(2,1)S(1)} %get-tuple-element.337), channel_id=1, source_target_pairs={{0,16},{4,20},{8,24},{12,28},{16,0},{20,4},{24,8},{28,12},{1,17},{... | collective-permute-start | bytes 393224 | tf_op jit(solution)/shard_map/ppermute | solution.py:1058
  396.1 57.8 %collective-permute-start.81 = (bf16[512,1024]{1,0:T(8,128)(2,1)S(1)}, bf16[512,1024]{1,0:T(8,128)(2,1)S(1)}, u32[]{:S(2)}, u32[]{:S(2)}) collective-permute-start(bf16[512,1024]{1,0:T(8,128)(2,1)S(1)} %bitcast.38), channel_id=1, source_target_pairs={{0,4},{4,0},{8,12},{12,8},{16,20},{20,16},{24,28},{28,24},{1,5},{5... | collective-permute-start | bytes 3145736 | tf_op jit(solution)/shard_map/ppermute | solution.py:1058
  409.3 53.9 %collective-permute-start.80 = (bf16[512,1024]{1,0:T(8,128)(2,1)S(1)}, bf16[512,1024]{1,0:T(8,128)(2,1)S(1)}, u32[]{:S(2)}, u32[]{:S(2)}) collective-permute-start(bf16[512,1024]{1,0:T(8,128)(2,1)S(1)} %bitcast.40), channel_id=1, source_target_pairs={{0,4},{4,0},{8,12},{12,8},{16,20},{20,16},{24,28},{28,24},{1,5},{5... | collective-permute-start | bytes 3145736 | tf_op jit(solution)/shard_map/ppermute | solution.py:1058
  426.0 24.3 %collective-permute-start.78 = (bf16[256,512]{1,0:T(8,128)(2,1)S(1)}, bf16[256,512]{1,0:T(8,128)(2,1)S(1)}, u32[]{:S(2)}, u32[]{:S(2)}) collective-permute-start(bf16[256,512]{1,0:T(8,128)(2,1)S(1)} %bitcast.52), channel_id=1, source_target_pairs={{0,4},{4,0},{8,12},{12,8},{16,20},{20,16},{24,28},{28,24},{1,5},{5... | collective-permute-start | bytes 786440 | tf_op jit(solution)/shard_map/ppermute | solution.py:1058
  432.5 25.2 %collective-permute-start.77 = (bf16[512,512]{1,0:T(8,128)(2,1)S(1)}, bf16[512,512]{1,0:T(8,128)(2,1)S(1)}, u32[]{:S(2)}, u32[]{:S(2)}) collective-permute-start(bf16[512,512]{1,0:T(8,128)(2,1)S(1)} %bitcast.46), channel_id=1, source_target_pairs={{0,4},{4,0},{8,12},{12,8},{16,20},{20,16},{24,28},{28,24},{1,5},{5... | collective-permute-start | bytes 1572872 | tf_op jit(solution)/shard_map/ppermute | solution.py:1058
  (102 other events, 1349.6 us)

commit v3 on v2

--- a/solution.py
+++ b/solution.py
@@ -17,7 +17,7 @@
 F32 = jnp.float32
 BF16 = jnp.bfloat16
 MIB = 1 << 20
-LIMIT, SMALL = 40, 16
+LIMIT, SMALL = 52, 14
 COST = 0.02
 NN = (((1,), (0,)), ((), ()))
 NT = (((1,), (1,)), ((), ()))
@@ -60,6 +60,7 @@
 
 ANY = pl.BlockSpec(memory_space=pl.ANY)
 HBM = pl.BlockSpec(memory_space=pltpu.HBM)
+SMEM = pl.BlockSpec(memory_space=pltpu.SMEM)
 DMA = pltpu.SemaphoreType.DMA
 
 
@@ -207,7 +208,7 @@
             z, rstd = norm_stats(v_ref[at, :])
             w = got * g[...]
             inner = rstd * (w - jnp.mean(w, axis=-1, keepdims=True) - z * jnp.mean(w * z, axis=-1, keepdims=True))
-            old = base_ref[at, :] if final else base_ref[0, at, :]
+            old = base_ref[at, :]
             new = old + inner
             if final:
                 out[0, at, :] = new
@@ -237,7 +238,7 @@
         body,
         outs,
         specs,
-        [block] * 4 + [whole((1, feats)), block if final else seq_block] + [ANY] * len(extra),
+        [block] * 4 + [whole((1, feats)), block] + [ANY] * len(extra),
         grid=(ROW_STEPS,),
         nbytes=rows * feats * 20,
         aliases={6: 0} if extra else None,
@@ -259,12 +260,16 @@
         pltpu.make_async_copy(src, ref, sems.at[r]).wait()
 
 
+def block_at(rel, rows):
+    return pl.ds(pl.multiple_of(rel * rows, rows), rows)
+
+
 def lane_pair(first, second, rows):
     lanes = lax.broadcasted_iota(jnp.int32, (rows, 128), 1)
     return jnp.where(lanes == 0, first, second)
 
 
-def attend_forward(seq, seqs, place, docs_row, blocks, wqkv, q_shift, v_shift, wo, previous):
+def attend_forward(seq, place, docs, vecs, blocks, wqkv, wo, previous):
     rows, feats = blocks[0].shape
     parts = len(blocks)
     length = rows * parts
@@ -273,9 +278,12 @@
     heads = width // size
     scale = LOG2E * size ** (-0.5)
 
-    def body(t_ref, dr, qb, vb, *rest):
+    seqs = docs.shape[0]
+
+    def body(t_ref, doc_ref, vec, *rest):
+        dr = doc_ref[seq : seq + 1, :].astype(F32)
         x_refs, (w_ref, wo_ref), rest = rest[:4], rest[4:6], rest[6:]
-        p_refs, (cat, qkv_out, att_out, lse_out), rest = rest[-19:-15], rest[-15:-11], rest[-11:]
+        p_refs, (saved, lse_out), rest = rest[-17:-13], rest[-13:-11], rest[-11:]
         xs, w, wov, qkv, att, lse, ps, in_sem, p_sem, c_sem, o_sem = rest
         t = t_ref[0]
         load_w = move(w_ref, w, in_sem.at[4])
@@ -288,12 +296,12 @@
         def project(i):
             pltpu.make_async_copy(x_refs[0], xs.at[i], in_sem.at[i]).wait()
             rel = lax.bitwise_xor(jnp.int32(i), t)
-            pending.append(move(xs.at[i], cat.at[seq, pl.ds(pl.multiple_of(rel * rows, rows), rows)], c_sem.at[i]))
+            pending.append(move(xs.at[i], saved.at[seq, block_at(rel, rows), pl.ds(0, feats)], c_sem.at[i]))
             x = xs[i]
             at = slice(i * rows, (i + 1) * rows)
-            qkv[0, at, :] = (dot(x, w[0]) + qb[...]).astype(BF16)
+            qkv[0, at, :] = (dot(x, w[0]) + vec[:, :width]).astype(BF16)
             qkv[1, at, :] = dot(x, w[1]).astype(BF16)
-            qkv[2, at, :] = (dot(x, w[2]) + vb[...]).astype(BF16)
+            qkv[2, at, :] = (dot(x, w[2]) + vec[:, width:]).astype(BF16)
 
         load_w.wait()
         project(0)
@@ -322,26 +330,25 @@
             rel = lax.bitwise_xor(jnp.int32(i), t)
             send_block(p_refs, rel, ps.at[i], p_sem)
             pending.append(
-                move(att.at[i], att_out.at[seq, pl.ds(pl.multiple_of(rel * rows, rows), rows)], o_sem.at[i])
+                move(att.at[i], saved.at[seq, block_at(rel, rows), pl.ds(feats + 3 * width, width)], o_sem.at[i])
             )
-        pending.append(move(qkv, qkv_out, in_sem.at[4]))
+        for c in range(3):
+            pending.append(move(qkv.at[c], saved.at[seq, :, pl.ds(feats + c * width, width)], o_sem.at[parts + c]))
         pending.append(move(lse, lse_out, in_sem.at[5]))
         for copy in pending:
             copy.wait()
         wait_blocks(p_refs, ps.at[0], p_sem)
 
-    extra = [] if previous is None else list(previous)
+    extra = [] if previous is None else [previous]
     return kernel_call(
         body,
         (
             *[struct((rows, feats), BF16)] * 4,
-            struct((seqs, length, feats), BF16),
-            struct((3, length, width), BF16),
-            struct((seqs, length, width), BF16),
+            struct((2 * seqs, length, feats + 4 * width), BF16),
             struct((length, 128), F32),
         ),
-        (ANY,) * 4 + (HBM,) * 4,
-        [pl.BlockSpec(memory_space=pltpu.SMEM), whole((1, length)), whole((1, width)), whole((1, width))]
+        (ANY,) * 4 + (HBM,) * 2,
+        [SMEM, whole(docs.shape), whole(vecs.shape)]
         + [ANY] * 4
         + [HBM] * (2 + len(extra)),
         scratch=[
@@ -355,17 +362,17 @@
             DMA((6,)),
             DMA((4,)),
             DMA((4,)),
-            DMA((4,)),
+            DMA((7,)),
         ],
         flops=2 * length * feats * width * 4 + 5 * length * length * width,
         nbytes=length * feats * 8,
         trans=length * length * heads // 2,
-        aliases={10: 4, 11: 6} if extra else None,
+        aliases={9: 4} if extra else None,
         name="attend_forward",
-    )(place, docs_row, q_shift, v_shift, *blocks, wqkv, wo, *extra)
-
-
-def attend_backward(seq, seqs, place, docs_row, blocks, qkv, att, lse, wqkv, wo, previous):
+    )(place, docs, vecs, *blocks, wqkv, wo, *extra)
+
+
+def attend_backward(seq, place, docs, blocks, saved, lse, wqkv, wo, previous):
     rows, feats = blocks[0].shape
     parts = len(blocks)
     length = rows * parts
@@ -375,29 +382,32 @@
     root = size ** (-0.5)
     scale = LOG2E * root
 
-    def body(t_ref, dr, *rest):
-        x_refs, (qkv_ref, att_ref, lse_ref, w_ref, wo_ref), rest = rest[:4], rest[4:9], rest[9:]
-        p_refs, (cat, gq_out, gk_out, gv_out, sums), rest = rest[-23:-19], rest[-19:-14], rest[-14:]
+    seqs = docs.shape[0]
+
+    def body(t_ref, doc_ref, *rest):
+        dr = doc_ref[seq : seq + 1, :].astype(F32)
+        x_refs, (saved_ref, lse_ref, w_ref, wo_ref), rest = rest[:4], rest[4:8], rest[8:]
+        p_refs, (out, sums), rest = rest[-20:-16], rest[-16:-14], rest[-14:]
         xs, w, wov, qkvv, attv, lsev, gk, gv, ga, low, ps, in_sem, p_sem, o_sem = rest
         t = t_ref[0]
         load_wo = move(wo_ref, wov, in_sem.at[4])
         for r in (3, 2, 1, 0):
             at = lax.bitwise_xor(jnp.int32(r), t)
             move(x_refs[r], xs.at[at], in_sem.at[at])
-        loads = [move(qkv_ref, qkvv, in_sem.at[5]), move(lse_ref, lsev, in_sem.at[6])]
+        loads = [move(lse_ref, lsev, in_sem.at[6])]
+        for c in range(3):
+            loads.append(move(saved_ref.at[seq, :, pl.ds(feats + c * width, width)], qkvv.at[c], in_sem.at[12 + c]))
         for i in range(parts):
             rel = lax.bitwise_xor(jnp.int32(i), t)
-            at = pl.ds(pl.multiple_of(rel * rows, rows), rows)
-            loads.append(move(att_ref.at[seq, at], attv.at[i], in_sem.at[8 + i]))
+            att_ref = saved_ref.at[seq, block_at(rel, rows), pl.ds(feats + 3 * width, width)]
+            loads.append(move(att_ref, attv.at[i], in_sem.at[8 + i]))
         load_w = move(w_ref, w, in_sem.at[7])
         pending = []
 
         def project(i):
             pltpu.make_async_copy(x_refs[0], xs.at[i], in_sem.at[i]).wait()
             rel = lax.bitwise_xor(jnp.int32(i), t)
-            pending.append(
-                move(xs.at[i], cat.at[seq, pl.ds(pl.multiple_of(rel * rows, rows), rows)], o_sem.at[i])
-            )
+            pending.append(move(xs.at[i], out.at[seq, block_at(rel, rows), pl.ds(0, feats)], o_sem.at[i]))
             ga[i] = dot(xs[i], wov[...], NT).astype(BF16)
 
         load_wo.wait()
@@ -445,26 +455,25 @@
             ).astype(BF16)
             rel = lax.bitwise_xor(jnp.int32(i), t)
             send_block(p_refs, rel, ps.at[i], p_sem)
-            at = pl.ds(pl.multiple_of(rel * rows, rows), rows)
-            for c, out in enumerate((gq_out, gk_out, gv_out)):
-                pending.append(move(low.at[c, own], out.at[seq, at], o_sem.at[4 + 3 * i + c]))
+            for c in range(3):
+                dst = out.at[seq, block_at(rel, rows), pl.ds(feats + c * width, width)]
+                pending.append(move(low.at[c, own], dst, o_sem.at[4 + 3 * i + c]))
         sums[0:1, :] = q_sum
         sums[1:2, :] = v_sum
         for copy in pending:
             copy.wait()
         wait_blocks(p_refs, ps.at[0], p_sem)
 
-    extra = [] if previous is None else list(previous)
+    extra = [] if previous is None else [previous]
     return kernel_call(
         body,
         (
             *[struct((rows, feats), BF16)] * 4,
-            struct((seqs, length, feats), BF16),
-            *[struct((seqs, length, width), BF16)] * 3,
+            struct((2 * seqs, length, feats + 4 * width), BF16),
             struct((2, width), F32),
         ),
-        (ANY,) * 4 + (HBM,) * 4 + (whole((2, width)),),
-        [pl.BlockSpec(memory_space=pltpu.SMEM), whole((1, length))] + [ANY] * 4 + [HBM] * (5 + len(extra)),
+        (ANY,) * 4 + (HBM, whole((2, width))),
+        [SMEM, whole(docs.shape)] + [ANY] * 4 + [HBM] * (4 + len(extra)),
         scratch=[
             VMEM((parts, rows, feats), BF16),
             VMEM(wqkv.shape, BF16),
@@ -477,31 +486,34 @@
             VMEM((parts, rows, width), BF16),
             VMEM((3, length, width), BF16),
             VMEM((parts, rows, feats), BF16),
-            DMA((12,)),
+            DMA((15,)),
             DMA((4,)),
             DMA((16,)),
         ],
         flops=2 * length * feats * width * 4 + 10 * length * length * width,
         nbytes=length * feats * 8,
         trans=length * length * heads // 2,
-        aliases={11: 4, 12: 5, 13: 6, 14: 7} if extra else None,
+        aliases={10: 4} if extra else None,
         name="attend_backward",
-    )(place, docs_row, *blocks, qkv, att, lse, wqkv, wo, *extra)
+    )(place, docs, *blocks, saved, lse, wqkv, wo, *extra)
 
 
 ORDER = (3, 1, 2, 0)
 
 
-def feed_forward(seq, seqs, blocks, w_up, b_up, w_down, previous):
+ROWS, ACT, SLOPE, GRAD = range(4)
+
+
+def feed_forward(seq, seqs, blocks, vecs, w_up, w_down, previous):
     rows, feats = blocks[0].shape
     parts = len(blocks)
     length = rows * parts
     units = w_up.shape[1]
     root = math.sqrt(2.0 / math.pi)
 
-    def body(bu, *rest):
+    def body(vec, *rest):
         x_refs, (up_ref, down_ref), rest = rest[:4], rest[4:6], rest[6:]
-        p_refs, (cat, act_out, slope_out), rest = rest[-17:-13], rest[-13:-10], rest[-10:]
+        p_refs, saved, rest = rest[-15:-11], rest[-11], rest[-10:]
         xs, up, down, u, act, slope, ps, in_sem, p_sem, o_sem = rest
         load_up = move(up_ref, up, in_sem.at[4])
         loads = {r: move(x_refs[r], xs.at[r], in_sem.at[r]) for r in ORDER}
@@ -511,8 +523,8 @@
         def project(k):
             r = ORDER[k]
             loads[r].wait()
-            pending.append(move(xs.at[r], cat.at[seq, pl.ds(r * rows, rows)], o_sem.at[r]))
-            u[k % 2] = dot(xs[r], up[...]) + bu[...]
+            pending.append(move(xs.at[r], saved.at[ROWS, seq, pl.ds(r * rows, rows)], o_sem.at[r]))
+            u[k % 2] = dot(xs[r], up[...]) + vec[...]
 
         load_up.wait()
         project(0)
@@ -530,22 +542,20 @@
             ps[r] = dot(g, down[...]).astype(BF16)
             at = pl.ds(r * rows, rows)
             pending.append(move(ps.at[r], p_refs[r], p_sem.at[r]))
-            pending.append(move(act.at[r], act_out.at[seq, at], o_sem.at[4 + r]))
-            pending.append(move(slope.at[r], slope_out.at[seq, at], o_sem.at[8 + r]))
+            pending.append(move(act.at[r], saved.at[ACT, seq, at], o_sem.at[4 + r]))
+            pending.append(move(slope.at[r], saved.at[SLOPE, seq, at], o_sem.at[8 + r]))
         for copy in pending:
             copy.wait()
 
-    extra = [] if previous is None else list(previous)
+    extra = [] if previous is None else [previous]
     return kernel_call(
         body,
         (
             *[struct((rows, feats), BF16)] * 4,
-            struct((seqs, length, feats), BF16),
-            struct((seqs, length, units), BF16),
-            struct((seqs, length, units), BF16),
+            struct((4, seqs, length, units), BF16),
         ),
-        (ANY,) * 4 + (HBM,) * 3,
-        [whole((1, units))] + [ANY] * 4 + [HBM] * (2 + len(extra)),
+        (ANY,) * 4 + (HBM,),
+        [whole(vecs.shape)] + [ANY] * 4 + [HBM] * (2 + len(extra)),
         scratch=[
             VMEM((parts, rows, feats), BF16),
             VMEM(w_up.shape, BF16),
@@ -561,25 +571,26 @@
         flops=4 * length * feats * units,
         nbytes=length * feats * 14,
         trans=length * units,
-        aliases={7: 4, 8: 5, 9: 6} if extra else None,
+        aliases={7: 4} if extra else None,
         name="feed_forward",
-    )(b_up, *blocks, w_up, w_down, *extra)
-
-
-def feed_backward(seq, seqs, own, got, slope, w_up, w_down, previous):
+    )(vecs, *blocks, w_up, w_down, *extra)
+
+
+def feed_backward(seq, own, got, saved, w_up, w_down, earlier):
     rows, feats = own.shape[1:]
     parts = 4
     length = rows * parts
     units = w_up.shape[1]
-
-    def body(own_ref, got_ref, slope_ref, up_ref, down_ref, *rest):
+    seqs = saved.shape[1]
+
+    def body(own_ref, got_ref, saved_ref, up_ref, down_ref, *rest):
         p_refs, (grad_out, sums), rest = rest[-16:-12], rest[-12:-10], rest[-10:]
         ys, up, down, slopes, u, grad, ps, in_sem, p_sem, o_sem = rest
         load_down = move(down_ref, down, in_sem.at[4])
         loads, slope_loads = {}, {}
         for r in ORDER:
             loads[r] = move((got_ref if r % 2 else own_ref).at[r // 2], ys.at[r], in_sem.at[r])
-            slope_loads[r] = move(slope_ref.at[seq, pl.ds(r * rows, rows)], slopes.at[r], in_sem.at[6 + r])
+            slope_loads[r] = move(saved_ref.at[SLOPE, seq, pl.ds(r * rows, rows)], slopes.at[r], in_sem.at[6 + r])
         load_up = move(up_ref, up, in_sem.at[5])
         pending = []
 
@@ -601,21 +612,20 @@
             total += jnp.sum(gu.astype(F32).reshape(rows // 8, 8, units), axis=0)
             ps[r] = dot(gu, up[...], NT).astype(BF16)
             pending.append(move(ps.at[r], p_refs[r], p_sem.at[r]))
-            pending.append(move(grad.at[r], grad_out.at[seq, pl.ds(r * rows, rows)], o_sem.at[4 + r]))
+            pending.append(move(grad.at[r], grad_out.at[GRAD, seq, pl.ds(r * rows, rows)], o_sem.at[4 + r]))
         sums[...] = jnp.sum(total, axis=0, keepdims=True)
         for copy in pending:
             copy.wait()
 
-    extra = [] if previous is None else [previous]
     return kernel_call(
         body,
         (
             *[struct((rows, feats), BF16)] * 4,
-            struct((seqs, length, units), BF16),
+            struct((4, seqs, length, units), BF16),
             struct((1, units), F32),
         ),
         (ANY,) * 4 + (HBM, whole((1, units))),
-        [ANY] * 2 + [HBM] * (3 + len(extra)),
+        [ANY] * 2 + [HBM] * 3 + [ANY] * len(earlier),
         scratch=[
             VMEM((parts, rows, feats), BF16),
             VMEM(w_up.shape, BF16),
@@ -630,48 +640,65 @@
         ],
         flops=4 * length * feats * units,
         nbytes=length * feats * 14,
-        aliases={5: 4} if extra else None,
+        aliases={2: 4},
         name="feed_backward",
-    )(own, got, slope, w_up, w_down, *extra)
-
-
-def contrast_scores(place, docs, labels, units):
+    )(own, got, saved, w_up, w_down, *earlier)
+
+
+def entries(ref, seq, part, place, rows):
+    at = lax.bitwise_xor(jnp.int32(part), place) * rows
+    return ref[seq : seq + 1, pl.ds(pl.multiple_of(at, rows), rows)].astype(F32)
+
+
+def contrast_scores(place, ends, docs, labels, units):
     rows, feats = units[0].shape[0] - EXTRA, units[0].shape[1]
     factor = CONTRAST_SCALE / feats * LOG2E
     count = len(units)
     seqs = count // 4
 
-    def body(t_ref, doc_ref, lab_ref, *rest):
-        refs, (exp_out, col_out, row_out, loss_out, both, exps, in_sem, out_sem) = rest[:count], rest[count:]
+    def body(t_ref, end_ref, doc_ref, lab_ref, *rest):
+        refs, rest = rest[:count], rest[count:]
+        exp_out, col_out, row_out, loss_out, both, exps, sums, in_sem, out_sem = rest
         t = t_ref[0]
         loads = [move(refs[k].at[pl.ds(0, rows)], both.at[k], in_sem.at[k]) for k in range(count)]
+        for copy in loads:
+            copy.wait()
         pending = []
         for s in range(4):
             seq, part = s // 2, s % 2 * 2
-            if s == 0:
-                loads[0].wait()
-            own_at = lax.bitwise_xor(jnp.int32(part), t)
-            own_doc = column(doc_ref[seq, own_at])
-            own_lab = column(lab_ref[seq, own_at])
-            total = jnp.zeros((rows, 128), F32)
-            total_pos = jnp.zeros((rows, 128), F32)
-            for k in range(count):
-                if s == 0 and k:
-                    loads[k].wait()
-                other = k // 4
+            own_lab = column(entries(lab_ref, seq, part, t, rows))
+
+            def block(k, own_doc, seq=seq, part=part, s=s, own_lab=own_lab):
                 e = jnp.exp2(dot(both[seq * 4 + part], both[k], NT) * factor)
-                at = lax.bitwise_xor(jnp.int32(k % 4), t)
-                if seq == other:
-                    e = jnp.where(own_doc != doc_ref[other, at], e, 0.0)
-                picked = jnp.where(own_lab == lab_ref[other, at], e, 0.0)
-                for c in range(rows // 128):
-                    lanes = slice(c * 128, (c + 1) * 128)
-                    total += e[:, lanes]
-                    total_pos += picked[:, lanes]
+                if own_doc is not None:
+                    e = jnp.where(own_doc != entries(doc_ref, seq, k % 4, t, rows), e, 0.0)
                 exps[s, :, k * rows : (k + 1) * rows] = e.astype(BF16)
+                picked = jnp.where(own_lab == entries(lab_ref, k // 4, k % 4, t, rows), e, 0.0)
+                lanes = [slice(c * 128, (c + 1) * 128) for c in range(rows // 128)]
+                fold = lambda v: functools.reduce(jnp.add, [v[:, lane] for lane in lanes])
+                return fold(e), fold(picked)
+
+            terms = [block(k, None) for k in range(count) if k // 4 != seq]
+            sums[0] = functools.reduce(jnp.add, [a for a, _ in terms])
+            sums[1] = functools.reduce(jnp.add, [b for _, b in terms])
+            single = end_ref[seq, 0] == end_ref[seq, 1]
+            inner = slice(seq * 4 * rows, (seq + 1) * 4 * rows)
+
+            @pl.when(single)
+            def _(s=s, inner=inner):
+                exps[s, :, inner] = jnp.zeros((rows, 4 * rows), BF16)
+
+            @pl.when(jnp.logical_not(single))
+            def _(seq=seq, part=part, block=block):
+                own_doc = column(entries(doc_ref, seq, part, t, rows))
+                for k in range(seq * 4, seq * 4 + 4):
+                    a, b = block(k, own_doc)
+                    sums[0] += a
+                    sums[1] += b
+
             pending.append(move(exps.at[s], exp_out.at[s], out_sem.at[s]))
             wide = lane_pair(
-                jnp.sum(total, axis=-1, keepdims=True), jnp.sum(total_pos, axis=-1, keepdims=True), rows
+                jnp.sum(sums[0], axis=-1, keepdims=True), jnp.sum(sums[1], axis=-1, keepdims=True), rows
             )
             col_out[s * rows : (s + 1) * rows, :] = wide
             flat = jnp.transpose(wide)[:8, :]
@@ -685,96 +712,109 @@
     return kernel_call(
         body,
         (
-            struct((4, rows, count * rows), BF16),
+            struct((16, rows, count * rows), BF16),
             struct((4 * rows, 128), F32),
             struct((8, 4 * rows), F32),
             struct((seqs, rows), F32),
         ),
         (HBM, whole((4 * rows, 128)), whole((8, 4 * rows)), whole((seqs, rows))),
-        [pl.BlockSpec(memory_space=pltpu.SMEM), whole(docs.shape), whole(labels.shape)] + [ANY] * count,
-        scratch=[VMEM((count, rows, feats), BF16), VMEM((4, rows, count * rows), BF16), DMA((count,)), DMA((4,))],
+        [SMEM, SMEM, whole(docs.shape), whole(labels.shape)] + [ANY] * count,
+        scratch=[
+            VMEM((count, rows, feats), BF16),
+            VMEM((4, rows, count * rows), BF16),
+            VMEM((2, rows, 128), F32),
+            DMA((count,)),
+            DMA((4,)),
+        ],
         flops=2 * 4 * rows * count * rows * feats,
         nbytes=count * rows * feats * 4,
         trans=4 * rows * count * rows,
         name="contrast_scores",
-    )(place, docs, labels, *units)
-
-
-def contrast_grads(place, labels, units, exps, col_sums, row_own, row_got, cot, cot_got):
+    )(place, ends, docs, labels, *units)
+
+
+def contrast_grads(seq, place, ends, labels, units, exps, col_sums, row_own, row_got, cot, cot_got):
     rows, feats = units[0].shape[0] - EXTRA, units[0].shape[1]
     factor = CONTRAST_SCALE / feats
     count = len(units)
-    seqs = count // 4
-
-    def body(t_ref, lab_ref, col, own, got, *rest):
-        refs, (e_ref, cot_ref, *other_refs), rest = rest[:count], rest[count : count + 4], rest[count + 4 :]
-        full, low0, low1, both, exps, scales, cots, grad, full_v, low_v, in_sem, e_sem, q_sem, c_sem, o_sem = rest
+    span = 4 * rows
+
+    def body(t_ref, end_ref, lab_ref, col, own, got, *rest):
+        refs, (e_ref, cot_ref, other_ref), rest = rest[:count], rest[count : count + 3], rest[count + 3 :]
+        full, low, both, exps, scales, cots, grad, gn, full_v, low_v, in_sem, e_sem, q_sem, c_sem, o_sem = rest
         t = t_ref[0]
-        e_loads = [move(e_ref.at[0], exps.at[0], e_sem.at[0])]
-        loads = [
-            move(refs[k].at[pl.ds(0, rows)], both.at[pl.ds(k * rows, rows)], in_sem.at[k]) for k in range(count)
+        order = [k for k in range(count) if k // 4 != seq] + [k for k in range(count) if k // 4 == seq]
+        e_loads = [move(e_ref.at[2 * seq + h], exps.at[h], e_sem.at[h]) for h in range(2)]
+        loads = {
+            k: move(refs[k].at[pl.ds(0, rows)], both.at[pl.ds(k * rows, rows)], in_sem.at[k]) for k in order
+        }
+        small = [
+            (
+                move(refs[seq * 4 + h * 2].at[pl.ds(rows, EXTRA)], scales.at[h], q_sem.at[h]),
+                move(other_ref if h else cot_ref.at[seq], cots.at[h], c_sem.at[h]),
+            )
+            for h in range(2)
         ]
-        e_loads += [move(e_ref.at[s], exps.at[s], e_sem.at[s]) for s in range(1, 4)]
-        small = []
-        for s in range(4):
-            seq, half = s // 2, s % 2
-            small.append(
-                (
-                    move(refs[seq * 4 + half * 2].at[pl.ds(rows, EXTRA)], scales.at[s], q_sem.at[s]),
-                    move(other_refs[seq] if half else cot_ref.at[seq], cots.at[s], c_sem.at[s]),
-                )
-            )
-        pending = []
-
-        def weigh(s):
-            seq, half = s // 2, s % 2
-            own_lab = column(lab_ref[seq, lax.bitwise_xor(jnp.int32(half * 2), t)])
+        single = end_ref[seq, 0] == end_ref[seq, 1]
+
+        def weigh(h, blocks):
+            s = 2 * seq + h
+            own_lab = column(entries(lab_ref, seq, h * 2, t, rows))
             inv = CONTRAST_WEIGHT / col[s * rows : (s + 1) * rows, :]
             all_i, pos_i = inv[:, 0:1], inv[:, 1:2]
-            e_loads[s].wait()
-            for k in range(count):
+            for k in blocks:
                 other, piece = k // 4, k % 4
                 source = own if piece % 2 == 0 else got
                 at = (other * 2 + piece // 2) * rows
                 inv_j = CONTRAST_WEIGHT / source[0:2, at : at + rows]
-                same = own_lab == lab_ref[other, lax.bitwise_xor(jnp.int32(piece), t)]
+                same = own_lab == entries(lab_ref, other, piece, t, rows)
                 coef = (all_i + inv_j[0:1]) - jnp.where(same, pos_i + inv_j[1:2], 0.0)
                 cols = slice(k * rows, (k + 1) * rows)
-                grad[s % 2, :, cols] = (exps[s, :, cols].astype(F32) * coef).astype(BF16)
-
-        weigh(0)
-        for copy in loads:
-            copy.wait()
-        for s in range(4):
-            seq, half = s // 2, s % 2
-            if s + 1 < 4:
-                weigh(s + 1)
-            gn = dot(grad[s % 2], both[...]) * factor
-            first = (seq * 4 + half * 2) * rows
+                grad[h, :, cols] = (exps[h, :, cols].astype(F32) * coef).astype(BF16)
+
+        outer = slice((1 - seq) * span, (2 - seq) * span)
+        inner = slice(seq * span, (seq + 1) * span)
+        for h in range(2):
+            e_loads[h].wait()
+        weigh(0, order[:4])
+        for k in order:
+            loads[k].wait()
+        for h in range(2):
+            if h == 0:
+                weigh(1, order[:4])
+            gn[h] = dot(grad[h, :, outer], both[outer, :])
+
+        @pl.when(jnp.logical_not(single))
+        def _():
+            for h in range(2):
+                weigh(h, order[4:])
+                gn[h] += dot(grad[h, :, inner], both[inner, :])
+
+        pending = []
+        for h in range(2):
+            first = (seq * 4 + h * 2) * rows
             n = both[first : first + rows, :].astype(F32)
-            inner = gn - n * jnp.mean(gn * n, axis=-1, keepdims=True)
-            for copy in small[s]:
+            g = gn[h] * factor
+            change = g - n * jnp.mean(g * n, axis=-1, keepdims=True)
+            for copy in small[h]:
                 copy.wait()
-            pieces = scales[s, :, :rows].astype(F32)
-            gy = cots[s].astype(F32) + column(pieces[0:1] + pieces[1:2]) * inner
-            low_v[s] = gy.astype(BF16)
-            pending.append(move(low_v.at[s], (low1 if seq else low0).at[half], o_sem.at[s]))
-            if half == 0:
-                full_v[seq] = gy
-                pending.append(move(full_v.at[seq], full.at[seq], o_sem.at[4 + seq]))
+            pieces = scales[h, :, :rows].astype(F32)
+            gy = cots[h].astype(F32) + column(pieces[0:1] + pieces[1:2]) * change
+            low_v[h] = gy.astype(BF16)
+            pending.append(move(low_v.at[h], low.at[h], o_sem.at[h]))
+            if h == 0:
+                full_v[...] = gy
+                pending.append(move(full_v, full, o_sem.at[2]))
         for copy in pending:
             copy.wait()
 
     return kernel_call(
         body,
-        (
-            struct((seqs, rows, feats), F32),
-            struct((2, rows, feats), BF16),
-            struct((2, rows, feats), BF16),
-        ),
-        (ANY,) * 3,
+        (struct((rows, feats), F32), struct((2, rows, feats), BF16)),
+        (ANY,) * 2,
         [
-            pl.BlockSpec(memory_space=pltpu.SMEM),
+            SMEM,
+            SMEM,
             whole(labels.shape),
             whole((4 * rows, 128)),
             whole((8, 4 * rows)),
@@ -782,59 +822,58 @@
         ]
         + [ANY] * count
         + [HBM] * 2
-        + [ANY] * 2,
+        + [ANY],
         scratch=[
             VMEM((count * rows, feats), BF16),
-            VMEM((4, rows, count * rows), BF16),
-            VMEM((4, EXTRA, feats), BF16),
-            VMEM((4, rows, feats), BF16),
             VMEM((2, rows, count * rows), BF16),
-            VMEM((seqs, rows, feats), F32),
-            VMEM((4, rows, feats), BF16),
+            VMEM((2, EXTRA, feats), BF16),
+            VMEM((2, rows, feats), BF16),
+            VMEM((2, rows, count * rows), BF16),
+            VMEM((2, rows, feats), F32),
+            VMEM((rows, feats), F32),
+            VMEM((2, rows, feats), BF16),
             DMA((count,)),
-            DMA((4,)),
-            DMA((4,)),
-            DMA((4,)),
-            DMA((4 + seqs,)),
+            DMA((2,)),
+            DMA((2,)),
+            DMA((2,)),
+            DMA((3,)),
         ],
-        flops=2 * 4 * rows * count * rows * feats,
-        nbytes=count * rows * feats * 5,
+        flops=4 * rows * count * rows * feats,
+        nbytes=count * rows * feats * 4,
         name="contrast_grads",
-    )(place, labels, col_sums, row_own, row_got, *units, exps, cot, *cot_got)
-
-
-def down_grad(act, own, got, flags, bit):
-    seqs, length, units = act.shape
+    )(place, ends, labels, col_sums, row_own, row_got, *units, exps, cot, cot_got)
+
+
+def down_grad(saved, own, got):
+    seqs, length, units = saved.shape[1:]
     rows, feats = own[0].shape[1:]
     tiles = units // TILE
 
-    def body(flag, a_ref, *rest):
+    def body(a_ref, *rest):
         own_refs, got_refs = rest[:seqs], rest[seqs : 2 * seqs]
-        other_ref, kept_ref, a, b, out, a_sem, b_sem, o_sem = rest[2 * seqs :]
+        out_ref, a, b, out, a_sem, b_sem, o_sem = rest[2 * seqs :]
         b_loads = []
         for s in range(seqs):
             for r in range(4):
                 src = (got_refs if r % 2 else own_refs)[s].at[r // 2]
                 b_loads.append(move(src, b.at[s, pl.ds(r * rows, rows)], b_sem.at[4 * s + r]))
         columns = [pl.ds(i * TILE, TILE) for i in range(tiles)]
-        a_loads = [move(a_ref.at[:, :, columns[i]], a.at[i], a_sem.at[i]) for i in range(tiles)]
+        a_loads = [move(a_ref.at[ACT, :, :, columns[i]], a.at[i], a_sem.at[i]) for i in range(tiles)]
         for copy in b_loads:
             copy.wait()
         stores = []
         for i in range(tiles):
             a_loads[i].wait()
             out[i] = functools.reduce(jnp.add, [dot(a[i, s], b[s], TN) for s in range(seqs)]).astype(BF16)
-            stores.append(
-                send_half(i, tiles, flag[bit], out.at[i], other_ref, kept_ref, pl.ds(0, feats), o_sem.at[i])
-            )
+            stores.append(move(out.at[i], out_ref.at[columns[i]], o_sem.at[i]))
         for copy in stores:
             copy.wait()
 
     return kernel_call(
         body,
-        (struct((units // 2, feats), BF16),) * 2,
-        (ANY,) * 2,
-        [pl.BlockSpec(memory_space=pltpu.SMEM), HBM] + [ANY] * (2 * seqs),
+        struct((units, feats), BF16),
+        ANY,
+        [HBM] + [ANY] * (2 * seqs),
         scratch=[
             VMEM((tiles, seqs, length, TILE), BF16),
             VMEM((seqs, length, feats), BF16),
@@ -846,7 +885,7 @@
         flops=2 * seqs * length * units * feats,
         nbytes=4 * seqs * length * feats,
         name="down_grad",
-    )(flags, act, *own, *got)
+    )(saved, *own, *got)
 
 
 TILE = 256
@@ -867,15 +906,15 @@
     return pltpu.make_async_copy(src, kept.at[rows, at], sem)
 
 
-def weight_grad(lhs, rhs, flags, bit):
-    seqs, length, out_rows = lhs.shape
-    cols = rhs.shape[2]
+def weight_grad(saved, flags, bit):
+    seqs, length, out_rows = saved.shape[1:]
+    cols = out_rows
     tiles = out_rows // TILE
 
-    def body(flag, a_ref, b_ref, other_ref, kept_ref, a, b, out, a_sem, b_sem, o_sem):
-        b_loads = [move(b_ref.at[s], b.at[s], b_sem.at[s]) for s in range(seqs)]
+    def body(flag, s_ref, other_ref, kept_ref, a, b, out, a_sem, b_sem, o_sem):
+        b_loads = [move(s_ref.at[GRAD, s], b.at[s], b_sem.at[s]) for s in range(seqs)]
         columns = [pl.ds(i * TILE, TILE) for i in range(tiles)]
-        a_loads = [move(a_ref.at[:, :, columns[i]], a.at[i], a_sem.at[i]) for i in range(tiles)]
+        a_loads = [move(s_ref.at[ROWS, :, :, columns[i]], a.at[i], a_sem.at[i]) for i in range(tiles)]
         for copy in b_loads:
             copy.wait()
         stores = []
@@ -892,7 +931,7 @@
         body,
         (struct((out_rows // 2, cols), BF16),) * 2,
         (ANY,) * 2,
-        [pl.BlockSpec(memory_space=pltpu.SMEM)] + [HBM] * 2,
+        [pl.BlockSpec(memory_space=pltpu.SMEM)] + [HBM],
         scratch=[
             VMEM((tiles, seqs, length, TILE), BF16),
             VMEM((seqs, length, cols), BF16),
@@ -904,24 +943,27 @@
         flops=2 * seqs * length * out_rows * cols,
         nbytes=4 * seqs * length * cols,
         name="weight_grad",
-    )(flags, lhs, rhs)
-
-
-def head_grads(lhs, grads, att, rows_r, flags, bits):
-    seqs, length, feats = lhs.shape
-    width = att.shape[2]
+    )(flags, saved)
+
+
+def head_grads(saved, grads, seqs, feats, flags, bits):
+    length = saved.shape[1]
+    width = (saved.shape[2] - feats) // 4
     tiles = feats // width
 
     def body(*refs):
-        flag, a_ref, *g_refs, r_ref = refs[:7]
-        first_refs, second_refs = refs[7:9], refs[9:11]
-        a, g, r, first, second, a_sem, g_sem, r_sem, o_sem = refs[11:]
+        flag, s_ref, h_ref = refs[:3]
+        first_refs, second_refs = refs[3:5], refs[5:7]
+        a, g, r, first, second, a_sem, g_sem, r_sem, o_sem = refs[7:]
+        both = pl.ds(0, seqs)
         columns = [pl.ds(i * width, width) for i in range(tiles)]
-        g_loads = [move(ref, g.at[n], g_sem.at[n]) for n, ref in enumerate(g_refs)]
+        g_loads = []
+        for n, ref in enumerate((h_ref, h_ref, h_ref, s_ref)):
+            g_loads.append(move(ref.at[both, :, pl.ds(feats + n * width, width)], g.at[n], g_sem.at[n]))
         a_loads, r_loads = [], []
         for i in range(tiles):
-            a_loads.append(move(a_ref.at[:, :, columns[i]], a.at[i], a_sem.at[i]))
-            r_loads.append(move(r_ref.at[:, :, columns[i]], r.at[i], r_sem.at[i]))
+            a_loads.append(move(s_ref.at[both, :, columns[i]], a.at[i], a_sem.at[i]))
+            r_loads.append(move(h_ref.at[both, :, columns[i]], r.at[i], r_sem.at[i]))
         for copy in g_loads:
             copy.wait()
 
@@ -947,7 +989,7 @@
         body,
         (struct((feats // 2, 2 * width), BF16),) * 4,
         (ANY,) * 4,
-        [pl.BlockSpec(memory_space=pltpu.SMEM)] + [HBM] * 6,
+        [pl.BlockSpec(memory_space=pltpu.SMEM)] + [HBM] * 2,
         scratch=[
             VMEM((tiles, seqs, length, width), BF16),
             VMEM((4, seqs, length, width), BF16),
@@ -962,7 +1004,7 @@
         flops=2 * seqs * length * feats * width * 4,
         nbytes=4 * seqs * length * feats,
         name="head_grads",
-    )(flags, lhs, *grads, att, rows_r)
+    )(flags, saved, grads)
 
 
 def halve_step(flags, bit, keep, got):
@@ -1017,6 +1059,30 @@
         limit=SMALL,
         name="join_step",
     )(flags, own, got).reshape(2 * rows, cols)
+
+
+def part_outputs(parts, order):
+    rows, cols = parts.shape
+    step = rows >> len(order)
+
+    def place(i):
+        return functools.reduce(
+            jnp.add, [((i >> bit) & 1) << (len(order) - 1 - n) for n, bit in enumerate(order)]
+        )
+
+    def body(part, out):
+        out[...] = part[...].astype(F32)
+
+    return kernel_call(
+        body,
+        struct((rows, cols), F32),
+        pl.BlockSpec((step, cols), lambda i: (place(i), 0)),
+        [pl.BlockSpec((step, cols), lambda i: (i, 0))],
+        grid=(1 << len(order),),
+        nbytes=6 * rows * cols,
+        limit=SMALL,
+        name="part_outputs",
+    )(parts)
 
 
 def head_outputs(flags, bits, first, second):
@@ -1141,7 +1207,8 @@
     vec = lambda v: v.astype(F32).reshape(1, -1)
     gain_one, shift_one, gain_two, shift_two = vec(ln1_gain), vec(ln1_bias), vec(ln2_gain), vec(ln2_bias)
     out_offset, down_offset, up_shift = vec(out_bias), vec(down_bias), vec(up_bias)
-    q_shift, v_shift = vec(query_bias), vec(value_bias)
+    head_shift = vec(jnp.concatenate([query_bias, value_bias]))
+    ends = doc_ids[:, :: length - 1]
 
     fine = 16
     paired = (jnp.arange(feats, dtype=jnp.int32) // 2).astype(F32)
@@ -1152,21 +1219,14 @@
     sin_a, cos_a = jnp.sin(coarse_at), jnp.cos(coarse_at)
     tables = (jnp.where(odd, cos_a, sin_a), jnp.where(odd, -sin_a, cos_a), jnp.cos(fine_at), jnp.sin(fine_at))
 
-    docs_f, labels_f = doc_ids.astype(F32), targets.astype(F32)
-    docs4 = docs_f.reshape(seqs, parts, 1, rows)
-    labels4 = labels_f.reshape(seqs, parts, 1, rows)
-    docs_row = [docs_f[s : s + 1] for s in range(seqs)]
-
     hidden, stream, grad_r = [None] * 2, [None] * 2, [None] * 2
     kept, up_sums, head_sums, sums_one, sums_two = [None] * 2, [None] * 2, [None] * 2, [None] * 2, [None] * 2
-    shared = {"attend": None, "feed": None, "act": None, "up": None, "heads": None, "input": None}
+    shared = {"attend": None, "feed": None, "act": None, "heads": None, "input": None}
 
     def attend(s, gathered, *earlier):
-        *blocks, cat, qkv, att, logs = attend_forward(
-            s, seqs, tie(place, *earlier), docs_row[s], gathered, qkv_weight, q_shift, v_shift, output_weight,
-            shared["attend"],
+        *blocks, shared["attend"], kept[s] = attend_forward(
+            s, tie(place, *earlier), doc_ids, head_shift, gathered, qkv_weight, output_weight, shared["attend"]
         )
-        shared["attend"], kept[s] = (cat, att), (qkv, logs)
         return Scatter(blocks)
 
     def middle_rows(s, scatter, *earlier):
@@ -1174,10 +1234,9 @@
         return normed, Gather(normed)
 
     def feed(s, gathered, *earlier):
-        *blocks, cat, act, slope = feed_forward(
-            s, seqs, gathered, up_weight, tie(up_shift, *earlier), down_weight, shared["feed"]
+        *blocks, shared["feed"] = feed_forward(
+            s, seqs, gathered, tie(up_shift, *earlier), up_weight, down_weight, shared["feed"]
         )
-        shared["feed"] = (cat, act, slope)
         return Scatter(blocks)
 
     def last_rows(s, scatter, *earlier):
@@ -1203,35 +1262,34 @@
     block = ff_b.cross(unit)
     unit, units_b = last_rows(1, ff_b, block)
     cots = [tensor_swap(tie(cotangent[s], unit), CROSS) for s in range(2)]
-    cat_one, att = shared["attend"]
-    cat_two, hidden_act, slope = shared["feed"]
 
     units = units_a.blocks() + units_b.blocks()
-    exps, col_sums, row_sums, loss = contrast_scores(place, docs4, labels4, units)
+    exps, col_sums, row_sums, loss = contrast_scores(place, ends, doc_ids, targets, units)
     row_got = tensor_swap(row_sums, CORE)
-    grad_y, *low_y = contrast_grads(
-        place, labels4, units, exps, col_sums, row_sums, row_got, cotangent, cots
-    )
-    got_y = [tensor_swap(v, CORE) for v in low_y]
+    grad_y, low_y, got_y = [None] * 2, [None] * 2, [None] * 2
+    for s in range(2):
+        grad_y[s], low_y[s] = contrast_grads(
+            s, tie(place, *low_y[:s]), ends, targets, units, exps, col_sums, row_sums, row_got, cotangent, cots[s]
+        )
+        got_y[s] = tensor_swap(tie(low_y[s], cots[1]), CORE)
 
     def feed_back(s, *earlier):
-        *blocks, shared["up"], up_sums[s] = feed_backward(
-            s, seqs, low_y[s], got_y[s], slope, tie(up_weight, *earlier), down_weight, shared["up"]
+        *blocks, shared["feed"], up_sums[s] = feed_backward(
+            s, low_y[s], got_y[s], shared["feed"], up_weight, down_weight, earlier
         )
         return Scatter(blocks)
 
     def middle_back(s, scatter, *earlier):
         grad_r[s], low, sums_two[s] = norm_backward(
-            s, seqs, stream[s], scatter.parts, tie(gain_two, *earlier), grad_y, False, None
+            s, seqs, stream[s], scatter.parts, tie(gain_two, *earlier), grad_y[s], False, None
         )
         return low, Gather(low)
 
     def attend_back(s, gathered, *earlier):
-        *blocks, cat, gq, gk, gv, head_sums[s] = attend_backward(
-            s, seqs, tie(place, *earlier), docs_row[s], gathered, kept[s][0], att, kept[s][1], qkv_weight,
-            output_weight, shared["heads"],
+        *blocks, shared["heads"], head_sums[s] = attend_backward(
+            s, tie(place, *earlier), doc_ids, gathered, shared["attend"], kept[s], qkv_weight, output_weight,
+            shared["heads"],
         )
-        shared["heads"] = (cat, gq, gk, gv)
         return Scatter(blocks)
 
     def first_back(s, scatter, *earlier):
@@ -1243,32 +1301,30 @@
     bits = list(range(dp_size.bit_length() - 1))
     other_bits = bits[1::-1] + bits[2:]
     flags = (lax.axis_index("dp") >> jnp.arange(len(bits), dtype=jnp.int32)) & 1
-    fb_a = feed_back(0)
-    block = fb_a.cross()
-    fb_b = feed_back(1, block)
-    block = fb_b.cross()
-    low, rows_a = middle_back(0, fb_a, block)
-    down_sum = DpSum(*down_grad(tie(hidden_act, low), low_y, got_y, flags, bits[0]), flags, dp_size, bits)
-    sent = down_sum.advance()
-    low, rows_b = middle_back(1, fb_b, sent)
-    up_sum = DpSum(*weight_grad(tie(cat_two, low), shared["up"], flags, bits[0]), flags, dp_size, bits)
+    grad_down_w = down_grad(shared["feed"], low_y, got_y)
+    down_part = lax.psum_scatter(grad_down_w, "dp", scatter_dimension=0, tiled=True)
+    fb_a = feed_back(0, grad_down_w)
+    fb_b = feed_back(1, fb_a.cross())
+    low, rows_a = middle_back(0, fb_a, fb_b.mark)
+    block = fb_b.cross(low)
+    up_sum = DpSum(*weight_grad(tie(shared["feed"], block), flags, bits[0]), flags, dp_size, bits)
     sent = up_sum.advance()
     ab_a = attend_back(0, rows_a.blocks(sent), sent)
-    sent = down_sum.advance(ab_a.mark)
-    block = ab_a.cross(sent)
-    ab_b = attend_back(1, rows_b.blocks(block), block)
-    sent = up_sum.advance(down_sum.advance(ab_b.mark))
+    low, rows_b = middle_back(1, fb_b, ab_a.mark)
+    block = ab_a.cross(low)
+    sent = up_sum.advance(block)
+    ab_b = attend_back(1, rows_b.blocks(sent), sent, down_part)
+    down_all = lax.all_gather(tie(down_part, sent), "dp", axis=0, tiled=True)
+    sent = up_sum.advance(ab_b.mark)
     sums = first_back(0, ab_a, sent)
     block = ab_b.cross(sums)
-    cat_r, *grad_qkv = shared["heads"]
     first_send, first_keep, second_send, second_keep = head_grads(
-        tie(cat_one, block), grad_qkv, att, cat_r, flags, (bits[0], other_bits[0])
+        tie(shared["attend"], block), shared["heads"], seqs, feats, flags, (bits[0], other_bits[0])
     )
     first = DpSum(first_send, first_keep, flags, dp_size, bits)
     second = DpSum(second_send, second_keep, flags, dp_size, other_bits)
     sent = (first.advance(), second.advance())
-    sent = up_sum.advance(down_sum.advance(*sent))
-    sums = first_back(1, ab_b, sent)
+    sums = first_back(1, ab_b, *sent)
     sent = (sums,)
 
     total = lambda items: functools.reduce(jnp.add, items)
@@ -1277,21 +1333,23 @@
     small = jnp.concatenate([total(sums_one)[:2], total(sums_two), total(up_sums), heads_row])
     swaps = [("dp", dp_size, 1 << bit) for bit in bits] + [("tensor", 4, CORE), ("tensor", 4, CROSS)]
     local = None
-    while swaps or first.left or up_sum.left or down_sum.left:
+    while swaps or first.left:
         if swaps:
             axis, size, bit = swaps.pop(0)
             if axis == "tensor" and local is None:
                 local, small = small[6:], small[:6]
             small = small + swap(tie(small, *sent), axis, size, bit)
-        sent = ()
+        sent = (small,)
+        if up_sum.left:
+            sent += (up_sum.advance(*sent),)
         if first.left:
-            sent += (first.advance(small), second.advance(small))
-        for other in (down_sum, up_sum):
-            if other.left:
-                sent += (other.advance(small, *sent),)
+            sent = (first.advance(*sent), second.advance(*sent))
+        if len(first.left) == 2:
+            grad_down_w = tie(down_all, *sent).astype(F32)
+            sent += (grad_down_w,)
+    own, got = up_sum.halves()
+    grad_up_w = join_step(flags, bits[0], tie(own, *sent), got, F32)
     grad_qkv_w, grad_out_w = head_outputs(flags, (bits[0], other_bits[0]), first.halves(), second.halves())
-    grad_down_w = join_step(flags, bits[0], *down_sum.halves(), F32)
-    grad_up_w = join_step(flags, bits[0], *up_sum.halves(), F32)
     return (
         shared["act"],
         loss,

time: 470 us -> 453 us (0.964); the launches traced: 466 us -> 444 us
  waiting for transfers between devices: 202 us -> 180 us
  between operations: 2.04 us -> 15.5 us
  local copies, waits for them, and re-layouts: 26 us -> 15 us
  starting transfers between devices: 62.2 us -> 54.3 us
    ppermute x82 -> x76, waiting for transfers between devices: 202 us -> 180 us  [swap(): return lax.ppermute(value, axis, [(i, i ^ bit) for i in range(size)])]
    unnamed x137 -> x109, local copies, waits for them, and re-layouts: 23.1 us -> 10.8 us
    ppermute x82 -> x76, starting transfers between devices: 62.2 us -> 53.9 us  [swap(): return lax.ppermute(value, axis, [(i, i ^ bit) for i in range(size)])]
    pallas_call x10 -> x7, Pallas kernels: 10.2 us -> 6.24 us  [join_step(): kernel_call(body, struct((2, rows, cols), dtype), pl.BlockSpec((2, part,...]
    pallas_call x15 -> x16, Pallas kernels: 123 us -> 126 us  [the longest x2 24.5 us: attend_backward(): kernel_call(body, (*[struct((rows, feats), BF16)] * 4, struct((2 * seqs,...]
  transfers between devices with their start and end apart: 82 -> 78, of which waited for: 34 -> 35; matrix products, arithmetic and copies ran while one was open for 2% -> 3% of each run, Pallas kernels for 30% -> 33%
where the time goes in v3:
time: 453 us; the launch traced here: 444 us
  waiting for transfers between devices  180 us (40%)
  Pallas kernels  170 us (38%)
  starting transfers between devices  54.3 us (12%)
  between operations  15.5 us (3%)
  local copies, waits for them, and re-layouts  15 us (3%)
  other arithmetic  9.46 us (2%)
    ppermute x76, waiting for transfers between devices, swap(): return lax.ppermute(value, axis, [(i, i ^ bit) for i in range(size)])  180 us
    ppermute x76, starting transfers between devices, swap(): return lax.ppermute(value, axis, [(i, i ^ bit) for i in range(size)])  53.9 us
    pallas_call x2, Pallas kernels, attend_backward(): kernel_call(body, (*[struct((rows, feats), BF16)] * 4, struct((2 * seqs,...  24.5 us
    pallas_call x2, Pallas kernels, feed_forward(): kernel_call(body, (*[struct((rows, feats), BF16)] * 4, struct((4, seqs, l...  20.3 us
    pallas_call x2, Pallas kernels, attend_forward(): kernel_call(body, (*[struct((rows, feats), BF16)] * 4, struct((2 * seqs,...  20.1 us
    pallas_call x2, Pallas kernels, feed_backward(): kernel_call(body, (*[struct((rows, feats), BF16)] * 4, struct((4, seqs, l...  18.8 us
    pallas_call x2, Pallas kernels, contrast_grads(): kernel_call(body, (struct((rows, feats), F32), struct((2, rows, feats), B...  15.6 us
    pallas_call x1, Pallas kernels, head_grads(): kernel_call(body, (struct((feats // 2, 2 * width), BF16),) * 4, (ANY,) *...  13.3 us
  transfers between devices with their start and end apart: 78, of which 35 were waited for; matrix products, arithmetic and copies ran while one was open for 3% of the time, Pallas kernels for 33%

profile of v3, /device:TPU:0, one launch (start us, length us, event | category | flops | bytes accessed | tf_op | source)
XLA Modules:
  0.0 444.2 jit_solution(13741003944518476766)
XLA Ops:
  11.5 3.0 collective-permute-start.1
  15.5 10.9 %collective-permute-done.1.rest_2_ = bf16[256,1024]{1,0:T(8,128)(2,1)S(1)} collective-permute-done((bf16[256,1024]{1,0:T(8,128)(2,1)S(1)}, bf16[256,1024]{1,0:T(8,128)(2,1)S(1)}, u32[]{:S(2)}, u32[]{:S(2)}) %collective-permute-start.1) | collective-permute-done | bytes 524320 | tf_op jit(solution)/shard_map/ppermute | solution.py:1124
  31.1 9.8 %attend_forward.2 = (bf16[256,1024]{1,0:T(8,128)(2,1)S(1)}, bf16[256,1024]{1,0:T(8,128)(2,1)S(1)}, bf16[256,1024]{1,0:T(8,128)(2,1)S(1)}, bf16[256,1024]{1,0:T(8...) custom-call(s32[1]{0:T(128)} %bitcast.2.t_ref, s32[2,1024]{1,0:T(2,128)S(1)} %copy-done.24, ...), custom_call_target="tpu_custom_call" | custom-call | flops 69793216 | bytes 167772 | tf_op jit(solution)/shard_map/attend_forward/pallas_call | solution.py:343
  45.3 10.2 %attend_forward.3 = (bf16[256,1024]{1,0:T(8,128)(2,1)S(1)}, bf16[256,1024]{1,0:T(8,128)(2,1)S(1)}, bf16[256,1024]{1,0:T(8,128)(2,1)S(1)}, bf16[256,1024]{1,0:T(8...) custom-call(s32[1]{0:T(128)} %bitcast.2.t_ref, ...), custom_call_target="tpu_custom_call", output_to_operand_aliasing={{4}: (9, {})} | custom-call | flops 69793216 | bytes 167772 | tf_op jit(solution)/shard_map/attend_forward/pallas_call | solution.py:343
  55.5 2.1 collective-permute-done.9.x_ref
  59.8 12.2 %collective-permute-done.13.rest_2_ = bf16[256,1024]{1,0:T(8,128)(2,1)S(1)} collective-permute-done((bf16[256,1024]{1,0:T(8,128)(2,1)S(1)}, bf16[256,1024]{1,0:T(8,128)(2,1)S(1)}, u32[]{:S(2)}, u32[]{:S(2)}) %collective-permute-start.13) | collective-permute-done | bytes 524320 | tf_op jit(solution)/shard_map/ppermute | solution.py:1124
  74.7 10.0 %feed_forward.2 = (bf16[256,1024]{1,0:T(8,128)(2,1)S(1)}, bf16[256,1024]{1,0:T(8,128)(2,1)S(1)}, bf16[256,1024]{1,0:T(8,128)(2,1)S(1)}, bf16[256,1024]{1,0:T(8,128)(2,1)}, bf16[4,2,1024,1024]{3,2,1,0:T(8,128)(2,1)}) custom-call(f32[1,1024]{1,0:T(1,128)S(1)} %bitcast.59, bf16[256,1024]{1,0:T(8,128)(2,1)} %copy-done.22, bf16[256,1024]{1,0:T(8,128)(2,1)} %copy-done.46, ...), custom_call_target="tpu_custom_call" | custom-call | flops 85899344 | bytes 293601 | tf_op jit(solution)/shard_map/feed_forward/pallas_call | solution.py:551
  88.9 12.4 %collective-permute-done.17.rest_2_ = bf16[256,1024]{1,0:T(8,128)(2,1)S(1)} collective-permute-done((bf16[256,1024]{1,0:T(8,128)(2,1)S(1)}, bf16[256,1024]{1,0:T(8,128)(2,1)S(1)}, u32[]{:S(2)}, u32[]{:S(2)}) %collective-permute-start.17) | collective-permute-done | bytes 524320 | tf_op jit(solution)/shard_map/ppermute | solution.py:1124
  104.0 10.2 %feed_forward.3 = (bf16[256,1024]{1,0:T(8,128)(2,1)S(1)}, bf16[256,1024]{1,0:T(8,128)(2,1)S(1)}, bf16[256,1024]{1,0:T(8,128)(2,1)S(1)}, bf16[256,1024]{1,0:T(8,128)(2,1)}, bf16[4,2,1024,1024]{3,2,1,0:T(8,128)(2,1)}) custom-call(f32[1,1024]{1,0:T(1,128)S(1)} %bitcast.60, bf16[256,1024]{1,0:T(8,128)(2,1)} %copy-done.18, ...), custom_call_target="tpu_custom_call", output_to_operand_aliasing={{4}: (7, {})} | custom-call | flops 85899344 | bytes 293601 | tf_op jit(solution)/shard_map/feed_forward/pallas_call | solution.py:551
  119.5 12.8 %collective-permute-done.23.x_ref = bf16[256,1024]{1,0:T(8,128)(2,1)S(1)} collective-permute-done((bf16[256,1024]{1,0:T(8,128)(2,1)S(1)}, bf16[256,1024]{1,0:T(8,128)(2,1)S(1)}, u32[]{:S(2)}, u32[]{:S(2)}) %collective-permute-start.23) | collective-permute-done | bytes 524320 | tf_op jit(solution)/shard_map/ppermute | solution.py:1124
  134.2 10.2 %collective-permute-done.25.rest_2_ = bf16[272,1024]{1,0:T(8,128)(2,1)} collective-permute-done((bf16[272,1024]{1,0:T(8,128)(2,1)S(1)}, bf16[272,1024]{1,0:T(8,128)(2,1)}, u32[]{:S(2)}, u32[]{:S(2)}) %collective-permute-start.25) | collective-permute-done | bytes 557088 | tf_op jit(solution)/shard_map/ppermute | solution.py:1124
  144.9 9.7 %collective-permute-done.28.rest_6_ = bf16[272,1024]{1,0:T(8,128)(2,1)} collective-permute-done((bf16[272,1024]{1,0:T(8,128)(2,1)S(1)}, bf16[272,1024]{1,0:T(8,128)(2,1)}, u32[]{:S(2)}, u32[]{:S(2)}) %collective-permute-start.28) | collective-permute-done | bytes 557088 | tf_op jit(solution)/shard_map/ppermute | solution.py:1124
  157.8 9.6 %contrast_scores.1 = (bf16[16,256,2048]{2,1,0:T(8,128)(2,1)}, f32[1024,128]{1,0:T(8,128)S(1)}, f32[8,1024]{1,0:T(8,128)S(1)}, f32[2,256]{1,0:T(2,128)}) custom-call(s32[1]{0:T(128)} %bitcast.2.t_ref, s32[2,2]{1,0:T(2,128)S(1)} %slice.46.end_ref, s32[2,1024]{1,0:T(2,128)S(1)} %copy-done.25, s32[2,1024]{1,0:T(2,128)S(1)} %copy-done.26, ...), custom_call_target="tpu_custom_call" | custom-call | flops 85899344 | bytes 167772 | tf_op jit(solution)/shard_map/contrast_scores/pallas_call | solution.py:712
  167.5 3.2 collective-permute-done.31.rest_10_
  170.7 8.8 %contrast_grads.2 = (f32[256,1024]{1,0:T(8,128)}, bf16[2,256,1024]{2,1,0:T(8,128)(2,1)}) custom-call(s32[1]{0:T(128)} %bitcast.2.t_ref, s32[2,2]{1,0:T(2,128)S(1)} %slice.46.end_ref, s32[2,1024]{1,0:T(2,128)S(1)} %copy-done.26, f32[1024,128]{1,0:T(8,128)S(1)} %get-tuple-element.210.col, f32[8,1024]{1,0:T(8,128)S(1)} %get-tuple-element.211.own, ...), custom_call_target="tpu_custom_call" | custom-call | flops 42949672 | bytes 167772 | tf_op jit(solution)/shard_map/contrast_grads/pallas_call | solution.py:811
  181.5 6.8 %contrast_grads.3 = (f32[256,1024]{1,0:T(8,128)}, bf16[2,256,1024]{2,1,0:T(8,128)(2,1)}) custom-call(s32[1]{0:T(128)} %bitcast.2.t_ref, s32[2,2]{1,0:T(2,128)S(1)} %slice.46.end_ref, s32[2,1024]{1,0:T(2,128)S(1)} %copy-done.26, f32[1024,128]{1,0:T(8,128)S(1)} %get-tuple-element.210.col, f32[8,1024]{1,0:T(8,128)S(1)} %get-tuple-element.211.own, ...), custom_call_target="tpu_custom_call" | custom-call | flops 42949672 | bytes 167772 | tf_op jit(solution)/shard_map/contrast_grads/pallas_call | solution.py:811
  188.8 3.0 collective-permute-done.33.rest_3_.got_ref
  193.5 8.9 %down_grad.1.rest_0_ = bf16[1024,1024]{1,0:T(8,128)(2,1)} custom-call(bf16[4,2,1024,1024]{3,2,1,0:T(8,128)(2,1)} %get-tuple-element.220.a_ref.saved_ref, bf16[2,256,1024]{2,1,0:T(8,128)(2,1)S(1)} %copy-done.2, bf16[2,256,1024]{2,1,0:T(8,128)(2,1)} %get-tuple-element.218.rest_1_.own_ref, bf16[2,256,1024]{2,1,0:T(8,128)(2,1)} %copy-done.31, ...), custom_call_target="tpu_custom_call" | custom-call | flops 85899344 | bytes 167772 | tf_op jit(solution)/shard_map/down_grad/pallas_call | solution.py:872
  202.8 9.3 %feed_backward.2 = (bf16[256,1024]{1,0:T(8,128)(2,1)S(1)}, bf16[256,1024]{1,0:T(8,128)(2,1)S(1)}, bf16[256,1024]{1,0:T(8,128)(2,1)S(1)}, bf16[256,1024]{1,0:T(8,...) custom-call(bf16[2,256,1024]{2,1,0:T(8,128)(2,1)} %get-tuple-element.219.res, ...), custom_call_target="tpu_custom_call", output_to_operand_aliasing={{4}: (2, {})} | custom-call | flops 85899344 | bytes 293601 | tf_op jit(solution)/shard_map/feed_backward/pallas_call | solution.py:620
  215.7 9.5 %feed_backward.3 = (bf16[256,1024]{1,0:T(8,128)(2,1)S(1)}, bf16[256,1024]{1,0:T(8,128)(2,1)S(1)}, bf16[256,1024]{1,0:T(8,128)(2,1)S(1)}, bf16[256,1024]{1,0:T(8,...) custom-call(bf16[2,256,1024]{2,1,0:T(8,128)(2,1)} %get-tuple-element.218.res, ...), custom_call_target="tpu_custom_call", output_to_operand_aliasing={{4}: (2, {})} | custom-call | flops 85899344 | bytes 293601 | tf_op jit(solution)/shard_map/feed_backward/pallas_call | solution.py:620
  225.3 3.3 collective-permute-done.37.x_ref
  233.3 9.4 %weight_grad.1 = (bf16[512,1024]{1,0:T(8,128)(2,1)S(1)}, bf16[512,1024]{1,0:T(8,128)(2,1)}) custom-call(s32[3]{0:T(128)S(1)} %shift-right-arithmetic_and_fusion.flag.refs_0_.h_ref, bf16[4,2,1024,1024]{3,2,1,0:T(8,128)(2,1)} %get-tuple-element.233.s_ref), custom_call_target="tpu_custom_call" | custom-call | flops 85899344 | bytes 167772 | tf_op jit(solution)/shard_map/weight_grad/pallas_call | solution.py:930
  244.4 3.4 collective-permute-start.45
  250.1 12.2 %attend_backward.2 = (bf16[256,1024]{1,0:T(8,128)(2,1)S(1)}, bf16[256,1024]{1,0:T(8,128)(2,1)S(1)}, bf16[256,1024]{1,0:T(8,128)(2,1)S(1)}, bf16[256,1024]{1,0:T(...) custom-call(s32[1]{0:T(128)} %bitcast.2.t_ref, s32[2,1024]{1,0:T(2,128)S(1)} %copy-done.25, ...), custom_call_target="tpu_custom_call" | custom-call | flops 96636768 | bytes 167772 | tf_op jit(solution)/shard_map/attend_backward/pallas_call | solution.py:468
  266.9 7.5 %collective-permute-done.45.g_ref = bf16[512,1024]{1,0:T(8,128)(2,1)S(1)} collective-permute-done((bf16[512,1024]{1,0:T(8,128)(2,1)S(1)}, bf16[512,1024]{1,0:T(8,128)(2,1)S(1)}, u32[]{:S(2)}, u32[]{:S(2)}) %collective-permute-start.45) | collective-permute-done | bytes 1048608 | tf_op jit(solution)/shard_map/ppermute | solution.py:1124
  276.4 2.8 collective-permute-done.47.rest_2_
  283.2 12.3 %attend_backward.3 = (bf16[256,1024]{1,0:T(8,128)(2,1)S(1)}, bf16[256,1024]{1,0:T(8,128)(2,1)S(1)}, bf16[256,1024]{1,0:T(8,128)(2,1)S(1)}, bf16[256,1024]{1,0:T(...) custom-call(s32[1]{0:T(128)} %bitcast.2.t_ref, ...), custom_call_target="tpu_custom_call", output_to_operand_aliasing={{4}: (10, {})} | custom-call | flops 96636768 | bytes 167772 | tf_op jit(solution)/shard_map/attend_backward/pallas_call | solution.py:468
  296.1 6.8 %collective-permute-done.52.g_ref = bf16[256,1024]{1,0:T(8,128)(2,1)S(1)} collective-permute-done((bf16[256,1024]{1,0:T(8,128)(2,1)}, bf16[256,1024]{1,0:T(8,128)(2,1)S(1)}, u32[]{:S(2)}, u32[]{:S(2)}) %collective-permute-start.52) | collective-permute-done | bytes 524320 | tf_op jit(solution)/shard_map/ppermute | solution.py:1124
  303.6 2.4 norm_backward.6
  307.5 13.3 %head_grads.1 = (bf16[512,512]{1,0:T(8,128)(2,1)S(1)}, bf16[512,512]{1,0:T(8,128)(2,1)S(1)}, bf16[512,512]{1,0:T(8,128)(2,1)S(1)}, bf16[512,512]{1,0:T(8,128)(2,1)}) custom-call(s32[3]{0:T(128)S(1)} %shift-right-arithmetic_and_fusion.flag.refs_0_.h_ref, bf16[4,1024,2048]{2,1,0:T(8,128)(2,1)} %get-tuple-element.267.rest_4_.refs_1_, ...), custom_call_target="tpu_custom_call" | custom-call | flops 85899344 | bytes 167772 | tf_op jit(solution)/shard_map/head_grads/pallas_call | solution.py:988
  322.2 2.3 collective-permute-start.58
  324.5 2.4 norm_backward.7
  328.4 4.6 %collective-permute-done.55 = f32[8,1024]{1,0:T(8,128)S(1)} collective-permute-done((f32[8,1024]{1,0:T(8,128)S(1)}, f32[8,1024]{1,0:T(8,128)S(1)}, u32[]{:S(2)}, u32[]{:S(2)}) %collective-permute-start.55) | collective-permute-done | bytes 32800 | tf_op jit(solution)/shard_map/ppermute | solution.py:1124
  333.7 2.7 collective-permute-start.60
  337.0 14.5 %collective-permute-done.58.g_ref = bf16[512,512]{1,0:T(8,128)(2,1)S(1)} collective-permute-done((bf16[512,512]{1,0:T(8,128)(2,1)S(1)}, bf16[512,512]{1,0:T(8,128)(2,1)S(1)}, u32[]{:S(2)}, u32[]{:S(2)}) %collective-permute-start.58) | collective-permute-done | bytes 524320 | tf_op jit(solution)/shard_map/ppermute | solution.py:1124
  352.3 3.9 collective-permute-done.59
  360.0 14.5 %collective-permute-done.61.g_ref = bf16[256,512]{1,0:T(8,128)(2,1)S(1)} collective-permute-done((bf16[256,512]{1,0:T(8,128)(2,1)S(1)}, bf16[256,512]{1,0:T(8,128)(2,1)S(1)}, u32[]{:S(2)}, u32[]{:S(2)}) %collective-permute-start.61) | collective-permute-done | bytes 262176 | tf_op jit(solution)/shard_map/ppermute | solution.py:1124
  376.6 2.3 collective-permute-start.66
  379.6 9.2 %collective-permute-done.63 = f32[8,1024]{1,0:T(8,128)S(1)} collective-permute-done((f32[8,1024]{1,0:T(8,128)S(1)}, f32[8,1024]{1,0:T(8,128)S(1)}, u32[]{:S(2)}, u32[]{:S(2)}) %collective-permute-start.63) | collective-permute-done | bytes 32800 | tf_op jit(solution)/shard_map/ppermute | solution.py:1124
  389.4 2.1 collective-permute-start.75
  392.7 4.1 convert_element_type.157
  396.8 2.9 collective-permute-start.69
  399.7 8.8 %collective-permute-done.68.got_ref = bf16[128,512]{1,0:T(8,128)(2,1)S(1)} collective-permute-done((bf16[128,512]{1,0:T(8,128)(2,1)S(1)}, bf16[128,512]{1,0:T(8,128)(2,1)S(1)}, u32[]{:S(2)}, u32[]{:S(2)}) %collective-permute-start.68) | collective-permute-done | bytes 131104 | tf_op jit(solution)/shard_map/ppermute | solution.py:1124
  409.1 2.1 collective-permute-done.69.got_ref
  422.9 2.7 join_step.13
  425.7 5.8 %collective-permute-done.72.b_ref = bf16[512,512]{1,0:T(8,128)(2,1)S(1)} collective-permute-done((bf16[512,512]{1,0:T(8,128)(2,1)S(1)}, bf16[512,512]{1,0:T(8,128)(2,1)S(1)}, u32[]{:S(2)}, u32[]{:S(2)}) %collective-permute-start.72) | collective-permute-done | bytes 524320 | tf_op jit(solution)/shard_map/ppermute | solution.py:1124
  431.4 2.5 collective-permute-done.74.d_ref
  433.9 3.0 head_outputs.1
  (299 shorter events, 92.3 us)
Async XLA Ops:
  7.2 269.1 %reduce-scatter.2.cloned.1.call-start = ((), (), s32[]{:S(2)}) async-start(), calls=%async_computation.1 | async-start | bytes 2359296 | tf_op jit(solution)/shard_map/reduce_scatter | solution.py:1305
  11.5 14.9 %collective-permute-start.1 = (bf16[256,1024]{1,0:T(8,128)(2,1)S(1)}, bf16[256,1024]{1,0:T(8,128)(2,1)S(1)}, u32[]{:S(2)}, u32[]{:S(2)}) collective-permute-start(bf16[256,1024]{1,0:T(8,128)(2,1)S(1)} %get-tuple-element.166.rest_0_), channel_id=1, source_target_pairs={{0,2},{1,3},{2,0},{3,1},{4,6},{5,7},{6,4},{7,5},{8,10},{9,11},{10,... | collective-permute-start | bytes 1572872 | tf_op jit(solution)/shard_map/ppermute | solution.py:1124
  14.5 15.0 %collective-permute-start = (bf16[256,1024]{1,0:T(8,128)(2,1)S(1)}, bf16[256,1024]{1,0:T(8,128)(2,1)S(1)}, u32[]{:S(2)}, u32[]{:S(2)}) collective-permute-start(bf16[256,1024]{1,0:T(8,128)(2,1)S(1)} %get-tuple-element.166.rest_0_), channel_id=1, source_target_pairs={{0,1},{1,0},{2,3},{3,2},{4,5},{5,4},{6,7},{7,6},{8,9},{9,8},{10,11... | collective-permute-start | bytes 1572872 | tf_op jit(solution)/shard_map/ppermute | solution.py:1124
  26.4 15.2 %collective-permute-start.3 = (bf16[256,1024]{1,0:T(8,128)(2,1)S(1)}, bf16[256,1024]{1,0:T(8,128)(2,1)S(1)}, u32[]{:S(2)}, u32[]{:S(2)}) collective-permute-start(bf16[256,1024]{1,0:T(8,128)(2,1)S(1)} %get-tuple-element.169.rest_0_), channel_id=1, source_target_pairs={{0,2},{1,3},{2,0},{3,1},{4,6},{5,7},{6,4},{7,5},{8,10},{9,11},{10,... | collective-permute-start | bytes 1572872 | tf_op jit(solution)/shard_map/ppermute | solution.py:1124
  41.9 13.6 %collective-permute-start.8 = (bf16[256,1024]{1,0:T(8,128)(2,1)S(1)}, bf16[256,1024]{1,0:T(8,128)(2,1)S(1)}, u32[]{:S(2)}, u32[]{:S(2)}) collective-permute-start(bf16[256,1024]{1,0:T(8,128)(2,1)S(1)} %get-tuple-element.181), channel_id=1, source_target_pairs={{0,1},{1,0},{2,3},{3,2},{4,5},{5,4},{6,7},{7,6},{8,9},{9,8},{10,11... | collective-permute-start | bytes 1572872 | tf_op jit(solution)/shard_map/ppermute | solution.py:1124
  43.4 14.2 %collective-permute-start.9 = (bf16[256,1024]{1,0:T(8,128)(2,1)S(1)}, bf16[256,1024]{1,0:T(8,128)(2,1)S(1)}, u32[]{:S(2)}, u32[]{:S(2)}) collective-permute-start(bf16[256,1024]{1,0:T(8,128)(2,1)S(1)} %add_convert_fusion.7), channel_id=1, source_target_pairs={{0,2},{1,3},{2,0},{3,1},{4,6},{5,7},{6,4},{7,5},{8,10},{9,11},{10,... | collective-permute-start | bytes 1572872 | tf_op jit(solution)/shard_map/ppermute | solution.py:1124
  58.6 13.4 %collective-permute-start.13 = (bf16[256,1024]{1,0:T(8,128)(2,1)S(1)}, bf16[256,1024]{1,0:T(8,128)(2,1)S(1)}, u32[]{:S(2)}, u32[]{:S(2)}) collective-permute-start(bf16[256,1024]{1,0:T(8,128)(2,1)S(1)} %get-tuple-element.184.rest_0_), channel_id=1, source_target_pairs={{0,2},{1,3},{2,0},{3,1},{4,6},{5,7},{6,4},{7,5},{8,10},{9,11},{10,... | collective-permute-start | bytes 1572872 | tf_op jit(solution)/shard_map/ppermute | solution.py:1124
  59.3 25.5 %collective-permute-start.7 = (bf16[256,1024]{1,0:T(8,128)(2,1)S(1)}, bf16[256,1024]{1,0:T(8,128)(2,1)S(1)}, u32[]{:S(2)}, u32[]{:S(2)}) collective-permute-start(bf16[256,1024]{1,0:T(8,128)(2,1)S(1)} %get-tuple-element.177), channel_id=1, source_target_pairs={{0,1},{1,0},{2,3},{3,2},{4,5},{5,4},{6,7},{7,6},{8,9},{9,8},{10,11... | collective-permute-start | bytes 1572872 | tf_op jit(solution)/shard_map/ppermute | solution.py:1124
  59.8 13.1 %collective-permute-start.12 = (bf16[256,1024]{1,0:T(8,128)(2,1)S(1)}, bf16[256,1024]{1,0:T(8,128)(2,1)S(1)}, u32[]{:S(2)}, u32[]{:S(2)}) collective-permute-start(bf16[256,1024]{1,0:T(8,128)(2,1)S(1)} %get-tuple-element.184.rest_0_), channel_id=1, source_target_pairs={{0,1},{1,0},{2,3},{3,2},{4,5},{5,4},{6,7},{7,6},{8,9},{9,8},{10,11... | collective-permute-start | bytes 1572872 | tf_op jit(solution)/shard_map/ppermute | solution.py:1124
  72.2 14.4 %collective-permute-start.11 = (bf16[256,1024]{1,0:T(8,128)(2,1)S(1)}, bf16[256,1024]{1,0:T(8,128)(2,1)S(1)}, u32[]{:S(2)}, u32[]{:S(2)}) collective-permute-start(bf16[256,1024]{1,0:T(8,128)(2,1)S(1)} %add_convert_fusion.6), channel_id=1, source_target_pairs={{0,2},{1,3},{2,0},{3,1},{4,6},{5,7},{6,4},{7,5},{8,10},{9,11},{10,... | collective-permute-start | bytes 1572872 | tf_op jit(solution)/shard_map/ppermute | solution.py:1124
  87.7 13.6 %collective-permute-start.17 = (bf16[256,1024]{1,0:T(8,128)(2,1)S(1)}, bf16[256,1024]{1,0:T(8,128)(2,1)S(1)}, u32[]{:S(2)}, u32[]{:S(2)}) collective-permute-start(bf16[256,1024]{1,0:T(8,128)(2,1)S(1)} %get-tuple-element.191.rest_0_), channel_id=1, source_target_pairs={{0,2},{1,3},{2,0},{3,1},{4,6},{5,7},{6,4},{7,5},{8,10},{9,11},{10,... | collective-permute-start | bytes 1572872 | tf_op jit(solution)/shard_map/ppermute | solution.py:1124
  88.4 13.4 %collective-permute-start.15 = (bf16[256,1024]{1,0:T(8,128)(2,1)}, bf16[256,1024]{1,0:T(8,128)(2,1)S(1)}, u32[]{:S(2)}, u32[]{:S(2)}) collective-permute-start(bf16[256,1024]{1,0:T(8,128)(2,1)} %get-tuple-element.187), channel_id=1, source_target_pairs={{0,1},{1,0},{2,3},{3,2},{4,5},{5,4},{6,7},{7,6},{8,9},{9,8},{10,11... | collective-permute-start | bytes 1572872 | tf_op jit(solution)/shard_map/ppermute | solution.py:1124
  88.4 14.3 %collective-permute-start.16 = (bf16[256,1024]{1,0:T(8,128)(2,1)S(1)}, bf16[256,1024]{1,0:T(8,128)(2,1)S(1)}, u32[]{:S(2)}, u32[]{:S(2)}) collective-permute-start(bf16[256,1024]{1,0:T(8,128)(2,1)S(1)} %get-tuple-element.191.rest_0_), channel_id=1, source_target_pairs={{0,1},{1,0},{2,3},{3,2},{4,5},{5,4},{6,7},{7,6},{8,9},{9,8},{10,11... | collective-permute-start | bytes 1572872 | tf_op jit(solution)/shard_map/ppermute | solution.py:1124
  101.3 13.5 %collective-permute-start.20 = (bf16[256,1024]{1,0:T(8,128)(2,1)S(1)}, bf16[256,1024]{1,0:T(8,128)(2,1)S(1)}, u32[]{:S(2)}, u32[]{:S(2)}) collective-permute-start(bf16[256,1024]{1,0:T(8,128)(2,1)S(1)} %get-tuple-element.200), channel_id=1, source_target_pairs={{0,1},{1,0},{2,3},{3,2},{4,5},{5,4},{6,7},{7,6},{8,9},{9,8},{10,11... | collective-permute-start | bytes 1572872 | tf_op jit(solution)/shard_map/ppermute | solution.py:1124
  102.0 13.9 %collective-permute-start.21 = (bf16[256,1024]{1,0:T(8,128)(2,1)S(1)}, bf16[256,1024]{1,0:T(8,128)(2,1)S(1)}, u32[]{:S(2)}, u32[]{:S(2)}) collective-permute-start(bf16[256,1024]{1,0:T(8,128)(2,1)S(1)} %add_convert_fusion.5), channel_id=1, source_target_pairs={{0,2},{1,3},{2,0},{3,1},{4,6},{5,7},{6,4},{7,5},{8,10},{9,11},{10,... | collective-permute-start | bytes 1572872 | tf_op jit(solution)/shard_map/ppermute | solution.py:1124
  117.4 14.9 %collective-permute-start.23 = (bf16[256,1024]{1,0:T(8,128)(2,1)S(1)}, bf16[256,1024]{1,0:T(8,128)(2,1)S(1)}, u32[]{:S(2)}, u32[]{:S(2)}) collective-permute-start(bf16[256,1024]{1,0:T(8,128)(2,1)S(1)} %add_convert_fusion.4), channel_id=1, source_target_pairs={{0,2},{1,3},{2,0},{3,1},{4,6},{5,7},{6,4},{7,5},{8,10},{9,11},{10,... | collective-permute-start | bytes 1572872 | tf_op jit(solution)/shard_map/ppermute | solution.py:1124
  118.1 26.3 %collective-permute-start.25 = (bf16[272,1024]{1,0:T(8,128)(2,1)S(1)}, bf16[272,1024]{1,0:T(8,128)(2,1)}, u32[]{:S(2)}, u32[]{:S(2)}) collective-permute-start(bf16[272,1024]{1,0:T(8,128)(2,1)S(1)} %get-tuple-element.203.rest_0_), channel_id=1, source_target_pairs={{0,2},{1,3},{2,0},{3,1},{4,6},{5,7},{6,4},{7,5},{8,10},{9,11},{10,... | collective-permute-start | bytes 1671176 | tf_op jit(solution)/shard_map/ppermute | solution.py:1124
  133.6 21.0 %collective-permute-start.28 = (bf16[272,1024]{1,0:T(8,128)(2,1)S(1)}, bf16[272,1024]{1,0:T(8,128)(2,1)}, u32[]{:S(2)}, u32[]{:S(2)}) collective-permute-start(bf16[272,1024]{1,0:T(8,128)(2,1)S(1)} %get-tuple-element.208.rest_4_), channel_id=1, source_target_pairs={{0,2},{1,3},{2,0},{3,1},{4,6},{5,7},{6,4},{7,5},{8,10},{9,11},{10,... | collective-permute-start | bytes 1671176 | tf_op jit(solution)/shard_map/ppermute | solution.py:1124
  134.2 22.5 %collective-permute-start.24 = (bf16[272,1024]{1,0:T(8,128)(2,1)S(1)}, bf16[272,1024]{1,0:T(8,128)(2,1)S(1)}, u32[]{:S(2)}, u32[]{:S(2)}) collective-permute-start(bf16[272,1024]{1,0:T(8,128)(2,1)S(1)} %get-tuple-element.203.rest_0_), channel_id=1, source_target_pairs={{0,1},{1,0},{2,3},{3,2},{4,5},{5,4},{6,7},{7,6},{8,9},{9,8},{10,11... | collective-permute-start | bytes 1671176 | tf_op jit(solution)/shard_map/ppermute | solution.py:1124
  144.4 13.4 %collective-permute-start.26 = (bf16[272,1024]{1,0:T(8,128)(2,1)}, bf16[272,1024]{1,0:T(8,128)(2,1)}, u32[]{:S(2)}, u32[]{:S(2)}) collective-permute-start(bf16[272,1024]{1,0:T(8,128)(2,1)} %collective-permute-done.25.rest_2_), channel_id=1, source_target_pairs={{0,1},{1,0},{2,3},{3,2},{4,5},{5,4},{6,7},{7,6},{8,9},{9,8},{10,11... | collective-permute-start | bytes 1671176 | tf_op jit(solution)/shard_map/ppermute | solution.py:1124
  144.4 13.4 %collective-permute-start.27 = (bf16[272,1024]{1,0:T(8,128)(2,1)S(1)}, bf16[272,1024]{1,0:T(8,128)(2,1)}, u32[]{:S(2)}, u32[]{:S(2)}) collective-permute-start(bf16[272,1024]{1,0:T(8,128)(2,1)S(1)} %get-tuple-element.208.rest_4_), channel_id=1, source_target_pairs={{0,1},{1,0},{2,3},{3,2},{4,5},{5,4},{6,7},{7,6},{8,9},{9,8},{10,11... | collective-permute-start | bytes 1671176 | tf_op jit(solution)/shard_map/ppermute | solution.py:1124
  155.7 15.0 %collective-permute-start.31 = (bf16[256,1024]{1,0:T(8,128)(2,1)}, bf16[256,1024]{1,0:T(8,128)(2,1)}, u32[]{:S(2)}, u32[]{:S(2)}) collective-permute-start(bf16[256,1024]{1,0:T(8,128)(2,1)} %get-tuple-element.213), channel_id=1, source_target_pairs={{0,2},{1,3},{2,0},{3,1},{4,6},{5,7},{6,4},{7,5},{8,10},{9,11},{10,... | collective-permute-start | bytes 1572872 | tf_op jit(solution)/shard_map/ppermute | solution.py:1124
  156.8 24.7 %collective-permute-start.32 = (bf16[256,1024]{1,0:T(8,128)(2,1)}, bf16[256,1024]{1,0:T(8,128)(2,1)S(1)}, u32[]{:S(2)}, u32[]{:S(2)}) collective-permute-start(bf16[256,1024]{1,0:T(8,128)(2,1)} %get-tuple-element.216), channel_id=1, source_target_pairs={{0,2},{1,3},{2,0},{3,1},{4,6},{5,7},{6,4},{7,5},{8,10},{9,11},{10,... | collective-permute-start | bytes 1572872 | tf_op jit(solution)/shard_map/ppermute | solution.py:1124
  202.4 190.3 %all-gather.2.cloned.1.call-start = ((), (), s32[]{:S(2)}) async-start(), calls=%async_computation.2 | async-start | bytes 2359296 | tf_op jit(solution)/shard_map/all_gather | solution.py:1317
  214.6 14.0 %collective-permute-start.37 = (bf16[256,1024]{1,0:T(8,128)(2,1)S(1)}, bf16[256,1024]{1,0:T(8,128)(2,1)S(1)}, u32[]{:S(2)}, u32[]{:S(2)}) collective-permute-start(bf16[256,1024]{1,0:T(8,128)(2,1)S(1)} %add_convert_fusion.3.rest_0_), channel_id=1, source_target_pairs={{0,2},{1,3},{2,0},{3,1},{4,6},{5,7},{6,4},{7,5},{8,10},{9,11},{10,... | collective-permute-start | bytes 1572872 | tf_op jit(solution)/shard_map/ppermute | solution.py:1124
  231.1 13.3 %collective-permute-start.40 = (bf16[256,1024]{1,0:T(8,128)(2,1)S(1)}, bf16[256,1024]{1,0:T(8,128)(2,1)}, u32[]{:S(2)}, u32[]{:S(2)}) collective-permute-start(bf16[256,1024]{1,0:T(8,128)(2,1)S(1)} %get-tuple-element.231.rest_0_), channel_id=1, source_target_pairs={{0,2},{1,3},{2,0},{3,1},{4,6},{5,7},{6,4},{7,5},{8,10},{9,11},{10,... | collective-permute-start | bytes 1572872 | tf_op jit(solution)/shard_map/ppermute | solution.py:1124
  232.1 17.0 %collective-permute-start.39 = (bf16[256,1024]{1,0:T(8,128)(2,1)S(1)}, bf16[256,1024]{1,0:T(8,128)(2,1)S(1)}, u32[]{:S(2)}, u32[]{:S(2)}) collective-permute-start(bf16[256,1024]{1,0:T(8,128)(2,1)S(1)} %get-tuple-element.231.rest_0_), channel_id=1, source_target_pairs={{0,1},{1,0},{2,3},{3,2},{4,5},{5,4},{6,7},{7,6},{8,9},{9,8},{10,11... | collective-permute-start | bytes 1572872 | tf_op jit(solution)/shard_map/ppermute | solution.py:1124
  244.4 30.0 %collective-permute-start.45 = (bf16[512,1024]{1,0:T(8,128)(2,1)S(1)}, bf16[512,1024]{1,0:T(8,128)(2,1)S(1)}, u32[]{:S(2)}, u32[]{:S(2)}) collective-permute-start(bf16[512,1024]{1,0:T(8,128)(2,1)S(1)} %get-tuple-element.235), channel_id=1, source_target_pairs={{0,4},{4,0},{8,12},{12,8},{16,20},{20,16},{24,28},{28,24},{1,5},{5... | collective-permute-start | bytes 3145736 | tf_op jit(solution)/shard_map/ppermute | solution.py:1124
  247.8 15.3 %collective-permute-start.42 = (bf16[256,1024]{1,0:T(8,128)(2,1)S(1)}, bf16[256,1024]{1,0:T(8,128)(2,1)S(1)}, u32[]{:S(2)}, u32[]{:S(2)}) collective-permute-start(bf16[256,1024]{1,0:T(8,128)(2,1)S(1)} %get-tuple-element.242), channel_id=1, source_target_pairs={{0,1},{1,0},{2,3},{3,2},{4,5},{5,4},{6,7},{7,6},{8,9},{9,8},{10,11... | collective-permute-start | bytes 1572872 | tf_op jit(solution)/shard_map/ppermute | solution.py:1124
  248.0 15.1 %collective-permute-start.43 = (bf16[256,1024]{1,0:T(8,128)(2,1)S(1)}, bf16[256,1024]{1,0:T(8,128)(2,1)S(1)}, u32[]{:S(2)}, u32[]{:S(2)}) collective-permute-start(bf16[256,1024]{1,0:T(8,128)(2,1)S(1)} %add_convert_fusion.2), channel_id=1, source_target_pairs={{0,2},{1,3},{2,0},{3,1},{4,6},{5,7},{6,4},{7,5},{8,10},{9,11},{10,... | collective-permute-start | bytes 1572872 | tf_op jit(solution)/shard_map/ppermute | solution.py:1124
  264.7 14.5 %collective-permute-start.47 = (bf16[256,1024]{1,0:T(8,128)(2,1)S(1)}, bf16[256,1024]{1,0:T(8,128)(2,1)}, u32[]{:S(2)}, u32[]{:S(2)}) collective-permute-start(bf16[256,1024]{1,0:T(8,128)(2,1)S(1)} %get-tuple-element.246.rest_0_), channel_id=1, source_target_pairs={{0,2},{1,3},{2,0},{3,1},{4,6},{5,7},{6,4},{7,5},{8,10},{9,11},{10,... | collective-permute-start | bytes 1572872 | tf_op jit(solution)/shard_map/ppermute | solution.py:1124
  279.2 24.4 %collective-permute-start.50 = (bf16[256,1024]{1,0:T(8,128)(2,1)}, bf16[256,1024]{1,0:T(8,128)(2,1)S(1)}, u32[]{:S(2)}, u32[]{:S(2)}) collective-permute-start(bf16[256,1024]{1,0:T(8,128)(2,1)} %copy-done.27), channel_id=1, source_target_pairs={{0,1},{1,0},{2,3},{3,2},{4,5},{5,4},{6,7},{7,6},{8,9},{9,8},{10,11... | collective-permute-start | bytes 1572872 | tf_op jit(solution)/shard_map/ppermute | solution.py:1124
  279.7 23.9 %collective-permute-start.51 = (bf16[256,1024]{1,0:T(8,128)(2,1)}, bf16[256,1024]{1,0:T(8,128)(2,1)S(1)}, u32[]{:S(2)}, u32[]{:S(2)}) collective-permute-start(bf16[256,1024]{1,0:T(8,128)(2,1)} %add_convert_fusion.1), channel_id=1, source_target_pairs={{0,2},{1,3},{2,0},{3,1},{4,6},{5,7},{6,4},{7,5},{8,10},{9,11},{10,... | collective-permute-start | bytes 1572872 | tf_op jit(solution)/shard_map/ppermute | solution.py:1124
  280.6 22.2 %collective-permute-start.52 = (bf16[256,1024]{1,0:T(8,128)(2,1)}, bf16[256,1024]{1,0:T(8,128)(2,1)S(1)}, u32[]{:S(2)}, u32[]{:S(2)}) collective-permute-start(bf16[256,1024]{1,0:T(8,128)(2,1)} %copy-done.28), channel_id=1, source_target_pairs={{0,8},{4,12},{8,0},{12,4},{16,24},{20,28},{24,16},{28,20},{1,9},{5... | collective-permute-start | bytes 1572872 | tf_op jit(solution)/shard_map/ppermute | solution.py:1124
  295.6 29.0 %collective-permute-start.49 = (bf16[256,1024]{1,0:T(8,128)(2,1)S(1)}, bf16[256,1024]{1,0:T(8,128)(2,1)S(1)}, u32[]{:S(2)}, u32[]{:S(2)}) collective-permute-start(bf16[256,1024]{1,0:T(8,128)(2,1)S(1)} %get-tuple-element.255), channel_id=1, source_target_pairs={{0,1},{1,0},{2,3},{3,2},{4,5},{5,4},{6,7},{7,6},{8,9},{9,8},{10,11... | collective-permute-start | bytes 1572872 | tf_op jit(solution)/shard_map/ppermute | solution.py:1124
  306.2 18.3 %collective-permute-start.54 = (bf16[256,1024]{1,0:T(8,128)(2,1)S(1)}, bf16[256,1024]{1,0:T(8,128)(2,1)S(1)}, u32[]{:S(2)}, u32[]{:S(2)}) collective-permute-start(bf16[256,1024]{1,0:T(8,128)(2,1)S(1)} %add_convert_fusion), channel_id=1, source_target_pairs={{0,2},{1,3},{2,0},{3,1},{4,6},{5,7},{6,4},{7,5},{8,10},{9,11},{10,... | collective-permute-start | bytes 1572872 | tf_op jit(solution)/shard_map/ppermute | solution.py:1124
  307.3 25.7 %collective-permute-start.56 = (bf16[128,1024]{1,0:T(8,128)(2,1)S(1)}, bf16[128,1024]{1,0:T(8,128)(2,1)S(1)}, u32[]{:S(2)}, u32[]{:S(2)}) collective-permute-start(bf16[128,1024]{1,0:T(8,128)(2,1)S(1)} %get-tuple-element.262), channel_id=1, source_target_pairs={{0,16},{4,20},{8,24},{12,28},{16,0},{20,4},{24,8},{28,12},{1,17},{... | collective-permute-start | bytes 786440 | tf_op jit(solution)/shard_map/ppermute | solution.py:1124
  320.8 15.5 %collective-permute-start.57 = (bf16[512,512]{1,0:T(8,128)(2,1)S(1)}, bf16[512,512]{1,0:T(8,128)(2,1)S(1)}, u32[]{:S(2)}, u32[]{:S(2)}) collective-permute-start(bf16[512,512]{1,0:T(8,128)(2,1)S(1)} %get-tuple-element.269), channel_id=1, source_target_pairs={{0,4},{4,0},{8,12},{12,8},{16,20},{20,16},{24,28},{28,24},{1,5},{5... | collective-permute-start | bytes 1572872 | tf_op jit(solution)/shard_map/ppermute | solution.py:1124
  322.2 29.3 %collective-permute-start.58 = (bf16[512,512]{1,0:T(8,128)(2,1)S(1)}, bf16[512,512]{1,0:T(8,128)(2,1)S(1)}, u32[]{:S(2)}, u32[]{:S(2)}) collective-permute-start(bf16[512,512]{1,0:T(8,128)(2,1)S(1)} %get-tuple-element.270), channel_id=1, source_target_pairs={{0,8},{4,12},{8,0},{12,4},{16,24},{20,28},{24,16},{28,20},{1,9},{5... | collective-permute-start | bytes 1572872 | tf_op jit(solution)/shard_map/ppermute | solution.py:1124
  333.7 22.5 %collective-permute-start.60 = (bf16[128,1024]{1,0:T(8,128)(2,1)S(1)}, bf16[128,1024]{1,0:T(8,128)(2,1)S(1)}, u32[]{:S(2)}, u32[]{:S(2)}) collective-permute-start(bf16[128,1024]{1,0:T(8,128)(2,1)S(1)} %halve_step.11.own_ref), channel_id=1, source_target_pairs={{0,16},{4,20},{8,24},{12,28},{16,0},{20,4},{24,8},{28,12},{1,17},{... | collective-permute-start | bytes 786440 | tf_op jit(solution)/shard_map/ppermute | solution.py:1124
  356.8 32.0 %collective-permute-start.64 = (bf16[256,1024]{1,0:T(8,128)(2,1)S(1)}, bf16[256,1024]{1,0:T(8,128)(2,1)S(1)}, u32[]{:S(2)}, u32[]{:S(2)}) collective-permute-start(bf16[256,1024]{1,0:T(8,128)(2,1)S(1)} %bitcast.35), channel_id=1, source_target_pairs={{0,8},{4,12},{8,0},{12,4},{16,24},{20,28},{24,16},{28,20},{1,9},{5... | collective-permute-start | bytes 1572872 | tf_op jit(solution)/shard_map/ppermute | solution.py:1124
  356.8 17.7 %collective-permute-start.61 = (bf16[256,512]{1,0:T(8,128)(2,1)S(1)}, bf16[256,512]{1,0:T(8,128)(2,1)S(1)}, u32[]{:S(2)}, u32[]{:S(2)}) collective-permute-start(bf16[256,512]{1,0:T(8,128)(2,1)S(1)} %get-tuple-element.287), channel_id=1, source_target_pairs={{0,8},{4,12},{8,0},{12,4},{16,24},{20,28},{24,16},{28,20},{1,9},{5... | collective-permute-start | bytes 786440 | tf_op jit(solution)/shard_map/ppermute | solution.py:1124
  358.9 17.1 %collective-permute-start.62 = (bf16[256,512]{1,0:T(8,128)(2,1)S(1)}, bf16[256,512]{1,0:T(8,128)(2,1)S(1)}, u32[]{:S(2)}, u32[]{:S(2)}) collective-permute-start(bf16[256,512]{1,0:T(8,128)(2,1)S(1)} %get-tuple-element.290), channel_id=1, source_target_pairs={{0,4},{4,0},{8,12},{12,8},{16,20},{20,16},{24,28},{28,24},{1,5},{5... | collective-permute-start | bytes 786440 | tf_op jit(solution)/shard_map/ppermute | solution.py:1124
  375.2 16.3 %collective-permute-start.65 = (bf16[128,512]{1,0:T(8,128)(2,1)S(1)}, bf16[128,512]{1,0:T(8,128)(2,1)S(1)}, u32[]{:S(2)}, u32[]{:S(2)}) collective-permute-start(bf16[128,512]{1,0:T(8,128)(2,1)S(1)} %get-tuple-element.295), channel_id=1, source_target_pairs={{0,16},{4,20},{8,24},{12,28},{16,0},{20,4},{24,8},{28,12},{1,17},{... | collective-permute-start | bytes 393224 | tf_op jit(solution)/shard_map/ppermute | solution.py:1124
  376.6 15.5 %collective-permute-start.66 = (bf16[128,512]{1,0:T(8,128)(2,1)S(1)}, bf16[128,512]{1,0:T(8,128)(2,1)S(1)}, u32[]{:S(2)}, u32[]{:S(2)}) collective-permute-start(bf16[128,512]{1,0:T(8,128)(2,1)S(1)} %get-tuple-element.298), channel_id=1, source_target_pairs={{0,16},{4,20},{8,24},{12,28},{16,0},{20,4},{24,8},{28,12},{1,17},{... | collective-permute-start | bytes 393224 | tf_op jit(solution)/shard_map/ppermute | solution.py:1124
  389.4 33.6 %collective-permute-start.75 = (bf16[512,1024]{1,0:T(8,128)(2,1)S(1)}, bf16[512,1024]{1,0:T(8,128)(2,1)S(1)}, u32[]{:S(2)}, u32[]{:S(2)}) collective-permute-start(bf16[512,1024]{1,0:T(8,128)(2,1)S(1)} %bitcast.33), channel_id=1, source_target_pairs={{0,4},{4,0},{8,12},{12,8},{16,20},{20,16},{24,28},{28,24},{1,5},{5... | collective-permute-start | bytes 3145736 | tf_op jit(solution)/shard_map/ppermute | solution.py:1124
  396.8 14.5 %collective-permute-start.69 = (bf16[128,512]{1,0:T(8,128)(2,1)S(1)}, bf16[128,512]{1,0:T(8,128)(2,1)S(1)}, u32[]{:S(2)}, u32[]{:S(2)}) collective-permute-start(bf16[128,512]{1,0:T(8,128)(2,1)S(1)} %halve_step.17.own_ref), channel_id=1, source_target_pairs={{0,16},{4,20},{8,24},{12,28},{16,0},{20,4},{24,8},{28,12},{1,17},{... | collective-permute-start | bytes 393224 | tf_op jit(solution)/shard_map/ppermute | solution.py:1124
  418.0 13.4 %collective-permute-start.72 = (bf16[512,512]{1,0:T(8,128)(2,1)S(1)}, bf16[512,512]{1,0:T(8,128)(2,1)S(1)}, u32[]{:S(2)}, u32[]{:S(2)}) collective-permute-start(bf16[512,512]{1,0:T(8,128)(2,1)S(1)} %bitcast.37), channel_id=1, source_target_pairs={{0,4},{4,0},{8,12},{12,8},{16,20},{20,16},{24,28},{28,24},{1,5},{5... | collective-permute-start | bytes 1572872 | tf_op jit(solution)/shard_map/ppermute | solution.py:1124
  (84 other events, 913.5 us)
Sparse Core Ops, SparseCore 0:
  202.5 71.1 reduce-scatter.1
  276.4 67.0 all-gather.1

commit v4 on v3

--- a/solution.py
+++ b/solution.py
@@ -1312,7 +1312,7 @@
     ab_a = attend_back(0, rows_a.blocks(sent), sent)
     low, rows_b = middle_back(1, fb_b, ab_a.mark)
     block = ab_a.cross(low)
-    sent = up_sum.advance(block)
+    sent = up_sum.advance(block, rows_b.cross)
     ab_b = attend_back(1, rows_b.blocks(sent), sent, down_part)
     down_all = lax.all_gather(tie(down_part, sent), "dp", axis=0, tiled=True)
     sent = up_sum.advance(ab_b.mark)
@@ -1324,7 +1324,8 @@
     first = DpSum(first_send, first_keep, flags, dp_size, bits)
     second = DpSum(second_send, second_keep, flags, dp_size, other_bits)
     sent = (first.advance(), second.advance())
-    sums = first_back(1, ab_b, *sent)
+    sent = up_sum.advance(*sent)
+    sums = first_back(1, ab_b, sent)
     sent = (sums,)
 
     total = lambda items: functools.reduce(jnp.add, items)
@@ -1333,23 +1334,34 @@
     small = jnp.concatenate([total(sums_one)[:2], total(sums_two), total(up_sums), heads_row])
     swaps = [("dp", dp_size, 1 << bit) for bit in bits] + [("tensor", 4, CORE), ("tensor", 4, CROSS)]
     local = None
-    while swaps or first.left:
+    axis, size, bit = swaps.pop(0)
+    arriving = swap(small, axis, size, bit)
+    sent = ()
+    while first.left or arriving is not None or up_sum.left:
+        if first.left:
+            sent = (first.advance(*sent),)
+            sent = (second.advance(*sent),)
+        if len(first.left) == 2:
+            grad_down_w = tie(down_all, *sent).astype(F32)
+            sent += (grad_down_w,)
+        small = tie(small, *sent)
+        if arriving is not None:
+            small = small + arriving
+        arriving = None
         if swaps:
             axis, size, bit = swaps.pop(0)
             if axis == "tensor" and local is None:
                 local, small = small[6:], small[:6]
-            small = small + swap(tie(small, *sent), axis, size, bit)
+            arriving = swap(small, axis, size, bit)
         sent = (small,)
         if up_sum.left:
             sent += (up_sum.advance(*sent),)
-        if first.left:
-            sent = (first.advance(*sent), second.advance(*sent))
-        if len(first.left) == 2:
-            grad_down_w = tie(down_all, *sent).astype(F32)
-            sent += (grad_down_w,)
     own, got = up_sum.halves()
     grad_up_w = join_step(flags, bits[0], tie(own, *sent), got, F32)
-    grad_qkv_w, grad_out_w = head_outputs(flags, (bits[0], other_bits[0]), first.halves(), second.halves())
+    own, got = first.halves()
+    grad_qkv_w, grad_out_w = head_outputs(
+        flags, (bits[0], other_bits[0]), (tie(own, grad_up_w), got), second.halves()
+    )
     return (
         shared["act"],
         loss,

time: 453 us -> 445 us (0.982)
  starting transfers between devices: 54.3 us -> 46.1 us
    ppermute x76, starting transfers between devices: 53.9 us -> 45.6 us  [swap(): return lax.ppermute(value, axis, [(i, i ^ bit) for i in range(size)])]
    unnamed x109 -> x111, local copies, waits for them, and re-layouts: 10.8 us -> 11.2 us
  transfers between devices with their start and end apart: 78 -> 78, of which waited for: 35 -> 36; matrix products, arithmetic and copies ran while one was open for 3% -> 3% of each run, Pallas kernels for 33% -> 33%
where the time goes in v4:
time: 445 us; the launch traced here: 437 us
  waiting for transfers between devices  181 us (41%)
  Pallas kernels  170 us (38%)
  starting transfers between devices  46.1 us (10%)
  local copies, waits for them, and re-layouts  15.5 us (3%)
  between operations  15.5 us (3%)
  other arithmetic  9.42 us (2%)
    ppermute x76, waiting for transfers between devices, swap(): return lax.ppermute(value, axis, [(i, i ^ bit) for i in range(size)])  181 us
    ppermute x76, starting transfers between devices, swap(): return lax.ppermute(value, axis, [(i, i ^ bit) for i in range(size)])  45.6 us
    pallas_call x2, Pallas kernels, attend_backward(): kernel_call(body, (*[struct((rows, feats), BF16)] * 4, struct((2 * seqs,...  24.5 us
    pallas_call x2, Pallas kernels, feed_forward(): kernel_call(body, (*[struct((rows, feats), BF16)] * 4, struct((4, seqs, l...  20.3 us
    pallas_call x2, Pallas kernels, attend_forward(): kernel_call(body, (*[struct((rows, feats), BF16)] * 4, struct((2 * seqs,...  20 us
    pallas_call x2, Pallas kernels, feed_backward(): kernel_call(body, (*[struct((rows, feats), BF16)] * 4, struct((4, seqs, l...  18.8 us
    pallas_call x2, Pallas kernels, contrast_grads(): kernel_call(body, (struct((rows, feats), F32), struct((2, rows, feats), B...  15.6 us
    pallas_call x1, Pallas kernels, head_grads(): kernel_call(body, (struct((feats // 2, 2 * width), BF16),) * 4, (ANY,) *...  13.2 us
  transfers between devices with their start and end apart: 78, of which 36 were waited for; matrix products, arithmetic and copies ran while one was open for 3% of the time, Pallas kernels for 33%

profile of v4, /device:TPU:0, one launch (start us, length us, event | category | flops | bytes accessed | tf_op | source)
XLA Modules:
  0.0 437.0 jit_solution(8150523453551421278)
XLA Ops:
  11.5 3.0 collective-permute-start.1
  15.5 10.9 %collective-permute-done.1.rest_2_ = bf16[256,1024]{1,0:T(8,128)(2,1)S(1)} collective-permute-done((bf16[256,1024]{1,0:T(8,128)(2,1)S(1)}, bf16[256,1024]{1,0:T(8,128)(2,1)S(1)}, u32[]{:S(2)}, u32[]{:S(2)}) %collective-permute-start.1) | collective-permute-done | bytes 524320 | tf_op jit(solution)/shard_map/ppermute | solution.py:1124
  31.1 9.8 %attend_forward.2 = (bf16[256,1024]{1,0:T(8,128)(2,1)S(1)}, bf16[256,1024]{1,0:T(8,128)(2,1)S(1)}, bf16[256,1024]{1,0:T(8,128)(2,1)S(1)}, bf16[256,1024]{1,0:T(8...) custom-call(s32[1]{0:T(128)} %bitcast.2.t_ref, s32[2,1024]{1,0:T(2,128)S(1)} %copy-done.24, ...), custom_call_target="tpu_custom_call" | custom-call | flops 69793216 | bytes 167772 | tf_op jit(solution)/shard_map/attend_forward/pallas_call | solution.py:343
  45.3 10.2 %attend_forward.3 = (bf16[256,1024]{1,0:T(8,128)(2,1)S(1)}, bf16[256,1024]{1,0:T(8,128)(2,1)S(1)}, bf16[256,1024]{1,0:T(8,128)(2,1)S(1)}, bf16[256,1024]{1,0:T(8...) custom-call(s32[1]{0:T(128)} %bitcast.2.t_ref, ...), custom_call_target="tpu_custom_call", output_to_operand_aliasing={{4}: (9, {})} | custom-call | flops 69793216 | bytes 167772 | tf_op jit(solution)/shard_map/attend_forward/pallas_call | solution.py:343
  55.5 2.0 collective-permute-done.9.x_ref
  59.8 12.1 %collective-permute-done.13.rest_2_ = bf16[256,1024]{1,0:T(8,128)(2,1)S(1)} collective-permute-done((bf16[256,1024]{1,0:T(8,128)(2,1)S(1)}, bf16[256,1024]{1,0:T(8,128)(2,1)S(1)}, u32[]{:S(2)}, u32[]{:S(2)}) %collective-permute-start.13) | collective-permute-done | bytes 524320 | tf_op jit(solution)/shard_map/ppermute | solution.py:1124
  74.7 10.0 %feed_forward.2 = (bf16[256,1024]{1,0:T(8,128)(2,1)S(1)}, bf16[256,1024]{1,0:T(8,128)(2,1)S(1)}, bf16[256,1024]{1,0:T(8,128)(2,1)S(1)}, bf16[256,1024]{1,0:T(8,128)(2,1)}, bf16[4,2,1024,1024]{3,2,1,0:T(8,128)(2,1)}) custom-call(f32[1,1024]{1,0:T(1,128)S(1)} %bitcast.59, bf16[256,1024]{1,0:T(8,128)(2,1)} %copy-done.22, bf16[256,1024]{1,0:T(8,128)(2,1)} %copy-done.47, ...), custom_call_target="tpu_custom_call" | custom-call | flops 85899344 | bytes 293601 | tf_op jit(solution)/shard_map/feed_forward/pallas_call | solution.py:551
  84.7 1.8 collective-permute-done.11.x_ref
  88.8 12.4 %collective-permute-done.17.rest_2_ = bf16[256,1024]{1,0:T(8,128)(2,1)S(1)} collective-permute-done((bf16[256,1024]{1,0:T(8,128)(2,1)S(1)}, bf16[256,1024]{1,0:T(8,128)(2,1)S(1)}, u32[]{:S(2)}, u32[]{:S(2)}) %collective-permute-start.17) | collective-permute-done | bytes 524320 | tf_op jit(solution)/shard_map/ppermute | solution.py:1124
  104.0 10.2 %feed_forward.3 = (bf16[256,1024]{1,0:T(8,128)(2,1)S(1)}, bf16[256,1024]{1,0:T(8,128)(2,1)S(1)}, bf16[256,1024]{1,0:T(8,128)(2,1)S(1)}, bf16[256,1024]{1,0:T(8,128)(2,1)}, bf16[4,2,1024,1024]{3,2,1,0:T(8,128)(2,1)}) custom-call(f32[1,1024]{1,0:T(1,128)S(1)} %bitcast.60, bf16[256,1024]{1,0:T(8,128)(2,1)} %copy-done.18, ...), custom_call_target="tpu_custom_call", output_to_operand_aliasing={{4}: (7, {})} | custom-call | flops 85899344 | bytes 293601 | tf_op jit(solution)/shard_map/feed_forward/pallas_call | solution.py:551
  119.5 12.8 %collective-permute-done.23.x_ref = bf16[256,1024]{1,0:T(8,128)(2,1)S(1)} collective-permute-done((bf16[256,1024]{1,0:T(8,128)(2,1)S(1)}, bf16[256,1024]{1,0:T(8,128)(2,1)S(1)}, u32[]{:S(2)}, u32[]{:S(2)}) %collective-permute-start.23) | collective-permute-done | bytes 524320 | tf_op jit(solution)/shard_map/ppermute | solution.py:1124
  134.2 10.1 %collective-permute-done.25.rest_2_ = bf16[272,1024]{1,0:T(8,128)(2,1)} collective-permute-done((bf16[272,1024]{1,0:T(8,128)(2,1)S(1)}, bf16[272,1024]{1,0:T(8,128)(2,1)}, u32[]{:S(2)}, u32[]{:S(2)}) %collective-permute-start.25) | collective-permute-done | bytes 557088 | tf_op jit(solution)/shard_map/ppermute | solution.py:1124
  144.8 9.7 %collective-permute-done.28.rest_6_ = bf16[272,1024]{1,0:T(8,128)(2,1)} collective-permute-done((bf16[272,1024]{1,0:T(8,128)(2,1)S(1)}, bf16[272,1024]{1,0:T(8,128)(2,1)}, u32[]{:S(2)}, u32[]{:S(2)}) %collective-permute-start.28) | collective-permute-done | bytes 557088 | tf_op jit(solution)/shard_map/ppermute | solution.py:1124
  157.8 9.6 %contrast_scores.1 = (bf16[16,256,2048]{2,1,0:T(8,128)(2,1)}, f32[1024,128]{1,0:T(8,128)S(1)}, f32[8,1024]{1,0:T(8,128)S(1)}, f32[2,256]{1,0:T(2,128)}) custom-call(s32[1]{0:T(128)} %bitcast.2.t_ref, s32[2,2]{1,0:T(2,128)S(1)} %slice.46.end_ref, s32[2,1024]{1,0:T(2,128)S(1)} %copy-done.25, s32[2,1024]{1,0:T(2,128)S(1)} %copy-done.26, ...), custom_call_target="tpu_custom_call" | custom-call | flops 85899344 | bytes 167772 | tf_op jit(solution)/shard_map/contrast_scores/pallas_call | solution.py:712
  167.4 3.2 collective-permute-done.31.rest_10_
  170.7 7.0 %contrast_grads.2 = (f32[256,1024]{1,0:T(8,128)}, bf16[2,256,1024]{2,1,0:T(8,128)(2,1)}) custom-call(s32[1]{0:T(128)} %bitcast.2.t_ref, s32[2,2]{1,0:T(2,128)S(1)} %slice.46.end_ref, s32[2,1024]{1,0:T(2,128)S(1)} %copy-done.26, f32[1024,128]{1,0:T(8,128)S(1)} %get-tuple-element.210.col, f32[8,1024]{1,0:T(8,128)S(1)} %get-tuple-element.211.own, ...), custom_call_target="tpu_custom_call" | custom-call | flops 42949672 | bytes 167772 | tf_op jit(solution)/shard_map/contrast_grads/pallas_call | solution.py:811
  177.7 3.8 collective-permute-done.32.rest_10_
  181.4 8.6 %contrast_grads.3 = (f32[256,1024]{1,0:T(8,128)}, bf16[2,256,1024]{2,1,0:T(8,128)(2,1)}) custom-call(s32[1]{0:T(128)} %bitcast.2.t_ref, s32[2,2]{1,0:T(2,128)S(1)} %slice.46.end_ref, s32[2,1024]{1,0:T(2,128)S(1)} %copy-done.26, f32[1024,128]{1,0:T(8,128)S(1)} %get-tuple-element.210.col, f32[8,1024]{1,0:T(8,128)S(1)} %get-tuple-element.211.own, ...), custom_call_target="tpu_custom_call" | custom-call | flops 42949672 | bytes 167772 | tf_op jit(solution)/shard_map/contrast_grads/pallas_call | solution.py:811
  190.6 3.0 collective-permute-done.33.rest_3_.got_ref
  195.3 8.9 %down_grad.1.rest_0_ = bf16[1024,1024]{1,0:T(8,128)(2,1)} custom-call(bf16[4,2,1024,1024]{3,2,1,0:T(8,128)(2,1)} %get-tuple-element.220.a_ref.saved_ref, bf16[2,256,1024]{2,1,0:T(8,128)(2,1)S(1)} %copy-done.2, bf16[2,256,1024]{2,1,0:T(8,128)(2,1)} %get-tuple-element.218.rest_1_.own_ref, bf16[2,256,1024]{2,1,0:T(8,128)(2,1)} %copy-done.31, ...), custom_call_target="tpu_custom_call" | custom-call | flops 85899344 | bytes 167772 | tf_op jit(solution)/shard_map/down_grad/pallas_call | solution.py:872
  204.6 9.3 %feed_backward.2 = (bf16[256,1024]{1,0:T(8,128)(2,1)S(1)}, bf16[256,1024]{1,0:T(8,128)(2,1)S(1)}, bf16[256,1024]{1,0:T(8,128)(2,1)S(1)}, bf16[256,1024]{1,0:T(8,...) custom-call(bf16[2,256,1024]{2,1,0:T(8,128)(2,1)} %get-tuple-element.219.res, ...), custom_call_target="tpu_custom_call", output_to_operand_aliasing={{4}: (2, {})} | custom-call | flops 85899344 | bytes 293601 | tf_op jit(solution)/shard_map/feed_backward/pallas_call | solution.py:620
  217.5 9.5 %feed_backward.3 = (bf16[256,1024]{1,0:T(8,128)(2,1)S(1)}, bf16[256,1024]{1,0:T(8,128)(2,1)S(1)}, bf16[256,1024]{1,0:T(8,128)(2,1)S(1)}, bf16[256,1024]{1,0:T(8,...) custom-call(bf16[2,256,1024]{2,1,0:T(8,128)(2,1)} %get-tuple-element.218.res, ...), custom_call_target="tpu_custom_call", output_to_operand_aliasing={{4}: (2, {})} | custom-call | flops 85899344 | bytes 293601 | tf_op jit(solution)/shard_map/feed_backward/pallas_call | solution.py:620
  227.1 3.3 collective-permute-done.37.x_ref
  235.2 9.3 %weight_grad.1 = (bf16[512,1024]{1,0:T(8,128)(2,1)S(1)}, bf16[512,1024]{1,0:T(8,128)(2,1)}) custom-call(s32[3]{0:T(128)S(1)} %shift-right-arithmetic_and_fusion.flag.refs_0_.h_ref, bf16[4,2,1024,1024]{3,2,1,0:T(8,128)(2,1)} %get-tuple-element.233.s_ref), custom_call_target="tpu_custom_call" | custom-call | flops 85899344 | bytes 167772 | tf_op jit(solution)/shard_map/weight_grad/pallas_call | solution.py:930
  244.4 1.8 collective-permute-done.40.rest_2_
  249.8 12.2 %attend_backward.2 = (bf16[256,1024]{1,0:T(8,128)(2,1)S(1)}, bf16[256,1024]{1,0:T(8,128)(2,1)S(1)}, bf16[256,1024]{1,0:T(8,128)(2,1)S(1)}, bf16[256,1024]{1,0:T(...) custom-call(s32[1]{0:T(128)} %bitcast.2.t_ref, s32[2,1024]{1,0:T(2,128)S(1)} %copy-done.25, ...), custom_call_target="tpu_custom_call" | custom-call | flops 96636768 | bytes 167772 | tf_op jit(solution)/shard_map/attend_backward/pallas_call | solution.py:468
  266.9 12.0 %collective-permute-done.45.rest_2_ = bf16[256,1024]{1,0:T(8,128)(2,1)S(1)} collective-permute-done((bf16[256,1024]{1,0:T(8,128)(2,1)S(1)}, bf16[256,1024]{1,0:T(8,128)(2,1)S(1)}, u32[]{:S(2)}, u32[]{:S(2)}) %collective-permute-start.45) | collective-permute-done | bytes 524320 | tf_op jit(solution)/shard_map/ppermute | solution.py:1124
  285.2 12.3 %attend_backward.3 = (bf16[256,1024]{1,0:T(8,128)(2,1)S(1)}, bf16[256,1024]{1,0:T(8,128)(2,1)S(1)}, bf16[256,1024]{1,0:T(8,128)(2,1)S(1)}, bf16[256,1024]{1,0:T(...) custom-call(s32[1]{0:T(128)} %bitcast.2.t_ref, ...), custom_call_target="tpu_custom_call", output_to_operand_aliasing={{4}: (10, {})} | custom-call | flops 96636768 | bytes 167772 | tf_op jit(solution)/shard_map/attend_backward/pallas_call | solution.py:468
  298.1 6.7 %collective-permute-done.52.g_ref = bf16[256,1024]{1,0:T(8,128)(2,1)S(1)} collective-permute-done((bf16[256,1024]{1,0:T(8,128)(2,1)}, bf16[256,1024]{1,0:T(8,128)(2,1)S(1)}, u32[]{:S(2)}, u32[]{:S(2)}) %collective-permute-start.52) | collective-permute-done | bytes 524320 | tf_op jit(solution)/shard_map/ppermute | solution.py:1124
  305.5 2.4 norm_backward.6
  310.0 13.2 %head_grads.1 = (bf16[512,512]{1,0:T(8,128)(2,1)S(1)}, bf16[512,512]{1,0:T(8,128)(2,1)S(1)}, bf16[512,512]{1,0:T(8,128)(2,1)S(1)}, bf16[512,512]{1,0:T(8,128)(2,1)}) custom-call(s32[3]{0:T(128)S(1)} %shift-right-arithmetic_and_fusion.flag.refs_0_.h_ref, bf16[4,1024,2048]{2,1,0:T(8,128)(2,1)} %get-tuple-element.268.rest_4_.refs_1_, ...), custom_call_target="tpu_custom_call" | custom-call | flops 85899344 | bytes 167772 | tf_op jit(solution)/shard_map/head_grads/pallas_call | solution.py:988
  324.5 3.1 collective-permute-start.57
  327.7 5.5 %collective-permute-done.55.g_ref = bf16[128,1024]{1,0:T(8,128)(2,1)S(1)} collective-permute-done((bf16[128,1024]{1,0:T(8,128)(2,1)S(1)}, bf16[128,1024]{1,0:T(8,128)(2,1)S(1)}, u32[]{:S(2)}, u32[]{:S(2)}) %collective-permute-start.55) | collective-permute-done | bytes 262176 | tf_op jit(solution)/shard_map/ppermute | solution.py:1124
  333.9 2.4 norm_backward.7
  337.2 16.7 %collective-permute-done.57.g_ref = bf16[512,512]{1,0:T(8,128)(2,1)S(1)} collective-permute-done((bf16[512,512]{1,0:T(8,128)(2,1)S(1)}, bf16[512,512]{1,0:T(8,128)(2,1)S(1)}, u32[]{:S(2)}, u32[]{:S(2)}) %collective-permute-start.57) | collective-permute-done | bytes 524320 | tf_op jit(solution)/shard_map/ppermute | solution.py:1124
  355.3 2.0 collective-permute-start.60
  357.6 17.2 %collective-permute-done.60.g_ref = bf16[256,512]{1,0:T(8,128)(2,1)S(1)} collective-permute-done((bf16[256,512]{1,0:T(8,128)(2,1)S(1)}, bf16[256,512]{1,0:T(8,128)(2,1)S(1)}, u32[]{:S(2)}, u32[]{:S(2)}) %collective-permute-start.60) | collective-permute-done | bytes 262176 | tf_op jit(solution)/shard_map/ppermute | solution.py:1124
  378.1 2.0 collective-permute-start.65
  380.1 7.6 %collective-permute-done.64.g_ref = bf16[128,512]{1,0:T(8,128)(2,1)S(1)} collective-permute-done((bf16[128,512]{1,0:T(8,128)(2,1)S(1)}, bf16[128,512]{1,0:T(8,128)(2,1)S(1)}, u32[]{:S(2)}, u32[]{:S(2)}) %collective-permute-start.64) | collective-permute-done | bytes 131104 | tf_op jit(solution)/shard_map/ppermute | solution.py:1124
  388.4 2.0 collective-permute-done.65.g_ref
  391.9 2.0 collective-permute-start.66
  393.9 4.1 convert_element_type.157
  398.0 5.4 %collective-permute-done.66 = f32[8,1024]{1,0:T(8,128)S(1)} collective-permute-done((f32[8,1024]{1,0:T(8,128)S(1)}, f32[8,1024]{1,0:T(8,128)S(1)}, u32[]{:S(2)}, u32[]{:S(2)}) %collective-permute-start.66) | collective-permute-done | bytes 32800 | tf_op jit(solution)/shard_map/ppermute | solution.py:1124
  407.0 5.3 %collective-permute-done.70.got_ref = bf16[256,512]{1,0:T(8,128)(2,1)S(1)} collective-permute-done((bf16[256,512]{1,0:T(8,128)(2,1)S(1)}, bf16[256,512]{1,0:T(8,128)(2,1)S(1)}, u32[]{:S(2)}, u32[]{:S(2)}) %collective-permute-start.70) | collective-permute-done | bytes 262176 | tf_op jit(solution)/shard_map/ppermute | solution.py:1124
  415.3 1.8 collective-permute-start.72
  419.2 2.7 join_step.13
  422.6 3.3 collective-permute-done.74.b_ref
  426.7 3.0 head_outputs.1
  (301 shorter events, 84.2 us)
Async XLA Ops:
  7.2 274.3 %reduce-scatter.2.cloned.1.call-start = ((), (), s32[]{:S(2)}) async-start(), calls=%async_computation.1 | async-start | bytes 2359296 | tf_op jit(solution)/shard_map/reduce_scatter | solution.py:1305
  11.5 14.9 %collective-permute-start.1 = (bf16[256,1024]{1,0:T(8,128)(2,1)S(1)}, bf16[256,1024]{1,0:T(8,128)(2,1)S(1)}, u32[]{:S(2)}, u32[]{:S(2)}) collective-permute-start(bf16[256,1024]{1,0:T(8,128)(2,1)S(1)} %get-tuple-element.166.rest_0_), channel_id=1, source_target_pairs={{0,2},{1,3},{2,0},{3,1},{4,6},{5,7},{6,4},{7,5},{8,10},{9,11},{10,... | collective-permute-start | bytes 1572872 | tf_op jit(solution)/shard_map/ppermute | solution.py:1124
  14.5 15.0 %collective-permute-start = (bf16[256,1024]{1,0:T(8,128)(2,1)S(1)}, bf16[256,1024]{1,0:T(8,128)(2,1)S(1)}, u32[]{:S(2)}, u32[]{:S(2)}) collective-permute-start(bf16[256,1024]{1,0:T(8,128)(2,1)S(1)} %get-tuple-element.166.rest_0_), channel_id=1, source_target_pairs={{0,1},{1,0},{2,3},{3,2},{4,5},{5,4},{6,7},{7,6},{8,9},{9,8},{10,11... | collective-permute-start | bytes 1572872 | tf_op jit(solution)/shard_map/ppermute | solution.py:1124
  26.4 15.2 %collective-permute-start.3 = (bf16[256,1024]{1,0:T(8,128)(2,1)S(1)}, bf16[256,1024]{1,0:T(8,128)(2,1)S(1)}, u32[]{:S(2)}, u32[]{:S(2)}) collective-permute-start(bf16[256,1024]{1,0:T(8,128)(2,1)S(1)} %get-tuple-element.169.rest_0_), channel_id=1, source_target_pairs={{0,2},{1,3},{2,0},{3,1},{4,6},{5,7},{6,4},{7,5},{8,10},{9,11},{10,... | collective-permute-start | bytes 1572872 | tf_op jit(solution)/shard_map/ppermute | solution.py:1124
  41.9 13.6 %collective-permute-start.8 = (bf16[256,1024]{1,0:T(8,128)(2,1)S(1)}, bf16[256,1024]{1,0:T(8,128)(2,1)S(1)}, u32[]{:S(2)}, u32[]{:S(2)}) collective-permute-start(bf16[256,1024]{1,0:T(8,128)(2,1)S(1)} %get-tuple-element.181), channel_id=1, source_target_pairs={{0,1},{1,0},{2,3},{3,2},{4,5},{5,4},{6,7},{7,6},{8,9},{9,8},{10,11... | collective-permute-start | bytes 1572872 | tf_op jit(solution)/shard_map/ppermute | solution.py:1124
  43.4 14.2 %collective-permute-start.9 = (bf16[256,1024]{1,0:T(8,128)(2,1)S(1)}, bf16[256,1024]{1,0:T(8,128)(2,1)S(1)}, u32[]{:S(2)}, u32[]{:S(2)}) collective-permute-start(bf16[256,1024]{1,0:T(8,128)(2,1)S(1)} %add_convert_fusion.7), channel_id=1, source_target_pairs={{0,2},{1,3},{2,0},{3,1},{4,6},{5,7},{6,4},{7,5},{8,10},{9,11},{10,... | collective-permute-start | bytes 1572872 | tf_op jit(solution)/shard_map/ppermute | solution.py:1124
  58.6 13.3 %collective-permute-start.13 = (bf16[256,1024]{1,0:T(8,128)(2,1)S(1)}, bf16[256,1024]{1,0:T(8,128)(2,1)S(1)}, u32[]{:S(2)}, u32[]{:S(2)}) collective-permute-start(bf16[256,1024]{1,0:T(8,128)(2,1)S(1)} %get-tuple-element.184.rest_0_), channel_id=1, source_target_pairs={{0,2},{1,3},{2,0},{3,1},{4,6},{5,7},{6,4},{7,5},{8,10},{9,11},{10,... | collective-permute-start | bytes 1572872 | tf_op jit(solution)/shard_map/ppermute | solution.py:1124
  59.3 25.4 %collective-permute-start.7 = (bf16[256,1024]{1,0:T(8,128)(2,1)S(1)}, bf16[256,1024]{1,0:T(8,128)(2,1)S(1)}, u32[]{:S(2)}, u32[]{:S(2)}) collective-permute-start(bf16[256,1024]{1,0:T(8,128)(2,1)S(1)} %get-tuple-element.177), channel_id=1, source_target_pairs={{0,1},{1,0},{2,3},{3,2},{4,5},{5,4},{6,7},{7,6},{8,9},{9,8},{10,11... | collective-permute-start | bytes 1572872 | tf_op jit(solution)/shard_map/ppermute | solution.py:1124
  72.2 14.4 %collective-permute-start.11 = (bf16[256,1024]{1,0:T(8,128)(2,1)S(1)}, bf16[256,1024]{1,0:T(8,128)(2,1)S(1)}, u32[]{:S(2)}, u32[]{:S(2)}) collective-permute-start(bf16[256,1024]{1,0:T(8,128)(2,1)S(1)} %add_convert_fusion.6), channel_id=1, source_target_pairs={{0,2},{1,3},{2,0},{3,1},{4,6},{5,7},{6,4},{7,5},{8,10},{9,11},{10,... | collective-permute-start | bytes 1572872 | tf_op jit(solution)/shard_map/ppermute | solution.py:1124
  87.6 13.6 %collective-permute-start.17 = (bf16[256,1024]{1,0:T(8,128)(2,1)S(1)}, bf16[256,1024]{1,0:T(8,128)(2,1)S(1)}, u32[]{:S(2)}, u32[]{:S(2)}) collective-permute-start(bf16[256,1024]{1,0:T(8,128)(2,1)S(1)} %get-tuple-element.191.rest_0_), channel_id=1, source_target_pairs={{0,2},{1,3},{2,0},{3,1},{4,6},{5,7},{6,4},{7,5},{8,10},{9,11},{10,... | collective-permute-start | bytes 1572872 | tf_op jit(solution)/shard_map/ppermute | solution.py:1124
  88.3 13.4 %collective-permute-start.15 = (bf16[256,1024]{1,0:T(8,128)(2,1)}, bf16[256,1024]{1,0:T(8,128)(2,1)S(1)}, u32[]{:S(2)}, u32[]{:S(2)}) collective-permute-start(bf16[256,1024]{1,0:T(8,128)(2,1)} %get-tuple-element.187), channel_id=1, source_target_pairs={{0,1},{1,0},{2,3},{3,2},{4,5},{5,4},{6,7},{7,6},{8,9},{9,8},{10,11... | collective-permute-start | bytes 1572872 | tf_op jit(solution)/shard_map/ppermute | solution.py:1124
  88.3 14.3 %collective-permute-start.16 = (bf16[256,1024]{1,0:T(8,128)(2,1)S(1)}, bf16[256,1024]{1,0:T(8,128)(2,1)S(1)}, u32[]{:S(2)}, u32[]{:S(2)}) collective-permute-start(bf16[256,1024]{1,0:T(8,128)(2,1)S(1)} %get-tuple-element.191.rest_0_), channel_id=1, source_target_pairs={{0,1},{1,0},{2,3},{3,2},{4,5},{5,4},{6,7},{7,6},{8,9},{9,8},{10,11... | collective-permute-start | bytes 1572872 | tf_op jit(solution)/shard_map/ppermute | solution.py:1124
  101.3 13.5 %collective-permute-start.20 = (bf16[256,1024]{1,0:T(8,128)(2,1)S(1)}, bf16[256,1024]{1,0:T(8,128)(2,1)S(1)}, u32[]{:S(2)}, u32[]{:S(2)}) collective-permute-start(bf16[256,1024]{1,0:T(8,128)(2,1)S(1)} %get-tuple-element.200), channel_id=1, source_target_pairs={{0,1},{1,0},{2,3},{3,2},{4,5},{5,4},{6,7},{7,6},{8,9},{9,8},{10,11... | collective-permute-start | bytes 1572872 | tf_op jit(solution)/shard_map/ppermute | solution.py:1124
  102.0 13.9 %collective-permute-start.21 = (bf16[256,1024]{1,0:T(8,128)(2,1)S(1)}, bf16[256,1024]{1,0:T(8,128)(2,1)S(1)}, u32[]{:S(2)}, u32[]{:S(2)}) collective-permute-start(bf16[256,1024]{1,0:T(8,128)(2,1)S(1)} %add_convert_fusion.5), channel_id=1, source_target_pairs={{0,2},{1,3},{2,0},{3,1},{4,6},{5,7},{6,4},{7,5},{8,10},{9,11},{10,... | collective-permute-start | bytes 1572872 | tf_op jit(solution)/shard_map/ppermute | solution.py:1124
  117.4 14.9 %collective-permute-start.23 = (bf16[256,1024]{1,0:T(8,128)(2,1)S(1)}, bf16[256,1024]{1,0:T(8,128)(2,1)S(1)}, u32[]{:S(2)}, u32[]{:S(2)}) collective-permute-start(bf16[256,1024]{1,0:T(8,128)(2,1)S(1)} %add_convert_fusion.4), channel_id=1, source_target_pairs={{0,2},{1,3},{2,0},{3,1},{4,6},{5,7},{6,4},{7,5},{8,10},{9,11},{10,... | collective-permute-start | bytes 1572872 | tf_op jit(solution)/shard_map/ppermute | solution.py:1124
  118.1 26.3 %collective-permute-start.25 = (bf16[272,1024]{1,0:T(8,128)(2,1)S(1)}, bf16[272,1024]{1,0:T(8,128)(2,1)}, u32[]{:S(2)}, u32[]{:S(2)}) collective-permute-start(bf16[272,1024]{1,0:T(8,128)(2,1)S(1)} %get-tuple-element.203.rest_0_), channel_id=1, source_target_pairs={{0,2},{1,3},{2,0},{3,1},{4,6},{5,7},{6,4},{7,5},{8,10},{9,11},{10,... | collective-permute-start | bytes 1671176 | tf_op jit(solution)/shard_map/ppermute | solution.py:1124
  133.6 21.0 %collective-permute-start.28 = (bf16[272,1024]{1,0:T(8,128)(2,1)S(1)}, bf16[272,1024]{1,0:T(8,128)(2,1)}, u32[]{:S(2)}, u32[]{:S(2)}) collective-permute-start(bf16[272,1024]{1,0:T(8,128)(2,1)S(1)} %get-tuple-element.208.rest_4_), channel_id=1, source_target_pairs={{0,2},{1,3},{2,0},{3,1},{4,6},{5,7},{6,4},{7,5},{8,10},{9,11},{10,... | collective-permute-start | bytes 1671176 | tf_op jit(solution)/shard_map/ppermute | solution.py:1124
  134.2 22.5 %collective-permute-start.24 = (bf16[272,1024]{1,0:T(8,128)(2,1)S(1)}, bf16[272,1024]{1,0:T(8,128)(2,1)S(1)}, u32[]{:S(2)}, u32[]{:S(2)}) collective-permute-start(bf16[272,1024]{1,0:T(8,128)(2,1)S(1)} %get-tuple-element.203.rest_0_), channel_id=1, source_target_pairs={{0,1},{1,0},{2,3},{3,2},{4,5},{5,4},{6,7},{7,6},{8,9},{9,8},{10,11... | collective-permute-start | bytes 1671176 | tf_op jit(solution)/shard_map/ppermute | solution.py:1124
  144.3 13.4 %collective-permute-start.26 = (bf16[272,1024]{1,0:T(8,128)(2,1)}, bf16[272,1024]{1,0:T(8,128)(2,1)}, u32[]{:S(2)}, u32[]{:S(2)}) collective-permute-start(bf16[272,1024]{1,0:T(8,128)(2,1)} %collective-permute-done.25.rest_2_), channel_id=1, source_target_pairs={{0,1},{1,0},{2,3},{3,2},{4,5},{5,4},{6,7},{7,6},{8,9},{9,8},{10,11... | collective-permute-start | bytes 1671176 | tf_op jit(solution)/shard_map/ppermute | solution.py:1124
  144.3 13.4 %collective-permute-start.27 = (bf16[272,1024]{1,0:T(8,128)(2,1)S(1)}, bf16[272,1024]{1,0:T(8,128)(2,1)}, u32[]{:S(2)}, u32[]{:S(2)}) collective-permute-start(bf16[272,1024]{1,0:T(8,128)(2,1)S(1)} %get-tuple-element.208.rest_4_), channel_id=1, source_target_pairs={{0,1},{1,0},{2,3},{3,2},{4,5},{5,4},{6,7},{7,6},{8,9},{9,8},{10,11... | collective-permute-start | bytes 1671176 | tf_op jit(solution)/shard_map/ppermute | solution.py:1124
  155.6 15.0 %collective-permute-start.31 = (bf16[256,1024]{1,0:T(8,128)(2,1)}, bf16[256,1024]{1,0:T(8,128)(2,1)}, u32[]{:S(2)}, u32[]{:S(2)}) collective-permute-start(bf16[256,1024]{1,0:T(8,128)(2,1)} %get-tuple-element.213), channel_id=1, source_target_pairs={{0,2},{1,3},{2,0},{3,1},{4,6},{5,7},{6,4},{7,5},{8,10},{9,11},{10,... | collective-permute-start | bytes 1572872 | tf_op jit(solution)/shard_map/ppermute | solution.py:1124
  156.7 24.7 %collective-permute-start.32 = (bf16[256,1024]{1,0:T(8,128)(2,1)}, bf16[256,1024]{1,0:T(8,128)(2,1)S(1)}, u32[]{:S(2)}, u32[]{:S(2)}) collective-permute-start(bf16[256,1024]{1,0:T(8,128)(2,1)} %get-tuple-element.216), channel_id=1, source_target_pairs={{0,2},{1,3},{2,0},{3,1},{4,6},{5,7},{6,4},{7,5},{8,10},{9,11},{10,... | collective-permute-start | bytes 1572872 | tf_op jit(solution)/shard_map/ppermute | solution.py:1124
  204.2 189.7 %all-gather.2.cloned.1.call-start = ((), (), s32[]{:S(2)}) async-start(), calls=%async_computation.2 | async-start | bytes 2359296 | tf_op jit(solution)/shard_map/all_gather | solution.py:1317
  216.3 14.0 %collective-permute-start.37 = (bf16[256,1024]{1,0:T(8,128)(2,1)S(1)}, bf16[256,1024]{1,0:T(8,128)(2,1)S(1)}, u32[]{:S(2)}, u32[]{:S(2)}) collective-permute-start(bf16[256,1024]{1,0:T(8,128)(2,1)S(1)} %add_convert_fusion.3.rest_0_), channel_id=1, source_target_pairs={{0,2},{1,3},{2,0},{3,1},{4,6},{5,7},{6,4},{7,5},{8,10},{9,11},{10,... | collective-permute-start | bytes 1572872 | tf_op jit(solution)/shard_map/ppermute | solution.py:1124
  232.9 13.3 %collective-permute-start.40 = (bf16[256,1024]{1,0:T(8,128)(2,1)S(1)}, bf16[256,1024]{1,0:T(8,128)(2,1)}, u32[]{:S(2)}, u32[]{:S(2)}) collective-permute-start(bf16[256,1024]{1,0:T(8,128)(2,1)S(1)} %get-tuple-element.231.rest_0_), channel_id=1, source_target_pairs={{0,2},{1,3},{2,0},{3,1},{4,6},{5,7},{6,4},{7,5},{8,10},{9,11},{10,... | collective-permute-start | bytes 1572872 | tf_op jit(solution)/shard_map/ppermute | solution.py:1124
  234.0 13.9 %collective-permute-start.39 = (bf16[256,1024]{1,0:T(8,128)(2,1)S(1)}, bf16[256,1024]{1,0:T(8,128)(2,1)S(1)}, u32[]{:S(2)}, u32[]{:S(2)}) collective-permute-start(bf16[256,1024]{1,0:T(8,128)(2,1)S(1)} %get-tuple-element.231.rest_0_), channel_id=1, source_target_pairs={{0,1},{1,0},{2,3},{3,2},{4,5},{5,4},{6,7},{7,6},{8,9},{9,8},{10,11... | collective-permute-start | bytes 1572872 | tf_op jit(solution)/shard_map/ppermute | solution.py:1124
  246.2 16.8 %collective-permute-start.42 = (bf16[256,1024]{1,0:T(8,128)(2,1)S(1)}, bf16[256,1024]{1,0:T(8,128)(2,1)S(1)}, u32[]{:S(2)}, u32[]{:S(2)}) collective-permute-start(bf16[256,1024]{1,0:T(8,128)(2,1)S(1)} %get-tuple-element.242), channel_id=1, source_target_pairs={{0,1},{1,0},{2,3},{3,2},{4,5},{5,4},{6,7},{7,6},{8,9},{9,8},{10,11... | collective-permute-start | bytes 1572872 | tf_op jit(solution)/shard_map/ppermute | solution.py:1124
  246.7 16.3 %collective-permute-start.43 = (bf16[256,1024]{1,0:T(8,128)(2,1)S(1)}, bf16[256,1024]{1,0:T(8,128)(2,1)S(1)}, u32[]{:S(2)}, u32[]{:S(2)}) collective-permute-start(bf16[256,1024]{1,0:T(8,128)(2,1)S(1)} %add_convert_fusion.2), channel_id=1, source_target_pairs={{0,2},{1,3},{2,0},{3,1},{4,6},{5,7},{6,4},{7,5},{8,10},{9,11},{10,... | collective-permute-start | bytes 1572872 | tf_op jit(solution)/shard_map/ppermute | solution.py:1124
  247.8 31.8 %collective-permute-start.46 = (bf16[512,1024]{1,0:T(8,128)(2,1)S(1)}, bf16[512,1024]{1,0:T(8,128)(2,1)S(1)}, u32[]{:S(2)}, u32[]{:S(2)}) collective-permute-start(bf16[512,1024]{1,0:T(8,128)(2,1)S(1)} %get-tuple-element.235), channel_id=1, source_target_pairs={{0,4},{4,0},{8,12},{12,8},{16,20},{20,16},{24,28},{28,24},{1,5},{5... | collective-permute-start | bytes 3145736 | tf_op jit(solution)/shard_map/ppermute | solution.py:1124
  264.5 14.3 %collective-permute-start.45 = (bf16[256,1024]{1,0:T(8,128)(2,1)S(1)}, bf16[256,1024]{1,0:T(8,128)(2,1)S(1)}, u32[]{:S(2)}, u32[]{:S(2)}) collective-permute-start(bf16[256,1024]{1,0:T(8,128)(2,1)S(1)} %get-tuple-element.246.rest_0_), channel_id=1, source_target_pairs={{0,2},{1,3},{2,0},{3,1},{4,6},{5,7},{6,4},{7,5},{8,10},{9,11},{10,... | collective-permute-start | bytes 1572872 | tf_op jit(solution)/shard_map/ppermute | solution.py:1124
  282.0 23.4 %collective-permute-start.50 = (bf16[256,1024]{1,0:T(8,128)(2,1)}, bf16[256,1024]{1,0:T(8,128)(2,1)S(1)}, u32[]{:S(2)}, u32[]{:S(2)}) collective-permute-start(bf16[256,1024]{1,0:T(8,128)(2,1)} %copy-done.27), channel_id=1, source_target_pairs={{0,1},{1,0},{2,3},{3,2},{4,5},{5,4},{6,7},{7,6},{8,9},{9,8},{10,11... | collective-permute-start | bytes 1572872 | tf_op jit(solution)/shard_map/ppermute | solution.py:1124
  282.1 23.3 %collective-permute-start.51 = (bf16[256,1024]{1,0:T(8,128)(2,1)}, bf16[256,1024]{1,0:T(8,128)(2,1)S(1)}, u32[]{:S(2)}, u32[]{:S(2)}) collective-permute-start(bf16[256,1024]{1,0:T(8,128)(2,1)} %add_convert_fusion.1), channel_id=1, source_target_pairs={{0,2},{1,3},{2,0},{3,1},{4,6},{5,7},{6,4},{7,5},{8,10},{9,11},{10,... | collective-permute-start | bytes 1572872 | tf_op jit(solution)/shard_map/ppermute | solution.py:1124
  283.2 21.6 %collective-permute-start.52 = (bf16[256,1024]{1,0:T(8,128)(2,1)}, bf16[256,1024]{1,0:T(8,128)(2,1)S(1)}, u32[]{:S(2)}, u32[]{:S(2)}) collective-permute-start(bf16[256,1024]{1,0:T(8,128)(2,1)} %copy-done.28), channel_id=1, source_target_pairs={{0,8},{4,12},{8,0},{12,4},{16,24},{20,28},{24,16},{28,20},{1,9},{5... | collective-permute-start | bytes 1572872 | tf_op jit(solution)/shard_map/ppermute | solution.py:1124
  297.7 36.2 %collective-permute-start.49 = (bf16[256,1024]{1,0:T(8,128)(2,1)S(1)}, bf16[256,1024]{1,0:T(8,128)(2,1)S(1)}, u32[]{:S(2)}, u32[]{:S(2)}) collective-permute-start(bf16[256,1024]{1,0:T(8,128)(2,1)S(1)} %get-tuple-element.255), channel_id=1, source_target_pairs={{0,1},{1,0},{2,3},{3,2},{4,5},{5,4},{6,7},{7,6},{8,9},{9,8},{10,11... | collective-permute-start | bytes 1572872 | tf_op jit(solution)/shard_map/ppermute | solution.py:1124
  308.1 25.8 %collective-permute-start.54 = (bf16[256,1024]{1,0:T(8,128)(2,1)S(1)}, bf16[256,1024]{1,0:T(8,128)(2,1)S(1)}, u32[]{:S(2)}, u32[]{:S(2)}) collective-permute-start(bf16[256,1024]{1,0:T(8,128)(2,1)S(1)} %add_convert_fusion), channel_id=1, source_target_pairs={{0,2},{1,3},{2,0},{3,1},{4,6},{5,7},{6,4},{7,5},{8,10},{9,11},{10,... | collective-permute-start | bytes 1572872 | tf_op jit(solution)/shard_map/ppermute | solution.py:1124
  308.7 24.6 %collective-permute-start.55 = (bf16[128,1024]{1,0:T(8,128)(2,1)S(1)}, bf16[128,1024]{1,0:T(8,128)(2,1)S(1)}, u32[]{:S(2)}, u32[]{:S(2)}) collective-permute-start(bf16[128,1024]{1,0:T(8,128)(2,1)S(1)} %get-tuple-element.262), channel_id=1, source_target_pairs={{0,16},{4,20},{8,24},{12,28},{16,0},{20,4},{24,8},{28,12},{1,17},{... | collective-permute-start | bytes 786440 | tf_op jit(solution)/shard_map/ppermute | solution.py:1124
  323.1 13.3 %collective-permute-start.56 = (bf16[512,512]{1,0:T(8,128)(2,1)S(1)}, bf16[512,512]{1,0:T(8,128)(2,1)S(1)}, u32[]{:S(2)}, u32[]{:S(2)}) collective-permute-start(bf16[512,512]{1,0:T(8,128)(2,1)S(1)} %get-tuple-element.270), channel_id=1, source_target_pairs={{0,4},{4,0},{8,12},{12,8},{16,20},{20,16},{24,28},{28,24},{1,5},{5... | collective-permute-start | bytes 1572872 | tf_op jit(solution)/shard_map/ppermute | solution.py:1124
  324.5 29.4 %collective-permute-start.57 = (bf16[512,512]{1,0:T(8,128)(2,1)S(1)}, bf16[512,512]{1,0:T(8,128)(2,1)S(1)}, u32[]{:S(2)}, u32[]{:S(2)}) collective-permute-start(bf16[512,512]{1,0:T(8,128)(2,1)S(1)} %get-tuple-element.271), channel_id=1, source_target_pairs={{0,8},{4,12},{8,0},{12,4},{16,24},{20,28},{24,16},{28,20},{1,9},{5... | collective-permute-start | bytes 1572872 | tf_op jit(solution)/shard_map/ppermute | solution.py:1124
  333.8 20.8 %collective-permute-start.59 = (bf16[128,1024]{1,0:T(8,128)(2,1)S(1)}, bf16[128,1024]{1,0:T(8,128)(2,1)S(1)}, u32[]{:S(2)}, u32[]{:S(2)}) collective-permute-start(bf16[128,1024]{1,0:T(8,128)(2,1)S(1)} %halve_step.11.own_ref), channel_id=1, source_target_pairs={{0,16},{4,20},{8,24},{12,28},{16,0},{20,4},{24,8},{28,12},{1,17},{... | collective-permute-start | bytes 786440 | tf_op jit(solution)/shard_map/ppermute | solution.py:1124
  336.4 18.2 %collective-permute-start.58 = (f32[8,1024]{1,0:T(8,128)S(1)}, f32[8,1024]{1,0:T(8,128)S(1)}, u32[]{:S(2)}, u32[]{:S(2)}) collective-permute-start(f32[8,1024]{1,0:T(8,128)S(1)} %select_maximum_fusion), channel_id=1, source_target_pairs={{0,4},{4,0},{8,12},{12,8},{16,20},{20,16},{24,28},{28,24},{1,5},{5... | collective-permute-start | bytes 98312 | tf_op jit(solution)/shard_map/ppermute | solution.py:1124
  355.2 20.9 %collective-permute-start.63 = (bf16[256,1024]{1,0:T(8,128)(2,1)S(1)}, bf16[256,1024]{1,0:T(8,128)(2,1)S(1)}, u32[]{:S(2)}, u32[]{:S(2)}) collective-permute-start(bf16[256,1024]{1,0:T(8,128)(2,1)S(1)} %bitcast.37), channel_id=1, source_target_pairs={{0,8},{4,12},{8,0},{12,4},{16,24},{20,28},{24,16},{28,20},{1,9},{5... | collective-permute-start | bytes 1572872 | tf_op jit(solution)/shard_map/ppermute | solution.py:1124
  355.3 19.5 %collective-permute-start.60 = (bf16[256,512]{1,0:T(8,128)(2,1)S(1)}, bf16[256,512]{1,0:T(8,128)(2,1)S(1)}, u32[]{:S(2)}, u32[]{:S(2)}) collective-permute-start(bf16[256,512]{1,0:T(8,128)(2,1)S(1)} %get-tuple-element.286), channel_id=1, source_target_pairs={{0,8},{4,12},{8,0},{12,4},{16,24},{20,28},{24,16},{28,20},{1,9},{5... | collective-permute-start | bytes 786440 | tf_op jit(solution)/shard_map/ppermute | solution.py:1124
  357.3 18.1 %collective-permute-start.61 = (bf16[256,512]{1,0:T(8,128)(2,1)S(1)}, bf16[256,512]{1,0:T(8,128)(2,1)S(1)}, u32[]{:S(2)}, u32[]{:S(2)}) collective-permute-start(bf16[256,512]{1,0:T(8,128)(2,1)S(1)} %get-tuple-element.288), channel_id=1, source_target_pairs={{0,4},{4,0},{8,12},{12,8},{16,20},{20,16},{24,28},{28,24},{1,5},{5... | collective-permute-start | bytes 786440 | tf_op jit(solution)/shard_map/ppermute | solution.py:1124
  357.6 18.5 %collective-permute-start.62 = (f32[8,1024]{1,0:T(8,128)S(1)}, f32[8,1024]{1,0:T(8,128)S(1)}, u32[]{:S(2)}, u32[]{:S(2)}) collective-permute-start(f32[8,1024]{1,0:T(8,128)S(1)} %add.97), channel_id=1, source_target_pairs={{0,8},{4,12},{8,0},{12,4},{16,24},{20,28},{24,16},{28,20},{1,9},{5... | collective-permute-start | bytes 98312 | tf_op jit(solution)/shard_map/ppermute | solution.py:1124
  376.7 42.5 %collective-permute-start.73 = (bf16[512,1024]{1,0:T(8,128)(2,1)S(1)}, bf16[512,1024]{1,0:T(8,128)(2,1)S(1)}, u32[]{:S(2)}, u32[]{:S(2)}) collective-permute-start(bf16[512,1024]{1,0:T(8,128)(2,1)S(1)} %bitcast.33), channel_id=1, source_target_pairs={{0,4},{4,0},{8,12},{12,8},{16,20},{20,16},{24,28},{28,24},{1,5},{5... | collective-permute-start | bytes 3145736 | tf_op jit(solution)/shard_map/ppermute | solution.py:1124
  388.3 15.1 %collective-permute-start.67 = (bf16[128,512]{1,0:T(8,128)(2,1)S(1)}, bf16[128,512]{1,0:T(8,128)(2,1)S(1)}, u32[]{:S(2)}, u32[]{:S(2)}) collective-permute-start(bf16[128,512]{1,0:T(8,128)(2,1)S(1)} %halve_step.16.own_ref), channel_id=1, source_target_pairs={{0,16},{4,20},{8,24},{12,28},{16,0},{20,4},{24,8},{28,12},{1,17},{... | collective-permute-start | bytes 393224 | tf_op jit(solution)/shard_map/ppermute | solution.py:1124
  390.9 13.1 %collective-permute-start.68 = (bf16[128,512]{1,0:T(8,128)(2,1)S(1)}, bf16[128,512]{1,0:T(8,128)(2,1)S(1)}, u32[]{:S(2)}, u32[]{:S(2)}) collective-permute-start(bf16[128,512]{1,0:T(8,128)(2,1)S(1)} %halve_step.17.own_ref), channel_id=1, source_target_pairs={{0,16},{4,20},{8,24},{12,28},{16,0},{20,4},{24,8},{28,12},{1,17},{... | collective-permute-start | bytes 393224 | tf_op jit(solution)/shard_map/ppermute | solution.py:1124
  412.9 13.1 %collective-permute-start.74 = (bf16[512,512]{1,0:T(8,128)(2,1)S(1)}, bf16[512,512]{1,0:T(8,128)(2,1)S(1)}, u32[]{:S(2)}, u32[]{:S(2)}) collective-permute-start(bf16[512,512]{1,0:T(8,128)(2,1)S(1)} %bitcast.35), channel_id=1, source_target_pairs={{0,4},{4,0},{8,12},{12,8},{16,20},{20,16},{24,28},{28,24},{1,5},{5... | collective-permute-start | bytes 1572872 | tf_op jit(solution)/shard_map/ppermute | solution.py:1124
  (85 other events, 939.3 us)
Sparse Core Ops, SparseCore 0:
  204.3 69.5 reduce-scatter.1
  281.6 64.7 all-gather.1

commit v5 on v4

--- a/solution.py
+++ b/solution.py
@@ -372,7 +372,7 @@
     )(place, docs, vecs, *blocks, wqkv, wo, *extra)
 
 
-def attend_backward(seq, place, docs, blocks, saved, lse, wqkv, wo, previous):
+def attend_backward(seq, place, docs, blocks, saved, lse, wqkv, wo, previous, earlier=()):
     rows, feats = blocks[0].shape
     parts = len(blocks)
     length = rows * parts
@@ -473,7 +473,7 @@
             struct((2, width), F32),
         ),
         (ANY,) * 4 + (HBM, whole((2, width))),
-        [SMEM, whole(docs.shape)] + [ANY] * 4 + [HBM] * (4 + len(extra)),
+        [SMEM, whole(docs.shape)] + [ANY] * 4 + [HBM] * (4 + len(extra)) + [ANY] * len(earlier),
         scratch=[
             VMEM((parts, rows, feats), BF16),
             VMEM(wqkv.shape, BF16),
@@ -495,7 +495,7 @@
         trans=length * length * heads // 2,
         aliases={10: 4} if extra else None,
         name="attend_backward",
-    )(place, docs, *blocks, saved, lse, wqkv, wo, *extra)
+    )(place, docs, *blocks, saved, lse, wqkv, wo, *extra, *earlier)
 
 
 ORDER = (3, 1, 2, 0)
@@ -946,38 +946,93 @@
     )(flags, saved)
 
 
-def head_grads(saved, grads, seqs, feats, flags, bits):
+def head_terms(seq, s_ref, h_ref, feats, width, a, g, r, a_sem, g_sem, r_sem):
+    tiles = feats // width
+    columns = [pl.ds(i * width, width) for i in range(tiles)]
+    a_load = lambda i: move(s_ref.at[seq, :, columns[i]], a.at[i], a_sem.at[i])
+    r_load = lambda i: move(h_ref.at[seq, :, columns[i]], r.at[i], r_sem.at[i])
+    g_load = lambda n: move(
+        (s_ref if n == 3 else h_ref).at[seq, :, pl.ds(feats + n * width, width)], g.at[n], g_sem.at[n]
+    )
+    a_loads = [a_load(0)]
+    g_loads = [g_load(n) for n in range(4)]
+    r_loads = [r_load(0)]
+    for i in range(1, tiles):
+        a_loads.append(a_load(i))
+        r_loads.append(r_load(i))
+
+    def tile(i):
+        a_loads[i].wait()
+        values = []
+        for n in range(3):
+            if i == 0:
+                g_loads[n].wait()
+            values.append(dot(a[i], g[n], TN))
+        if i == 0:
+            g_loads[3].wait()
+        r_loads[i].wait()
+        values.append(dot(g[3], r[i], TN))
+        return values
+
+    return tile, columns
+
+
+def head_scratch(length, feats, width):
+    tiles = feats // width
+    return [
+        VMEM((tiles, length, width), BF16),
+        VMEM((4, length, width), BF16),
+        VMEM((tiles, length, width), BF16),
+        DMA((tiles,)),
+        DMA((4,)),
+        DMA((tiles,)),
+    ]
+
+
+def head_part(saved, grads, feats):
     length = saved.shape[1]
     width = (saved.shape[2] - feats) // 4
     tiles = feats // width
 
-    def body(*refs):
-        flag, s_ref, h_ref = refs[:3]
-        first_refs, second_refs = refs[3:5], refs[5:7]
-        a, g, r, first, second, a_sem, g_sem, r_sem, o_sem = refs[7:]
-        both = pl.ds(0, seqs)
-        columns = [pl.ds(i * width, width) for i in range(tiles)]
-        g_loads = []
-        for n, ref in enumerate((h_ref, h_ref, h_ref, s_ref)):
-            g_loads.append(move(ref.at[both, :, pl.ds(feats + n * width, width)], g.at[n], g_sem.at[n]))
-        a_loads, r_loads = [], []
-        for i in range(tiles):
-            a_loads.append(move(s_ref.at[both, :, columns[i]], a.at[i], a_sem.at[i]))
-            r_loads.append(move(h_ref.at[both, :, columns[i]], r.at[i], r_sem.at[i]))
-        for copy in g_loads:
-            copy.wait()
-
-        def total(x, y):
-            return functools.reduce(jnp.add, [dot(x[s], y[s], TN) for s in range(seqs)]).astype(BF16)
-
+    def body(s_ref, h_ref, out_ref, a, g, r, a_sem, g_sem, r_sem, out, o_sem):
+        tile, _ = head_terms(0, s_ref, h_ref, feats, width, a, g, r, a_sem, g_sem, r_sem)
         stores = []
         for i in range(tiles):
-            a_loads[i].wait()
-            first[i, :, :width] = total(a[i], g[0])
-            first[i, :, width:] = total(a[i], g[1])
-            second[i, :, :width] = total(a[i], g[2])
-            r_loads[i].wait()
-            second[i, :, width:] = total(g[3], r[i])
+            for n, value in enumerate(tile(i)):
+                out[i, :, n * width : (n + 1) * width] = value
+            stores.append(move(out.at[i], out_ref.at[i], o_sem.at[i]))
+        for copy in stores:
+            copy.wait()
+
+    return kernel_call(
+        body,
+        struct((tiles, width, 4 * width), F32),
+        ANY,
+        [HBM] * 2,
+        scratch=head_scratch(length, feats, width) + [VMEM((tiles, width, 4 * width), F32), DMA((tiles,))],
+        flops=8 * length * feats * width,
+        nbytes=4 * length * feats,
+        name="head_part",
+    )(saved, grads)
+
+
+def head_grads(saved, grads, part, feats, flags, bits):
+    length = saved.shape[1]
+    width = (saved.shape[2] - feats) // 4
+    tiles = feats // width
+
+    def body(flag, s_ref, h_ref, part_ref, *refs):
+        first_refs, second_refs = refs[:2], refs[2:4]
+        a, g, r, a_sem, g_sem, r_sem, old, first, second, p_sem, o_sem = refs[4:]
+        tile, columns = head_terms(1, s_ref, h_ref, feats, width, a, g, r, a_sem, g_sem, r_sem)
+        p_loads = [move(part_ref.at[i], old.at[i], p_sem.at[i]) for i in range(tiles)]
+        stores = []
+        for i in range(tiles):
+            values = tile(i)
+            p_loads[i].wait()
+            for n, value in enumerate(values):
+                total = value + old[i, :, n * width : (n + 1) * width]
+                (first, second)[n // 2][i, :, n % 2 * width : (n % 2 + 1) * width] = total.astype(BF16)
             for n, (src, outs) in enumerate(((first, first_refs), (second, second_refs))):
                 stores.append(
                     send_half(i, tiles, flag[bits[n]], src.at[i], *outs, pl.ds(0, 2 * width), o_sem.at[2 * i + n])
@@ -989,22 +1044,19 @@
         body,
         (struct((feats // 2, 2 * width), BF16),) * 4,
         (ANY,) * 4,
-        [pl.BlockSpec(memory_space=pltpu.SMEM)] + [HBM] * 2,
-        scratch=[
-            VMEM((tiles, seqs, length, width), BF16),
-            VMEM((4, seqs, length, width), BF16),
-            VMEM((tiles, seqs, length, width), BF16),
+        [SMEM] + [HBM] * 2 + [ANY],
+        scratch=head_scratch(length, feats, width)
+        + [
+            VMEM((tiles, width, 4 * width), F32),
             VMEM((tiles, width, 2 * width), BF16),
             VMEM((tiles, width, 2 * width), BF16),
             DMA((tiles,)),
-            DMA((4,)),
-            DMA((tiles,)),
             DMA((2 * tiles,)),
         ],
-        flops=2 * seqs * length * feats * width * 4,
-        nbytes=4 * seqs * length * feats,
+        flops=8 * length * feats * width,
+        nbytes=4 * length * feats,
         name="head_grads",
-    )(flags, saved, grads)
+    )(flags, saved, grads, part)
 
 
 def halve_step(flags, bit, keep, got):
@@ -1285,10 +1337,10 @@
         )
         return low, Gather(low)
 
-    def attend_back(s, gathered, *earlier):
+    def attend_back(s, gathered, *earlier, after=()):
         *blocks, shared["heads"], head_sums[s] = attend_backward(
             s, tie(place, *earlier), doc_ids, gathered, shared["attend"], kept[s], qkv_weight, output_weight,
-            shared["heads"],
+            shared["heads"], after,
         )
         return Scatter(blocks)
 
@@ -1312,50 +1364,50 @@
     ab_a = attend_back(0, rows_a.blocks(sent), sent)
     low, rows_b = middle_back(1, fb_b, ab_a.mark)
     block = ab_a.cross(low)
-    sent = up_sum.advance(block, rows_b.cross)
-    ab_b = attend_back(1, rows_b.blocks(sent), sent, down_part)
+    part = head_part(tie(shared["attend"], block), shared["heads"], feats)
+    sent = up_sum.advance(part, rows_b.cross)
+    ab_b = attend_back(1, rows_b.blocks(sent), sent, down_part, after=(part,))
     down_all = lax.all_gather(tie(down_part, sent), "dp", axis=0, tiled=True)
     sent = up_sum.advance(ab_b.mark)
     sums = first_back(0, ab_a, sent)
     block = ab_b.cross(sums)
     first_send, first_keep, second_send, second_keep = head_grads(
-        tie(shared["attend"], block), shared["heads"], seqs, feats, flags, (bits[0], other_bits[0])
+        tie(shared["attend"], block), shared["heads"], part, feats, flags, (bits[0], other_bits[0])
     )
     first = DpSum(first_send, first_keep, flags, dp_size, bits)
     second = DpSum(second_send, second_keep, flags, dp_size, other_bits)
     sent = (first.advance(), second.advance())
-    sent = up_sum.advance(*sent)
-    sums = first_back(1, ab_b, sent)
+    sums = first_back(1, ab_b, *sent)
     sent = (sums,)
 
     total = lambda items: functools.reduce(jnp.add, items)
     heads_sum = total(head_sums)
     heads_row = jnp.pad(heads_sum.reshape(1, -1), ((0, 0), (0, feats - heads_sum.size)))
     small = jnp.concatenate([total(sums_one)[:2], total(sums_two), total(up_sums), heads_row])
-    swaps = [("dp", dp_size, 1 << bit) for bit in bits] + [("tensor", 4, CORE), ("tensor", 4, CROSS)]
-    local = None
+    swaps = [("tensor", 4, CROSS)] + [("dp", dp_size, 1 << bit) for bit in bits] + [("tensor", 4, CORE)]
+    shared_rows = (jnp.arange(small.shape[0]) < 6).astype(F32)[:, None]
     axis, size, bit = swaps.pop(0)
     arriving = swap(small, axis, size, bit)
     sent = ()
     while first.left or arriving is not None or up_sum.left:
         if first.left:
             sent = (first.advance(*sent),)
+        if up_sum.left:
+            sent = (up_sum.advance(*sent),)
+        if second.left:
             sent = (second.advance(*sent),)
         if len(first.left) == 2:
             grad_down_w = tie(down_all, *sent).astype(F32)
             sent += (grad_down_w,)
         small = tie(small, *sent)
         if arriving is not None:
-            small = small + arriving
+            small = small + (arriving * shared_rows if axis == "tensor" else arriving)
         arriving = None
         if swaps:
             axis, size, bit = swaps.pop(0)
-            if axis == "tensor" and local is None:
-                local, small = small[6:], small[:6]
             arriving = swap(small, axis, size, bit)
         sent = (small,)
-        if up_sum.left:
-            sent += (up_sum.advance(*sent),)
+    local, small = small[6:], small[:6]
     own, got = up_sum.halves()
     grad_up_w = join_step(flags, bits[0], tie(own, *sent), got, F32)
     own, got = first.halves()

time: 445 us -> 442 us (level)
  waiting for transfers between devices: 181 us -> 163 us
  starting transfers between devices: 46.1 us -> 57.9 us
    ppermute x76, waiting for transfers between devices: 181 us -> 163 us  [swap(): return lax.ppermute(value, axis, [(i, i ^ bit) for i in range(size)])]
    ppermute x76, starting transfers between devices: 45.6 us -> 57.4 us  [swap(): return lax.ppermute(value, axis, [(i, i ^ bit) for i in range(size)])]
    pallas_call x0 -> x1, Pallas kernels: none -> 7.95 us  [head_part(): kernel_call(body, struct((tiles, width, 4 * width), F32), ANY, [HBM] * 2,...]
    pallas_call x1, Pallas kernels: 13.2 us -> 8.02 us  [head_grads(): kernel_call(body, (struct((feats // 2, 2 * width), BF16),) * 4, (ANY,) *...]
  transfers between devices with their start and end apart: 78 -> 78, of which waited for: 36 -> 33; matrix products, arithmetic and copies ran while one was open for 3% -> 3% of each run, Pallas kernels for 33% -> 34%
where the time goes in v5:
time: 442 us; the launch traced here: 434 us
  Pallas kernels  173 us (39%)
  waiting for transfers between devices  163 us (37%)
  starting transfers between devices  57.9 us (13%)
  between operations  15.4 us (3%)
  local copies, waits for them, and re-layouts  15.2 us (3%)
  other arithmetic  9.53 us (2%)
    ppermute x76, waiting for transfers between devices, swap(): return lax.ppermute(value, axis, [(i, i ^ bit) for i in range(size)])  163 us
    ppermute x76, starting transfers between devices, swap(): return lax.ppermute(value, axis, [(i, i ^ bit) for i in range(size)])  57.4 us
    pallas_call x2, Pallas kernels, attend_backward(): kernel_call(body, (*[struct((rows, feats), BF16)] * 4, struct((2 * seqs,...  25 us
    pallas_call x2, Pallas kernels, feed_forward(): kernel_call(body, (*[struct((rows, feats), BF16)] * 4, struct((4, seqs, l...  20.3 us
    pallas_call x2, Pallas kernels, attend_forward(): kernel_call(body, (*[struct((rows, feats), BF16)] * 4, struct((2 * seqs,...  20 us
    pallas_call x2, Pallas kernels, feed_backward(): kernel_call(body, (*[struct((rows, feats), BF16)] * 4, struct((4, seqs, l...  18.8 us
    pallas_call x2, Pallas kernels, contrast_grads(): kernel_call(body, (struct((rows, feats), F32), struct((2, rows, feats), B...  15.6 us
    unnamed x111, local copies, waits for them, and re-layouts  11.6 us
  transfers between devices with their start and end apart: 78, of which 33 were waited for; matrix products, arithmetic and copies ran while one was open for 3% of the time, Pallas kernels for 34%

profile of v5, /device:TPU:0, one launch (start us, length us, event | category | flops | bytes accessed | tf_op | source)
XLA Modules:
  0.0 433.8 jit_solution(3070560507254139226)
XLA Ops:
  11.5 3.0 collective-permute-start.1
  15.5 10.9 %collective-permute-done.1.rest_2_ = bf16[256,1024]{1,0:T(8,128)(2,1)S(1)} collective-permute-done((bf16[256,1024]{1,0:T(8,128)(2,1)S(1)}, bf16[256,1024]{1,0:T(8,128)(2,1)S(1)}, u32[]{:S(2)}, u32[]{:S(2)}) %collective-permute-start.1) | collective-permute-done | bytes 524320 | tf_op jit(solution)/shard_map/ppermute | solution.py:1176
  31.1 9.8 %attend_forward.2 = (bf16[256,1024]{1,0:T(8,128)(2,1)S(1)}, bf16[256,1024]{1,0:T(8,128)(2,1)S(1)}, bf16[256,1024]{1,0:T(8,128)(2,1)S(1)}, bf16[256,1024]{1,0:T(8...) custom-call(s32[1]{0:T(128)} %bitcast.2.t_ref, s32[2,1024]{1,0:T(2,128)S(1)} %copy-done.24, ...), custom_call_target="tpu_custom_call" | custom-call | flops 69793216 | bytes 167772 | tf_op jit(solution)/shard_map/attend_forward/pallas_call | solution.py:343
  45.3 10.2 %attend_forward.3 = (bf16[256,1024]{1,0:T(8,128)(2,1)S(1)}, bf16[256,1024]{1,0:T(8,128)(2,1)S(1)}, bf16[256,1024]{1,0:T(8,128)(2,1)S(1)}, bf16[256,1024]{1,0:T(8...) custom-call(s32[1]{0:T(128)} %bitcast.2.t_ref, ...), custom_call_target="tpu_custom_call", output_to_operand_aliasing={{4}: (9, {})} | custom-call | flops 69793216 | bytes 167772 | tf_op jit(solution)/shard_map/attend_forward/pallas_call | solution.py:343
  55.5 2.0 collective-permute-done.9.x_ref
  59.8 12.1 %collective-permute-done.13.rest_2_ = bf16[256,1024]{1,0:T(8,128)(2,1)S(1)} collective-permute-done((bf16[256,1024]{1,0:T(8,128)(2,1)S(1)}, bf16[256,1024]{1,0:T(8,128)(2,1)S(1)}, u32[]{:S(2)}, u32[]{:S(2)}) %collective-permute-start.13) | collective-permute-done | bytes 524320 | tf_op jit(solution)/shard_map/ppermute | solution.py:1176
  74.7 10.0 %feed_forward.2 = (bf16[256,1024]{1,0:T(8,128)(2,1)S(1)}, bf16[256,1024]{1,0:T(8,128)(2,1)S(1)}, bf16[256,1024]{1,0:T(8,128)(2,1)S(1)}, bf16[256,1024]{1,0:T(8,128)(2,1)}, bf16[4,2,1024,1024]{3,2,1,0:T(8,128)(2,1)}) custom-call(f32[1,1024]{1,0:T(1,128)S(1)} %bitcast.58, bf16[256,1024]{1,0:T(8,128)(2,1)} %copy-done.22, bf16[256,1024]{1,0:T(8,128)(2,1)} %copy-done.47, ...), custom_call_target="tpu_custom_call" | custom-call | flops 85899344 | bytes 293601 | tf_op jit(solution)/shard_map/feed_forward/pallas_call | solution.py:551
  88.8 12.4 %collective-permute-done.17.rest_2_ = bf16[256,1024]{1,0:T(8,128)(2,1)S(1)} collective-permute-done((bf16[256,1024]{1,0:T(8,128)(2,1)S(1)}, bf16[256,1024]{1,0:T(8,128)(2,1)S(1)}, u32[]{:S(2)}, u32[]{:S(2)}) %collective-permute-start.17) | collective-permute-done | bytes 524320 | tf_op jit(solution)/shard_map/ppermute | solution.py:1176
  104.0 10.2 %feed_forward.3 = (bf16[256,1024]{1,0:T(8,128)(2,1)S(1)}, bf16[256,1024]{1,0:T(8,128)(2,1)S(1)}, bf16[256,1024]{1,0:T(8,128)(2,1)S(1)}, bf16[256,1024]{1,0:T(8,128)(2,1)}, bf16[4,2,1024,1024]{3,2,1,0:T(8,128)(2,1)}) custom-call(f32[1,1024]{1,0:T(1,128)S(1)} %bitcast.59, bf16[256,1024]{1,0:T(8,128)(2,1)} %copy-done.18, ...), custom_call_target="tpu_custom_call", output_to_operand_aliasing={{4}: (7, {})} | custom-call | flops 85899344 | bytes 293601 | tf_op jit(solution)/shard_map/feed_forward/pallas_call | solution.py:551
  119.5 12.8 %collective-permute-done.23.x_ref = bf16[256,1024]{1,0:T(8,128)(2,1)S(1)} collective-permute-done((bf16[256,1024]{1,0:T(8,128)(2,1)S(1)}, bf16[256,1024]{1,0:T(8,128)(2,1)S(1)}, u32[]{:S(2)}, u32[]{:S(2)}) %collective-permute-start.23) | collective-permute-done | bytes 524320 | tf_op jit(solution)/shard_map/ppermute | solution.py:1176
  134.2 10.1 %collective-permute-done.25.rest_2_ = bf16[272,1024]{1,0:T(8,128)(2,1)} collective-permute-done((bf16[272,1024]{1,0:T(8,128)(2,1)S(1)}, bf16[272,1024]{1,0:T(8,128)(2,1)}, u32[]{:S(2)}, u32[]{:S(2)}) %collective-permute-start.25) | collective-permute-done | bytes 557088 | tf_op jit(solution)/shard_map/ppermute | solution.py:1176
  144.8 9.7 %collective-permute-done.28.rest_6_ = bf16[272,1024]{1,0:T(8,128)(2,1)} collective-permute-done((bf16[272,1024]{1,0:T(8,128)(2,1)S(1)}, bf16[272,1024]{1,0:T(8,128)(2,1)}, u32[]{:S(2)}, u32[]{:S(2)}) %collective-permute-start.28) | collective-permute-done | bytes 557088 | tf_op jit(solution)/shard_map/ppermute | solution.py:1176
  157.8 9.6 %contrast_scores.1 = (bf16[16,256,2048]{2,1,0:T(8,128)(2,1)}, f32[1024,128]{1,0:T(8,128)S(1)}, f32[8,1024]{1,0:T(8,128)S(1)}, f32[2,256]{1,0:T(2,128)}) custom-call(s32[1]{0:T(128)} %bitcast.2.t_ref, s32[2,2]{1,0:T(2,128)S(1)} %slice.50.end_ref, s32[2,1024]{1,0:T(2,128)S(1)} %copy-done.25, s32[2,1024]{1,0:T(2,128)S(1)} %copy-done.26, ...), custom_call_target="tpu_custom_call" | custom-call | flops 85899344 | bytes 167772 | tf_op jit(solution)/shard_map/contrast_scores/pallas_call | solution.py:712
  167.4 3.2 collective-permute-done.31.rest_10_
  170.7 7.0 %contrast_grads.2 = (f32[256,1024]{1,0:T(8,128)}, bf16[2,256,1024]{2,1,0:T(8,128)(2,1)}) custom-call(s32[1]{0:T(128)} %bitcast.2.t_ref, s32[2,2]{1,0:T(2,128)S(1)} %slice.50.end_ref, s32[2,1024]{1,0:T(2,128)S(1)} %copy-done.26, f32[1024,128]{1,0:T(8,128)S(1)} %get-tuple-element.211.col, f32[8,1024]{1,0:T(8,128)S(1)} %get-tuple-element.212.own, ...), custom_call_target="tpu_custom_call" | custom-call | flops 42949672 | bytes 167772 | tf_op jit(solution)/shard_map/contrast_grads/pallas_call | solution.py:811
  177.7 3.8 collective-permute-done.32.rest_10_
  181.4 8.6 %contrast_grads.3 = (f32[256,1024]{1,0:T(8,128)}, bf16[2,256,1024]{2,1,0:T(8,128)(2,1)}) custom-call(s32[1]{0:T(128)} %bitcast.2.t_ref, s32[2,2]{1,0:T(2,128)S(1)} %slice.50.end_ref, s32[2,1024]{1,0:T(2,128)S(1)} %copy-done.26, f32[1024,128]{1,0:T(8,128)S(1)} %get-tuple-element.211.col, f32[8,1024]{1,0:T(8,128)S(1)} %get-tuple-element.212.own, ...), custom_call_target="tpu_custom_call" | custom-call | flops 42949672 | bytes 167772 | tf_op jit(solution)/shard_map/contrast_grads/pallas_call | solution.py:811
  190.6 3.0 collective-permute-done.33.rest_3_.got_ref
  195.3 8.9 %down_grad.1.rest_0_ = bf16[1024,1024]{1,0:T(8,128)(2,1)} custom-call(bf16[4,2,1024,1024]{3,2,1,0:T(8,128)(2,1)} %get-tuple-element.221.a_ref.saved_ref, bf16[2,256,1024]{2,1,0:T(8,128)(2,1)S(1)} %copy-done.2, bf16[2,256,1024]{2,1,0:T(8,128)(2,1)} %get-tuple-element.219.rest_1_.own_ref, bf16[2,256,1024]{2,1,0:T(8,128)(2,1)} %copy-done.31, ...), custom_call_target="tpu_custom_call" | custom-call | flops 85899344 | bytes 167772 | tf_op jit(solution)/shard_map/down_grad/pallas_call | solution.py:872
  204.6 9.3 %feed_backward.2 = (bf16[256,1024]{1,0:T(8,128)(2,1)S(1)}, bf16[256,1024]{1,0:T(8,128)(2,1)S(1)}, bf16[256,1024]{1,0:T(8,128)(2,1)S(1)}, bf16[256,1024]{1,0:T(8,...) custom-call(bf16[2,256,1024]{2,1,0:T(8,128)(2,1)} %get-tuple-element.220.res, ...), custom_call_target="tpu_custom_call", output_to_operand_aliasing={{4}: (2, {})} | custom-call | flops 85899344 | bytes 293601 | tf_op jit(solution)/shard_map/feed_backward/pallas_call | solution.py:620
  217.5 9.5 %feed_backward.3 = (bf16[256,1024]{1,0:T(8,128)(2,1)S(1)}, bf16[256,1024]{1,0:T(8,128)(2,1)S(1)}, bf16[256,1024]{1,0:T(8,128)(2,1)S(1)}, bf16[256,1024]{1,0:T(8,...) custom-call(bf16[2,256,1024]{2,1,0:T(8,128)(2,1)} %get-tuple-element.219.res, ...), custom_call_target="tpu_custom_call", output_to_operand_aliasing={{4}: (2, {})} | custom-call | flops 85899344 | bytes 293601 | tf_op jit(solution)/shard_map/feed_backward/pallas_call | solution.py:620
  227.1 3.3 collective-permute-done.37.x_ref
  235.2 9.3 %weight_grad.1 = (bf16[512,1024]{1,0:T(8,128)(2,1)S(1)}, bf16[512,1024]{1,0:T(8,128)(2,1)}) custom-call(s32[3]{0:T(128)S(1)} %shift-right-arithmetic_and_fusion.flag.h_ref, bf16[4,2,1024,1024]{3,2,1,0:T(8,128)(2,1)} %get-tuple-element.234.s_ref), custom_call_target="tpu_custom_call" | custom-call | flops 85899344 | bytes 167772 | tf_op jit(solution)/shard_map/weight_grad/pallas_call | solution.py:930
  249.8 12.4 %attend_backward.2 = (bf16[256,1024]{1,0:T(8,128)(2,1)S(1)}, bf16[256,1024]{1,0:T(8,128)(2,1)S(1)}, bf16[256,1024]{1,0:T(8,128)(2,1)S(1)}, bf16[256,1024]{1,0:T(...) custom-call(s32[1]{0:T(128)} %bitcast.2.t_ref, s32[2,1024]{1,0:T(2,128)S(1)} %copy-done.25, ...), custom_call_target="tpu_custom_call" | custom-call | flops 96636768 | bytes 167772 | tf_op jit(solution)/shard_map/attend_backward/pallas_call | solution.py:468
  266.9 7.9 %head_part.1.rest_9_.part_ref = f32[4,256,1024]{2,1,0:T(8,128)} custom-call(bf16[4,1024,2048]{2,1,0:T(8,128)(2,1)} %get-tuple-element.269.rest_4_.s_ref, bf16[4,1024,2048]{2,1,0:T(8,128)(2,1)} %get-tuple-element.250.h_ref.rest_8_), custom_call_target="tpu_custom_call" | custom-call | flops 42949672 | bytes 83886 | tf_op jit(solution)/shard_map/head_part/pallas_call | solution.py:1007
  274.9 4.1 collective-permute-done.45.rest_2_
  285.8 12.5 %attend_backward.3 = (bf16[256,1024]{1,0:T(8,128)(2,1)S(1)}, bf16[256,1024]{1,0:T(8,128)(2,1)S(1)}, bf16[256,1024]{1,0:T(8,128)(2,1)S(1)}, bf16[256,1024]{1,0:T(...) custom-call(s32[1]{0:T(128)} %bitcast.2.t_ref, ...), custom_call_target="tpu_custom_call", output_to_operand_aliasing={{4}: (10, {})} | custom-call | flops 96636768 | bytes 167772 | tf_op jit(solution)/shard_map/attend_backward/pallas_call | solution.py:468
  298.4 5.2 %collective-permute-done.52.g_ref = bf16[256,1024]{1,0:T(8,128)(2,1)S(1)} collective-permute-done((bf16[256,1024]{1,0:T(8,128)(2,1)}, bf16[256,1024]{1,0:T(8,128)(2,1)S(1)}, u32[]{:S(2)}, u32[]{:S(2)}) %collective-permute-start.52) | collective-permute-done | bytes 524320 | tf_op jit(solution)/shard_map/ppermute | solution.py:1176
  304.3 2.4 norm_backward.6
  307.0 8.0 %head_grads.1 = (bf16[512,512]{1,0:T(8,128)(2,1)S(1)}, bf16[512,512]{1,0:T(8,128)(2,1)S(1)}, bf16[512,512]{1,0:T(8,128)(2,1)S(1)}, bf16[512,512]{1,0:T(8,128)(2,1)}) custom-call(s32[3]{0:T(128)S(1)} %shift-right-arithmetic_and_fusion.flag.h_ref, bf16[4,1024,2048]{2,1,0:T(8,128)(2,1)} %get-tuple-element.269.rest_4_.s_ref, ...), custom_call_target="tpu_custom_call" | custom-call | flops 42949672 | bytes 83886 | tf_op jit(solution)/shard_map/head_grads/pallas_call | solution.py:1043
  315.9 3.8 collective-permute-start.56
  319.7 2.1 collective-permute-start.57
  321.8 15.2 %collective-permute-done.55.g_ref = bf16[512,512]{1,0:T(8,128)(2,1)S(1)} collective-permute-done((bf16[512,512]{1,0:T(8,128)(2,1)S(1)}, bf16[512,512]{1,0:T(8,128)(2,1)S(1)}, u32[]{:S(2)}, u32[]{:S(2)}) %collective-permute-start.55) | collective-permute-done | bytes 524320 | tf_op jit(solution)/shard_map/ppermute | solution.py:1176
  339.3 2.4 norm_backward.7
  343.8 2.5 collective-permute-start.60
  346.3 8.1 %collective-permute-done.57.g_ref = bf16[512,512]{1,0:T(8,128)(2,1)S(1)} collective-permute-done((bf16[512,512]{1,0:T(8,128)(2,1)S(1)}, bf16[512,512]{1,0:T(8,128)(2,1)S(1)}, u32[]{:S(2)}, u32[]{:S(2)}) %collective-permute-start.57) | collective-permute-done | bytes 524320 | tf_op jit(solution)/shard_map/ppermute | solution.py:1176
  355.2 4.3 %collective-permute-done.59.g_ref = bf16[256,512]{1,0:T(8,128)(2,1)S(1)} collective-permute-done((bf16[256,512]{1,0:T(8,128)(2,1)S(1)}, bf16[256,512]{1,0:T(8,128)(2,1)S(1)}, u32[]{:S(2)}, u32[]{:S(2)}) %collective-permute-start.59) | collective-permute-done | bytes 262176 | tf_op jit(solution)/shard_map/ppermute | solution.py:1176
  365.8 5.0 %collective-permute-done.61.g_ref = bf16[256,512]{1,0:T(8,128)(2,1)S(1)} collective-permute-done((bf16[256,512]{1,0:T(8,128)(2,1)S(1)}, bf16[256,512]{1,0:T(8,128)(2,1)S(1)}, u32[]{:S(2)}, u32[]{:S(2)}) %collective-permute-start.61) | collective-permute-done | bytes 262176 | tf_op jit(solution)/shard_map/ppermute | solution.py:1176
  371.5 5.2 %collective-permute-done.63.g_ref = bf16[128,512]{1,0:T(8,128)(2,1)S(1)} collective-permute-done((bf16[128,512]{1,0:T(8,128)(2,1)S(1)}, bf16[128,512]{1,0:T(8,128)(2,1)S(1)}, u32[]{:S(2)}, u32[]{:S(2)}) %collective-permute-start.63) | collective-permute-done | bytes 131104 | tf_op jit(solution)/shard_map/ppermute | solution.py:1176
  379.5 3.2 collective-permute-start.65
  382.8 10.3 %collective-permute-done.65.g_ref = bf16[128,512]{1,0:T(8,128)(2,1)S(1)} collective-permute-done((bf16[128,512]{1,0:T(8,128)(2,1)S(1)}, bf16[128,512]{1,0:T(8,128)(2,1)S(1)}, u32[]{:S(2)}, u32[]{:S(2)}) %collective-permute-start.65) | collective-permute-done | bytes 131104 | tf_op jit(solution)/shard_map/ppermute | solution.py:1176
  393.7 1.9 collective-permute-start.66
  395.6 4.1 convert_element_type.167
  402.0 2.8 collective-permute-start.69
  404.9 2.1 collective-permute-done.69
  411.2 2.7 join_step.13
  415.2 6.8 %collective-permute-done.74.b_ref = bf16[512,512]{1,0:T(8,128)(2,1)S(1)} collective-permute-done((bf16[512,512]{1,0:T(8,128)(2,1)S(1)}, bf16[512,512]{1,0:T(8,128)(2,1)S(1)}, u32[]{:S(2)}, u32[]{:S(2)}) %collective-permute-start.74) | collective-permute-done | bytes 524320 | tf_op jit(solution)/shard_map/ppermute | solution.py:1176
  423.5 3.0 head_outputs.1
  (302 shorter events, 91.1 us)
Async XLA Ops:
  7.2 274.3 %reduce-scatter.2.cloned.1.call-start = ((), (), s32[]{:S(2)}) async-start(), calls=%async_computation.1 | async-start | bytes 2359296 | tf_op jit(solution)/shard_map/reduce_scatter | solution.py:1357
  11.5 14.9 %collective-permute-start.1 = (bf16[256,1024]{1,0:T(8,128)(2,1)S(1)}, bf16[256,1024]{1,0:T(8,128)(2,1)S(1)}, u32[]{:S(2)}, u32[]{:S(2)}) collective-permute-start(bf16[256,1024]{1,0:T(8,128)(2,1)S(1)} %get-tuple-element.167.rest_0_), channel_id=1, source_target_pairs={{0,2},{1,3},{2,0},{3,1},{4,6},{5,7},{6,4},{7,5},{8,10},{9,11},{10,... | collective-permute-start | bytes 1572872 | tf_op jit(solution)/shard_map/ppermute | solution.py:1176
  14.5 15.0 %collective-permute-start = (bf16[256,1024]{1,0:T(8,128)(2,1)S(1)}, bf16[256,1024]{1,0:T(8,128)(2,1)S(1)}, u32[]{:S(2)}, u32[]{:S(2)}) collective-permute-start(bf16[256,1024]{1,0:T(8,128)(2,1)S(1)} %get-tuple-element.167.rest_0_), channel_id=1, source_target_pairs={{0,1},{1,0},{2,3},{3,2},{4,5},{5,4},{6,7},{7,6},{8,9},{9,8},{10,11... | collective-permute-start | bytes 1572872 | tf_op jit(solution)/shard_map/ppermute | solution.py:1176
  26.4 15.2 %collective-permute-start.3 = (bf16[256,1024]{1,0:T(8,128)(2,1)S(1)}, bf16[256,1024]{1,0:T(8,128)(2,1)S(1)}, u32[]{:S(2)}, u32[]{:S(2)}) collective-permute-start(bf16[256,1024]{1,0:T(8,128)(2,1)S(1)} %get-tuple-element.170.rest_0_), channel_id=1, source_target_pairs={{0,2},{1,3},{2,0},{3,1},{4,6},{5,7},{6,4},{7,5},{8,10},{9,11},{10,... | collective-permute-start | bytes 1572872 | tf_op jit(solution)/shard_map/ppermute | solution.py:1176
  41.9 13.6 %collective-permute-start.8 = (bf16[256,1024]{1,0:T(8,128)(2,1)S(1)}, bf16[256,1024]{1,0:T(8,128)(2,1)S(1)}, u32[]{:S(2)}, u32[]{:S(2)}) collective-permute-start(bf16[256,1024]{1,0:T(8,128)(2,1)S(1)} %get-tuple-element.182), channel_id=1, source_target_pairs={{0,1},{1,0},{2,3},{3,2},{4,5},{5,4},{6,7},{7,6},{8,9},{9,8},{10,11... | collective-permute-start | bytes 1572872 | tf_op jit(solution)/shard_map/ppermute | solution.py:1176
  43.4 14.2 %collective-permute-start.9 = (bf16[256,1024]{1,0:T(8,128)(2,1)S(1)}, bf16[256,1024]{1,0:T(8,128)(2,1)S(1)}, u32[]{:S(2)}, u32[]{:S(2)}) collective-permute-start(bf16[256,1024]{1,0:T(8,128)(2,1)S(1)} %add_convert_fusion.7), channel_id=1, source_target_pairs={{0,2},{1,3},{2,0},{3,1},{4,6},{5,7},{6,4},{7,5},{8,10},{9,11},{10,... | collective-permute-start | bytes 1572872 | tf_op jit(solution)/shard_map/ppermute | solution.py:1176
  58.6 13.3 %collective-permute-start.13 = (bf16[256,1024]{1,0:T(8,128)(2,1)S(1)}, bf16[256,1024]{1,0:T(8,128)(2,1)S(1)}, u32[]{:S(2)}, u32[]{:S(2)}) collective-permute-start(bf16[256,1024]{1,0:T(8,128)(2,1)S(1)} %get-tuple-element.185.rest_0_), channel_id=1, source_target_pairs={{0,2},{1,3},{2,0},{3,1},{4,6},{5,7},{6,4},{7,5},{8,10},{9,11},{10,... | collective-permute-start | bytes 1572872 | tf_op jit(solution)/shard_map/ppermute | solution.py:1176
  59.3 25.4 %collective-permute-start.7 = (bf16[256,1024]{1,0:T(8,128)(2,1)S(1)}, bf16[256,1024]{1,0:T(8,128)(2,1)S(1)}, u32[]{:S(2)}, u32[]{:S(2)}) collective-permute-start(bf16[256,1024]{1,0:T(8,128)(2,1)S(1)} %get-tuple-element.178), channel_id=1, source_target_pairs={{0,1},{1,0},{2,3},{3,2},{4,5},{5,4},{6,7},{7,6},{8,9},{9,8},{10,11... | collective-permute-start | bytes 1572872 | tf_op jit(solution)/shard_map/ppermute | solution.py:1176
  59.8 13.1 %collective-permute-start.12 = (bf16[256,1024]{1,0:T(8,128)(2,1)S(1)}, bf16[256,1024]{1,0:T(8,128)(2,1)S(1)}, u32[]{:S(2)}, u32[]{:S(2)}) collective-permute-start(bf16[256,1024]{1,0:T(8,128)(2,1)S(1)} %get-tuple-element.185.rest_0_), channel_id=1, source_target_pairs={{0,1},{1,0},{2,3},{3,2},{4,5},{5,4},{6,7},{7,6},{8,9},{9,8},{10,11... | collective-permute-start | bytes 1572872 | tf_op jit(solution)/shard_map/ppermute | solution.py:1176
  72.2 14.4 %collective-permute-start.11 = (bf16[256,1024]{1,0:T(8,128)(2,1)S(1)}, bf16[256,1024]{1,0:T(8,128)(2,1)S(1)}, u32[]{:S(2)}, u32[]{:S(2)}) collective-permute-start(bf16[256,1024]{1,0:T(8,128)(2,1)S(1)} %add_convert_fusion.6), channel_id=1, source_target_pairs={{0,2},{1,3},{2,0},{3,1},{4,6},{5,7},{6,4},{7,5},{8,10},{9,11},{10,... | collective-permute-start | bytes 1572872 | tf_op jit(solution)/shard_map/ppermute | solution.py:1176
  87.6 13.6 %collective-permute-start.17 = (bf16[256,1024]{1,0:T(8,128)(2,1)S(1)}, bf16[256,1024]{1,0:T(8,128)(2,1)S(1)}, u32[]{:S(2)}, u32[]{:S(2)}) collective-permute-start(bf16[256,1024]{1,0:T(8,128)(2,1)S(1)} %get-tuple-element.192.rest_0_), channel_id=1, source_target_pairs={{0,2},{1,3},{2,0},{3,1},{4,6},{5,7},{6,4},{7,5},{8,10},{9,11},{10,... | collective-permute-start | bytes 1572872 | tf_op jit(solution)/shard_map/ppermute | solution.py:1176
  88.3 13.4 %collective-permute-start.15 = (bf16[256,1024]{1,0:T(8,128)(2,1)}, bf16[256,1024]{1,0:T(8,128)(2,1)S(1)}, u32[]{:S(2)}, u32[]{:S(2)}) collective-permute-start(bf16[256,1024]{1,0:T(8,128)(2,1)} %get-tuple-element.188), channel_id=1, source_target_pairs={{0,1},{1,0},{2,3},{3,2},{4,5},{5,4},{6,7},{7,6},{8,9},{9,8},{10,11... | collective-permute-start | bytes 1572872 | tf_op jit(solution)/shard_map/ppermute | solution.py:1176
  88.3 14.3 %collective-permute-start.16 = (bf16[256,1024]{1,0:T(8,128)(2,1)S(1)}, bf16[256,1024]{1,0:T(8,128)(2,1)S(1)}, u32[]{:S(2)}, u32[]{:S(2)}) collective-permute-start(bf16[256,1024]{1,0:T(8,128)(2,1)S(1)} %get-tuple-element.192.rest_0_), channel_id=1, source_target_pairs={{0,1},{1,0},{2,3},{3,2},{4,5},{5,4},{6,7},{7,6},{8,9},{9,8},{10,11... | collective-permute-start | bytes 1572872 | tf_op jit(solution)/shard_map/ppermute | solution.py:1176
  101.3 13.5 %collective-permute-start.20 = (bf16[256,1024]{1,0:T(8,128)(2,1)S(1)}, bf16[256,1024]{1,0:T(8,128)(2,1)S(1)}, u32[]{:S(2)}, u32[]{:S(2)}) collective-permute-start(bf16[256,1024]{1,0:T(8,128)(2,1)S(1)} %get-tuple-element.201), channel_id=1, source_target_pairs={{0,1},{1,0},{2,3},{3,2},{4,5},{5,4},{6,7},{7,6},{8,9},{9,8},{10,11... | collective-permute-start | bytes 1572872 | tf_op jit(solution)/shard_map/ppermute | solution.py:1176
  102.0 13.9 %collective-permute-start.21 = (bf16[256,1024]{1,0:T(8,128)(2,1)S(1)}, bf16[256,1024]{1,0:T(8,128)(2,1)S(1)}, u32[]{:S(2)}, u32[]{:S(2)}) collective-permute-start(bf16[256,1024]{1,0:T(8,128)(2,1)S(1)} %add_convert_fusion.5), channel_id=1, source_target_pairs={{0,2},{1,3},{2,0},{3,1},{4,6},{5,7},{6,4},{7,5},{8,10},{9,11},{10,... | collective-permute-start | bytes 1572872 | tf_op jit(solution)/shard_map/ppermute | solution.py:1176
  117.4 14.9 %collective-permute-start.23 = (bf16[256,1024]{1,0:T(8,128)(2,1)S(1)}, bf16[256,1024]{1,0:T(8,128)(2,1)S(1)}, u32[]{:S(2)}, u32[]{:S(2)}) collective-permute-start(bf16[256,1024]{1,0:T(8,128)(2,1)S(1)} %add_convert_fusion.4), channel_id=1, source_target_pairs={{0,2},{1,3},{2,0},{3,1},{4,6},{5,7},{6,4},{7,5},{8,10},{9,11},{10,... | collective-permute-start | bytes 1572872 | tf_op jit(solution)/shard_map/ppermute | solution.py:1176
  118.1 26.3 %collective-permute-start.25 = (bf16[272,1024]{1,0:T(8,128)(2,1)S(1)}, bf16[272,1024]{1,0:T(8,128)(2,1)}, u32[]{:S(2)}, u32[]{:S(2)}) collective-permute-start(bf16[272,1024]{1,0:T(8,128)(2,1)S(1)} %get-tuple-element.204.rest_0_), channel_id=1, source_target_pairs={{0,2},{1,3},{2,0},{3,1},{4,6},{5,7},{6,4},{7,5},{8,10},{9,11},{10,... | collective-permute-start | bytes 1671176 | tf_op jit(solution)/shard_map/ppermute | solution.py:1176
  133.6 21.0 %collective-permute-start.28 = (bf16[272,1024]{1,0:T(8,128)(2,1)S(1)}, bf16[272,1024]{1,0:T(8,128)(2,1)}, u32[]{:S(2)}, u32[]{:S(2)}) collective-permute-start(bf16[272,1024]{1,0:T(8,128)(2,1)S(1)} %get-tuple-element.209.rest_4_), channel_id=1, source_target_pairs={{0,2},{1,3},{2,0},{3,1},{4,6},{5,7},{6,4},{7,5},{8,10},{9,11},{10,... | collective-permute-start | bytes 1671176 | tf_op jit(solution)/shard_map/ppermute | solution.py:1176
  134.2 22.5 %collective-permute-start.24 = (bf16[272,1024]{1,0:T(8,128)(2,1)S(1)}, bf16[272,1024]{1,0:T(8,128)(2,1)S(1)}, u32[]{:S(2)}, u32[]{:S(2)}) collective-permute-start(bf16[272,1024]{1,0:T(8,128)(2,1)S(1)} %get-tuple-element.204.rest_0_), channel_id=1, source_target_pairs={{0,1},{1,0},{2,3},{3,2},{4,5},{5,4},{6,7},{7,6},{8,9},{9,8},{10,11... | collective-permute-start | bytes 1671176 | tf_op jit(solution)/shard_map/ppermute | solution.py:1176
  144.3 13.4 %collective-permute-start.26 = (bf16[272,1024]{1,0:T(8,128)(2,1)}, bf16[272,1024]{1,0:T(8,128)(2,1)}, u32[]{:S(2)}, u32[]{:S(2)}) collective-permute-start(bf16[272,1024]{1,0:T(8,128)(2,1)} %collective-permute-done.25.rest_2_), channel_id=1, source_target_pairs={{0,1},{1,0},{2,3},{3,2},{4,5},{5,4},{6,7},{7,6},{8,9},{9,8},{10,11... | collective-permute-start | bytes 1671176 | tf_op jit(solution)/shard_map/ppermute | solution.py:1176
  144.3 13.4 %collective-permute-start.27 = (bf16[272,1024]{1,0:T(8,128)(2,1)S(1)}, bf16[272,1024]{1,0:T(8,128)(2,1)}, u32[]{:S(2)}, u32[]{:S(2)}) collective-permute-start(bf16[272,1024]{1,0:T(8,128)(2,1)S(1)} %get-tuple-element.209.rest_4_), channel_id=1, source_target_pairs={{0,1},{1,0},{2,3},{3,2},{4,5},{5,4},{6,7},{7,6},{8,9},{9,8},{10,11... | collective-permute-start | bytes 1671176 | tf_op jit(solution)/shard_map/ppermute | solution.py:1176
  155.6 15.0 %collective-permute-start.31 = (bf16[256,1024]{1,0:T(8,128)(2,1)}, bf16[256,1024]{1,0:T(8,128)(2,1)}, u32[]{:S(2)}, u32[]{:S(2)}) collective-permute-start(bf16[256,1024]{1,0:T(8,128)(2,1)} %get-tuple-element.214), channel_id=1, source_target_pairs={{0,2},{1,3},{2,0},{3,1},{4,6},{5,7},{6,4},{7,5},{8,10},{9,11},{10,... | collective-permute-start | bytes 1572872 | tf_op jit(solution)/shard_map/ppermute | solution.py:1176
  156.7 24.7 %collective-permute-start.32 = (bf16[256,1024]{1,0:T(8,128)(2,1)}, bf16[256,1024]{1,0:T(8,128)(2,1)S(1)}, u32[]{:S(2)}, u32[]{:S(2)}) collective-permute-start(bf16[256,1024]{1,0:T(8,128)(2,1)} %get-tuple-element.217), channel_id=1, source_target_pairs={{0,2},{1,3},{2,0},{3,1},{4,6},{5,7},{6,4},{7,5},{8,10},{9,11},{10,... | collective-permute-start | bytes 1572872 | tf_op jit(solution)/shard_map/ppermute | solution.py:1176
  204.2 191.4 %all-gather.2.cloned.1.call-start = ((), (), s32[]{:S(2)}) async-start(), calls=%async_computation.2 | async-start | bytes 2359296 | tf_op jit(solution)/shard_map/all_gather | solution.py:1370
  216.3 14.0 %collective-permute-start.37 = (bf16[256,1024]{1,0:T(8,128)(2,1)S(1)}, bf16[256,1024]{1,0:T(8,128)(2,1)S(1)}, u32[]{:S(2)}, u32[]{:S(2)}) collective-permute-start(bf16[256,1024]{1,0:T(8,128)(2,1)S(1)} %add_convert_fusion.3.rest_0_), channel_id=1, source_target_pairs={{0,2},{1,3},{2,0},{3,1},{4,6},{5,7},{6,4},{7,5},{8,10},{9,11},{10,... | collective-permute-start | bytes 1572872 | tf_op jit(solution)/shard_map/ppermute | solution.py:1176
  232.9 13.2 %collective-permute-start.40 = (bf16[256,1024]{1,0:T(8,128)(2,1)S(1)}, bf16[256,1024]{1,0:T(8,128)(2,1)}, u32[]{:S(2)}, u32[]{:S(2)}) collective-permute-start(bf16[256,1024]{1,0:T(8,128)(2,1)S(1)} %get-tuple-element.232.rest_0_), channel_id=1, source_target_pairs={{0,2},{1,3},{2,0},{3,1},{4,6},{5,7},{6,4},{7,5},{8,10},{9,11},{10,... | collective-permute-start | bytes 1572872 | tf_op jit(solution)/shard_map/ppermute | solution.py:1176
  234.0 13.8 %collective-permute-start.39 = (bf16[256,1024]{1,0:T(8,128)(2,1)S(1)}, bf16[256,1024]{1,0:T(8,128)(2,1)S(1)}, u32[]{:S(2)}, u32[]{:S(2)}) collective-permute-start(bf16[256,1024]{1,0:T(8,128)(2,1)S(1)} %get-tuple-element.232.rest_0_), channel_id=1, source_target_pairs={{0,1},{1,0},{2,3},{3,2},{4,5},{5,4},{6,7},{7,6},{8,9},{9,8},{10,11... | collective-permute-start | bytes 1572872 | tf_op jit(solution)/shard_map/ppermute | solution.py:1176
  246.1 17.0 %collective-permute-start.42 = (bf16[256,1024]{1,0:T(8,128)(2,1)S(1)}, bf16[256,1024]{1,0:T(8,128)(2,1)S(1)}, u32[]{:S(2)}, u32[]{:S(2)}) collective-permute-start(bf16[256,1024]{1,0:T(8,128)(2,1)S(1)} %get-tuple-element.243), channel_id=1, source_target_pairs={{0,1},{1,0},{2,3},{3,2},{4,5},{5,4},{6,7},{7,6},{8,9},{9,8},{10,11... | collective-permute-start | bytes 1572872 | tf_op jit(solution)/shard_map/ppermute | solution.py:1176
  246.6 16.5 %collective-permute-start.43 = (bf16[256,1024]{1,0:T(8,128)(2,1)S(1)}, bf16[256,1024]{1,0:T(8,128)(2,1)S(1)}, u32[]{:S(2)}, u32[]{:S(2)}) collective-permute-start(bf16[256,1024]{1,0:T(8,128)(2,1)S(1)} %add_convert_fusion.2), channel_id=1, source_target_pairs={{0,2},{1,3},{2,0},{3,1},{4,6},{5,7},{6,4},{7,5},{8,10},{9,11},{10,... | collective-permute-start | bytes 1572872 | tf_op jit(solution)/shard_map/ppermute | solution.py:1176
  247.7 32.1 %collective-permute-start.46 = (bf16[512,1024]{1,0:T(8,128)(2,1)S(1)}, bf16[512,1024]{1,0:T(8,128)(2,1)S(1)}, u32[]{:S(2)}, u32[]{:S(2)}) collective-permute-start(bf16[512,1024]{1,0:T(8,128)(2,1)S(1)} %get-tuple-element.237), channel_id=1, source_target_pairs={{0,4},{4,0},{8,12},{12,8},{16,20},{20,16},{24,28},{28,24},{1,5},{5... | collective-permute-start | bytes 3145736 | tf_op jit(solution)/shard_map/ppermute | solution.py:1176
  264.7 14.3 %collective-permute-start.45 = (bf16[256,1024]{1,0:T(8,128)(2,1)S(1)}, bf16[256,1024]{1,0:T(8,128)(2,1)S(1)}, u32[]{:S(2)}, u32[]{:S(2)}) collective-permute-start(bf16[256,1024]{1,0:T(8,128)(2,1)S(1)} %get-tuple-element.247.rest_0_), channel_id=1, source_target_pairs={{0,2},{1,3},{2,0},{3,1},{4,6},{5,7},{6,4},{7,5},{8,10},{9,11},{10,... | collective-permute-start | bytes 1572872 | tf_op jit(solution)/shard_map/ppermute | solution.py:1176
  282.0 22.2 %collective-permute-start.50 = (bf16[256,1024]{1,0:T(8,128)(2,1)}, bf16[256,1024]{1,0:T(8,128)(2,1)S(1)}, u32[]{:S(2)}, u32[]{:S(2)}) collective-permute-start(bf16[256,1024]{1,0:T(8,128)(2,1)} %copy-done.27), channel_id=1, source_target_pairs={{0,1},{1,0},{2,3},{3,2},{4,5},{5,4},{6,7},{7,6},{8,9},{9,8},{10,11... | collective-permute-start | bytes 1572872 | tf_op jit(solution)/shard_map/ppermute | solution.py:1176
  282.1 22.2 %collective-permute-start.51 = (bf16[256,1024]{1,0:T(8,128)(2,1)}, bf16[256,1024]{1,0:T(8,128)(2,1)S(1)}, u32[]{:S(2)}, u32[]{:S(2)}) collective-permute-start(bf16[256,1024]{1,0:T(8,128)(2,1)} %add_convert_fusion.1), channel_id=1, source_target_pairs={{0,2},{1,3},{2,0},{3,1},{4,6},{5,7},{6,4},{7,5},{8,10},{9,11},{10,... | collective-permute-start | bytes 1572872 | tf_op jit(solution)/shard_map/ppermute | solution.py:1176
  283.2 20.4 %collective-permute-start.52 = (bf16[256,1024]{1,0:T(8,128)(2,1)}, bf16[256,1024]{1,0:T(8,128)(2,1)S(1)}, u32[]{:S(2)}, u32[]{:S(2)}) collective-permute-start(bf16[256,1024]{1,0:T(8,128)(2,1)} %copy-done.28), channel_id=1, source_target_pairs={{0,8},{4,12},{8,0},{12,4},{16,24},{20,28},{24,16},{28,20},{1,9},{5... | collective-permute-start | bytes 1572872 | tf_op jit(solution)/shard_map/ppermute | solution.py:1176
  315.0 22.0 %collective-permute-start.55 = (bf16[512,512]{1,0:T(8,128)(2,1)S(1)}, bf16[512,512]{1,0:T(8,128)(2,1)S(1)}, u32[]{:S(2)}, u32[]{:S(2)}) collective-permute-start(bf16[512,512]{1,0:T(8,128)(2,1)S(1)} %get-tuple-element.271), channel_id=1, source_target_pairs={{0,4},{4,0},{8,12},{12,8},{16,20},{20,16},{24,28},{28,24},{1,5},{5... | collective-permute-start | bytes 1572872 | tf_op jit(solution)/shard_map/ppermute | solution.py:1176
  315.2 24.1 %collective-permute-start.49 = (bf16[256,1024]{1,0:T(8,128)(2,1)S(1)}, bf16[256,1024]{1,0:T(8,128)(2,1)S(1)}, u32[]{:S(2)}, u32[]{:S(2)}) collective-permute-start(bf16[256,1024]{1,0:T(8,128)(2,1)S(1)} %get-tuple-element.257), channel_id=1, source_target_pairs={{0,1},{1,0},{2,3},{3,2},{4,5},{5,4},{6,7},{7,6},{8,9},{9,8},{10,11... | collective-permute-start | bytes 1572872 | tf_op jit(solution)/shard_map/ppermute | solution.py:1176
  315.2 24.1 %collective-permute-start.54 = (bf16[256,1024]{1,0:T(8,128)(2,1)S(1)}, bf16[256,1024]{1,0:T(8,128)(2,1)S(1)}, u32[]{:S(2)}, u32[]{:S(2)}) collective-permute-start(bf16[256,1024]{1,0:T(8,128)(2,1)S(1)} %add_convert_fusion), channel_id=1, source_target_pairs={{0,2},{1,3},{2,0},{3,1},{4,6},{5,7},{6,4},{7,5},{8,10},{9,11},{10,... | collective-permute-start | bytes 1572872 | tf_op jit(solution)/shard_map/ppermute | solution.py:1176
  315.9 27.4 %collective-permute-start.56 = (bf16[128,1024]{1,0:T(8,128)(2,1)S(1)}, bf16[128,1024]{1,0:T(8,128)(2,1)S(1)}, u32[]{:S(2)}, u32[]{:S(2)}) collective-permute-start(bf16[128,1024]{1,0:T(8,128)(2,1)S(1)} %get-tuple-element.264), channel_id=1, source_target_pairs={{0,16},{4,20},{8,24},{12,28},{16,0},{20,4},{24,8},{28,12},{1,17},{... | collective-permute-start | bytes 786440 | tf_op jit(solution)/shard_map/ppermute | solution.py:1176
  319.7 34.8 %collective-permute-start.57 = (bf16[512,512]{1,0:T(8,128)(2,1)S(1)}, bf16[512,512]{1,0:T(8,128)(2,1)S(1)}, u32[]{:S(2)}, u32[]{:S(2)}) collective-permute-start(bf16[512,512]{1,0:T(8,128)(2,1)S(1)} %get-tuple-element.272), channel_id=1, source_target_pairs={{0,8},{4,12},{8,0},{12,4},{16,24},{20,28},{24,16},{28,20},{1,9},{5... | collective-permute-start | bytes 1572872 | tf_op jit(solution)/shard_map/ppermute | solution.py:1176
  337.7 21.9 %collective-permute-start.59 = (bf16[256,512]{1,0:T(8,128)(2,1)S(1)}, bf16[256,512]{1,0:T(8,128)(2,1)S(1)}, u32[]{:S(2)}, u32[]{:S(2)}) collective-permute-start(bf16[256,512]{1,0:T(8,128)(2,1)S(1)} %get-tuple-element.287), channel_id=1, source_target_pairs={{0,8},{4,12},{8,0},{12,4},{16,24},{20,28},{24,16},{28,20},{1,9},{5... | collective-permute-start | bytes 786440 | tf_op jit(solution)/shard_map/ppermute | solution.py:1176
  341.7 13.5 %collective-permute-start.58 = (f32[8,1024]{1,0:T(8,128)S(1)}, f32[8,1024]{1,0:T(8,128)S(1)}, u32[]{:S(2)}, u32[]{:S(2)}) collective-permute-start(f32[8,1024]{1,0:T(8,128)S(1)} %select_maximum_fusion), channel_id=1, source_target_pairs={{0,2},{1,3},{2,0},{3,1},{4,6},{5,7},{6,4},{7,5},{8,10},{9,11},{10,... | collective-permute-start | bytes 98312 | tf_op jit(solution)/shard_map/ppermute | solution.py:1176
  343.8 16.4 %collective-permute-start.60 = (bf16[128,1024]{1,0:T(8,128)(2,1)S(1)}, bf16[128,1024]{1,0:T(8,128)(2,1)S(1)}, u32[]{:S(2)}, u32[]{:S(2)}) collective-permute-start(bf16[128,1024]{1,0:T(8,128)(2,1)S(1)} %halve_step.12.own_ref), channel_id=1, source_target_pairs={{0,16},{4,20},{8,24},{12,28},{16,0},{20,4},{24,8},{28,12},{1,17},{... | collective-permute-start | bytes 786440 | tf_op jit(solution)/shard_map/ppermute | solution.py:1176
  360.8 16.6 %collective-permute-start.64 = (bf16[256,1024]{1,0:T(8,128)(2,1)S(1)}, bf16[256,1024]{1,0:T(8,128)(2,1)S(1)}, u32[]{:S(2)}, u32[]{:S(2)}) collective-permute-start(bf16[256,1024]{1,0:T(8,128)(2,1)S(1)} %bitcast.36), channel_id=1, source_target_pairs={{0,8},{4,12},{8,0},{12,4},{16,24},{20,28},{24,16},{28,20},{1,9},{5... | collective-permute-start | bytes 1572872 | tf_op jit(solution)/shard_map/ppermute | solution.py:1176
  378.0 33.2 %collective-permute-start.73 = (bf16[512,1024]{1,0:T(8,128)(2,1)S(1)}, bf16[512,1024]{1,0:T(8,128)(2,1)S(1)}, u32[]{:S(2)}, u32[]{:S(2)}) collective-permute-start(bf16[512,1024]{1,0:T(8,128)(2,1)S(1)} %bitcast.32), channel_id=1, source_target_pairs={{0,4},{4,0},{8,12},{12,8},{16,20},{20,16},{24,28},{28,24},{1,5},{5... | collective-permute-start | bytes 3145736 | tf_op jit(solution)/shard_map/ppermute | solution.py:1176
  379.5 13.5 %collective-permute-start.65 = (bf16[128,512]{1,0:T(8,128)(2,1)S(1)}, bf16[128,512]{1,0:T(8,128)(2,1)S(1)}, u32[]{:S(2)}, u32[]{:S(2)}) collective-permute-start(bf16[128,512]{1,0:T(8,128)(2,1)S(1)} %get-tuple-element.298), channel_id=1, source_target_pairs={{0,16},{4,20},{8,24},{12,28},{16,0},{20,4},{24,8},{28,12},{1,17},{... | collective-permute-start | bytes 393224 | tf_op jit(solution)/shard_map/ppermute | solution.py:1176
  382.7 16.9 %collective-permute-start.67 = (bf16[128,512]{1,0:T(8,128)(2,1)S(1)}, bf16[128,512]{1,0:T(8,128)(2,1)S(1)}, u32[]{:S(2)}, u32[]{:S(2)}) collective-permute-start(bf16[128,512]{1,0:T(8,128)(2,1)S(1)} %halve_step.16.own_ref), channel_id=1, source_target_pairs={{0,16},{4,20},{8,24},{12,28},{16,0},{20,4},{24,8},{28,12},{1,17},{... | collective-permute-start | bytes 393224 | tf_op jit(solution)/shard_map/ppermute | solution.py:1176
  407.6 14.4 %collective-permute-start.74 = (bf16[512,512]{1,0:T(8,128)(2,1)S(1)}, bf16[512,512]{1,0:T(8,128)(2,1)S(1)}, u32[]{:S(2)}, u32[]{:S(2)}) collective-permute-start(bf16[512,512]{1,0:T(8,128)(2,1)S(1)} %bitcast.34), channel_id=1, source_target_pairs={{0,4},{4,0},{8,12},{12,8},{16,20},{20,16},{24,28},{28,24},{1,5},{5... | collective-permute-start | bytes 1572872 | tf_op jit(solution)/shard_map/ppermute | solution.py:1176
  409.3 14.2 %collective-permute-start.75 = (bf16[512,512]{1,0:T(8,128)(2,1)S(1)}, bf16[512,512]{1,0:T(8,128)(2,1)S(1)}, u32[]{:S(2)}, u32[]{:S(2)}) collective-permute-start(bf16[512,512]{1,0:T(8,128)(2,1)S(1)} %bitcast.38), channel_id=1, source_target_pairs={{0,8},{4,12},{8,0},{12,4},{16,24},{20,28},{24,16},{28,20},{1,9},{5... | collective-permute-start | bytes 1572872 | tf_op jit(solution)/shard_map/ppermute | solution.py:1176
  (85 other events, 904.3 us)
Sparse Core Ops, SparseCore 0:
  204.3 70.3 reduce-scatter.1
  281.6 66.5 all-gather.1

commit v6 on v5

--- a/solution.py
+++ b/solution.py
@@ -1299,7 +1299,7 @@
 
     hidden[0], normed_a = first_norm(0, tokens, tables, gain_one, shift_one)
     rows_a = Gather(normed_a)
-    hidden[1], normed_b = first_norm(1, tie(tokens, normed_a), tables, gain_one, shift_one)
+    hidden[1], normed_b = first_norm(1, tie(tokens, normed_a, head_shift), tables, gain_one, shift_one)
     rows_b = Gather(normed_b)
     at_a = attend(0, rows_a.blocks(normed_b))
     block = at_a.cross(rows_b.cross)
@@ -1312,8 +1312,9 @@
     ff_b = feed(1, rows_b.blocks(), block)
     unit, units_a = last_rows(0, ff_a, ff_b.mark)
     block = ff_b.cross(unit)
-    unit, units_b = last_rows(1, ff_b, block)
-    cots = [tensor_swap(tie(cotangent[s], unit), CROSS) for s in range(2)]
+    cot_rows = [cotangent[s] for s in range(2)]
+    unit, units_b = last_rows(1, ff_b, block, *cot_rows)
+    cots = [tensor_swap(tie(cot_rows[s], unit), CROSS) for s in range(2)]
 
     units = units_a.blocks() + units_b.blocks()
     exps, col_sums, row_sums, loss = contrast_scores(place, ends, doc_ids, targets, units)

time: 442 us -> 442 us (level)
  waiting for transfers between devices: 163 us -> 149 us
  starting transfers between devices: 57.9 us -> 70.4 us
    ppermute x76, waiting for transfers between devices: 163 us -> 149 us  [swap(): return lax.ppermute(value, axis, [(i, i ^ bit) for i in range(size)])]
    ppermute x76, starting transfers between devices: 57.4 us -> 69.9 us  [swap(): return lax.ppermute(value, axis, [(i, i ^ bit) for i in range(size)])]
  transfers between devices with their start and end apart: 78 -> 78, of which waited for: 33 -> 33; matrix products, arithmetic and copies ran while one was open for 3% -> 3% of each run, Pallas kernels for 34% -> 35%
where the time goes in v6:
time: 442 us; the launch traced here: 433 us
  Pallas kernels  173 us (39%)
  waiting for transfers between devices  149 us (34%)
  starting transfers between devices  70.4 us (16%)
  local copies, waits for them, and re-layouts  16.2 us (4%)
  between operations  15.5 us (4%)
  other arithmetic  9.54 us (2%)
    ppermute x76, waiting for transfers between devices, swap(): return lax.ppermute(value, axis, [(i, i ^ bit) for i in range(size)])  149 us
    ppermute x76, starting transfers between devices, swap(): return lax.ppermute(value, axis, [(i, i ^ bit) for i in range(size)])  69.9 us
    pallas_call x2, Pallas kernels, attend_backward(): kernel_call(body, (*[struct((rows, feats), BF16)] * 4, struct((2 * seqs,...  24.9 us
    pallas_call x2, Pallas kernels, feed_forward(): kernel_call(body, (*[struct((rows, feats), BF16)] * 4, struct((4, seqs, l...  20.3 us
    pallas_call x2, Pallas kernels, attend_forward(): kernel_call(body, (*[struct((rows, feats), BF16)] * 4, struct((2 * seqs,...  20 us
    pallas_call x2, Pallas kernels, feed_backward(): kernel_call(body, (*[struct((rows, feats), BF16)] * 4, struct((4, seqs, l...  18.8 us
    pallas_call x2, Pallas kernels, contrast_grads(): kernel_call(body, (struct((rows, feats), F32), struct((2, rows, feats), B...  15.6 us
    unnamed x111, local copies, waits for them, and re-layouts  12.5 us
  transfers between devices with their start and end apart: 78, of which 33 were waited for; matrix products, arithmetic and copies ran while one was open for 3% of the time, Pallas kernels for 35%

profile of v6, /device:TPU:0, one launch (start us, length us, event | category | flops | bytes accessed | tf_op | source)
XLA Modules:
  0.0 433.2 jit_solution(5375236576366921570)
XLA Ops:
  11.5 3.0 collective-permute-start.1
  16.9 9.5 %collective-permute-done.1.rest_2_ = bf16[256,1024]{1,0:T(8,128)(2,1)S(1)} collective-permute-done((bf16[256,1024]{1,0:T(8,128)(2,1)S(1)}, bf16[256,1024]{1,0:T(8,128)(2,1)S(1)}, u32[]{:S(2)}, u32[]{:S(2)}) %collective-permute-start.1) | collective-permute-done | bytes 524320 | tf_op jit(solution)/shard_map/ppermute | solution.py:1176
  29.8 9.8 %attend_forward.2 = (bf16[256,1024]{1,0:T(8,128)(2,1)S(1)}, bf16[256,1024]{1,0:T(8,128)(2,1)S(1)}, bf16[256,1024]{1,0:T(8,128)(2,1)S(1)}, bf16[256,1024]{1,0:T(8...) custom-call(s32[1]{0:T(128)} %bitcast.2.t_ref, s32[2,1024]{1,0:T(2,128)S(1)} %copy-done.24, ...), custom_call_target="tpu_custom_call" | custom-call | flops 69793216 | bytes 167772 | tf_op jit(solution)/shard_map/attend_forward/pallas_call | solution.py:343
  42.1 2.0 collective-permute-start.9
  45.1 10.2 %attend_forward.3 = (bf16[256,1024]{1,0:T(8,128)(2,1)S(1)}, bf16[256,1024]{1,0:T(8,128)(2,1)S(1)}, bf16[256,1024]{1,0:T(8,128)(2,1)S(1)}, bf16[256,1024]{1,0:T(8...) custom-call(s32[1]{0:T(128)} %bitcast.2.t_ref, ...), custom_call_target="tpu_custom_call", output_to_operand_aliasing={{4}: (9, {})} | custom-call | flops 69793216 | bytes 167772 | tf_op jit(solution)/shard_map/attend_forward/pallas_call | solution.py:343
  59.8 11.3 %collective-permute-done.13.rest_2_ = bf16[256,1024]{1,0:T(8,128)(2,1)S(1)} collective-permute-done((bf16[256,1024]{1,0:T(8,128)(2,1)S(1)}, bf16[256,1024]{1,0:T(8,128)(2,1)S(1)}, u32[]{:S(2)}, u32[]{:S(2)}) %collective-permute-start.13) | collective-permute-done | bytes 524320 | tf_op jit(solution)/shard_map/ppermute | solution.py:1176
  74.5 10.0 %feed_forward.2 = (bf16[256,1024]{1,0:T(8,128)(2,1)S(1)}, bf16[256,1024]{1,0:T(8,128)(2,1)S(1)}, bf16[256,1024]{1,0:T(8,128)(2,1)S(1)}, bf16[256,1024]{1,0:T(8,128)(2,1)}, bf16[4,2,1024,1024]{3,2,1,0:T(8,128)(2,1)}) custom-call(f32[1,1024]{1,0:T(1,128)S(1)} %bitcast.58, bf16[256,1024]{1,0:T(8,128)(2,1)} %copy-done.22, bf16[256,1024]{1,0:T(8,128)(2,1)} %copy-done.47, ...), custom_call_target="tpu_custom_call" | custom-call | flops 85899344 | bytes 293601 | tf_op jit(solution)/shard_map/feed_forward/pallas_call | solution.py:551
  88.9 11.5 %collective-permute-done.17.rest_2_ = bf16[256,1024]{1,0:T(8,128)(2,1)S(1)} collective-permute-done((bf16[256,1024]{1,0:T(8,128)(2,1)S(1)}, bf16[256,1024]{1,0:T(8,128)(2,1)S(1)}, u32[]{:S(2)}, u32[]{:S(2)}) %collective-permute-start.17) | collective-permute-done | bytes 524320 | tf_op jit(solution)/shard_map/ppermute | solution.py:1176
  103.7 10.2 %feed_forward.3 = (bf16[256,1024]{1,0:T(8,128)(2,1)S(1)}, bf16[256,1024]{1,0:T(8,128)(2,1)S(1)}, bf16[256,1024]{1,0:T(8,128)(2,1)S(1)}, bf16[256,1024]{1,0:T(8,128)(2,1)}, bf16[4,2,1024,1024]{3,2,1,0:T(8,128)(2,1)}) custom-call(f32[1,1024]{1,0:T(1,128)S(1)} %bitcast.59, bf16[256,1024]{1,0:T(8,128)(2,1)} %copy-done.18, ...), custom_call_target="tpu_custom_call", output_to_operand_aliasing={{4}: (7, {})} | custom-call | flops 85899344 | bytes 293601 | tf_op jit(solution)/shard_map/feed_forward/pallas_call | solution.py:551
  119.6 11.7 %collective-permute-done.23.x_ref = bf16[256,1024]{1,0:T(8,128)(2,1)S(1)} collective-permute-done((bf16[256,1024]{1,0:T(8,128)(2,1)S(1)}, bf16[256,1024]{1,0:T(8,128)(2,1)S(1)}, u32[]{:S(2)}, u32[]{:S(2)}) %collective-permute-start.23) | collective-permute-done | bytes 524320 | tf_op jit(solution)/shard_map/ppermute | solution.py:1176
  134.2 9.2 %collective-permute-done.25.rest_2_ = bf16[272,1024]{1,0:T(8,128)(2,1)} collective-permute-done((bf16[272,1024]{1,0:T(8,128)(2,1)S(1)}, bf16[272,1024]{1,0:T(8,128)(2,1)}, u32[]{:S(2)}, u32[]{:S(2)}) %collective-permute-start.25) | collective-permute-done | bytes 557088 | tf_op jit(solution)/shard_map/ppermute | solution.py:1176
  143.9 10.4 %collective-permute-done.28.rest_6_ = bf16[272,1024]{1,0:T(8,128)(2,1)} collective-permute-done((bf16[272,1024]{1,0:T(8,128)(2,1)S(1)}, bf16[272,1024]{1,0:T(8,128)(2,1)}, u32[]{:S(2)}, u32[]{:S(2)}) %collective-permute-start.28) | collective-permute-done | bytes 557088 | tf_op jit(solution)/shard_map/ppermute | solution.py:1176
  156.6 9.6 %contrast_scores.1 = (bf16[16,256,2048]{2,1,0:T(8,128)(2,1)}, f32[1024,128]{1,0:T(8,128)S(1)}, f32[8,1024]{1,0:T(8,128)S(1)}, f32[2,256]{1,0:T(2,128)}) custom-call(s32[1]{0:T(128)} %bitcast.2.t_ref, s32[2,2]{1,0:T(2,128)S(1)} %slice.52.end_ref, s32[2,1024]{1,0:T(2,128)S(1)} %copy-done.25, s32[2,1024]{1,0:T(2,128)S(1)} %copy-done.26, ...), custom_call_target="tpu_custom_call" | custom-call | flops 85899344 | bytes 167772 | tf_op jit(solution)/shard_map/contrast_scores/pallas_call | solution.py:712
  166.4 3.0 collective-permute-done.31.rest_10_
  169.3 8.8 %contrast_grads.2 = (f32[256,1024]{1,0:T(8,128)}, bf16[2,256,1024]{2,1,0:T(8,128)(2,1)}) custom-call(s32[1]{0:T(128)} %bitcast.2.t_ref, s32[2,2]{1,0:T(2,128)S(1)} %slice.52.end_ref, s32[2,1024]{1,0:T(2,128)S(1)} %copy-done.26, f32[1024,128]{1,0:T(8,128)S(1)} %get-tuple-element.211.col, f32[8,1024]{1,0:T(8,128)S(1)} %get-tuple-element.212.own, ...), custom_call_target="tpu_custom_call" | custom-call | flops 42949672 | bytes 167772 | tf_op jit(solution)/shard_map/contrast_grads/pallas_call | solution.py:811
  180.1 6.8 %contrast_grads.3 = (f32[256,1024]{1,0:T(8,128)}, bf16[2,256,1024]{2,1,0:T(8,128)(2,1)}) custom-call(s32[1]{0:T(128)} %bitcast.2.t_ref, s32[2,2]{1,0:T(2,128)S(1)} %slice.52.end_ref, s32[2,1024]{1,0:T(2,128)S(1)} %copy-done.26, f32[1024,128]{1,0:T(8,128)S(1)} %get-tuple-element.211.col, f32[8,1024]{1,0:T(8,128)S(1)} %get-tuple-element.212.own, ...), custom_call_target="tpu_custom_call" | custom-call | flops 42949672 | bytes 167772 | tf_op jit(solution)/shard_map/contrast_grads/pallas_call | solution.py:811
  187.4 3.0 collective-permute-done.33.rest_3_.got_ref
  192.1 8.9 %down_grad.1.rest_0_ = bf16[1024,1024]{1,0:T(8,128)(2,1)} custom-call(bf16[4,2,1024,1024]{3,2,1,0:T(8,128)(2,1)} %get-tuple-element.221.a_ref.saved_ref, bf16[2,256,1024]{2,1,0:T(8,128)(2,1)S(1)} %copy-done.2, bf16[2,256,1024]{2,1,0:T(8,128)(2,1)} %get-tuple-element.219.rest_1_.own_ref, bf16[2,256,1024]{2,1,0:T(8,128)(2,1)} %copy-done.31, ...), custom_call_target="tpu_custom_call" | custom-call | flops 85899344 | bytes 167772 | tf_op jit(solution)/shard_map/down_grad/pallas_call | solution.py:872
  201.5 9.3 %feed_backward.2 = (bf16[256,1024]{1,0:T(8,128)(2,1)S(1)}, bf16[256,1024]{1,0:T(8,128)(2,1)S(1)}, bf16[256,1024]{1,0:T(8,128)(2,1)S(1)}, bf16[256,1024]{1,0:T(8,...) custom-call(bf16[2,256,1024]{2,1,0:T(8,128)(2,1)} %get-tuple-element.220.res, ...), custom_call_target="tpu_custom_call", output_to_operand_aliasing={{4}: (2, {})} | custom-call | flops 85899344 | bytes 293601 | tf_op jit(solution)/shard_map/feed_backward/pallas_call | solution.py:620
  214.2 9.5 %feed_backward.3 = (bf16[256,1024]{1,0:T(8,128)(2,1)S(1)}, bf16[256,1024]{1,0:T(8,128)(2,1)S(1)}, bf16[256,1024]{1,0:T(8,128)(2,1)S(1)}, bf16[256,1024]{1,0:T(8,...) custom-call(bf16[2,256,1024]{2,1,0:T(8,128)(2,1)} %get-tuple-element.219.res, ...), custom_call_target="tpu_custom_call", output_to_operand_aliasing={{4}: (2, {})} | custom-call | flops 85899344 | bytes 293601 | tf_op jit(solution)/shard_map/feed_backward/pallas_call | solution.py:620
  223.8 3.4 collective-permute-done.37.x_ref
  231.9 9.3 %weight_grad.1 = (bf16[512,1024]{1,0:T(8,128)(2,1)S(1)}, bf16[512,1024]{1,0:T(8,128)(2,1)}) custom-call(s32[3]{0:T(128)S(1)} %shift-right-arithmetic_and_fusion.flag.h_ref, bf16[4,2,1024,1024]{3,2,1,0:T(8,128)(2,1)} %get-tuple-element.234.s_ref), custom_call_target="tpu_custom_call" | custom-call | flops 85899344 | bytes 167772 | tf_op jit(solution)/shard_map/weight_grad/pallas_call | solution.py:930
  244.5 3.4 collective-permute-start.46
  248.9 12.5 %attend_backward.2 = (bf16[256,1024]{1,0:T(8,128)(2,1)S(1)}, bf16[256,1024]{1,0:T(8,128)(2,1)S(1)}, bf16[256,1024]{1,0:T(8,128)(2,1)S(1)}, bf16[256,1024]{1,0:T(...) custom-call(s32[1]{0:T(128)} %bitcast.2.t_ref, s32[2,1024]{1,0:T(2,128)S(1)} %copy-done.25, ...), custom_call_target="tpu_custom_call" | custom-call | flops 96636768 | bytes 167772 | tf_op jit(solution)/shard_map/attend_backward/pallas_call | solution.py:468
  265.8 8.0 %head_part.1.rest_9_.part_ref = f32[4,256,1024]{2,1,0:T(8,128)} custom-call(bf16[4,1024,2048]{2,1,0:T(8,128)(2,1)} %get-tuple-element.269.rest_4_.s_ref, bf16[4,1024,2048]{2,1,0:T(8,128)(2,1)} %get-tuple-element.250.h_ref.rest_8_), custom_call_target="tpu_custom_call" | custom-call | flops 42949672 | bytes 83886 | tf_op jit(solution)/shard_map/head_part/pallas_call | solution.py:1007
  273.8 4.3 collective-permute-done.45.rest_2_
  284.8 12.4 %attend_backward.3 = (bf16[256,1024]{1,0:T(8,128)(2,1)S(1)}, bf16[256,1024]{1,0:T(8,128)(2,1)S(1)}, bf16[256,1024]{1,0:T(8,128)(2,1)S(1)}, bf16[256,1024]{1,0:T(...) custom-call(s32[1]{0:T(128)} %bitcast.2.t_ref, ...), custom_call_target="tpu_custom_call", output_to_operand_aliasing={{4}: (10, {})} | custom-call | flops 96636768 | bytes 167772 | tf_op jit(solution)/shard_map/attend_backward/pallas_call | solution.py:468
  297.3 4.8 %collective-permute-done.52.g_ref = bf16[256,1024]{1,0:T(8,128)(2,1)S(1)} collective-permute-done((bf16[256,1024]{1,0:T(8,128)(2,1)}, bf16[256,1024]{1,0:T(8,128)(2,1)S(1)}, u32[]{:S(2)}, u32[]{:S(2)}) %collective-permute-start.52) | collective-permute-done | bytes 524320 | tf_op jit(solution)/shard_map/ppermute | solution.py:1176
  302.9 2.4 norm_backward.6
  305.5 8.0 %head_grads.1 = (bf16[512,512]{1,0:T(8,128)(2,1)S(1)}, bf16[512,512]{1,0:T(8,128)(2,1)S(1)}, bf16[512,512]{1,0:T(8,128)(2,1)S(1)}, bf16[512,512]{1,0:T(8,128)(2,1)}) custom-call(s32[3]{0:T(128)S(1)} %shift-right-arithmetic_and_fusion.flag.h_ref, bf16[4,1024,2048]{2,1,0:T(8,128)(2,1)} %get-tuple-element.269.rest_4_.s_ref, ...), custom_call_target="tpu_custom_call" | custom-call | flops 42949672 | bytes 83886 | tf_op jit(solution)/shard_map/head_grads/pallas_call | solution.py:1043
  315.0 4.8 %collective-permute-start.56 = (bf16[128,1024]{1,0:T(8,128)(2,1)S(1)}, bf16[128,1024]{1,0:T(8,128)(2,1)S(1)}, u32[]{:S(2)}, u32[]{:S(2)}) collective-permute-start(bf16[128,1024]{1,0:T(8,128)(2,1)S(1)} %get-tuple-element.264), channel_id=1, source_target_pairs={{0,16},{4,20},{8,24},{12,28},{16,0},{20,4},{24,8},{28,12},{1,17},{... | collective-permute-start | bytes 786440 | tf_op jit(solution)/shard_map/ppermute | solution.py:1176
  319.8 3.5 collective-permute-start.57
  323.3 12.3 %collective-permute-done.55.g_ref = bf16[512,512]{1,0:T(8,128)(2,1)S(1)} collective-permute-done((bf16[512,512]{1,0:T(8,128)(2,1)S(1)}, bf16[512,512]{1,0:T(8,128)(2,1)S(1)}, u32[]{:S(2)}, u32[]{:S(2)}) %collective-permute-start.55) | collective-permute-done | bytes 524320 | tf_op jit(solution)/shard_map/ppermute | solution.py:1176
  337.9 2.4 norm_backward.7
  342.5 2.5 collective-permute-start.60
  345.0 9.2 %collective-permute-done.57.g_ref = bf16[512,512]{1,0:T(8,128)(2,1)S(1)} collective-permute-done((bf16[512,512]{1,0:T(8,128)(2,1)S(1)}, bf16[512,512]{1,0:T(8,128)(2,1)S(1)}, u32[]{:S(2)}, u32[]{:S(2)}) %collective-permute-start.57) | collective-permute-done | bytes 524320 | tf_op jit(solution)/shard_map/ppermute | solution.py:1176
  355.0 4.2 collective-permute-done.59.g_ref
  366.1 3.5 collective-permute-done.61.g_ref
  370.2 5.2 %collective-permute-done.63.g_ref = bf16[128,512]{1,0:T(8,128)(2,1)S(1)} collective-permute-done((bf16[128,512]{1,0:T(8,128)(2,1)S(1)}, bf16[128,512]{1,0:T(8,128)(2,1)S(1)}, u32[]{:S(2)}, u32[]{:S(2)}) %collective-permute-start.63) | collective-permute-done | bytes 131104 | tf_op jit(solution)/shard_map/ppermute | solution.py:1176
  378.8 2.6 collective-permute-start.65
  381.8 10.6 %collective-permute-done.65.g_ref = bf16[128,512]{1,0:T(8,128)(2,1)S(1)} collective-permute-done((bf16[128,512]{1,0:T(8,128)(2,1)S(1)}, bf16[128,512]{1,0:T(8,128)(2,1)S(1)}, u32[]{:S(2)}, u32[]{:S(2)}) %collective-permute-start.65) | collective-permute-done | bytes 131104 | tf_op jit(solution)/shard_map/ppermute | solution.py:1176
  394.3 4.1 convert_element_type.167
  401.9 2.4 collective-permute-start.69
  404.3 2.4 collective-permute-done.69
  407.3 2.0 collective-permute-start.74
  410.8 2.7 join_step.13
  414.8 6.9 %collective-permute-done.74.b_ref = bf16[512,512]{1,0:T(8,128)(2,1)S(1)} collective-permute-done((bf16[512,512]{1,0:T(8,128)(2,1)S(1)}, bf16[512,512]{1,0:T(8,128)(2,1)S(1)}, u32[]{:S(2)}, u32[]{:S(2)}) %collective-permute-start.74) | collective-permute-done | bytes 524320 | tf_op jit(solution)/shard_map/ppermute | solution.py:1176
  422.9 3.0 head_outputs.1
  (302 shorter events, 96.9 us)
Async XLA Ops:
  7.2 273.4 %reduce-scatter.2.cloned.1.call-start = ((), (), s32[]{:S(2)}) async-start(), calls=%async_computation.1 | async-start | bytes 2359296 | tf_op jit(solution)/shard_map/reduce_scatter | solution.py:1358
  11.5 14.9 %collective-permute-start.1 = (bf16[256,1024]{1,0:T(8,128)(2,1)S(1)}, bf16[256,1024]{1,0:T(8,128)(2,1)S(1)}, u32[]{:S(2)}, u32[]{:S(2)}) collective-permute-start(bf16[256,1024]{1,0:T(8,128)(2,1)S(1)} %get-tuple-element.167.rest_0_), channel_id=1, source_target_pairs={{0,2},{1,3},{2,0},{3,1},{4,6},{5,7},{6,4},{7,5},{8,10},{9,11},{10,... | collective-permute-start | bytes 1572872 | tf_op jit(solution)/shard_map/ppermute | solution.py:1176
  14.5 13.7 %collective-permute-start = (bf16[256,1024]{1,0:T(8,128)(2,1)S(1)}, bf16[256,1024]{1,0:T(8,128)(2,1)S(1)}, u32[]{:S(2)}, u32[]{:S(2)}) collective-permute-start(bf16[256,1024]{1,0:T(8,128)(2,1)S(1)} %get-tuple-element.167.rest_0_), channel_id=1, source_target_pairs={{0,1},{1,0},{2,3},{3,2},{4,5},{5,4},{6,7},{7,6},{8,9},{9,8},{10,11... | collective-permute-start | bytes 1572872 | tf_op jit(solution)/shard_map/ppermute | solution.py:1176
  26.4 14.3 %collective-permute-start.3 = (bf16[256,1024]{1,0:T(8,128)(2,1)S(1)}, bf16[256,1024]{1,0:T(8,128)(2,1)S(1)}, u32[]{:S(2)}, u32[]{:S(2)}) collective-permute-start(bf16[256,1024]{1,0:T(8,128)(2,1)S(1)} %get-tuple-element.170.rest_0_), channel_id=1, source_target_pairs={{0,2},{1,3},{2,0},{3,1},{4,6},{5,7},{6,4},{7,5},{8,10},{9,11},{10,... | collective-permute-start | bytes 1572872 | tf_op jit(solution)/shard_map/ppermute | solution.py:1176
  40.8 14.5 %collective-permute-start.8 = (bf16[256,1024]{1,0:T(8,128)(2,1)S(1)}, bf16[256,1024]{1,0:T(8,128)(2,1)S(1)}, u32[]{:S(2)}, u32[]{:S(2)}) collective-permute-start(bf16[256,1024]{1,0:T(8,128)(2,1)S(1)} %get-tuple-element.182), channel_id=1, source_target_pairs={{0,1},{1,0},{2,3},{3,2},{4,5},{5,4},{6,7},{7,6},{8,9},{9,8},{10,11... | collective-permute-start | bytes 1572872 | tf_op jit(solution)/shard_map/ppermute | solution.py:1176
  42.1 14.4 %collective-permute-start.9 = (bf16[256,1024]{1,0:T(8,128)(2,1)S(1)}, bf16[256,1024]{1,0:T(8,128)(2,1)S(1)}, u32[]{:S(2)}, u32[]{:S(2)}) collective-permute-start(bf16[256,1024]{1,0:T(8,128)(2,1)S(1)} %add_convert_fusion.7), channel_id=1, source_target_pairs={{0,2},{1,3},{2,0},{3,1},{4,6},{5,7},{6,4},{7,5},{8,10},{9,11},{10,... | collective-permute-start | bytes 1572872 | tf_op jit(solution)/shard_map/ppermute | solution.py:1176
  57.5 13.6 %collective-permute-start.13 = (bf16[256,1024]{1,0:T(8,128)(2,1)S(1)}, bf16[256,1024]{1,0:T(8,128)(2,1)S(1)}, u32[]{:S(2)}, u32[]{:S(2)}) collective-permute-start(bf16[256,1024]{1,0:T(8,128)(2,1)S(1)} %get-tuple-element.185.rest_0_), channel_id=1, source_target_pairs={{0,2},{1,3},{2,0},{3,1},{4,6},{5,7},{6,4},{7,5},{8,10},{9,11},{10,... | collective-permute-start | bytes 1572872 | tf_op jit(solution)/shard_map/ppermute | solution.py:1176
  59.3 25.2 %collective-permute-start.7 = (bf16[256,1024]{1,0:T(8,128)(2,1)S(1)}, bf16[256,1024]{1,0:T(8,128)(2,1)S(1)}, u32[]{:S(2)}, u32[]{:S(2)}) collective-permute-start(bf16[256,1024]{1,0:T(8,128)(2,1)S(1)} %get-tuple-element.178), channel_id=1, source_target_pairs={{0,1},{1,0},{2,3},{3,2},{4,5},{5,4},{6,7},{7,6},{8,9},{9,8},{10,11... | collective-permute-start | bytes 1572872 | tf_op jit(solution)/shard_map/ppermute | solution.py:1176
  59.8 13.1 %collective-permute-start.12 = (bf16[256,1024]{1,0:T(8,128)(2,1)S(1)}, bf16[256,1024]{1,0:T(8,128)(2,1)S(1)}, u32[]{:S(2)}, u32[]{:S(2)}) collective-permute-start(bf16[256,1024]{1,0:T(8,128)(2,1)S(1)} %get-tuple-element.185.rest_0_), channel_id=1, source_target_pairs={{0,1},{1,0},{2,3},{3,2},{4,5},{5,4},{6,7},{7,6},{8,9},{9,8},{10,11... | collective-permute-start | bytes 1572872 | tf_op jit(solution)/shard_map/ppermute | solution.py:1176
  71.3 14.4 %collective-permute-start.11 = (bf16[256,1024]{1,0:T(8,128)(2,1)S(1)}, bf16[256,1024]{1,0:T(8,128)(2,1)S(1)}, u32[]{:S(2)}, u32[]{:S(2)}) collective-permute-start(bf16[256,1024]{1,0:T(8,128)(2,1)S(1)} %add_convert_fusion.6), channel_id=1, source_target_pairs={{0,2},{1,3},{2,0},{3,1},{4,6},{5,7},{6,4},{7,5},{8,10},{9,11},{10,... | collective-permute-start | bytes 1572872 | tf_op jit(solution)/shard_map/ppermute | solution.py:1176
  86.8 13.6 %collective-permute-start.17 = (bf16[256,1024]{1,0:T(8,128)(2,1)S(1)}, bf16[256,1024]{1,0:T(8,128)(2,1)S(1)}, u32[]{:S(2)}, u32[]{:S(2)}) collective-permute-start(bf16[256,1024]{1,0:T(8,128)(2,1)S(1)} %get-tuple-element.192.rest_0_), channel_id=1, source_target_pairs={{0,2},{1,3},{2,0},{3,1},{4,6},{5,7},{6,4},{7,5},{8,10},{9,11},{10,... | collective-permute-start | bytes 1572872 | tf_op jit(solution)/shard_map/ppermute | solution.py:1176
  88.4 14.3 %collective-permute-start.16 = (bf16[256,1024]{1,0:T(8,128)(2,1)S(1)}, bf16[256,1024]{1,0:T(8,128)(2,1)S(1)}, u32[]{:S(2)}, u32[]{:S(2)}) collective-permute-start(bf16[256,1024]{1,0:T(8,128)(2,1)S(1)} %get-tuple-element.192.rest_0_), channel_id=1, source_target_pairs={{0,1},{1,0},{2,3},{3,2},{4,5},{5,4},{6,7},{7,6},{8,9},{9,8},{10,11... | collective-permute-start | bytes 1572872 | tf_op jit(solution)/shard_map/ppermute | solution.py:1176
  100.4 14.1 %collective-permute-start.20 = (bf16[256,1024]{1,0:T(8,128)(2,1)S(1)}, bf16[256,1024]{1,0:T(8,128)(2,1)S(1)}, u32[]{:S(2)}, u32[]{:S(2)}) collective-permute-start(bf16[256,1024]{1,0:T(8,128)(2,1)S(1)} %get-tuple-element.201), channel_id=1, source_target_pairs={{0,1},{1,0},{2,3},{3,2},{4,5},{5,4},{6,7},{7,6},{8,9},{9,8},{10,11... | collective-permute-start | bytes 1572872 | tf_op jit(solution)/shard_map/ppermute | solution.py:1176
  101.1 13.9 %collective-permute-start.21 = (bf16[256,1024]{1,0:T(8,128)(2,1)S(1)}, bf16[256,1024]{1,0:T(8,128)(2,1)S(1)}, u32[]{:S(2)}, u32[]{:S(2)}) collective-permute-start(bf16[256,1024]{1,0:T(8,128)(2,1)S(1)} %add_convert_fusion.5), channel_id=1, source_target_pairs={{0,2},{1,3},{2,0},{3,1},{4,6},{5,7},{6,4},{7,5},{8,10},{9,11},{10,... | collective-permute-start | bytes 1572872 | tf_op jit(solution)/shard_map/ppermute | solution.py:1176
  116.5 14.9 %collective-permute-start.23 = (bf16[256,1024]{1,0:T(8,128)(2,1)S(1)}, bf16[256,1024]{1,0:T(8,128)(2,1)S(1)}, u32[]{:S(2)}, u32[]{:S(2)}) collective-permute-start(bf16[256,1024]{1,0:T(8,128)(2,1)S(1)} %add_convert_fusion.4), channel_id=1, source_target_pairs={{0,2},{1,3},{2,0},{3,1},{4,6},{5,7},{6,4},{7,5},{8,10},{9,11},{10,... | collective-permute-start | bytes 1572872 | tf_op jit(solution)/shard_map/ppermute | solution.py:1176
  119.1 24.3 %collective-permute-start.25 = (bf16[272,1024]{1,0:T(8,128)(2,1)S(1)}, bf16[272,1024]{1,0:T(8,128)(2,1)}, u32[]{:S(2)}, u32[]{:S(2)}) collective-permute-start(bf16[272,1024]{1,0:T(8,128)(2,1)S(1)} %get-tuple-element.204.rest_0_), channel_id=1, source_target_pairs={{0,2},{1,3},{2,0},{3,1},{4,6},{5,7},{6,4},{7,5},{8,10},{9,11},{10,... | collective-permute-start | bytes 1671176 | tf_op jit(solution)/shard_map/ppermute | solution.py:1176
  132.7 21.6 %collective-permute-start.28 = (bf16[272,1024]{1,0:T(8,128)(2,1)S(1)}, bf16[272,1024]{1,0:T(8,128)(2,1)}, u32[]{:S(2)}, u32[]{:S(2)}) collective-permute-start(bf16[272,1024]{1,0:T(8,128)(2,1)S(1)} %get-tuple-element.209.rest_4_), channel_id=1, source_target_pairs={{0,2},{1,3},{2,0},{3,1},{4,6},{5,7},{6,4},{7,5},{8,10},{9,11},{10,... | collective-permute-start | bytes 1671176 | tf_op jit(solution)/shard_map/ppermute | solution.py:1176
  134.2 21.0 %collective-permute-start.24 = (bf16[272,1024]{1,0:T(8,128)(2,1)S(1)}, bf16[272,1024]{1,0:T(8,128)(2,1)S(1)}, u32[]{:S(2)}, u32[]{:S(2)}) collective-permute-start(bf16[272,1024]{1,0:T(8,128)(2,1)S(1)} %get-tuple-element.204.rest_0_), channel_id=1, source_target_pairs={{0,1},{1,0},{2,3},{3,2},{4,5},{5,4},{6,7},{7,6},{8,9},{9,8},{10,11... | collective-permute-start | bytes 1671176 | tf_op jit(solution)/shard_map/ppermute | solution.py:1176
  143.4 13.0 %collective-permute-start.26 = (bf16[272,1024]{1,0:T(8,128)(2,1)}, bf16[272,1024]{1,0:T(8,128)(2,1)}, u32[]{:S(2)}, u32[]{:S(2)}) collective-permute-start(bf16[272,1024]{1,0:T(8,128)(2,1)} %collective-permute-done.25.rest_2_), channel_id=1, source_target_pairs={{0,1},{1,0},{2,3},{3,2},{4,5},{5,4},{6,7},{7,6},{8,9},{9,8},{10,11... | collective-permute-start | bytes 1671176 | tf_op jit(solution)/shard_map/ppermute | solution.py:1176
  143.4 13.0 %collective-permute-start.27 = (bf16[272,1024]{1,0:T(8,128)(2,1)S(1)}, bf16[272,1024]{1,0:T(8,128)(2,1)}, u32[]{:S(2)}, u32[]{:S(2)}) collective-permute-start(bf16[272,1024]{1,0:T(8,128)(2,1)S(1)} %get-tuple-element.209.rest_4_), channel_id=1, source_target_pairs={{0,1},{1,0},{2,3},{3,2},{4,5},{5,4},{6,7},{7,6},{8,9},{9,8},{10,11... | collective-permute-start | bytes 1671176 | tf_op jit(solution)/shard_map/ppermute | solution.py:1176
  154.3 15.0 %collective-permute-start.31 = (bf16[256,1024]{1,0:T(8,128)(2,1)}, bf16[256,1024]{1,0:T(8,128)(2,1)}, u32[]{:S(2)}, u32[]{:S(2)}) collective-permute-start(bf16[256,1024]{1,0:T(8,128)(2,1)} %get-tuple-element.214), channel_id=1, source_target_pairs={{0,2},{1,3},{2,0},{3,1},{4,6},{5,7},{6,4},{7,5},{8,10},{9,11},{10,... | collective-permute-start | bytes 1572872 | tf_op jit(solution)/shard_map/ppermute | solution.py:1176
  155.2 24.8 %collective-permute-start.32 = (bf16[256,1024]{1,0:T(8,128)(2,1)}, bf16[256,1024]{1,0:T(8,128)(2,1)S(1)}, u32[]{:S(2)}, u32[]{:S(2)}) collective-permute-start(bf16[256,1024]{1,0:T(8,128)(2,1)} %get-tuple-element.217), channel_id=1, source_target_pairs={{0,2},{1,3},{2,0},{3,1},{4,6},{5,7},{6,4},{7,5},{8,10},{9,11},{10,... | collective-permute-start | bytes 1572872 | tf_op jit(solution)/shard_map/ppermute | solution.py:1176
  201.0 193.3 %all-gather.2.cloned.1.call-start = ((), (), s32[]{:S(2)}) async-start(), calls=%async_computation.2 | async-start | bytes 2359296 | tf_op jit(solution)/shard_map/all_gather | solution.py:1371
  211.0 12.8 %collective-permute-start.36 = (bf16[256,1024]{1,0:T(8,128)(2,1)S(1)}, bf16[256,1024]{1,0:T(8,128)(2,1)S(1)}, u32[]{:S(2)}, u32[]{:S(2)}) collective-permute-start(bf16[256,1024]{1,0:T(8,128)(2,1)S(1)} %get-tuple-element.228), channel_id=1, source_target_pairs={{0,1},{1,0},{2,3},{3,2},{4,5},{5,4},{6,7},{7,6},{8,9},{9,8},{10,11... | collective-permute-start | bytes 1572872 | tf_op jit(solution)/shard_map/ppermute | solution.py:1176
  213.2 14.0 %collective-permute-start.37 = (bf16[256,1024]{1,0:T(8,128)(2,1)S(1)}, bf16[256,1024]{1,0:T(8,128)(2,1)S(1)}, u32[]{:S(2)}, u32[]{:S(2)}) collective-permute-start(bf16[256,1024]{1,0:T(8,128)(2,1)S(1)} %add_convert_fusion.3.rest_0_), channel_id=1, source_target_pairs={{0,2},{1,3},{2,0},{3,1},{4,6},{5,7},{6,4},{7,5},{8,10},{9,11},{10,... | collective-permute-start | bytes 1572872 | tf_op jit(solution)/shard_map/ppermute | solution.py:1176
  229.7 13.3 %collective-permute-start.40 = (bf16[256,1024]{1,0:T(8,128)(2,1)S(1)}, bf16[256,1024]{1,0:T(8,128)(2,1)}, u32[]{:S(2)}, u32[]{:S(2)}) collective-permute-start(bf16[256,1024]{1,0:T(8,128)(2,1)S(1)} %get-tuple-element.232.rest_0_), channel_id=1, source_target_pairs={{0,2},{1,3},{2,0},{3,1},{4,6},{5,7},{6,4},{7,5},{8,10},{9,11},{10,... | collective-permute-start | bytes 1572872 | tf_op jit(solution)/shard_map/ppermute | solution.py:1176
  230.7 17.2 %collective-permute-start.39 = (bf16[256,1024]{1,0:T(8,128)(2,1)S(1)}, bf16[256,1024]{1,0:T(8,128)(2,1)S(1)}, u32[]{:S(2)}, u32[]{:S(2)}) collective-permute-start(bf16[256,1024]{1,0:T(8,128)(2,1)S(1)} %get-tuple-element.232.rest_0_), channel_id=1, source_target_pairs={{0,1},{1,0},{2,3},{3,2},{4,5},{5,4},{6,7},{7,6},{8,9},{9,8},{10,11... | collective-permute-start | bytes 1572872 | tf_op jit(solution)/shard_map/ppermute | solution.py:1176
  243.0 19.1 %collective-permute-start.42 = (bf16[256,1024]{1,0:T(8,128)(2,1)S(1)}, bf16[256,1024]{1,0:T(8,128)(2,1)S(1)}, u32[]{:S(2)}, u32[]{:S(2)}) collective-permute-start(bf16[256,1024]{1,0:T(8,128)(2,1)S(1)} %get-tuple-element.243), channel_id=1, source_target_pairs={{0,1},{1,0},{2,3},{3,2},{4,5},{5,4},{6,7},{7,6},{8,9},{9,8},{10,11... | collective-permute-start | bytes 1572872 | tf_op jit(solution)/shard_map/ppermute | solution.py:1176
  243.5 18.6 %collective-permute-start.43 = (bf16[256,1024]{1,0:T(8,128)(2,1)S(1)}, bf16[256,1024]{1,0:T(8,128)(2,1)S(1)}, u32[]{:S(2)}, u32[]{:S(2)}) collective-permute-start(bf16[256,1024]{1,0:T(8,128)(2,1)S(1)} %add_convert_fusion.2), channel_id=1, source_target_pairs={{0,2},{1,3},{2,0},{3,1},{4,6},{5,7},{6,4},{7,5},{8,10},{9,11},{10,... | collective-permute-start | bytes 1572872 | tf_op jit(solution)/shard_map/ppermute | solution.py:1176
  244.5 34.4 %collective-permute-start.46 = (bf16[512,1024]{1,0:T(8,128)(2,1)S(1)}, bf16[512,1024]{1,0:T(8,128)(2,1)S(1)}, u32[]{:S(2)}, u32[]{:S(2)}) collective-permute-start(bf16[512,1024]{1,0:T(8,128)(2,1)S(1)} %get-tuple-element.237), channel_id=1, source_target_pairs={{0,4},{4,0},{8,12},{12,8},{16,20},{20,16},{24,28},{28,24},{1,5},{5... | collective-permute-start | bytes 3145736 | tf_op jit(solution)/shard_map/ppermute | solution.py:1176
  263.7 14.4 %collective-permute-start.45 = (bf16[256,1024]{1,0:T(8,128)(2,1)S(1)}, bf16[256,1024]{1,0:T(8,128)(2,1)S(1)}, u32[]{:S(2)}, u32[]{:S(2)}) collective-permute-start(bf16[256,1024]{1,0:T(8,128)(2,1)S(1)} %get-tuple-element.247.rest_0_), channel_id=1, source_target_pairs={{0,2},{1,3},{2,0},{3,1},{4,6},{5,7},{6,4},{7,5},{8,10},{9,11},{10,... | collective-permute-start | bytes 1572872 | tf_op jit(solution)/shard_map/ppermute | solution.py:1176
  281.1 21.7 %collective-permute-start.50 = (bf16[256,1024]{1,0:T(8,128)(2,1)}, bf16[256,1024]{1,0:T(8,128)(2,1)S(1)}, u32[]{:S(2)}, u32[]{:S(2)}) collective-permute-start(bf16[256,1024]{1,0:T(8,128)(2,1)} %copy-done.27), channel_id=1, source_target_pairs={{0,1},{1,0},{2,3},{3,2},{4,5},{5,4},{6,7},{7,6},{8,9},{9,8},{10,11... | collective-permute-start | bytes 1572872 | tf_op jit(solution)/shard_map/ppermute | solution.py:1176
  281.2 21.6 %collective-permute-start.51 = (bf16[256,1024]{1,0:T(8,128)(2,1)}, bf16[256,1024]{1,0:T(8,128)(2,1)S(1)}, u32[]{:S(2)}, u32[]{:S(2)}) collective-permute-start(bf16[256,1024]{1,0:T(8,128)(2,1)} %add_convert_fusion.1), channel_id=1, source_target_pairs={{0,2},{1,3},{2,0},{3,1},{4,6},{5,7},{6,4},{7,5},{8,10},{9,11},{10,... | collective-permute-start | bytes 1572872 | tf_op jit(solution)/shard_map/ppermute | solution.py:1176
  282.3 19.8 %collective-permute-start.52 = (bf16[256,1024]{1,0:T(8,128)(2,1)}, bf16[256,1024]{1,0:T(8,128)(2,1)S(1)}, u32[]{:S(2)}, u32[]{:S(2)}) collective-permute-start(bf16[256,1024]{1,0:T(8,128)(2,1)} %copy-done.28), channel_id=1, source_target_pairs={{0,8},{4,12},{8,0},{12,4},{16,24},{20,28},{24,16},{28,20},{1,9},{5... | collective-permute-start | bytes 1572872 | tf_op jit(solution)/shard_map/ppermute | solution.py:1176
  313.5 22.1 %collective-permute-start.55 = (bf16[512,512]{1,0:T(8,128)(2,1)S(1)}, bf16[512,512]{1,0:T(8,128)(2,1)S(1)}, u32[]{:S(2)}, u32[]{:S(2)}) collective-permute-start(bf16[512,512]{1,0:T(8,128)(2,1)S(1)} %get-tuple-element.271), channel_id=1, source_target_pairs={{0,4},{4,0},{8,12},{12,8},{16,20},{20,16},{24,28},{28,24},{1,5},{5... | collective-permute-start | bytes 1572872 | tf_op jit(solution)/shard_map/ppermute | solution.py:1176
  314.1 23.8 %collective-permute-start.49 = (bf16[256,1024]{1,0:T(8,128)(2,1)S(1)}, bf16[256,1024]{1,0:T(8,128)(2,1)S(1)}, u32[]{:S(2)}, u32[]{:S(2)}) collective-permute-start(bf16[256,1024]{1,0:T(8,128)(2,1)S(1)} %get-tuple-element.257), channel_id=1, source_target_pairs={{0,1},{1,0},{2,3},{3,2},{4,5},{5,4},{6,7},{7,6},{8,9},{9,8},{10,11... | collective-permute-start | bytes 1572872 | tf_op jit(solution)/shard_map/ppermute | solution.py:1176
  314.1 23.8 %collective-permute-start.54 = (bf16[256,1024]{1,0:T(8,128)(2,1)S(1)}, bf16[256,1024]{1,0:T(8,128)(2,1)S(1)}, u32[]{:S(2)}, u32[]{:S(2)}) collective-permute-start(bf16[256,1024]{1,0:T(8,128)(2,1)S(1)} %add_convert_fusion), channel_id=1, source_target_pairs={{0,2},{1,3},{2,0},{3,1},{4,6},{5,7},{6,4},{7,5},{8,10},{9,11},{10,... | collective-permute-start | bytes 1572872 | tf_op jit(solution)/shard_map/ppermute | solution.py:1176
  315.0 26.9 %collective-permute-start.56 = (bf16[128,1024]{1,0:T(8,128)(2,1)S(1)}, bf16[128,1024]{1,0:T(8,128)(2,1)S(1)}, u32[]{:S(2)}, u32[]{:S(2)}) collective-permute-start(bf16[128,1024]{1,0:T(8,128)(2,1)S(1)} %get-tuple-element.264), channel_id=1, source_target_pairs={{0,16},{4,20},{8,24},{12,28},{16,0},{20,4},{24,8},{28,12},{1,17},{... | collective-permute-start | bytes 786440 | tf_op jit(solution)/shard_map/ppermute | solution.py:1176
  319.8 34.4 %collective-permute-start.57 = (bf16[512,512]{1,0:T(8,128)(2,1)S(1)}, bf16[512,512]{1,0:T(8,128)(2,1)S(1)}, u32[]{:S(2)}, u32[]{:S(2)}) collective-permute-start(bf16[512,512]{1,0:T(8,128)(2,1)S(1)} %get-tuple-element.272), channel_id=1, source_target_pairs={{0,8},{4,12},{8,0},{12,4},{16,24},{20,28},{24,16},{28,20},{1,9},{5... | collective-permute-start | bytes 1572872 | tf_op jit(solution)/shard_map/ppermute | solution.py:1176
  336.4 22.8 %collective-permute-start.59 = (bf16[256,512]{1,0:T(8,128)(2,1)S(1)}, bf16[256,512]{1,0:T(8,128)(2,1)S(1)}, u32[]{:S(2)}, u32[]{:S(2)}) collective-permute-start(bf16[256,512]{1,0:T(8,128)(2,1)S(1)} %get-tuple-element.287), channel_id=1, source_target_pairs={{0,8},{4,12},{8,0},{12,4},{16,24},{20,28},{24,16},{28,20},{1,9},{5... | collective-permute-start | bytes 786440 | tf_op jit(solution)/shard_map/ppermute | solution.py:1176
  340.4 14.5 %collective-permute-start.58 = (f32[8,1024]{1,0:T(8,128)S(1)}, f32[8,1024]{1,0:T(8,128)S(1)}, u32[]{:S(2)}, u32[]{:S(2)}) collective-permute-start(f32[8,1024]{1,0:T(8,128)S(1)} %select_maximum_fusion), channel_id=1, source_target_pairs={{0,2},{1,3},{2,0},{3,1},{4,6},{5,7},{6,4},{7,5},{8,10},{9,11},{10,... | collective-permute-start | bytes 98312 | tf_op jit(solution)/shard_map/ppermute | solution.py:1176
  342.5 17.3 %collective-permute-start.60 = (bf16[128,1024]{1,0:T(8,128)(2,1)S(1)}, bf16[128,1024]{1,0:T(8,128)(2,1)S(1)}, u32[]{:S(2)}, u32[]{:S(2)}) collective-permute-start(bf16[128,1024]{1,0:T(8,128)(2,1)S(1)} %halve_step.12.own_ref), channel_id=1, source_target_pairs={{0,16},{4,20},{8,24},{12,28},{16,0},{20,4},{24,8},{28,12},{1,17},{... | collective-permute-start | bytes 786440 | tf_op jit(solution)/shard_map/ppermute | solution.py:1176
  360.4 16.2 %collective-permute-start.64 = (bf16[256,1024]{1,0:T(8,128)(2,1)S(1)}, bf16[256,1024]{1,0:T(8,128)(2,1)S(1)}, u32[]{:S(2)}, u32[]{:S(2)}) collective-permute-start(bf16[256,1024]{1,0:T(8,128)(2,1)S(1)} %bitcast.36), channel_id=1, source_target_pairs={{0,8},{4,12},{8,0},{12,4},{16,24},{20,28},{24,16},{28,20},{1,9},{5... | collective-permute-start | bytes 1572872 | tf_op jit(solution)/shard_map/ppermute | solution.py:1176
  377.2 33.7 %collective-permute-start.73 = (bf16[512,1024]{1,0:T(8,128)(2,1)S(1)}, bf16[512,1024]{1,0:T(8,128)(2,1)S(1)}, u32[]{:S(2)}, u32[]{:S(2)}) collective-permute-start(bf16[512,1024]{1,0:T(8,128)(2,1)S(1)} %bitcast.32), channel_id=1, source_target_pairs={{0,4},{4,0},{8,12},{12,8},{16,20},{20,16},{24,28},{28,24},{1,5},{5... | collective-permute-start | bytes 3145736 | tf_op jit(solution)/shard_map/ppermute | solution.py:1176
  378.8 13.5 %collective-permute-start.65 = (bf16[128,512]{1,0:T(8,128)(2,1)S(1)}, bf16[128,512]{1,0:T(8,128)(2,1)S(1)}, u32[]{:S(2)}, u32[]{:S(2)}) collective-permute-start(bf16[128,512]{1,0:T(8,128)(2,1)S(1)} %get-tuple-element.298), channel_id=1, source_target_pairs={{0,16},{4,20},{8,24},{12,28},{16,0},{20,4},{24,8},{28,12},{1,17},{... | collective-permute-start | bytes 393224 | tf_op jit(solution)/shard_map/ppermute | solution.py:1176
  381.5 17.0 %collective-permute-start.67 = (bf16[128,512]{1,0:T(8,128)(2,1)S(1)}, bf16[128,512]{1,0:T(8,128)(2,1)S(1)}, u32[]{:S(2)}, u32[]{:S(2)}) collective-permute-start(bf16[128,512]{1,0:T(8,128)(2,1)S(1)} %halve_step.16.own_ref), channel_id=1, source_target_pairs={{0,16},{4,20},{8,24},{12,28},{16,0},{20,4},{24,8},{28,12},{1,17},{... | collective-permute-start | bytes 393224 | tf_op jit(solution)/shard_map/ppermute | solution.py:1176
  407.3 14.4 %collective-permute-start.74 = (bf16[512,512]{1,0:T(8,128)(2,1)S(1)}, bf16[512,512]{1,0:T(8,128)(2,1)S(1)}, u32[]{:S(2)}, u32[]{:S(2)}) collective-permute-start(bf16[512,512]{1,0:T(8,128)(2,1)S(1)} %bitcast.34), channel_id=1, source_target_pairs={{0,4},{4,0},{8,12},{12,8},{16,20},{20,16},{24,28},{28,24},{1,5},{5... | collective-permute-start | bytes 1572872 | tf_op jit(solution)/shard_map/ppermute | solution.py:1176
  409.9 12.9 %collective-permute-start.75 = (bf16[512,512]{1,0:T(8,128)(2,1)S(1)}, bf16[512,512]{1,0:T(8,128)(2,1)S(1)}, u32[]{:S(2)}, u32[]{:S(2)}) collective-permute-start(bf16[512,512]{1,0:T(8,128)(2,1)S(1)} %bitcast.38), channel_id=1, source_target_pairs={{0,8},{4,12},{8,0},{12,4},{16,24},{20,28},{24,16},{28,20},{1,9},{5... | collective-permute-start | bytes 1572872 | tf_op jit(solution)/shard_map/ppermute | solution.py:1176
  (85 other events, 860.3 us)
Sparse Core Ops, SparseCore 0:
  201.1 73.2 reduce-scatter.1
  280.7 70.7 all-gather.1
